TPU v7x, 512 devices: a whole 4x8x8 slice. The times are simulated.
512 devices in a mesh: wide: 64 (over y, z_lo, core), narrow: 8 (over x, z_hi).
Axes of the slice: x: 4, y: 8, z: 8 (z_hi: 2, z_lo: 4; z = z_hi * 4 + z_lo), core: 2. Of those that a mesh axis runs over, the one named last changes fastest.
Arguments:
- tokens: bfloat16 [24576, 4096], P('wide', 'narrow'), may hold values from -6 to 6
- grad_out: bfloat16 [24576, 4096], P('wide', 'narrow'), may hold values from -6 to 6
- slot_token: int32 [16384], P('wide'), may hold values from 0 to 383, as said below
- slot_count: int32 [64], P('wide'), may hold values from 64 to 256, as said below
- slot_gate: float32 [16384], P('wide'), may hold values from 0.1 to 1
- w_gate: bfloat16 [4096, 1024], P('wide', 'narrow'), may hold values from -0.09375 to 0.09375
- w_up: bfloat16 [4096, 1024], P('wide', 'narrow'), may hold values from -0.09375 to 0.09375
- w_down: bfloat16 [4096, 1024], P('wide', 'narrow'), may hold values from -0.1875 to 0.1875
Outputs:
- mixed: bfloat16 [24576, 4096], P('wide', 'narrow')
- grad_tokens: bfloat16 [24576, 4096], P('wide', 'narrow')
- grad_gate: float32 [4096, 1024], P('wide', 'narrow')
- grad_up: float32 [4096, 1024], P('wide', 'narrow')
- grad_down: float32 [4096, 1024], P('wide', 'narrow')
Inputs may be any that keep to these rules, and one draw needn't show every extreme that they name: `slot_token`: the slots of one index of wide name distinct tokens of that index. `slot_count`: some index of wide fills all 256 slots in every draw.
All inputs are finite; a program needn't handle non-finite values.
Results may differ from a plain program's by a relative error of at most 0.017.
Values may be sent and summed in bfloat16 or wider, within the bound.
No kernel may reach another device: no remote copies, remote signals or barrier semaphores. Data moves between devices by JAX's collectives and lax.ppermute only.
A program may use at most 64 MiB of HBM per device.

v0:
```python
import jax
import jax.numpy as jnp
from jax import lax
from jax.sharding import PartitionSpec as P


def local(tokens, grad_out, slot_token, slot_count, slot_gate, w_gate, w_up, w_down):
    slot_total = slot_token.shape[0]
    f_block = w_gate.shape[1]
    cycle_size = lax.axis_size("wide")
    contract_last = (((1,), (1,)), ((), ()))
    contract_first = (((0,), (0,)), ((), ()))
    in_use = lax.iota(jnp.int32, slot_total) < slot_count[0]
    weight_use = jnp.where(in_use, slot_gate, jnp.zeros_like(slot_gate))
    local_rows = jnp.take(tokens, slot_token, axis=0)
    local_grads = (
        weight_use[:, None] * jnp.take(grad_out, slot_token, axis=0).astype(jnp.float32)
    ).astype(jnp.bfloat16)
    routed, grad_routed = (
        lax.all_gather(local_rows, "narrow", axis=1, tiled=True),
        lax.all_gather(local_grads, "narrow", axis=1, tiled=True),
    )
    joined = jnp.concatenate(
        (
            lax.all_gather(w_gate, "wide", axis=0, tiled=True),
            lax.all_gather(w_up, "wide", axis=0, tiled=True),
        ),
        axis=1,
    )
    slab = routed
    pre_both = jnp.dot(slab, joined, preferred_element_type=jnp.float32)
    pre_gate = pre_both[:, :f_block]
    pre_up = pre_both[:, f_block:]
    sigma = jax.nn.sigmoid(pre_gate)
    hidden = (pre_gate * sigma * pre_up).astype(jnp.bfloat16)
    expert_part = lax.dot_general(
        hidden,
        lax.all_gather(w_down, "wide", axis=0, tiled=True),
        contract_last,
        preferred_element_type=jnp.float32,
    )
    out_cols = lax.psum_scatter(
        expert_part.astype(jnp.bfloat16), "narrow", scatter_dimension=1, tiled=True
    ).astype(jnp.float32)
    mixed = (
        jnp.zeros((tokens.shape[0], out_cols.shape[1]), jnp.float32)
        .at[slot_token]
        .add(weight_use[:, None] * out_cols)
    )
    mixed = mixed.astype(jnp.bfloat16)
    term_down = lax.dot_general(
        grad_routed, hidden, contract_first, preferred_element_type=jnp.float32
    )
    slab = grad_routed
    grad_hidden = jnp.dot(
        slab, lax.all_gather(w_down, "wide", axis=0, tiled=True), preferred_element_type=jnp.float32
    )
    back_gate = (grad_hidden * pre_up * sigma * (1.0 + pre_gate * (1.0 - sigma))).astype(
        jnp.bfloat16
    )
    back_up = (grad_hidden * pre_gate * sigma).astype(jnp.bfloat16)
    term_gate = lax.dot_general(
        routed, back_gate, contract_first, preferred_element_type=jnp.float32
    )
    term_up = lax.dot_general(routed, back_up, contract_first, preferred_element_type=jnp.float32)
    grad_down, grad_gate, grad_up = jax.tree.map(
        lambda member: member.reshape(cycle_size, -1, member.shape[-1]).sum(axis=0),
        (
            lax.all_to_all(
                term_down.astype(jnp.bfloat16), "wide", split_axis=0, concat_axis=0, tiled=True
            ).astype(term_down.dtype),
            lax.all_to_all(
                term_gate.astype(jnp.bfloat16), "wide", split_axis=0, concat_axis=0, tiled=True
            ).astype(term_gate.dtype),
            lax.all_to_all(
                term_up.astype(jnp.bfloat16), "wide", split_axis=0, concat_axis=0, tiled=True
            ).astype(term_up.dtype),
        ),
    )
    pieces = lax.all_gather((w_gate, w_up), "wide", axis=0, tiled=True)
    first_term = lax.dot_general(
        back_gate, pieces[0], contract_last, preferred_element_type=jnp.float32
    )
    token_back = first_term + lax.dot_general(
        back_up, pieces[1], contract_last, preferred_element_type=jnp.float32
    )
    back_cols = lax.psum_scatter(
        token_back.astype(jnp.bfloat16), "narrow", scatter_dimension=1, tiled=True
    ).astype(jnp.float32)
    grad_tokens = (
        jnp.zeros((tokens.shape[0], back_cols.shape[1]), jnp.float32).at[slot_token].add(back_cols)
    )
    return (mixed, grad_tokens.astype(jnp.bfloat16), grad_gate, grad_up, grad_down)


def solution(mesh):
    in_specs = (
        P("wide", "narrow"),
        P("wide", "narrow"),
        P("wide"),
        P("wide"),
        P("wide"),
        P("wide", "narrow"),
        P("wide", "narrow"),
        P("wide", "narrow"),
    )
    out_specs = (
        P("wide", "narrow"),
        P("wide", "narrow"),
        P("wide", "narrow"),
        P("wide", "narrow"),
        P("wide", "narrow"),
    )
    return jax.shard_map(local, mesh=mesh, in_specs=in_specs, out_specs=out_specs, check_vma=False)
```

profile of v0, /device:TPU:1, one launch (start us, length us, event | category | flops | bytes accessed | tf_op | source)
XLA Modules:
  0.0 805.0 jit_solution(7973740187257303589)
XLA Ops:
  9.4 1.2 gather_fusion
  10.6 0.8 broadcast_select_fusion
  12.7 1.2 gather_fusion.1
  13.9 0.8 multiply_convert_fusion
  14.8 118.3 %all-gather.8.cloned.1.call-done = bf16[4096,128]{1,0:T(8,128)(2,1)} async-done(((bf16[64,128]{1,0:T(8,128)(2,1)}), bf16[4096,128]{1,0:T(8,128)(2,1)}) %all-gather.8.cloned.1.call-update) | async-done | bytes 1048592 | tf_op jit(solution)/shard_map/all_gather | solution.py:25
  133.1 116.7 %all-gather.10.cloned.1.call-done = bf16[4096,128]{1,0:T(8,128)(2,1)} async-done(((bf16[64,128]{1,0:T(8,128)(2,1)}), bf16[4096,128]{1,0:T(8,128)(2,1)}) %all-gather.10.cloned.1.call-update) | async-done | bytes 1048592 | tf_op jit(solution)/shard_map/all_gather | solution.py:26
  249.9 82.4 %all-gather.6.cloned.1.call-done = bf16[256,4096]{1,0:T(8,128)(2,1)} async-done(((bf16[256,512]{1,0:T(8,128)(2,1)}), bf16[256,4096]{1,0:T(8,128)(2,1)}) %all-gather.6.cloned.1.call-update) | async-done | bytes 2097168 | tf_op jit(solution)/shard_map/all_gather | solution.py:20
  332.3 2.9 fusion.1
  335.2 113.6 %all-gather.12.cloned.1.call-done = bf16[4096,128]{1,0:T(8,128)(2,1)} async-done(((bf16[64,128]{1,0:T(8,128)(2,1)}), bf16[4096,128]{1,0:T(8,128)(2,1)}) %all-gather.12.cloned.1.call-update) | async-done | bytes 1048592 | tf_op jit(solution)/shard_map/all_gather | solution.py:38
  448.7 82.3 %all-gather.14.cloned.1.call-done = bf16[256,4096]{1,0:T(8,128)(2,1)} async-done(((bf16[256,512]{1,0:T(8,128)(2,1)}), bf16[256,4096]{1,0:T(8,128)(2,1)}) %all-gather.14.cloned.1.call-update) | async-done | bytes 2097168 | tf_op jit(solution)/shard_map/all_gather | solution.py:21
  531.0 3.2 multiply_convert_fusion.1
  534.8 2.1 convolution_convert_fusion
  536.9 0.8 copy-done.7
  537.7 1.8 convolution_convert_fusion.1
  539.5 9.8 %all-to-all-start.2 = ((bf16[64,64,128]{2,1,0:T(8,128)(2,1)}), bf16[64,64,128]{2,1,0:T(8,128)(2,1)S(1)}, u32[]{:S(2)}, u32[]{:S(2)}) async-start(bf16[64,64,128]{2,1,0:T(8,128)(2,1)} %bitcast.3), calls=%async_computation.4 | async-start | bytes 2097152 | tf_op jit(solution)/shard_map/all_to_all | solution.py:69
  549.4 2.7 convolution_convert_fusion.2
  552.1 2.7 fusion.14
  554.8 28.2 %all-to-all-done.2 = bf16[64,64,128]{2,1,0:T(8,128)(2,1)S(1)} async-done(((bf16[64,64,128]{2,1,0:T(8,128)(2,1)}), bf16[64,64,128]{2,1,0:T(8,128)(2,1)S(1)}, u32[]{:S(2)}, u32[]{:S(2)}) %all-to-all-start.2) | async-done | bytes 1048608 | tf_op jit(solution)/shard_map/all_to_all | solution.py:69
  583.0 8.4 %all-to-all-start.1 = ((bf16[64,64,128]{2,1,0:T(8,128)(2,1)}), bf16[64,64,128]{2,1,0:T(8,128)(2,1)}, u32[]{:S(2)}, u32[]{:S(2)}) async-start(bf16[64,64,128]{2,1,0:T(8,128)(2,1)} %bitcast.2), calls=%async_computation.3 | async-start | bytes 2097152 | tf_op jit(solution)/shard_map/all_to_all | solution.py:75
  591.5 4.6 fusion
  596.1 2.7 convolution_convert_fusion.3
  598.8 21.7 %all-to-all-done.1 = bf16[64,64,128]{2,1,0:T(8,128)(2,1)} async-done(((bf16[64,64,128]{2,1,0:T(8,128)(2,1)}), bf16[64,64,128]{2,1,0:T(8,128)(2,1)}, u32[]{:S(2)}, u32[]{:S(2)}) %all-to-all-start.1) | async-done | bytes 1048608 | tf_op jit(solution)/shard_map/all_to_all | solution.py:75
  620.5 10.9 %all-to-all-start = ((bf16[64,64,128]{2,1,0:T(8,128)(2,1)}), bf16[64,64,128]{2,1,0:T(8,128)(2,1)S(1)}, u32[]{:S(2)}, u32[]{:S(2)}) async-start(bf16[64,64,128]{2,1,0:T(8,128)(2,1)} %bitcast.1), calls=%async_computation.2 | async-start | bytes 2097152 | tf_op jit(solution)/shard_map/all_to_all | solution.py:72
  631.5 0.8 convert_reduce_fusion
  632.2 2.0 convert_reduce_fusion.1
  634.3 25.8 %all-to-all-done = bf16[64,64,128]{2,1,0:T(8,128)(2,1)S(1)} async-done(((bf16[64,64,128]{2,1,0:T(8,128)(2,1)}), bf16[64,64,128]{2,1,0:T(8,128)(2,1)S(1)}, u32[]{:S(2)}, u32[]{:S(2)}) %all-to-all-start) | async-done | bytes 1048608 | tf_op jit(solution)/shard_map/all_to_all | solution.py:72
  660.8 31.6 %reduce-scatter.3.cloned.1.call-done = bf16[256,512]{1,0:T(8,128)(2,1)} async-done(((bf16[256,4096]{1,0:T(8,128)(2,1)}), bf16[256,512]{1,0:T(8,128)(2,1)}) %reduce-scatter.3.cloned.1.call-update) | async-done | bytes 262160 | tf_op jit(solution)/shard_map/reduce_scatter | solution.py:42
  692.4 2.8 scatter_custom_fusion
  695.2 0.8 convert_element_type.57
  696.0 98.7 %reduce-scatter.5.cloned.1.call-done = bf16[256,512]{1,0:T(8,128)(2,1)} async-done(((bf16[256,4096]{1,0:T(8,128)(2,1)}), bf16[256,512]{1,0:T(8,128)(2,1)}) %reduce-scatter.5.cloned.1.call-update) | async-done | bytes 262160 | tf_op jit(solution)/shard_map/reduce_scatter | solution.py:87
  794.6 2.7 scatter_custom_fusion.1
  797.3 0.8 convert_element_type.64
  (40 shorter events, 4.4 us)
Async XLA Ops:
  7.2 2.3 copy-start
  7.2 3.4 copy-start.9
  7.2 5.5 copy-start.2
  7.2 125.9 %all-gather.8.cloned.1.call-start = ((), (), s32[]{:S(2)}) async-start(), calls=%async_computation.6 | async-start | bytes 1064960 | tf_op jit(solution)/shard_map/all_gather | solution.py:25
  7.9 241.9 %all-gather.10.cloned.1.call-start = ((), (), s32[]{:S(2)}) async-start(), calls=%async_computation.7 | async-start | bytes 1064960 | tf_op jit(solution)/shard_map/all_gather | solution.py:26
  8.7 323.6 %all-gather.6.cloned.1.call-start = ((), (), s32[]{:S(2)}) async-start(), calls=%async_computation.5 | async-start | bytes 2359296 | tf_op jit(solution)/shard_map/all_gather | solution.py:20
  10.6 3.3 copy-start.10
  11.4 437.3 %all-gather.12.cloned.1.call-start = ((), (), s32[]{:S(2)}) async-start(), calls=%async_computation.8 | async-start | bytes 1064960 | tf_op jit(solution)/shard_map/all_gather | solution.py:38
  12.0 519.0 %all-gather.14.cloned.1.call-start = ((), (), s32[]{:S(2)}) async-start(), calls=%async_computation.10 | async-start | bytes 2359296 | tf_op jit(solution)/shard_map/all_gather | solution.py:21
  14.8 677.6 %reduce-scatter.3.cloned.1.call-start = ((), (), s32[]{:S(2)}) async-start(), calls=%async_computation.9 | async-start | bytes 2359296 | tf_op jit(solution)/shard_map/reduce_scatter | solution.py:42
  448.7 86.1 %copy-start.4 = (bf16[4096,128]{1,0:T(8,128)(2,1)S(1)}, bf16[4096,128]{1,0:T(8,128)(2,1)}, u32[]{:S(2)}) copy-start(bf16[4096,128]{1,0:T(8,128)(2,1)} %all-gather.12.cloned.1.call-done) | copy-start | bytes 3145732
  534.2 0.6 copy-start.6
  534.8 2.1 copy-start.3
  536.9 0.8 copy-start.7
  539.5 9.9 %copy-start.1 = (bf16[256,4096]{1,0:T(8,128)(2,1)S(1)}, bf16[256,4096]{1,0:T(8,128)(2,1)}, u32[]{:S(2)}) copy-start(bf16[256,4096]{1,0:T(8,128)(2,1)} %all-gather.6.cloned.1.call-done) | copy-start | bytes 6291460
  539.5 43.5 %all-to-all-start.2 = ((bf16[64,64,128]{2,1,0:T(8,128)(2,1)}), bf16[64,64,128]{2,1,0:T(8,128)(2,1)S(1)}, u32[]{:S(2)}, u32[]{:S(2)}) async-start(bf16[64,64,128]{2,1,0:T(8,128)(2,1)} %bitcast.3), calls=%async_computation.4 | async-start | bytes 2097152 | tf_op jit(solution)/shard_map/all_to_all | solution.py:69
  549.4 2.7 copy-start.5
  549.4 2.7 copy-start.8
  583.0 37.5 %all-to-all-start.1 = ((bf16[64,64,128]{2,1,0:T(8,128)(2,1)}), bf16[64,64,128]{2,1,0:T(8,128)(2,1)}, u32[]{:S(2)}, u32[]{:S(2)}) async-start(bf16[64,64,128]{2,1,0:T(8,128)(2,1)} %bitcast.2), calls=%async_computation.3 | async-start | bytes 2097152 | tf_op jit(solution)/shard_map/all_to_all | solution.py:75
  591.4 203.2 %reduce-scatter.5.cloned.1.call-start = ((), (), s32[]{:S(2)}) async-start(), calls=%async_computation.11 | async-start | bytes 2359296 | tf_op jit(solution)/shard_map/reduce_scatter | solution.py:87
  620.5 39.5 %all-to-all-start = ((bf16[64,64,128]{2,1,0:T(8,128)(2,1)}), bf16[64,64,128]{2,1,0:T(8,128)(2,1)S(1)}, u32[]{:S(2)}, u32[]{:S(2)}) async-start(bf16[64,64,128]{2,1,0:T(8,128)(2,1)} %bitcast.1), calls=%async_computation.2 | async-start | bytes 2097152 | tf_op jit(solution)/shard_map/all_to_all | solution.py:72
Sparse Core Ops, SparseCore 0:
  10.2 122.9 all-gather.7
  135.3 114.5 all-gather.9
  253.5 78.7 all-gather.5
  334.3 114.4 all-gather.11
  452.2 78.7 all-gather.13
  537.0 155.2 reduce-scatter.2
  697.7 96.8 reduce-scatter.4
where the time goes:
time: 806 us; the launch traced here: 805 us
  waiting for transfers between devices  721 us (89%)
  starting transfers between devices  29.5 us (4%)
  matrix products  22.6 us (3%)
  between operations  14.9 us (2%)
  other arithmetic  13 us (2%)
    all_gather x1, waiting for transfers between devices, local(): lax.all_gather(w_gate, 'wide', axis=0, tiled=True)  118 us
    all_gather x1, waiting for transfers between devices, local(): lax.all_gather(w_up, 'wide', axis=0, tiled=True)  117 us
    all_gather x1, waiting for transfers between devices, local(): lax.all_gather(w_down, 'wide', axis=0, tiled=True)  114 us
    reduce_scatter x1, waiting for transfers between devices, local(): lax.psum_scatter(token_back.astype(jnp.bfloat16), 'narrow', scatter_dimen...  98.7 us
    all_gather x1, waiting for transfers between devices, local(): lax.all_gather(local_rows, 'narrow', axis=1, tiled=True)  82.4 us
    all_gather x1, waiting for transfers between devices, local(): lax.all_gather(local_grads, 'narrow', axis=1, tiled=True)  82.3 us
    reduce_scatter x1, waiting for transfers between devices, local(): lax.psum_scatter(expert_part.astype(jnp.bfloat16), 'narrow', scatter_dime...  31.6 us
    all_to_all x1, waiting for transfers between devices, local(): lax.all_to_all(term_down.astype(jnp.bfloat16), 'wide', split_axis=0, conc...  28.2 us
  transfers between devices with their start and end apart: 10, of which 10 were waited for; matrix products, arithmetic and copies ran while one was open for 4% of the time, Pallas kernels for 0%

commit v1 on v0

v1 whole, which is shorter than its diff:
```python
import jax
import jax.numpy as jnp
from jax import lax
from jax.sharding import PartitionSpec as P

N_Y, N_Z, N_CORE, N_NARROW = 8, 4, 2, 8
F32, BF16 = jnp.float32, jnp.bfloat16


def wide_index(y, z, core):
    return (y * N_Z + z) * N_CORE + core


SWAP = [
    (
        wide_index(y, z, core) * N_NARROW + n,
        wide_index(core * 4 + n % 4, z, n // 4) * N_NARROW + y,
    )
    for y in range(N_Y)
    for z in range(N_Z)
    for core in range(N_CORE)
    for n in range(N_NARROW)
]
SWAP_BACK = [(b, a) for a, b in SWAP]
OTHER_CORE = [(w, w ^ 1) for w in range(N_Y * N_Z * N_CORE)]
CHIPS = [[wide_index(y, z, core) for y in range(N_Y) for z in range(N_Z)] for core in range(N_CORE)]


def dot(a, b, dims):
    return lax.dot_general(a, b, (dims, ((), ())), preferred_element_type=F32)


def spread(x, axis, groups=None):
    count = N_NARROW if groups is None else len(groups[0])
    return lax.all_to_all(
        jnp.broadcast_to(x[None], (count,) + x.shape), axis, 0, 0, axis_index_groups=groups
    )


def local(tokens, grad_out, slot_token, slot_count, slot_gate, w_gate, w_up, w_down):
    slots, tok = slot_token.shape[0], tokens.shape[0]
    feat = tokens.shape[1]
    rows, cols = w_gate.shape
    block = lax.ppermute(jnp.concatenate((w_gate, w_up, w_down), axis=0), ("wide", "narrow"), SWAP)
    pieces = spread(block, "wide", CHIPS).reshape(2, 4, N_Z, 3, rows, cols)
    weights = pieces.transpose(3, 2, 0, 4, 1, 5).reshape(3, feat, 4 * cols)
    wg, wu, wd = weights[0], weights[1], weights[2]

    weight_use = jnp.where(lax.iota(jnp.int32, slots) < slot_count[0], slot_gate, 0.0)
    pick = (slot_token[:, None] == lax.broadcasted_iota(jnp.int32, (slots, tok), 1)).astype(BF16)
    own_x = dot(pick, tokens, ((1,), (0,))).astype(BF16)
    own_g = (weight_use[:, None] * dot(pick, grad_out, ((1,), (0,)))).astype(BF16)
    other = lax.ppermute(jnp.stack((own_x, own_g)), "wide", OTHER_CORE)
    x = jnp.concatenate((own_x, other[0]), axis=0)
    g = jnp.concatenate((own_g, other[1]), axis=0)

    part = jnp.concatenate(
        (dot(x, wg, ((1,), (0,))), dot(x, wu, ((1,), (0,))), dot(g, wd, ((1,), (0,)))), axis=1
    ).astype(BF16)
    units = wg.shape[1]
    got = lax.all_to_all(part.reshape(N_NARROW, -1, 3 * units), "narrow", 0, 0)
    full = got.astype(F32).sum(axis=0)
    pre_gate, pre_up, grad_hidden = full[:, :units], full[:, units : 2 * units], full[:, 2 * units :]
    sigma = jax.nn.sigmoid(pre_gate)
    acts = jnp.concatenate(
        (
            grad_hidden * pre_up * sigma * (1.0 + pre_gate * (1.0 - sigma)),
            grad_hidden * pre_gate * sigma,
            pre_gate * sigma * pre_up,
        ),
        axis=1,
    ).astype(BF16)
    acts = spread(acts, "narrow").reshape(2 * slots, 3 * units)
    back_gate, back_up, hidden = acts[:, :units], acts[:, units : 2 * units], acts[:, 2 * units :]

    terms = jnp.stack(
        (
            dot(x, back_gate, ((0,), (0,))),
            dot(x, back_up, ((0,), (0,))),
            dot(g, hidden, ((0,), (0,))),
        )
    ).astype(BF16)
    terms = terms.reshape(3, N_Z, 2, rows, 4, cols).transpose(2, 4, 1, 0, 3, 5)
    terms = lax.all_to_all(terms.reshape(-1, 3 * rows, cols), "wide", 0, 0, axis_index_groups=CHIPS)
    grads = terms.astype(F32).sum(axis=0).astype(BF16)
    grads = lax.ppermute(grads, ("wide", "narrow"), SWAP_BACK).astype(F32)

    out = dot(hidden, wd, ((1,), (1,)))
    back = dot(back_gate, wg, ((1,), (1,))) + dot(back_up, wu, ((1,), (1,)))
    theirs = lax.ppermute(
        jnp.stack((out[slots:], back[slots:])).astype(BF16), "wide", OTHER_CORE
    ).astype(F32)
    out = (weight_use[:, None] * (out[:slots] + theirs[0])).astype(BF16)
    back = (back[:slots] + theirs[1]).astype(BF16)
    mixed = dot(pick, out, ((0,), (0,))).astype(BF16)
    grad_tokens = dot(pick, back, ((0,), (0,))).astype(BF16)
    return mixed, grad_tokens, grads[:rows], grads[rows : 2 * rows], grads[2 * rows :]


def solution(mesh):
    both = P("wide", "narrow")
    in_specs = (both, both, P("wide"), P("wide"), P("wide"), both, both, both)
    return jax.shard_map(
        local, mesh=mesh, in_specs=in_specs, out_specs=(both,) * 5, check_vma=False
    )
```

time: 806 us -> 238 us (0.30)
  the two profiles are of different devices: /device:TPU:1 before, /device:TPU:8 now
where the time goes in v1:
time: 238 us; the launch traced here: 237 us
  blocking collectives  77.4 us (33%)
  waiting for transfers between devices  75.9 us (32%)
  starting transfers between devices  55 us (23%)
  matrix products  12 us (5%)
  local copies, waits for them, and re-layouts  11.1 us (5%)
  other arithmetic  3.96 us (2%)
    all_to_all x1, blocking collectives, local(): got = lax.all_to_all(part.reshape(N_NARROW, -1, 3 * units), 'narrow', 0, 0)  52.3 us
    all_to_all x1, waiting for transfers between devices, spread(): lax.all_to_all(jnp.broadcast_to(x[None], (count,) + x.shape), axis, 0, 0,...  30.7 us
    all_to_all x1, waiting for transfers between devices, local(): lax.all_to_all(terms.reshape(-1, 3 * rows, cols), 'wide', 0, 0, axis_inde...  29 us
    all_to_all x1, blocking collectives, spread(): lax.all_to_all(jnp.broadcast_to(x[None], (count,) + x.shape), axis, 0, 0,...  25 us
    all_to_all x1, starting transfers between devices, local(): lax.all_to_all(terms.reshape(-1, 3 * rows, cols), 'wide', 0, 0, axis_inde...  20.9 us
    all_to_all x1, starting transfers between devices, spread(): lax.all_to_all(jnp.broadcast_to(x[None], (count,) + x.shape), axis, 0, 0,...  12.6 us
    dot_general x13, matrix products, dot(): return lax.dot_general(a, b, (dims, ((), ())), preferred_element_type=F32)  12 us
    ppermute x1, starting transfers between devices, local(): lax.ppermute(jnp.concatenate((w_gate, w_up, w_down), axis=0), ('wide', 'n...  10.8 us
  transfers between devices with their start and end apart: 6, of which 6 were waited for; matrix products, arithmetic and copies ran while one was open for 3% of the time, Pallas kernels for 0%

profile of v1, /device:TPU:8, one launch (start us, length us, event | category | flops | bytes accessed | tf_op | source)
XLA Modules:
  0.0 237.0 jit_solution(2015090380357692240)
XLA Ops:
  0.6 0.8 pad_maximum_fusion.7
  1.5 10.8 %collective-permute-start.1 = (bf16[192,128]{1,0:T(8,128)(2,1)S(1)}, bf16[192,128]{1,0:T(8,128)(2,1)S(1)}, u32[]{:S(2)}, u32[]{:S(2)}) collective-permute-start(bf16[192,128]{1,0:T(8,128)(2,1)S(1)} %pad_maximum_fusion.7), channel_id=1, source_target_pairs={{0,0},{1,64},{2,128},{3,192},{4,8},{5,72},{6,136},{7,200},{8,256},... | collective-permute-start | bytes 147464 | tf_op jit(solution)/shard_map/ppermute | solution.py:44
  12.2 2.6 %collective-permute-done.1 = bf16[192,128]{1,0:T(8,128)(2,1)S(1)} collective-permute-done((bf16[192,128]{1,0:T(8,128)(2,1)S(1)}, bf16[192,128]{1,0:T(8,128)(2,1)S(1)}, u32[]{:S(2)}, u32[]{:S(2)}) %collective-permute-start.1) | collective-permute-done | bytes 49184 | tf_op jit(solution)/shard_map/ppermute | solution.py:44
  14.8 1.5 broadcast_in_dim.9
  16.3 12.6 %all-to-all-start = ((bf16[32,192,128]{2,1,0:T(8,128)(2,1)}), bf16[32,192,128]{2,1,0:T(8,128)(2,1)S(1)}, u32[]{:S(2)}, u32[]{:S(2)}) async-start(bf16[32,192,128]{2,1,0:T(8,128)(2,1)} %broadcast_in_dim.9), calls=%async_computation | async-start | bytes 3145728 | tf_op jit(solution)/shard_map/all_to_all | solution.py:35
  30.4 3.3 %collective-permute-start = (bf16[2,256,512]{2,1,0:T(8,128)(2,1)S(1)}, bf16[2,256,512]{2,1,0:T(8,128)(2,1)S(1)}, u32[]{:S(2)}, u32[]{:S(2)}) collective-permute-start(bf16[2,256,512]{2,1,0:T(8,128)(2,1)S(1)} %pad_maximum_fusion.2), channel_id=1, source_target_pairs={{0,8},{8,0},{16,24},{24,16},{32,40},{40,32},{48,56},{56,48},{64,72... | collective-permute-start | bytes 1572872 | tf_op jit(solution)/shard_map/ppermute | solution.py:53
  33.7 1.5 collective-permute-done
  35.2 1.0 pad_maximum_fusion.3
  36.2 30.7 %all-to-all-done = bf16[32,192,128]{2,1,0:T(8,128)(2,1)S(1)} async-done(((bf16[32,192,128]{2,1,0:T(8,128)(2,1)}), bf16[32,192,128]{2,1,0:T(8,128)(2,1)S(1)}, u32[]{:S(2)}, u32[]{:S(2)}) %all-to-all-start) | async-done | bytes 1572896 | tf_op jit(solution)/shard_map/all_to_all | solution.py:35
  66.9 0.9 fusion.29
  68.9 1.5 copy.14
  70.4 1.0 reshape.72
  71.4 1.0 reshape.71
  72.4 1.6 convolution_convert_fusion.4
  75.0 52.3 %all_to_all.20 = bf16[8,64,1536]{2,1,0:T(8,128)(2,1)S(1)} all-to-all(bf16[8,64,1536]{2,1,0:T(8,128)(2,1)S(1)} %pad_maximum_fusion), channel_id=1, replica_groups=mesh['wide'=64,'narrow'=8] {'narrow'}, dimensions={0} | all-to-all | bytes 3145728 | tf_op jit(solution)/shard_map/all_to_all | solution.py:61
  127.8 25.0 %all_to_all.21 = bf16[8,64,1536]{2,1,0:T(8,128)(2,1)S(1)} all-to-all(bf16[8,64,1536]{2,1,0:T(8,128)(2,1)S(1)} %broadcast_in_dim.10), channel_id=1, replica_groups=mesh['wide'=64,'narrow'=8] {'narrow'}, dimensions={0} | all-to-all | bytes 3145728 | tf_op jit(solution)/shard_map/all_to_all | solution.py:35
  152.8 1.3 convolution_convert_fusion
  154.6 1.2 convolution_convert_fusion.2
  155.8 1.2 stack.41
  157.4 1.2 stack.39
  158.7 1.3 pad_maximum_fusion.1
  160.0 20.9 %all-to-all-start.3 = ((bf16[32,192,128]{2,1,0:T(8,128)(2,1)}), bf16[32,192,128]{2,1,0:T(8,128)(2,1)S(1)}, u32[]{:S(2)}, u32[]{:S(2)}) async-start(bf16[32,192,128]{2,1,0:T(8,128)(2,1)} %bitcast.16), calls=%async_computation.3 | async-start | bytes 3145728 | tf_op jit(solution)/shard_map/all_to_all | solution.py:84
  180.9 1.6 fusion.3
  183.0 0.5 copy-done.2
  184.1 1.9 collective-permute-start.2
  186.0 1.9 collective-permute-done.2
  188.0 1.2 convolution_convert_fusion.7
  189.2 29.0 %all-to-all-done.3 = bf16[32,192,128]{2,1,0:T(8,128)(2,1)S(1)} async-done(((bf16[32,192,128]{2,1,0:T(8,128)(2,1)}), bf16[32,192,128]{2,1,0:T(8,128)(2,1)S(1)}, u32[]{:S(2)}, u32[]{:S(2)}) %all-to-all-start.3) | async-done | bytes 1572896 | tf_op jit(solution)/shard_map/all_to_all | solution.py:84
  218.4 5.5 %collective-permute-start.3 = (bf16[192,128]{1,0:T(8,128)(2,1)S(1)}, bf16[192,128]{1,0:T(8,128)(2,1)S(1)}, u32[]{:S(2)}, u32[]{:S(2)}) collective-permute-start(bf16[192,128]{1,0:T(8,128)(2,1)S(1)} %reduce_sum.22), channel_id=1, source_target_pairs={{0,0},{64,1},{128,2},{192,3},{8,4},{72,5},{136,6},{200,7},{256,8},... | collective-permute-start | bytes 147464 | tf_op jit(solution)/shard_map/ppermute | solution.py:86
  224.0 2.2 convolution_convert_fusion.6
  226.1 10.2 %collective-permute-done.3 = bf16[192,128]{1,0:T(8,128)(2,1)S(1)} collective-permute-done((bf16[192,128]{1,0:T(8,128)(2,1)S(1)}, bf16[192,128]{1,0:T(8,128)(2,1)S(1)}, u32[]{:S(2)}, u32[]{:S(2)}) %collective-permute-start.3) | collective-permute-done | bytes 49184 | tf_op jit(solution)/shard_map/ppermute | solution.py:86
  236.3 0.6 fusion.30
  (58 shorter events, 5.6 us)
Async XLA Ops:
  0.6 28.9 %copy-start = (bf16[384,512]{1,0:T(8,128)(2,1)S(1)}, bf16[384,512]{1,0:T(8,128)(2,1)}, u32[]{:S(2)}) copy-start(bf16[384,512]{1,0:T(8,128)(2,1)} %param.8) | copy-start | bytes 1179652
  1.5 13.4 %collective-permute-start.1 = (bf16[192,128]{1,0:T(8,128)(2,1)S(1)}, bf16[192,128]{1,0:T(8,128)(2,1)S(1)}, u32[]{:S(2)}, u32[]{:S(2)}) collective-permute-start(bf16[192,128]{1,0:T(8,128)(2,1)S(1)} %pad_maximum_fusion.7), channel_id=1, source_target_pairs={{0,0},{1,64},{2,128},{3,192},{4,8},{5,72},{6,136},{7,200},{8,256},... | collective-permute-start | bytes 147464 | tf_op jit(solution)/shard_map/ppermute | solution.py:44
  16.3 13.2 %copy-start.14 = (f32[256]{0:T(256)S(1)}, f32[256]{0:T(256)}, u32[]{:S(2)}) copy-start(f32[256]{0:T(256)} %param.12) | copy-start | bytes 3076
  16.3 13.3 %copy-start.13 = (s32[256]{0:T(256)S(1)}, s32[256]{0:T(256)}, u32[]{:S(2)}) copy-start(s32[256]{0:T(256)} %param.10) | copy-start | bytes 3076
  16.3 13.6 %copy-start.15 = (bf16[384,512]{1,0:T(8,128)(2,1)S(1)}, bf16[384,512]{1,0:T(8,128)(2,1)}, u32[]{:S(2)}) copy-start(bf16[384,512]{1,0:T(8,128)(2,1)} %param.9) | copy-start | bytes 1179652
  16.3 50.6 %all-to-all-start = ((bf16[32,192,128]{2,1,0:T(8,128)(2,1)}), bf16[32,192,128]{2,1,0:T(8,128)(2,1)S(1)}, u32[]{:S(2)}, u32[]{:S(2)}) async-start(bf16[32,192,128]{2,1,0:T(8,128)(2,1)} %broadcast_in_dim.9), calls=%async_computation | async-start | bytes 3145728 | tf_op jit(solution)/shard_map/all_to_all | solution.py:35
  30.4 4.8 %collective-permute-start = (bf16[2,256,512]{2,1,0:T(8,128)(2,1)S(1)}, bf16[2,256,512]{2,1,0:T(8,128)(2,1)S(1)}, u32[]{:S(2)}, u32[]{:S(2)}) collective-permute-start(bf16[2,256,512]{2,1,0:T(8,128)(2,1)S(1)} %pad_maximum_fusion.2), channel_id=1, source_target_pairs={{0,8},{8,0},{16,24},{24,16},{32,40},{40,32},{48,56},{56,48},{64,72... | collective-permute-start | bytes 1572872 | tf_op jit(solution)/shard_map/ppermute | solution.py:53
  35.2 32.6 %copy-start.9 = (bf16[256,512]{1,0:T(8,128)(2,1)}, bf16[256,512]{1,0:T(8,128)(2,1)S(1)}, u32[]{:S(2)}) copy-start(bf16[256,512]{1,0:T(8,128)(2,1)S(1)} %get-tuple-element.8) | copy-start | bytes 786436
  35.2 32.6 %copy-start.11 = (bf16[256,512]{1,0:T(8,128)(2,1)}, bf16[256,512]{1,0:T(8,128)(2,1)S(1)}, u32[]{:S(2)}) copy-start(bf16[256,512]{1,0:T(8,128)(2,1)S(1)} %get-tuple-element.9) | copy-start | bytes 786436
  68.3 3.1 %copy-start.3 = (bf16[1,4,2,64,4,128]{5,4,3,2,1,0:T(4,128)(2,1)}, bf16[1,4,2,64,4,128]{5,4,3,2,1,0:T(4,128)(2,1)S(1)}, u32[]{:S(2)}) copy-start(bf16[1,4,2,64,4,128]{5,4,3,2,1,0:T(4,128)(2,1)S(1)} %copy.13) | copy-start | bytes 1572868
  68.7 2.7 %copy-start.1 = (bf16[1,4,2,64,4,128]{5,4,3,2,1,0:T(4,128)(2,1)}, bf16[1,4,2,64,4,128]{5,4,3,2,1,0:T(4,128)(2,1)S(1)}, u32[]{:S(2)}) copy-start(bf16[1,4,2,64,4,128]{5,4,3,2,1,0:T(4,128)(2,1)S(1)} %copy.15) | copy-start | bytes 1572868
  70.4 3.6 %copy-start.4 = (bf16[1,4,2,64,4,128]{5,4,3,2,1,0:T(4,128)(2,1)}, bf16[1,4,2,64,4,128]{5,4,3,2,1,0:T(4,128)(2,1)S(1)}, u32[]{:S(2)}) copy-start(bf16[1,4,2,64,4,128]{5,4,3,2,1,0:T(4,128)(2,1)S(1)} %copy.14) | copy-start | bytes 1572868
  72.4 1.6 copy-start.7
  72.4 2.0 copy-start.8
  127.8 25.1 %copy-start.12 = (bf16[256,512]{1,0:T(8,128)(2,1)S(1)}, bf16[256,512]{1,0:T(8,128)(2,1)}, u32[]{:S(2)}) copy-start(bf16[256,512]{1,0:T(8,128)(2,1)} %copy-done.11) | copy-start | bytes 786436
  152.8 1.3 copy-start.10
  160.0 58.2 %all-to-all-start.3 = ((bf16[32,192,128]{2,1,0:T(8,128)(2,1)}), bf16[32,192,128]{2,1,0:T(8,128)(2,1)S(1)}, u32[]{:S(2)}, u32[]{:S(2)}) async-start(bf16[32,192,128]{2,1,0:T(8,128)(2,1)} %bitcast.16), calls=%async_computation.3 | async-start | bytes 3145728 | tf_op jit(solution)/shard_map/all_to_all | solution.py:84
  180.9 1.6 copy-start.5
  182.5 1.0 copy-start.2
  182.9 1.1 copy-start.6
  184.1 3.8 %collective-permute-start.2 = (bf16[2,256,512]{2,1,0:T(8,128)(2,1)S(1)}, bf16[2,256,512]{2,1,0:T(8,128)(2,1)S(1)}, u32[]{:S(2)}, u32[]{:S(2)}) collective-permute-start(bf16[2,256,512]{2,1,0:T(8,128)(2,1)S(1)} %pad_maximum_fusion.5), channel_id=1, source_target_pairs={{0,8},{8,0},{16,24},{24,16},{32,40},{40,32},{48,56},{56,48},{64,72... | collective-permute-start | bytes 1572872 | tf_op jit(solution)/shard_map/ppermute | solution.py:90
  218.4 17.9 %collective-permute-start.3 = (bf16[192,128]{1,0:T(8,128)(2,1)S(1)}, bf16[192,128]{1,0:T(8,128)(2,1)S(1)}, u32[]{:S(2)}, u32[]{:S(2)}) collective-permute-start(bf16[192,128]{1,0:T(8,128)(2,1)S(1)} %reduce_sum.22), channel_id=1, source_target_pairs={{0,0},{64,1},{128,2},{192,3},{8,4},{72,5},{136,6},{200,7},{256,8},... | collective-permute-start | bytes 147464 | tf_op jit(solution)/shard_map/ppermute | solution.py:86

commit v2 on v1

v2 whole, which is shorter than its diff:
```python
import jax
import jax.numpy as jnp
from jax import lax
from jax.sharding import PartitionSpec as P

N_Y, N_Z, N_CORE, N_X = 8, 4, 2, 4
N_WIDE, N_NARROW = N_Y * N_Z * N_CORE, 2 * N_X
F32, BF16 = jnp.float32, jnp.bfloat16


def wide_index(y, z, core):
    return (y * N_Z + z) * N_CORE + core


def swap_pairs():
    pairs = []
    for y in range(N_Y):
        for z in range(N_Z):
            for core in range(N_CORE):
                for n in range(N_NARROW):
                    z_bit, to_core, half = n // 4, n // 2 % 2, n % 2
                    to = wide_index(half * 4 + z % 2 * 2 + core, z // 2 * 2 + z_bit, to_core)
                    pairs.append((wide_index(y, z, core) * N_NARROW + n, to * N_NARROW + y))
    return pairs


SWAP = swap_pairs()
SWAP_BACK = [(b, a) for a, b in SWAP]
OTHER_CORE = [(w, w ^ 1) for w in range(N_WIDE)]
OTHER_CHIP = [(w, w ^ 2) for w in range(N_WIDE)]
OTHER_HALF = [(n, n ^ 1) for n in range(N_NARROW)]
OWNERS = [
    [wide_index(y, 2 * pair + z_bit, core) for y in range(N_Y) for pair in range(2)]
    for z_bit in range(2)
    for core in range(N_CORE)
]
ALONG_X = [[2 * x + z_hi for x in range(N_X)] for z_hi in range(2)]


def dot(a, b, dims):
    return lax.dot_general(a, b, (dims, ((), ())), preferred_element_type=F32)


def exchange(x, axis, groups):
    return lax.all_to_all(x, axis, 0, 0, axis_index_groups=groups)


def spread(x, axis, groups):
    return exchange(jnp.broadcast_to(x[None], (len(groups[0]),) + x.shape), axis, groups)


def local(tokens, grad_out, slot_token, slot_count, slot_gate, w_gate, w_up, w_down):
    slots, tok = slot_token.shape[0], tokens.shape[0]
    feat = tokens.shape[1]
    rows, cols = w_gate.shape
    half = slots // 2
    z_hi = lax.axis_index("narrow") % 2

    def mine_first(a):
        return jnp.where(z_hi == 0, a, jnp.concatenate((a[half:], a[:half])))

    block = lax.ppermute(jnp.concatenate((w_gate, w_up, w_down), axis=0), ("wide", "narrow"), SWAP)
    pieces = spread(block, "wide", OWNERS).reshape(2, 2, 2, 2, 3, rows, cols)
    weights = pieces.transpose(4, 3, 1, 2, 5, 0, 6).reshape(3, feat, 2 * cols)
    wg, wu, wd = weights[0], weights[1], weights[2]

    weight_use = jnp.where(lax.iota(jnp.int32, slots) < slot_count[0], slot_gate, 0.0)
    weight_use, slot_token = mine_first(weight_use), mine_first(slot_token)
    pick = (slot_token[:, None] == lax.broadcasted_iota(jnp.int32, (slots, tok), 1)).astype(BF16)
    own_x = dot(pick, tokens, ((1,), (0,))).astype(BF16)
    own_g = (weight_use[:, None] * dot(pick, grad_out, ((1,), (0,)))).astype(BF16)
    own = jnp.stack((own_x, own_g))
    chip = jnp.concatenate((own, lax.ppermute(own, "wide", OTHER_CHIP)), axis=1)
    all_rows = jnp.concatenate((chip, lax.ppermute(chip, "wide", OTHER_CORE)), axis=1)
    x, g = all_rows[0], all_rows[1]

    part = jnp.concatenate(
        (dot(x, wg, ((1,), (0,))), dot(x, wu, ((1,), (0,))), dot(g, wd, ((1,), (0,)))), axis=1
    ).astype(BF16)
    units = wg.shape[1]
    got = exchange(part.reshape(N_X, slots, 3 * units), "narrow", ALONG_X)
    part = got.astype(F32).sum(axis=0)
    theirs = lax.ppermute(part[half:].astype(BF16), "narrow", OTHER_HALF)
    full = part[:half] + theirs.astype(F32)
    pre_gate, pre_up, grad_hidden = full[:, :units], full[:, units : 2 * units], full[:, 2 * units :]
    sigma = jax.nn.sigmoid(pre_gate)
    acts = jnp.concatenate(
        (
            grad_hidden * pre_up * sigma * (1.0 + pre_gate * (1.0 - sigma)),
            grad_hidden * pre_gate * sigma,
            pre_gate * sigma * pre_up,
        ),
        axis=1,
    ).astype(BF16)
    acts = jnp.concatenate((acts, lax.ppermute(acts, "narrow", OTHER_HALF)))
    acts = spread(acts, "narrow", ALONG_X).reshape(N_X * slots, 3 * units)
    back_gate, back_up, hidden = acts[:, :units], acts[:, units : 2 * units], acts[:, 2 * units :]

    terms = jnp.stack(
        (
            dot(x, back_gate, ((0,), (0,))),
            dot(x, back_up, ((0,), (0,))),
            dot(g, hidden, ((0,), (0,))),
        )
    ).astype(BF16)
    terms = terms.reshape(3, 2, 2, 2, rows, 2, cols).transpose(5, 2, 3, 1, 0, 4, 6)
    terms = exchange(terms.reshape(-1, 3 * rows, cols), "wide", OWNERS)
    grads = terms.astype(F32).sum(axis=0).astype(BF16)
    grads = lax.ppermute(grads, ("wide", "narrow"), SWAP_BACK).astype(F32)

    outs = jnp.stack(
        (
            dot(hidden, wd, ((1,), (1,))),
            dot(back_gate, wg, ((1,), (1,))) + dot(back_up, wu, ((1,), (1,))),
        )
    )
    theirs = lax.ppermute(outs[:, 2 * slots :].astype(BF16), "wide", OTHER_CORE)
    outs = outs[:, : 2 * slots] + theirs.astype(F32)
    theirs = lax.ppermute(outs[:, slots:].astype(BF16), "wide", OTHER_CHIP)
    outs = outs[:, :slots] + theirs.astype(F32)
    out = (weight_use[:, None] * outs[0]).astype(BF16)
    mixed = dot(pick, out, ((0,), (0,))).astype(BF16)
    grad_tokens = dot(pick, outs[1].astype(BF16), ((0,), (0,))).astype(BF16)
    return mixed, grad_tokens, grads[:rows], grads[rows : 2 * rows], grads[2 * rows :]


def solution(mesh):
    both = P("wide", "narrow")
    in_specs = (both, both, P("wide"), P("wide"), P("wide"), both, both, both)
    return jax.shard_map(
        local, mesh=mesh, in_specs=in_specs, out_specs=(both,) * 5, check_vma=False
    )
```

time: 238 us -> 216 us (0.908)
  the two profiles are of different devices: /device:TPU:8 before, /device:TPU:40 now
where the time goes in v2:
time: 216 us; the launch traced here: 215 us
  waiting for transfers between devices  76.5 us (35%)
  starting transfers between devices  69.3 us (32%)
  blocking collectives  23.7 us (11%)
  local copies, waits for them, and re-layouts  18.4 us (9%)
  matrix products  15.5 us (7%)
  other arithmetic  9.51 us (4%)
    all_to_all x3, waiting for transfers between devices, exchange(): return lax.all_to_all(x, axis, 0, 0, axis_index_groups=groups)  33 us
    all_to_all x3, starting transfers between devices, exchange(): return lax.all_to_all(x, axis, 0, 0, axis_index_groups=groups)  27 us
    all_to_all x1, blocking collectives, exchange(): return lax.all_to_all(x, axis, 0, 0, axis_index_groups=groups)  23.7 us
    ppermute x1, waiting for transfers between devices, local(): chip = jnp.concatenate((own, lax.ppermute(own, 'wide', OTHER_CHIP)), axis=1)  18.5 us
    dot_general x13, matrix products, dot(): return lax.dot_general(a, b, (dims, ((), ())), preferred_element_type=F32)  15.5 us
    ppermute x1, starting transfers between devices, local(): lax.ppermute(jnp.concatenate((w_gate, w_up, w_down), axis=0), ('wide', 'n...  12.8 us
    ppermute x1, waiting for transfers between devices, local(): grads = lax.ppermute(grads, ('wide', 'narrow'), SWAP_BACK).astype(F32)  12.5 us
    dot_general x7, local copies, waits for them, and re-layouts, dot(): return lax.dot_general(a, b, (dims, ((), ())), preferred_element_type=F32)  9.08 us
  transfers between devices with their start and end apart: 11, of which 7 were waited for; matrix products, arithmetic and copies ran while one was open for 6% of the time, Pallas kernels for 0%

profile of v2, /device:TPU:40, one launch (start us, length us, event | category | flops | bytes accessed | tf_op | source)
XLA Modules:
  0.0 214.8 jit_solution(5077901080084499467)
XLA Ops:
  1.5 12.8 %collective-permute-start.2 = (bf16[192,128]{1,0:T(8,128)(2,1)S(1)}, bf16[192,128]{1,0:T(8,128)(2,1)S(1)}, u32[]{:S(2)}, u32[]{:S(2)}) collective-permute-start(bf16[192,128]{1,0:T(8,128)(2,1)S(1)} %pad_maximum_fusion.7), channel_id=1, source_target_pairs={{0,0},{1,256},{2,8},{3,264},{4,16},{5,272},{6,24},{7,280},{8,64},{... | collective-permute-start | bytes 147464 | tf_op jit(solution)/shard_map/ppermute | solution.py:62
  18.1 1.3 fusion.5
  20.5 8.1 %all-to-all-start = ((bf16[16,192,128]{2,1,0:T(8,128)(2,1)}), bf16[16,192,128]{2,1,0:T(8,128)(2,1)S(1)}, u32[]{:S(2)}, u32[]{:S(2)}) async-start(bf16[16,192,128]{2,1,0:T(8,128)(2,1)} %broadcast_in_dim.9), calls=%async_computation | async-start | bytes 1572864 | tf_op jit(solution)/shard_map/all_to_all | solution.py:45
  28.7 5.1 %collective-permute-start = (bf16[2,256,512]{2,1,0:T(8,128)(2,1)S(1)}, bf16[2,256,512]{2,1,0:T(8,128)(2,1)S(1)}, u32[]{:S(2)}, u32[]{:S(2)}) collective-permute-start(bf16[2,256,512]{2,1,0:T(8,128)(2,1)S(1)} %pad_maximum_fusion.4), channel_id=1, source_target_pairs={{0,16},{8,24},{16,0},{24,8},{32,48},{40,56},{48,32},{56,40},{64,80... | collective-permute-start | bytes 1572872 | tf_op jit(solution)/shard_map/ppermute | solution.py:73
  33.8 18.5 %collective-permute-done = bf16[2,256,512]{2,1,0:T(8,128)(2,1)S(1)} collective-permute-done((bf16[2,256,512]{2,1,0:T(8,128)(2,1)S(1)}, bf16[2,256,512]{2,1,0:T(8,128)(2,1)S(1)}, u32[]{:S(2)}, u32[]{:S(2)}) %collective-permute-start) | collective-permute-done | bytes 524320 | tf_op jit(solution)/shard_map/ppermute | solution.py:73
  52.3 1.9 collective-permute-start.1
  55.2 1.8 collective-permute-done.1
  57.0 1.4 pad_maximum_fusion.1
  61.2 23.7 %all_to_all.20 = bf16[4,256,768]{1,2,0:T(8,128)(2,1)S(1)} all-to-all(bf16[4,256,768]{1,2,0:T(8,128)(2,1)S(1)} %pad_maximum_fusion.2), channel_id=1, replica_groups={{0,2,4,6},{1,3,5,7},{8,10,12,14},{9,11,13,15},{16,18,20,22},{17,19,21,2..., dimensions={0} | all-to-all | bytes 3145728 | tf_op jit(solution)/shard_map/all_to_all | solution.py:45
  85.3 6.9 %collective-permute-start.3 = (bf16[128,768]{0,1:T(8,128)(2,1)S(1)}, bf16[128,768]{0,1:T(8,128)(2,1)S(1)}, u32[]{:S(2)}, u32[]{:S(2)}) collective-permute-start(bf16[128,768]{0,1:T(8,128)(2,1)S(1)} %slice.174), channel_id=1, source_target_pairs={{0,1},{1,0},{2,3},{3,2},{4,5},{5,4},{6,7},{7,6},{8,9},{9,8},{10,11... | collective-permute-start | bytes 589832 | tf_op jit(solution)/shard_map/ppermute | solution.py:83
  92.2 5.3 %collective-permute-done.3 = bf16[128,768]{0,1:T(8,128)(2,1)S(1)} collective-permute-done((bf16[128,768]{0,1:T(8,128)(2,1)S(1)}, bf16[128,768]{0,1:T(8,128)(2,1)S(1)}, u32[]{:S(2)}, u32[]{:S(2)}) %collective-permute-start.3) | collective-permute-done | bytes 196640 | tf_op jit(solution)/shard_map/ppermute | solution.py:83
  97.7 6.2 %collective-permute-start.4 = (bf16[128,768]{0,1:T(8,128)(2,1)S(1)}, bf16[128,768]{0,1:T(8,128)(2,1)S(1)}, u32[]{:S(2)}, u32[]{:S(2)}) collective-permute-start(bf16[128,768]{0,1:T(8,128)(2,1)S(1)} %pad_maximum_fusion.6), channel_id=1, source_target_pairs={{0,1},{1,0},{2,3},{3,2},{4,5},{5,4},{6,7},{7,6},{8,9},{9,8},{10,11... | collective-permute-start | bytes 589832 | tf_op jit(solution)/shard_map/ppermute | solution.py:95
  103.8 5.4 %collective-permute-done.4 = bf16[128,768]{0,1:T(8,128)(2,1)S(1)} collective-permute-done((bf16[128,768]{0,1:T(8,128)(2,1)S(1)}, bf16[128,768]{0,1:T(8,128)(2,1)S(1)}, u32[]{:S(2)}, u32[]{:S(2)}) %collective-permute-start.4) | collective-permute-done | bytes 196640 | tf_op jit(solution)/shard_map/ppermute | solution.py:95
  110.6 3.6 %all-to-all-start.2 = ((bf16[4,256,768]{1,2,0:T(8,128)(2,1)}), bf16[4,256,768]{1,2,0:T(8,128)(2,1)S(1)}, u32[]{:S(2)}, u32[]{:S(2)}) async-start(bf16[4,256,768]{1,2,0:T(8,128)(2,1)} %broadcast_in_dim.10), calls=%async_computation.2 | async-start | bytes 3145728 | tf_op jit(solution)/shard_map/all_to_all | solution.py:45
  114.2 2.3 %copy.41 = bf16[512,1024]{1,0:T(8,128)(2,1)} copy(bf16[512,1024]{0,1:T(8,128)(2,1)} %get-tuple-element.5) | data formatting | bytes 2097152 | tf_op jit(solution)/shard_map/dot_general | solution.py:41
  116.5 1.3 copy.44
  117.8 15.6 %all-to-all-done.2 = bf16[4,256,768]{1,2,0:T(8,128)(2,1)S(1)} async-done(((bf16[4,256,768]{1,2,0:T(8,128)(2,1)}), bf16[4,256,768]{1,2,0:T(8,128)(2,1)S(1)}, u32[]{:S(2)}, u32[]{:S(2)}) %all-to-all-start.2) | async-done | bytes 1572896 | tf_op jit(solution)/shard_map/all_to_all | solution.py:45
  136.2 1.6 convolution_bitcast_fusion
  137.7 2.9 %fusion.12 = f32[1024,512]{1,0:T(8,128)} fusion(bf16[1024,768]{1,0:T(8,128)(2,1)} %bitcast.118, bf16[64,8,2,128]{3,2,1,0:T(2,128)(2,1)S(1)} %bitcast.128), kind=kOutput, calls=%fused_computation.39 | convolution fusion | flops 268435456 | bytes 2883584 | tf_op jit(solution)/shard_map/dot_general | solution.py:41
  140.6 2.1 copy.42
  143.9 2.0 fusion.6
  145.9 1.7 fusion.7
  147.6 1.5 add_bitcast_fusion
  150.8 1.9 collective-permute-start.5
  154.3 15.3 %all-to-all-start.3 = ((bf16[16,192,128]{2,1,0:T(8,128)(2,1)}), bf16[16,192,128]{2,1,0:T(8,128)(2,1)S(1)}, u32[]{:S(2)}, u32[]{:S(2)}) async-start(bf16[16,192,128]{2,1,0:T(8,128)(2,1)} %bitcast.124), calls=%async_computation.3 | async-start | bytes 1572864 | tf_op jit(solution)/shard_map/all_to_all | solution.py:45
  169.6 1.9 fusion.1
  171.5 1.3 copy-done.4
  172.9 1.9 collective-permute-start.6
  174.8 17.4 %all-to-all-done.3 = bf16[16,192,128]{2,1,0:T(8,128)(2,1)S(1)} async-done(((bf16[16,192,128]{2,1,0:T(8,128)(2,1)}), bf16[16,192,128]{2,1,0:T(8,128)(2,1)S(1)}, u32[]{:S(2)}, u32[]{:S(2)}) %all-to-all-start.3) | async-done | bytes 786464 | tf_op jit(solution)/shard_map/all_to_all | solution.py:45
  192.3 5.6 %collective-permute-start.7 = (bf16[192,128]{1,0:T(8,128)(2,1)S(1)}, bf16[192,128]{1,0:T(8,128)(2,1)S(1)}, u32[]{:S(2)}, u32[]{:S(2)}) collective-permute-start(bf16[192,128]{1,0:T(8,128)(2,1)S(1)} %reduce_sum.22), channel_id=1, source_target_pairs={{0,0},{256,1},{8,2},{264,3},{16,4},{272,5},{24,6},{280,7},{64,8},{... | collective-permute-start | bytes 147464 | tf_op jit(solution)/shard_map/ppermute | solution.py:109
  198.0 12.5 %collective-permute-done.7 = bf16[192,128]{1,0:T(8,128)(2,1)S(1)} collective-permute-done((bf16[192,128]{1,0:T(8,128)(2,1)S(1)}, bf16[192,128]{1,0:T(8,128)(2,1)S(1)}, u32[]{:S(2)}, u32[]{:S(2)}) %collective-permute-start.7) | collective-permute-done | bytes 49184 | tf_op jit(solution)/shard_map/ppermute | solution.py:109
  211.1 1.4 slice_add_fusion
  (68 shorter events, 20.9 us)
Async XLA Ops:
  0.6 17.1 %copy-start = (bf16[384,512]{1,0:T(8,128)(2,1)S(1)}, bf16[384,512]{1,0:T(8,128)(2,1)}, u32[]{:S(2)}) copy-start(bf16[384,512]{1,0:T(8,128)(2,1)} %param.9) | copy-start | bytes 1179652
  1.5 18.0 %collective-permute-start.2 = (bf16[192,128]{1,0:T(8,128)(2,1)S(1)}, bf16[192,128]{1,0:T(8,128)(2,1)S(1)}, u32[]{:S(2)}, u32[]{:S(2)}) collective-permute-start(bf16[192,128]{1,0:T(8,128)(2,1)S(1)} %pad_maximum_fusion.7), channel_id=1, source_target_pairs={{0,0},{1,256},{2,8},{3,264},{4,16},{5,272},{6,24},{7,280},{8,64},{... | collective-permute-start | bytes 147464 | tf_op jit(solution)/shard_map/ppermute | solution.py:62
  20.5 33.8 %all-to-all-start = ((bf16[16,192,128]{2,1,0:T(8,128)(2,1)}), bf16[16,192,128]{2,1,0:T(8,128)(2,1)S(1)}, u32[]{:S(2)}, u32[]{:S(2)}) async-start(bf16[16,192,128]{2,1,0:T(8,128)(2,1)} %broadcast_in_dim.9), calls=%async_computation | async-start | bytes 1572864 | tf_op jit(solution)/shard_map/all_to_all | solution.py:45
  28.7 23.6 %collective-permute-start = (bf16[2,256,512]{2,1,0:T(8,128)(2,1)S(1)}, bf16[2,256,512]{2,1,0:T(8,128)(2,1)S(1)}, u32[]{:S(2)}, u32[]{:S(2)}) collective-permute-start(bf16[2,256,512]{2,1,0:T(8,128)(2,1)S(1)} %pad_maximum_fusion.4), channel_id=1, source_target_pairs={{0,16},{8,24},{16,0},{24,8},{32,48},{40,56},{48,32},{56,40},{64,80... | collective-permute-start | bytes 1572872 | tf_op jit(solution)/shard_map/ppermute | solution.py:73
  52.3 4.7 %collective-permute-start.1 = (bf16[2,512,512]{2,1,0:T(8,128)(2,1)S(1)}, bf16[2,512,512]{2,1,0:T(8,128)(2,1)}, u32[]{:S(2)}, u32[]{:S(2)}) collective-permute-start(bf16[2,512,512]{2,1,0:T(8,128)(2,1)S(1)} %pad_maximum_fusion.3), channel_id=1, source_target_pairs={{0,8},{8,0},{16,24},{24,16},{32,40},{40,32},{48,56},{56,48},{64,72... | collective-permute-start | bytes 3145736 | tf_op jit(solution)/shard_map/ppermute | solution.py:74
  54.6 5.5 %copy-start.7 = (bf16[1,2,2,2,64,2,128]{6,5,4,3,2,1,0:T(2,128)(2,1)}, bf16[1,2,2,2,64,2,128]{6,5,4,3,2,1,0:T(2,128)(2,1)S(1)}, u32[]{:S(2)}) copy-start(bf16[1,2,2,2,64,2,128]{6,5,4,3,2,1,0:T(2,128)(2,1)S(1)} %copy.34) | copy-start | bytes 786436
  54.9 5.7 %copy-start.9 = (bf16[1,2,2,2,64,2,128]{6,5,4,3,2,1,0:T(2,128)(2,1)}, bf16[1,2,2,2,64,2,128]{6,5,4,3,2,1,0:T(2,128)(2,1)S(1)}, u32[]{:S(2)}) copy-start(bf16[1,2,2,2,64,2,128]{6,5,4,3,2,1,0:T(2,128)(2,1)S(1)} %copy.38) | copy-start | bytes 786436
  55.2 4.4 %copy-start.5 = (bf16[1,2,2,2,64,2,128]{6,5,4,3,2,1,0:T(2,128)(2,1)}, bf16[1,2,2,2,64,2,128]{6,5,4,3,2,1,0:T(2,128)(2,1)S(1)}, u32[]{:S(2)}) copy-start(bf16[1,2,2,2,64,2,128]{6,5,4,3,2,1,0:T(2,128)(2,1)S(1)} %copy.36) | copy-start | bytes 786436
  85.3 12.2 %collective-permute-start.3 = (bf16[128,768]{0,1:T(8,128)(2,1)S(1)}, bf16[128,768]{0,1:T(8,128)(2,1)S(1)}, u32[]{:S(2)}, u32[]{:S(2)}) collective-permute-start(bf16[128,768]{0,1:T(8,128)(2,1)S(1)} %slice.174), channel_id=1, source_target_pairs={{0,1},{1,0},{2,3},{3,2},{4,5},{5,4},{6,7},{7,6},{8,9},{9,8},{10,11... | collective-permute-start | bytes 589832 | tf_op jit(solution)/shard_map/ppermute | solution.py:83
  97.7 11.6 %collective-permute-start.4 = (bf16[128,768]{0,1:T(8,128)(2,1)S(1)}, bf16[128,768]{0,1:T(8,128)(2,1)S(1)}, u32[]{:S(2)}, u32[]{:S(2)}) collective-permute-start(bf16[128,768]{0,1:T(8,128)(2,1)S(1)} %pad_maximum_fusion.6), channel_id=1, source_target_pairs={{0,1},{1,0},{2,3},{3,2},{4,5},{5,4},{6,7},{7,6},{8,9},{9,8},{10,11... | collective-permute-start | bytes 589832 | tf_op jit(solution)/shard_map/ppermute | solution.py:95
  110.6 22.8 %all-to-all-start.2 = ((bf16[4,256,768]{1,2,0:T(8,128)(2,1)}), bf16[4,256,768]{1,2,0:T(8,128)(2,1)S(1)}, u32[]{:S(2)}, u32[]{:S(2)}) async-start(bf16[4,256,768]{1,2,0:T(8,128)(2,1)} %broadcast_in_dim.10), calls=%async_computation.2 | async-start | bytes 3145728 | tf_op jit(solution)/shard_map/all_to_all | solution.py:45
  134.1 1.1 copy-start.2
  134.1 2.0 copy-start.10
  136.2 1.6 copy-start.8
  143.9 3.7 %copy-start.3 = (f32[1024,512]{1,0:T(8,128)S(1)}, f32[1024,512]{1,0:T(8,128)}, u32[]{:S(2)}) copy-start(f32[1024,512]{1,0:T(8,128)} %fusion.12) | copy-start | bytes 6291460
  143.9 3.7 %copy-start.6 = (bf16[1,2,2,2,64,2,128]{6,5,4,3,2,1,0:T(2,128)(2,1)S(1)}, bf16[1,2,2,2,64,2,128]{6,5,4,3,2,1,0:T(2,128)(2,1)}, u32[]{:S(2)}) copy-start(bf16[1,2,2,2,64,2,128]{6,5,4,3,2,1,0:T(2,128)(2,1)} %copy-done.5) | copy-start | bytes 786436
  149.1 1.7 copy-start.1
  149.1 3.6 %copy-start.11 = (bf16[512,1024]{1,0:T(8,128)(2,1)S(1)}, bf16[512,1024]{1,0:T(8,128)(2,1)}, u32[]{:S(2)}) copy-start(bf16[512,1024]{1,0:T(8,128)(2,1)} %copy.44) | copy-start | bytes 3145732
  149.2 3.6 %copy-start.12 = (bf16[256,1024]{1,0:T(8,128)(2,1)S(1)}, bf16[256,1024]{1,0:T(8,128)(2,1)}, u32[]{:S(2)}) copy-start(bf16[256,1024]{1,0:T(8,128)(2,1)} %copy.45) | copy-start | bytes 1572868
  150.8 18.8 %collective-permute-start.5 = (bf16[2,512,512]{2,1,0:T(8,128)(2,1)}, bf16[2,512,512]{2,1,0:T(8,128)(2,1)}, u32[]{:S(2)}, u32[]{:S(2)}) collective-permute-start(bf16[2,512,512]{2,1,0:T(8,128)(2,1)} %fusion.2), channel_id=1, source_target_pairs={{0,8},{8,0},{16,24},{24,16},{32,40},{40,32},{48,56},{56,48},{64,72... | collective-permute-start | bytes 3145736 | tf_op jit(solution)/shard_map/ppermute | solution.py:117
  154.3 37.9 %all-to-all-start.3 = ((bf16[16,192,128]{2,1,0:T(8,128)(2,1)}), bf16[16,192,128]{2,1,0:T(8,128)(2,1)S(1)}, u32[]{:S(2)}, u32[]{:S(2)}) async-start(bf16[16,192,128]{2,1,0:T(8,128)(2,1)} %bitcast.124), calls=%async_computation.3 | async-start | bytes 1572864 | tf_op jit(solution)/shard_map/all_to_all | solution.py:45
  171.5 1.3 copy-start.4
  172.9 38.2 %collective-permute-start.6 = (bf16[2,256,512]{2,1,0:T(8,128)(2,1)S(1)}, bf16[2,256,512]{2,1,0:T(8,128)(2,1)S(1)}, u32[]{:S(2)}, u32[]{:S(2)}) collective-permute-start(bf16[2,256,512]{2,1,0:T(8,128)(2,1)S(1)} %slice.173), channel_id=1, source_target_pairs={{0,16},{8,24},{16,0},{24,8},{32,48},{40,56},{48,32},{56,40},{64,80... | collective-permute-start | bytes 1572872 | tf_op jit(solution)/shard_map/ppermute | solution.py:119
  192.3 18.1 %collective-permute-start.7 = (bf16[192,128]{1,0:T(8,128)(2,1)S(1)}, bf16[192,128]{1,0:T(8,128)(2,1)S(1)}, u32[]{:S(2)}, u32[]{:S(2)}) collective-permute-start(bf16[192,128]{1,0:T(8,128)(2,1)S(1)} %reduce_sum.22), channel_id=1, source_target_pairs={{0,0},{256,1},{8,2},{264,3},{16,4},{272,5},{24,6},{280,7},{64,8},{... | collective-permute-start | bytes 147464 | tf_op jit(solution)/shard_map/ppermute | solution.py:109

commit v3 on v2

v3 whole, which is shorter than its diff:
```python
import jax
import jax.numpy as jnp
from jax import lax
from jax.experimental import pallas as pl
from jax.experimental.pallas import tpu as pltpu
from jax.sharding import PartitionSpec as P

N_Y, N_Z, N_CORE, N_X = 8, 4, 2, 4
N_WIDE, N_NARROW = N_Y * N_Z * N_CORE, 2 * N_X
F32, BF16 = jnp.float32, jnp.bfloat16
FIRST, LAST, PLAIN = ((0,), (0,)), ((1,), (1,)), ((1,), (0,))


def wide_index(y, z, core):
    return (y * N_Z + z) * N_CORE + core


def swap_pairs():
    pairs = []
    for y in range(N_Y):
        for z in range(N_Z):
            for core in range(N_CORE):
                for n in range(N_NARROW):
                    z_bit, to_core, half = n // 4, n // 2 % 2, n % 2
                    to = wide_index(half * 4 + z % 2 * 2 + core, z // 2 * 2 + z_bit, to_core)
                    pairs.append((wide_index(y, z, core) * N_NARROW + n, to * N_NARROW + y))
    return pairs


PIECES = [(i // 8, (i % 2 * 2 + i // 4 % 2) * 2 + i // 2 % 2) for i in range(16)]
SWAP = swap_pairs()
SWAP_BACK = [(b, a) for a, b in SWAP]
OTHER_CORE = [(w, w ^ 1) for w in range(N_WIDE)]
OTHER_CHIP = [(w, w ^ 2) for w in range(N_WIDE)]
OTHER_HALF = [(n, n ^ 1) for n in range(N_NARROW)]
OWNERS = [
    [wide_index(y, 2 * pair + z_bit, core) for y in range(N_Y) for pair in range(2)]
    for z_bit in range(2)
    for core in range(N_CORE)
]
ALONG_X = [[2 * x + z_hi for x in range(N_X)] for z_hi in range(2)]


def dot(a, b, dims=PLAIN):
    return lax.dot_general(a, b, (dims, ((), ())), preferred_element_type=F32)


def exchange(x, axis, groups):
    return lax.all_to_all(x, axis, 0, 0, axis_index_groups=groups)


def call(body, outs, flops, *args):
    size = sum(a.size * a.dtype.itemsize for a in args)
    spec = pl.BlockSpec(memory_space=pltpu.VMEM)
    return pl.pallas_call(
        body,
        out_shape=[jax.ShapeDtypeStruct(shape, kind) for shape, kind in outs],
        in_specs=[spec] * len(args),
        out_specs=[spec] * len(outs),
        compiler_params=pltpu.CompilerParams(vmem_limit_bytes=32 * 1024 * 1024),
        cost_estimate=pl.CostEstimate(flops=flops, bytes_accessed=size, transcendentals=0),
    )(*args)


def use_of(gate, count):
    slots = gate.shape[1]
    lane = lax.broadcasted_iota(jnp.int32, (1, slots), 1)
    use = jnp.where(lane < count, gate, 0.0)
    square = lax.broadcasted_iota(jnp.int32, (slots, slots), 0) == lax.broadcasted_iota(
        jnp.int32, (slots, slots), 1
    )
    return jnp.sum(jnp.where(square, use, 0.0), axis=1, keepdims=True)


def pick_of(token, tok):
    slots = token.shape[1]
    return jnp.where(lax.broadcasted_iota(jnp.int32, (tok, slots), 0) == token, 1.0, 0.0).astype(BF16)


def rows_body(tokens, grad_out, token, count, gate, w_gate, w_up, w_down, own, block):
    rows = w_gate.shape[0]
    block[0:rows] = w_gate[...]
    block[rows : 2 * rows] = w_up[...]
    block[2 * rows : 3 * rows] = w_down[...]
    pick = pick_of(token[...], tokens.shape[0])
    own[0] = dot(pick, tokens[...], FIRST).astype(BF16)
    own[1] = (use_of(gate[...], count[...]) * dot(pick, grad_out[...], FIRST)).astype(BF16)


def forward_body(pieces, a0, a1, b0, b1, part_b, part_a, weights):
    rows = pieces.shape[1] // 3
    cols = pieces.shape[2]
    for i, (half, place) in enumerate(PIECES):
        for m in range(3):
            weights[m, rows * place : rows * (place + 1), cols * half : cols * (half + 1)] = pieces[
                i, rows * m : rows * (m + 1)
            ]
    units = 2 * cols
    slots = a0.shape[1]
    for part, x0, x1 in ((part_b, b0, b1), (part_a, a0, a1)):
        for which, x in enumerate((x0, x1)):
            at = slice(slots * which, slots * (which + 1))
            for m in range(3):
                part[at, units * m : units * (m + 1)] = dot(x[m // 2], weights[m]).astype(BF16)


def act_body(got, theirs, acts):
    total = got[0].astype(F32)
    for i in range(1, got.shape[0]):
        total = total + got[i].astype(F32)
    total = total + theirs[...].astype(F32)
    units = total.shape[1] // 3
    pre_gate, pre_up, grad_hidden = total[:, :units], total[:, units : 2 * units], total[:, 2 * units :]
    sigma = jax.nn.sigmoid(pre_gate)
    back_gate = (grad_hidden * pre_up * sigma * (1.0 + pre_gate * (1.0 - sigma))).astype(BF16)
    back_up = (grad_hidden * pre_gate * sigma).astype(BF16)
    hidden = (pre_gate * sigma * pre_up).astype(BF16)
    for i in range(got.shape[0]):
        acts[i, :, :units] = back_gate
        acts[i, :, units : 2 * units] = back_up
        acts[i, :, 2 * units :] = hidden


def outputs(acts, weights, which):
    units = weights.shape[2]
    if which == 0:
        return dot(acts[:, 2 * units :], weights[2], LAST)
    return dot(acts[:, :units], weights[0], LAST) + dot(acts[:, units : 2 * units], weights[1], LAST)


def term(acts, x0, x1, m, units):
    slots = x0.shape[1]
    cut = slice(units * m, units * (m + 1))
    return dot(x0[m // 2], acts[:slots, cut], FIRST) + dot(x1[m // 2], acts[slots:, cut], FIRST)


def theirs_body(acts, x0, x1, weights, send, terms):
    units = weights.shape[2]
    for which in range(2):
        send[which] = outputs(acts, weights, which).astype(BF16)
    for m in range(3):
        terms[:, units * m : units * (m + 1)] = term(acts, x0, x1, m, units)


def ours_body(acts, x0, x1, weights, terms, got, pieces, mine, send):
    units = weights.shape[2]
    rows, cols = pieces.shape[1] // 3, pieces.shape[2]
    slots = x0.shape[1]
    for m in range(3):
        total = (terms[:, units * m : units * (m + 1)] + term(acts, x0, x1, m, units)).astype(BF16)
        for i, (half, place) in enumerate(PIECES):
            pieces[i, rows * m : rows * (m + 1)] = total[
                rows * place : rows * (place + 1), cols * half : cols * (half + 1)
            ]
    for which in range(2):
        out = outputs(acts, weights, which) + got[which].astype(F32)
        mine[which] = out[:slots]
        send[which] = out[slots:].astype(BF16)


def tokens_body(mine, got, token, count, gate, mixed, grad_tokens):
    pick = pick_of(token[...], mixed.shape[0])
    out = use_of(gate[...], count[...]) * (mine[0] + got[0].astype(F32))
    mixed[...] = dot(pick, out.astype(BF16)).astype(BF16)
    back = mine[1] + got[1].astype(F32)
    grad_tokens[...] = dot(pick, back.astype(BF16)).astype(BF16)


def local(tokens, grad_out, slot_token, slot_count, slot_gate, w_gate, w_up, w_down):
    slots, (tok, feat) = slot_token.shape[0], tokens.shape
    rows, cols = w_gate.shape
    units = 2 * cols
    token, gate, count = slot_token[None], slot_gate[None], slot_count[None]
    pick_flops = 4 * slots * tok * feat
    own, block = call(
        rows_body,
        [((2, slots, feat), BF16), ((3 * rows, cols), BF16)],
        pick_flops,
        *(tokens, grad_out, token, count, gate, w_gate, w_up, w_down),
    )

    block = lax.ppermute(block, ("wide", "narrow"), SWAP)
    next_own = lax.ppermute(own, "wide", OTHER_CHIP)
    core_own = lax.ppermute(own, "wide", OTHER_CORE)
    core_next = lax.ppermute(next_own, "wide", OTHER_CORE)
    pieces = exchange(jnp.broadcast_to(block[None], (len(PIECES),) + block.shape), "wide", OWNERS)

    flops = 2 * 3 * 2 * slots * feat * units
    part_b, part_a, weights = call(
        forward_body,
        [((2 * slots, 3 * units), BF16)] * 2 + [((3, feat, units), BF16)],
        2 * flops,
        *(pieces, own, next_own, core_own, core_next),
    )
    portion = 2 * slots // N_X
    parts = (N_X, portion, 3 * units)

    def narrow_sum(part):
        got = exchange(part.reshape(parts), "narrow", ALONG_X)
        sent = got.astype(F32).sum(axis=0).astype(BF16)
        return got, lax.ppermute(sent, "narrow", OTHER_HALF)

    def activations(got, theirs):
        (acts,) = call(act_body, [(parts, BF16)], 20 * portion * 3 * units, got, theirs)
        return exchange(acts, "narrow", ALONG_X).reshape(2 * slots, 3 * units)

    got_b, theirs_b = narrow_sum(part_b)
    part_a, got_b = lax.optimization_barrier((part_a, got_b))
    got_a, theirs_a = narrow_sum(part_a)
    acts_b = activations(got_b, theirs_b)
    acts_a = activations(got_a, theirs_a)

    send, terms = call(
        theirs_body,
        [((2, 2 * slots, feat), BF16), ((feat, 3 * units), F32)],
        2 * flops,
        *(acts_b, core_own, core_next, weights),
    )
    got = lax.ppermute(send, "wide", OTHER_CORE)
    terms, mine, send = call(
        ours_body,
        [(pieces.shape, BF16), ((2, slots, feat), F32), ((2, slots, feat), BF16)],
        2 * flops,
        *(acts_a, own, next_own, weights, terms, got),
    )
    got = lax.ppermute(send, "wide", OTHER_CHIP)
    terms = exchange(terms, "wide", OWNERS)
    mixed, grad_tokens = call(
        tokens_body, [((tok, feat), BF16)] * 2, pick_flops, *(mine, got, token, count, gate)
    )
    terms, mixed, grad_tokens = lax.optimization_barrier((terms, mixed, grad_tokens))
    grads = terms.astype(F32).sum(axis=0).astype(BF16)
    grads = lax.ppermute(grads, ("wide", "narrow"), SWAP_BACK).astype(F32)
    return mixed, grad_tokens, grads[:rows], grads[rows : 2 * rows], grads[2 * rows :]


def solution(mesh):
    both = P("wide", "narrow")
    in_specs = (both, both, P("wide"), P("wide"), P("wide"), both, both, both)
    return jax.shard_map(
        local, mesh=mesh, in_specs=in_specs, out_specs=(both,) * 5, check_vma=False
    )
```

time: 216 us -> 212 us (0.981)
  blocking collectives: 23.7 us -> 44.8 us
  matrix products: 15.5 us -> 0 us
  waiting for transfers between devices: 76.5 us -> 66 us
  other arithmetic: 9.51 us -> 1.05 us
  Pallas kernels: 0 us -> 6.88 us
  starting transfers between devices: 69.3 us -> 75.9 us
  local copies, waits for them, and re-layouts: 18.4 us -> 14.9 us
    all_to_all x3, waiting for transfers between devices: 33 us -> 2.57 us  [exchange(): return lax.all_to_all(x, axis, 0, 0, axis_index_groups=groups)]
    all_to_all x1 -> x3, blocking collectives: 23.7 us -> 44.8 us  [exchange(): return lax.all_to_all(x, axis, 0, 0, axis_index_groups=groups)]
    dot_general x13 -> x0, matrix products: 15.5 us -> none  [dot(): return lax.dot_general(a, b, (dims, ((), ())), preferred_element_type=F32)]
    ppermute x7 -> x8, waiting for transfers between devices: 31 us -> 46 us  [the longest x1 18 us: local(): got = lax.ppermute(send, 'wide', OTHER_CHIP)]
    unnamed x26 -> x52, local copies, waits for them, and re-layouts: 2.98 us -> 13.2 us
    dot_general x7 -> x0, local copies, waits for them, and re-layouts: 9.08 us -> none  [dot(): return lax.dot_general(a, b, (dims, ((), ())), preferred_element_type=F32)]
    ppermute x7 -> x8, starting transfers between devices: 36.7 us -> 43.6 us  [the longest x2 14.8 us: narrow_sum(): return (got, lax.ppermute(sent, 'narrow', OTHER_HALF))]
    pallas_call x0 -> x7, Pallas kernels: none -> 6.88 us  [call(): pl.pallas_call(body, out_shape=[jax.ShapeDtypeStruct(shape, kind) for sha...]
  transfers between devices with their start and end apart: 11 -> 12, of which waited for: 7 -> 8; matrix products, arithmetic and copies ran while one was open for 6% -> 0% of each run, Pallas kernels for 0% -> 2%
where the time goes in v3:
time: 212 us; the launch traced here: 211 us
  starting transfers between devices  75.9 us (36%)
  waiting for transfers between devices  66 us (31%)
  blocking collectives  44.8 us (21%)
  local copies, waits for them, and re-layouts  14.9 us (7%)
  Pallas kernels  6.88 us (3%)
    all_to_all x3, blocking collectives, exchange(): return lax.all_to_all(x, axis, 0, 0, axis_index_groups=groups)  44.8 us
    all_to_all x3, starting transfers between devices, exchange(): return lax.all_to_all(x, axis, 0, 0, axis_index_groups=groups)  30.3 us
    ppermute x1, waiting for transfers between devices, local(): got = lax.ppermute(send, 'wide', OTHER_CHIP)  18 us
    ppermute x1, waiting for transfers between devices, local(): grads = lax.ppermute(grads, ('wide', 'narrow'), SWAP_BACK).astype(F32)  17.5 us
    ppermute x1, waiting for transfers between devices, local(): next_own = lax.ppermute(own, 'wide', OTHER_CHIP)  15.9 us
    ppermute x2, starting transfers between devices, narrow_sum(): return (got, lax.ppermute(sent, 'narrow', OTHER_HALF))  14.8 us
    unnamed x52, local copies, waits for them, and re-layouts  13.2 us
    ppermute x1, starting transfers between devices, local(): block = lax.ppermute(block, ('wide', 'narrow'), SWAP)  12.8 us
  transfers between devices with their start and end apart: 12, of which 8 were waited for; matrix products, arithmetic and copies ran while one was open for 0% of the time, Pallas kernels for 2%

profile of v3, /device:TPU:40, one launch (start us, length us, event | category | flops | bytes accessed | tf_op | source)
XLA Modules:
  0.0 211.0 jit_solution(7674654750328922192)
XLA Ops:
  7.3 12.8 %collective-permute-start = (bf16[192,128]{1,0:T(8,128)(2,1)S(1)}, bf16[192,128]{1,0:T(8,128)(2,1)S(1)}, u32[]{:S(2)}, u32[]{:S(2)}) collective-permute-start(bf16[192,128]{1,0:T(8,128)(2,1)S(1)} %get-tuple-element.22), channel_id=1, source_target_pairs={{0,0},{1,256},{2,8},{3,264},{4,16},{5,272},{6,24},{7,280},{8,64},{... | collective-permute-start | bytes 147464 | tf_op jit(solution)/shard_map/ppermute | solution.py:182
  20.1 1.7 collective-permute-done
  21.8 1.0 broadcast_in_dim.18
  22.9 11.1 %all-to-all-start = ((bf16[16,192,128]{2,1,0:T(8,128)(2,1)}), bf16[16,192,128]{2,1,0:T(8,128)(2,1)S(1)}, u32[]{:S(2)}, u32[]{:S(2)}) async-start(bf16[16,192,128]{2,1,0:T(8,128)(2,1)} %broadcast_in_dim.18), calls=%async_computation | async-start | bytes 1572864 | tf_op jit(solution)/shard_map/all_to_all | solution.py:49
  33.9 5.6 %collective-permute-start.1 = (bf16[2,256,512]{2,1,0:T(8,128)(2,1)S(1)}, bf16[2,256,512]{2,1,0:T(8,128)(2,1)S(1)}, u32[]{:S(2)}, u32[]{:S(2)}) collective-permute-start(bf16[2,256,512]{2,1,0:T(8,128)(2,1)S(1)} %get-tuple-element.23.a0.x0), channel_id=1, source_target_pairs={{0,16},{8,24},{16,0},{24,8},{32,48},{40,56},{48,32},{56,40},{64,80... | collective-permute-start | bytes 1572872 | tf_op jit(solution)/shard_map/ppermute | solution.py:183
  39.5 1.9 collective-permute-start.2
  41.4 15.9 %collective-permute-done.1.a1.x1 = bf16[2,256,512]{2,1,0:T(8,128)(2,1)S(1)} collective-permute-done((bf16[2,256,512]{2,1,0:T(8,128)(2,1)S(1)}, bf16[2,256,512]{2,1,0:T(8,128)(2,1)S(1)}, u32[]{:S(2)}, u32[]{:S(2)}) %collective-permute-start.1) | collective-permute-done | bytes 524320 | tf_op jit(solution)/shard_map/ppermute | solution.py:183
  57.4 1.9 collective-permute-start.3
  59.3 1.9 collective-permute-done.3.b1.x1
  62.0 1.0 copy-done.22
  63.0 1.9 shard_map.120
  64.9 15.5 %all_to_all.30.got = bf16[4,128,768]{2,1,0:T(8,128)(2,1)S(1)} all-to-all(bf16[4,128,768]{2,1,0:T(8,128)(2,1)S(1)} %bitcast.11), channel_id=1, replica_groups={{0,2,4,6},{1,3,5,7},{8,10,12,14},{9,11,13,15},{16,18,20,22},{17,19,21,2..., dimensions={0} | all-to-all | bytes 1572864 | tf_op jit(solution)/shard_map/all_to_all | solution.py:49
  80.6 7.3 %collective-permute-start.5 = (bf16[128,768]{1,0:T(8,128)(2,1)S(1)}, bf16[128,768]{1,0:T(8,128)(2,1)S(1)}, u32[]{:S(2)}, u32[]{:S(2)}) collective-permute-start(bf16[128,768]{1,0:T(8,128)(2,1)S(1)} %reduce_sum.37), channel_id=1, source_target_pairs={{0,1},{1,0},{2,3},{3,2},{4,5},{5,4},{6,7},{7,6},{8,9},{9,8},{10,11... | collective-permute-start | bytes 589832 | tf_op jit(solution)/shard_map/ppermute | solution.py:201
  87.9 4.2 %collective-permute-done.5.theirs = bf16[128,768]{1,0:T(8,128)(2,1)S(1)} collective-permute-done((bf16[128,768]{1,0:T(8,128)(2,1)S(1)}, bf16[128,768]{1,0:T(8,128)(2,1)S(1)}, u32[]{:S(2)}, u32[]{:S(2)}) %collective-permute-start.5) | collective-permute-done | bytes 196640 | tf_op jit(solution)/shard_map/ppermute | solution.py:201
  92.3 13.5 %all_to_all.31 = bf16[4,128,768]{2,1,0:T(8,128)(2,1)} all-to-all(bf16[4,128,768]{2,1,0:T(8,128)(2,1)S(1)} %shard_map.122), channel_id=1, replica_groups={{0,2,4,6},{1,3,5,7},{8,10,12,14},{9,11,13,15},{16,18,20,22},{17,19,21,2..., dimensions={0} | all-to-all | bytes 1572864 | tf_op jit(solution)/shard_map/all_to_all | solution.py:49
  105.7 3.5 %all-to-all-start.2 = ((bf16[4,128,768]{2,1,0:T(8,128)(2,1)}), bf16[4,128,768]{2,1,0:T(8,128)(2,1)S(1)}, u32[]{:S(2)}, u32[]{:S(2)}) async-start(bf16[4,128,768]{2,1,0:T(8,128)(2,1)} %bitcast.4), calls=%async_computation.2 | async-start | bytes 1572864 | tf_op jit(solution)/shard_map/all_to_all | solution.py:49
  109.3 1.1 copy-done.5
  110.4 1.0 copy-done.20
  111.4 1.0 copy-done.23
  112.5 1.7 shard_map.123
  114.2 1.9 collective-permute-start.6
  116.1 2.6 %all-to-all-done.2.got = bf16[4,128,768]{2,1,0:T(8,128)(2,1)S(1)} async-done(((bf16[4,128,768]{2,1,0:T(8,128)(2,1)}), bf16[4,128,768]{2,1,0:T(8,128)(2,1)S(1)}, u32[]{:S(2)}, u32[]{:S(2)}) %all-to-all-start.2) | async-done | bytes 786464 | tf_op jit(solution)/shard_map/all_to_all | solution.py:49
  119.5 7.5 %collective-permute-start.4 = (bf16[128,768]{1,0:T(8,128)(2,1)}, bf16[128,768]{1,0:T(8,128)(2,1)S(1)}, u32[]{:S(2)}, u32[]{:S(2)}) collective-permute-start(bf16[128,768]{1,0:T(8,128)(2,1)} %reduce_sum.36), channel_id=1, source_target_pairs={{0,1},{1,0},{2,3},{3,2},{4,5},{5,4},{6,7},{7,6},{8,9},{9,8},{10,11... | collective-permute-start | bytes 589832 | tf_op jit(solution)/shard_map/ppermute | solution.py:201
  127.0 4.3 %collective-permute-done.4.theirs = bf16[128,768]{1,0:T(8,128)(2,1)S(1)} collective-permute-done((bf16[128,768]{1,0:T(8,128)(2,1)}, bf16[128,768]{1,0:T(8,128)(2,1)S(1)}, u32[]{:S(2)}, u32[]{:S(2)}) %collective-permute-start.4) | collective-permute-done | bytes 196640 | tf_op jit(solution)/shard_map/ppermute | solution.py:201
  131.5 15.8 %all_to_all.32 = bf16[4,128,768]{2,1,0:T(8,128)(2,1)S(1)} all-to-all(bf16[4,128,768]{2,1,0:T(8,128)(2,1)S(1)} %shard_map.121), channel_id=1, replica_groups={{0,2,4,6},{1,3,5,7},{8,10,12,14},{9,11,13,15},{16,18,20,22},{17,19,21,2..., dimensions={0} | all-to-all | bytes 1572864 | tf_op jit(solution)/shard_map/all_to_all | solution.py:49
  147.3 1.0 shard_map.124
  151.0 15.8 %all-to-all-start.5 = ((bf16[16,192,128]{2,1,0:T(8,128)(2,1)}), bf16[16,192,128]{2,1,0:T(8,128)(2,1)S(1)}, u32[]{:S(2)}, u32[]{:S(2)}) async-start(bf16[16,192,128]{2,1,0:T(8,128)(2,1)} %copy-done.4), calls=%async_computation.5 | async-start | bytes 1572864 | tf_op jit(solution)/shard_map/all_to_all | solution.py:49
  166.8 4.7 %collective-permute-start.7 = (bf16[2,256,512]{2,1,0:T(8,128)(2,1)S(1)}, bf16[2,256,512]{2,1,0:T(8,128)(2,1)S(1)}, u32[]{:S(2)}, u32[]{:S(2)}) collective-permute-start(bf16[2,256,512]{2,1,0:T(8,128)(2,1)S(1)} %copy-done.25), channel_id=1, source_target_pairs={{0,16},{8,24},{16,0},{24,8},{32,48},{40,56},{48,32},{56,40},{64,80... | collective-permute-start | bytes 1572872 | tf_op jit(solution)/shard_map/ppermute | solution.py:226
  171.5 18.0 %collective-permute-done.7.got = bf16[2,256,512]{2,1,0:T(8,128)(2,1)S(1)} collective-permute-done((bf16[2,256,512]{2,1,0:T(8,128)(2,1)S(1)}, bf16[2,256,512]{2,1,0:T(8,128)(2,1)S(1)}, u32[]{:S(2)}, u32[]{:S(2)}) %collective-permute-start.7) | collective-permute-done | bytes 524320 | tf_op jit(solution)/shard_map/ppermute | solution.py:226
  189.5 1.3 shard_map.125
  191.0 1.9 collective-permute-start.8
  192.9 17.5 %collective-permute-done.8 = bf16[192,128]{1,0:T(8,128)(2,1)S(1)} collective-permute-done((bf16[192,128]{1,0:T(8,128)(2,1)S(1)}, bf16[192,128]{1,0:T(8,128)(2,1)S(1)}, u32[]{:S(2)}, u32[]{:S(2)}) %collective-permute-start.8) | collective-permute-done | bytes 49184 | tf_op jit(solution)/shard_map/ppermute | solution.py:233
  (59 shorter events, 11.5 us)
Async XLA Ops:
  1.3 1.0 copy-start.10
  2.3 1.0 copy-start.11
  7.3 57.7 %copy-start.6 = (bf16[2,256,512]{2,1,0:T(8,128)(2,1)}, bf16[2,256,512]{2,1,0:T(8,128)(2,1)S(1)}, u32[]{:S(2)}) copy-start(bf16[2,256,512]{2,1,0:T(8,128)(2,1)S(1)} %get-tuple-element.23.a0.x0) | copy-start | bytes 1572868
  7.3 14.5 %collective-permute-start = (bf16[192,128]{1,0:T(8,128)(2,1)S(1)}, bf16[192,128]{1,0:T(8,128)(2,1)S(1)}, u32[]{:S(2)}, u32[]{:S(2)}) collective-permute-start(bf16[192,128]{1,0:T(8,128)(2,1)S(1)} %get-tuple-element.22), channel_id=1, source_target_pairs={{0,0},{1,256},{2,8},{3,264},{4,16},{5,272},{6,24},{7,280},{8,64},{... | collective-permute-start | bytes 147464 | tf_op jit(solution)/shard_map/ppermute | solution.py:182
  22.9 39.1 %all-to-all-start = ((bf16[16,192,128]{2,1,0:T(8,128)(2,1)}), bf16[16,192,128]{2,1,0:T(8,128)(2,1)S(1)}, u32[]{:S(2)}, u32[]{:S(2)}) async-start(bf16[16,192,128]{2,1,0:T(8,128)(2,1)} %broadcast_in_dim.18), calls=%async_computation | async-start | bytes 1572864 | tf_op jit(solution)/shard_map/all_to_all | solution.py:49
  33.9 23.4 %collective-permute-start.1 = (bf16[2,256,512]{2,1,0:T(8,128)(2,1)S(1)}, bf16[2,256,512]{2,1,0:T(8,128)(2,1)S(1)}, u32[]{:S(2)}, u32[]{:S(2)}) collective-permute-start(bf16[2,256,512]{2,1,0:T(8,128)(2,1)S(1)} %get-tuple-element.23.a0.x0), channel_id=1, source_target_pairs={{0,16},{8,24},{16,0},{24,8},{32,48},{40,56},{48,32},{56,40},{64,80... | collective-permute-start | bytes 1572872 | tf_op jit(solution)/shard_map/ppermute | solution.py:183
  39.5 19.8 %collective-permute-start.2 = (bf16[2,256,512]{2,1,0:T(8,128)(2,1)S(1)}, bf16[2,256,512]{2,1,0:T(8,128)(2,1)S(1)}, u32[]{:S(2)}, u32[]{:S(2)}) collective-permute-start(bf16[2,256,512]{2,1,0:T(8,128)(2,1)S(1)} %get-tuple-element.23.a0.x0), channel_id=1, source_target_pairs={{0,8},{8,0},{16,24},{24,16},{32,40},{40,32},{48,56},{56,48},{64,72... | collective-permute-start | bytes 1572872 | tf_op jit(solution)/shard_map/ppermute | solution.py:184
  57.4 23.1 %copy-start.8 = (bf16[2,256,512]{2,1,0:T(8,128)(2,1)}, bf16[2,256,512]{2,1,0:T(8,128)(2,1)S(1)}, u32[]{:S(2)}) copy-start(bf16[2,256,512]{2,1,0:T(8,128)(2,1)S(1)} %collective-permute-done.1.a1.x1) | copy-start | bytes 1572868
  57.4 3.8 %collective-permute-start.3 = (bf16[2,256,512]{2,1,0:T(8,128)(2,1)S(1)}, bf16[2,256,512]{2,1,0:T(8,128)(2,1)S(1)}, u32[]{:S(2)}, u32[]{:S(2)}) collective-permute-start(bf16[2,256,512]{2,1,0:T(8,128)(2,1)S(1)} %collective-permute-done.1.a1.x1), channel_id=1, source_target_pairs={{0,8},{8,0},{16,24},{24,16},{32,40},{40,32},{48,56},{56,48},{64,72... | collective-permute-start | bytes 1572872 | tf_op jit(solution)/shard_map/ppermute | solution.py:185
  59.3 21.2 %copy-start.19 = (bf16[2,256,512]{2,1,0:T(8,128)(2,1)}, bf16[2,256,512]{2,1,0:T(8,128)(2,1)S(1)}, u32[]{:S(2)}) copy-start(bf16[2,256,512]{2,1,0:T(8,128)(2,1)S(1)} %collective-permute-done.2.b0.x0) | copy-start | bytes 1572868
  61.2 0.8 copy-start.21
  62.0 1.0 copy-start.22
  64.9 44.3 %copy-start.2 = (bf16[3,512,256]{2,1,0:T(8,128)(2,1)}, bf16[3,512,256]{2,1,0:T(8,128)(2,1)S(1)}, u32[]{:S(2)}) copy-start(bf16[3,512,256]{2,1,0:T(8,128)(2,1)S(1)} %get-tuple-element.27.weights) | copy-start | bytes 2359300
  80.6 11.5 %collective-permute-start.5 = (bf16[128,768]{1,0:T(8,128)(2,1)S(1)}, bf16[128,768]{1,0:T(8,128)(2,1)S(1)}, u32[]{:S(2)}, u32[]{:S(2)}) collective-permute-start(bf16[128,768]{1,0:T(8,128)(2,1)S(1)} %reduce_sum.37), channel_id=1, source_target_pairs={{0,1},{1,0},{2,3},{3,2},{4,5},{5,4},{6,7},{7,6},{8,9},{9,8},{10,11... | collective-permute-start | bytes 589832 | tf_op jit(solution)/shard_map/ppermute | solution.py:201
  105.7 13.0 %all-to-all-start.2 = ((bf16[4,128,768]{2,1,0:T(8,128)(2,1)}), bf16[4,128,768]{2,1,0:T(8,128)(2,1)S(1)}, u32[]{:S(2)}, u32[]{:S(2)}) async-start(bf16[4,128,768]{2,1,0:T(8,128)(2,1)} %bitcast.4), calls=%async_computation.2 | async-start | bytes 1572864 | tf_op jit(solution)/shard_map/all_to_all | solution.py:49
  109.2 1.1 copy-start.5
  110.4 1.0 copy-start.20
  111.4 1.0 copy-start.23
  114.2 33.1 %collective-permute-start.6 = (bf16[2,512,512]{2,1,0:T(8,128)(2,1)}, bf16[2,512,512]{2,1,0:T(8,128)(2,1)S(1)}, u32[]{:S(2)}, u32[]{:S(2)}) collective-permute-start(bf16[2,512,512]{2,1,0:T(8,128)(2,1)} %get-tuple-element.30), channel_id=1, source_target_pairs={{0,8},{8,0},{16,24},{24,16},{32,40},{40,32},{48,56},{56,48},{64,72... | collective-permute-start | bytes 3145736 | tf_op jit(solution)/shard_map/ppermute | solution.py:219
  119.5 27.8 %copy-start.3 = (bf16[3,512,256]{2,1,0:T(8,128)(2,1)S(1)}, bf16[3,512,256]{2,1,0:T(8,128)(2,1)}, u32[]{:S(2)}) copy-start(bf16[3,512,256]{2,1,0:T(8,128)(2,1)} %copy-done.2) | copy-start | bytes 2359300
  119.5 27.8 %copy-start.7 = (bf16[2,256,512]{2,1,0:T(8,128)(2,1)S(1)}, bf16[2,256,512]{2,1,0:T(8,128)(2,1)}, u32[]{:S(2)}) copy-start(bf16[2,256,512]{2,1,0:T(8,128)(2,1)} %copy-done.6) | copy-start | bytes 1572868
  119.5 27.8 %copy-start.9 = (bf16[2,256,512]{2,1,0:T(8,128)(2,1)S(1)}, bf16[2,256,512]{2,1,0:T(8,128)(2,1)}, u32[]{:S(2)}) copy-start(bf16[2,256,512]{2,1,0:T(8,128)(2,1)} %copy-done.8) | copy-start | bytes 1572868
  119.5 11.8 %collective-permute-start.4 = (bf16[128,768]{1,0:T(8,128)(2,1)}, bf16[128,768]{1,0:T(8,128)(2,1)S(1)}, u32[]{:S(2)}, u32[]{:S(2)}) collective-permute-start(bf16[128,768]{1,0:T(8,128)(2,1)} %reduce_sum.36), channel_id=1, source_target_pairs={{0,1},{1,0},{2,3},{3,2},{4,5},{5,4},{6,7},{7,6},{8,9},{9,8},{10,11... | collective-permute-start | bytes 589832 | tf_op jit(solution)/shard_map/ppermute | solution.py:201
  148.4 1.0 copy-start
  149.3 0.9 copy-start.4
  151.0 38.5 %copy-start.16 = (s32[256]{0:T(256)S(1)}, s32[256]{0:T(256)}, u32[]{:S(2)}) copy-start(s32[256]{0:T(256)} %param.10) | copy-start | bytes 3076
  151.0 38.5 %copy-start.18 = (f32[256]{0:T(256)S(1)}, f32[256]{0:T(256)}, u32[]{:S(2)}) copy-start(f32[256]{0:T(256)} %param.12) | copy-start | bytes 3076
  151.0 15.8 %copy-start.25 = (bf16[2,256,512]{2,1,0:T(8,128)(2,1)S(1)}, bf16[2,256,512]{2,1,0:T(8,128)(2,1)}, u32[]{:S(2)}) copy-start(bf16[2,256,512]{2,1,0:T(8,128)(2,1)} %copy-done.24) | copy-start | bytes 1572868
  151.0 38.5 %copy-start.1 = (f32[2,256,512]{2,1,0:T(8,128)S(1)}, f32[2,256,512]{2,1,0:T(8,128)}, u32[]{:S(2)}) copy-start(f32[2,256,512]{2,1,0:T(8,128)} %copy-done) | copy-start | bytes 3145732
  151.0 39.8 %all-to-all-start.5 = ((bf16[16,192,128]{2,1,0:T(8,128)(2,1)}), bf16[16,192,128]{2,1,0:T(8,128)(2,1)S(1)}, u32[]{:S(2)}, u32[]{:S(2)}) async-start(bf16[16,192,128]{2,1,0:T(8,128)(2,1)} %copy-done.4), calls=%async_computation.5 | async-start | bytes 1572864 | tf_op jit(solution)/shard_map/all_to_all | solution.py:49
  166.8 22.7 %collective-permute-start.7 = (bf16[2,256,512]{2,1,0:T(8,128)(2,1)S(1)}, bf16[2,256,512]{2,1,0:T(8,128)(2,1)S(1)}, u32[]{:S(2)}, u32[]{:S(2)}) collective-permute-start(bf16[2,256,512]{2,1,0:T(8,128)(2,1)S(1)} %copy-done.25), channel_id=1, source_target_pairs={{0,16},{8,24},{16,0},{24,8},{32,48},{40,56},{48,32},{56,40},{64,80... | collective-permute-start | bytes 1572872 | tf_op jit(solution)/shard_map/ppermute | solution.py:226
  191.0 19.4 %collective-permute-start.8 = (bf16[192,128]{1,0:T(8,128)(2,1)S(1)}, bf16[192,128]{1,0:T(8,128)(2,1)S(1)}, u32[]{:S(2)}, u32[]{:S(2)}) collective-permute-start(bf16[192,128]{1,0:T(8,128)(2,1)S(1)} %reduce_sum.38), channel_id=1, source_target_pairs={{0,0},{256,1},{8,2},{264,3},{16,4},{272,5},{24,6},{280,7},{64,8},{... | collective-permute-start | bytes 147464 | tf_op jit(solution)/shard_map/ppermute | solution.py:233
  (6 other events, 4.3 us)

commit v4 on v3

--- a/solution.py
+++ b/solution.py
@@ -49,17 +49,25 @@
     return lax.all_to_all(x, axis, 0, 0, axis_index_groups=groups)
 
 
-def call(body, outs, flops, *args):
+def call(body, outs, flops, *args, after=(), fetch=False):
     size = sum(a.size * a.dtype.itemsize for a in args)
-    spec = pl.BlockSpec(memory_space=pltpu.VMEM)
+    vmem, anywhere = pl.BlockSpec(memory_space=pltpu.VMEM), pl.BlockSpec(memory_space=pl.ANY)
+    scratch = ()
+    if fetch:
+        scratch = [pltpu.VMEM(a.shape, a.dtype) for a in args] + [pltpu.SemaphoreType.DMA((len(args),))]
+
+    def inner(*refs):
+        body(*refs[: len(args)], *refs[len(args) + len(after) :])
+
     return pl.pallas_call(
-        body,
+        inner,
         out_shape=[jax.ShapeDtypeStruct(shape, kind) for shape, kind in outs],
-        in_specs=[spec] * len(args),
-        out_specs=[spec] * len(outs),
-        compiler_params=pltpu.CompilerParams(vmem_limit_bytes=32 * 1024 * 1024),
+        in_specs=[pl.BlockSpec(memory_space=pltpu.HBM) if fetch else vmem] * len(args) + [anywhere] * len(after),
+        out_specs=[vmem] * len(outs),
+        scratch_shapes=scratch,
+        compiler_params=pltpu.CompilerParams(vmem_limit_bytes=(60 if fetch else 12) * 1024 * 1024),
         cost_estimate=pl.CostEstimate(flops=flops, bytes_accessed=size, transcendentals=0),
-    )(*args)
+    )(*args, *after)
 
 
 def use_of(gate, count):
@@ -77,31 +85,45 @@
     return jnp.where(lax.broadcasted_iota(jnp.int32, (tok, slots), 0) == token, 1.0, 0.0).astype(BF16)
 
 
-def rows_body(tokens, grad_out, token, count, gate, w_gate, w_up, w_down, own, block):
+def rows_body(*refs):
+    sources, (own, block), held, sem = refs[:8], refs[8:10], refs[10:18], refs[18]
+    copies = [pltpu.make_async_copy(s, h, sem.at[i]) for i, (s, h) in enumerate(zip(sources, held))]
+    for copy in copies:
+        copy.start()
+    tokens, grad_out, token, count, gate, w_gate, w_up, w_down = held
     rows = w_gate.shape[0]
-    block[0:rows] = w_gate[...]
-    block[rows : 2 * rows] = w_up[...]
-    block[2 * rows : 3 * rows] = w_down[...]
+    for i, weight in ((5, w_gate), (6, w_up), (7, w_down)):
+        copies[i].wait()
+        block[rows * (i - 5) : rows * (i - 4)] = weight[...]
+    for i in (2, 3, 4, 0):
+        copies[i].wait()
     pick = pick_of(token[...], tokens.shape[0])
     own[0] = dot(pick, tokens[...], FIRST).astype(BF16)
+    copies[1].wait()
     own[1] = (use_of(gate[...], count[...]) * dot(pick, grad_out[...], FIRST)).astype(BF16)
 
 
-def forward_body(pieces, a0, a1, b0, b1, part_b, part_a, weights):
-    rows = pieces.shape[1] // 3
-    cols = pieces.shape[2]
+def products(part, x0, x1, weights):
+    slots, units = x0.shape[1], weights.shape[2]
+    for which, x in enumerate((x0, x1)):
+        for m in range(3):
+            part[slots * which : slots * (which + 1), units * m : units * (m + 1)] = dot(
+                x[m // 2], weights[m]
+            ).astype(BF16)
+
+
+def first_body(pieces, x0, x1, part, weights):
+    rows, cols = pieces.shape[1] // 3, pieces.shape[2]
     for i, (half, place) in enumerate(PIECES):
         for m in range(3):
             weights[m, rows * place : rows * (place + 1), cols * half : cols * (half + 1)] = pieces[
                 i, rows * m : rows * (m + 1)
             ]
-    units = 2 * cols
-    slots = a0.shape[1]
-    for part, x0, x1 in ((part_b, b0, b1), (part_a, a0, a1)):
-        for which, x in enumerate((x0, x1)):
-            at = slice(slots * which, slots * (which + 1))
-            for m in range(3):
-                part[at, units * m : units * (m + 1)] = dot(x[m // 2], weights[m]).astype(BF16)
+    products(part, x0, x1, weights)
+
+
+def second_body(weights, x0, x1, part):
+    products(part, x0, x1, weights)
 
 
 def act_body(got, theirs, acts):
@@ -134,35 +156,39 @@
     return dot(x0[m // 2], acts[:slots, cut], FIRST) + dot(x1[m // 2], acts[slots:, cut], FIRST)
 
 
-def theirs_body(acts, x0, x1, weights, send, terms):
-    units = weights.shape[2]
+def near_body(acts, x0, x1, weights, mine, send, terms):
+    units, slots = weights.shape[2], x0.shape[1]
     for which in range(2):
-        send[which] = outputs(acts, weights, which).astype(BF16)
+        out = outputs(acts, weights, which)
+        mine[which] = out[:slots]
+        send[which] = out[slots:].astype(BF16)
     for m in range(3):
         terms[:, units * m : units * (m + 1)] = term(acts, x0, x1, m, units)
 
 
-def ours_body(acts, x0, x1, weights, terms, got, pieces, mine, send):
-    units = weights.shape[2]
+def far_body(acts, weights, mine, send):
+    slots = mine.shape[1]
+    for which in range(2):
+        out = outputs(acts, weights, which)
+        mine[which] = out[:slots]
+        send[which] = out[slots:].astype(BF16)
+
+
+def terms_body(acts, x0, x1, terms, pieces):
+    units = terms.shape[1] // 3
     rows, cols = pieces.shape[1] // 3, pieces.shape[2]
-    slots = x0.shape[1]
     for m in range(3):
         total = (terms[:, units * m : units * (m + 1)] + term(acts, x0, x1, m, units)).astype(BF16)
         for i, (half, place) in enumerate(PIECES):
             pieces[i, rows * m : rows * (m + 1)] = total[
                 rows * place : rows * (place + 1), cols * half : cols * (half + 1)
             ]
-    for which in range(2):
-        out = outputs(acts, weights, which) + got[which].astype(F32)
-        mine[which] = out[:slots]
-        send[which] = out[slots:].astype(BF16)
-
-
-def tokens_body(mine, got, token, count, gate, mixed, grad_tokens):
+
+
+def tokens_body(mine, core, chip, token, count, gate, mixed, grad_tokens):
     pick = pick_of(token[...], mixed.shape[0])
-    out = use_of(gate[...], count[...]) * (mine[0] + got[0].astype(F32))
-    mixed[...] = dot(pick, out.astype(BF16)).astype(BF16)
-    back = mine[1] + got[1].astype(F32)
+    out, back = [mine[i] + core[i].astype(F32) + chip[i].astype(F32) for i in range(2)]
+    mixed[...] = dot(pick, (use_of(gate[...], count[...]) * out).astype(BF16)).astype(BF16)
     grad_tokens[...] = dot(pick, back.astype(BF16)).astype(BF16)
 
 
@@ -177,21 +203,21 @@
         [((2, slots, feat), BF16), ((3 * rows, cols), BF16)],
         pick_flops,
         *(tokens, grad_out, token, count, gate, w_gate, w_up, w_down),
+        fetch=True,
     )
 
     block = lax.ppermute(block, ("wide", "narrow"), SWAP)
-    next_own = lax.ppermute(own, "wide", OTHER_CHIP)
+    chip_own = lax.ppermute(own, "wide", OTHER_CHIP)
     core_own = lax.ppermute(own, "wide", OTHER_CORE)
-    core_next = lax.ppermute(next_own, "wide", OTHER_CORE)
+    core_chip = lax.ppermute(chip_own, "wide", OTHER_CORE)
     pieces = exchange(jnp.broadcast_to(block[None], (len(PIECES),) + block.shape), "wide", OWNERS)
 
     flops = 2 * 3 * 2 * slots * feat * units
-    part_b, part_a, weights = call(
-        forward_body,
-        [((2 * slots, 3 * units), BF16)] * 2 + [((3, feat, units), BF16)],
-        2 * flops,
-        *(pieces, own, next_own, core_own, core_next),
-    )
+    wide_part = ((2 * slots, 3 * units), BF16)
+    part_1, weights = call(
+        first_body, [wide_part, ((3, feat, units), BF16)], flops, pieces, own, core_own
+    )
+    (part_2,) = call(second_body, [wide_part], flops, weights, chip_own, core_chip)
     portion = 2 * slots // N_X
     parts = (N_X, portion, 3 * units)
 
@@ -200,37 +226,38 @@
         sent = got.astype(F32).sum(axis=0).astype(BF16)
         return got, lax.ppermute(sent, "narrow", OTHER_HALF)
 
-    def activations(got, theirs):
-        (acts,) = call(act_body, [(parts, BF16)], 20 * portion * 3 * units, got, theirs)
+    def activations(got, theirs, after):
+        (acts,) = call(
+            act_body, [(parts, BF16)], 20 * portion * 3 * units, got, theirs, after=after
+        )
         return exchange(acts, "narrow", ALONG_X).reshape(2 * slots, 3 * units)
 
-    got_b, theirs_b = narrow_sum(part_b)
-    part_a, got_b = lax.optimization_barrier((part_a, got_b))
-    got_a, theirs_a = narrow_sum(part_a)
-    acts_b = activations(got_b, theirs_b)
-    acts_a = activations(got_a, theirs_a)
-
-    send, terms = call(
-        theirs_body,
-        [((2, 2 * slots, feat), BF16), ((feat, 3 * units), F32)],
+    got_1, theirs_1 = narrow_sum(part_1)
+    got_2, theirs_2 = narrow_sum(part_2)
+    acts_1 = activations(got_1, theirs_1, (got_2,))
+    acts_2 = activations(got_2, theirs_2, (acts_1,))
+
+    mine, send, terms = call(
+        near_body,
+        [((2, slots, feat), F32), ((2, slots, feat), BF16), ((feat, 3 * units), F32)],
         2 * flops,
-        *(acts_b, core_own, core_next, weights),
-    )
-    got = lax.ppermute(send, "wide", OTHER_CORE)
-    terms, mine, send = call(
-        ours_body,
-        [(pieces.shape, BF16), ((2, slots, feat), F32), ((2, slots, feat), BF16)],
-        2 * flops,
-        *(acts_a, own, next_own, weights, terms, got),
-    )
-    got = lax.ppermute(send, "wide", OTHER_CHIP)
+        *(acts_1, own, core_own, weights),
+    )
+    core = lax.ppermute(send, "wide", OTHER_CORE)
+    far, send = call(
+        far_body, [((2, slots, feat), F32), ((2, slots, feat), BF16)], flops, acts_2, weights
+    )
+    far = (far + lax.ppermute(send, "wide", OTHER_CORE).astype(F32)).astype(BF16)
+    (terms,) = call(
+        terms_body, [(pieces.shape, BF16)], flops, acts_2, chip_own, core_chip, terms
+    )
+    chip = lax.ppermute(far, "wide", OTHER_CHIP)
     terms = exchange(terms, "wide", OWNERS)
-    mixed, grad_tokens = call(
-        tokens_body, [((tok, feat), BF16)] * 2, pick_flops, *(mine, got, token, count, gate)
-    )
-    terms, mixed, grad_tokens = lax.optimization_barrier((terms, mixed, grad_tokens))
     grads = terms.astype(F32).sum(axis=0).astype(BF16)
     grads = lax.ppermute(grads, ("wide", "narrow"), SWAP_BACK).astype(F32)
+    mixed, grad_tokens = call(
+        tokens_body, [((tok, feat), BF16)] * 2, pick_flops, *(mine, core, chip, token, count, gate)
+    )
     return mixed, grad_tokens, grads[:rows], grads[rows : 2 * rows], grads[2 * rows :]
 
 

time: 212 us -> 180 us (0.85)
  the two profiles are of different devices: /device:TPU:40 before, /device:TPU:1 now
where the time goes in v4:
time: 180 us; the launch traced here: 178 us
  starting transfers between devices  103 us (57%)
  waiting for transfers between devices  47.6 us (26%)
  Pallas kernels  13.7 us (8%)
  local copies, waits for them, and re-layouts  8.99 us (5%)
  other arithmetic  3.06 us (2%)
    all_to_all x6, starting transfers between devices, exchange(): return lax.all_to_all(x, axis, 0, 0, axis_index_groups=groups)  55.8 us
    all_to_all x6, waiting for transfers between devices, exchange(): return lax.all_to_all(x, axis, 0, 0, axis_index_groups=groups)  29.3 us
    ppermute x2, starting transfers between devices, narrow_sum(): return (got, lax.ppermute(sent, 'narrow', OTHER_HALF))  14.3 us
    pallas_call x9, Pallas kernels, call(): pl.pallas_call(inner, out_shape=[jax.ShapeDtypeStruct(shape, kind) for sh...  13.7 us
    ppermute x1, waiting for transfers between devices, local(): chip = lax.ppermute(far, 'wide', OTHER_CHIP)  8.17 us
    unnamed x24, local copies, waits for them, and re-layouts  7.3 us
    ppermute x2, waiting for transfers between devices, narrow_sum(): return (got, lax.ppermute(sent, 'narrow', OTHER_HALF))  6.72 us
    ppermute x1, starting transfers between devices, local(): grads = lax.ppermute(grads, ('wide', 'narrow'), SWAP_BACK).astype(F32)  6.4 us
  transfers between devices with their start and end apart: 16, of which 10 were waited for; matrix products, arithmetic and copies ran while one was open for 2% of the time, Pallas kernels for 4%

profile of v4, /device:TPU:1, one launch (start us, length us, event | category | flops | bytes accessed | tf_op | source)
XLA Modules:
  0.0 178.0 jit_solution(6183470755152340449)
XLA Ops:
  1.3 2.5 %shard_map.119 = (bf16[2,256,512]{2,1,0:T(8,128)(2,1)}, bf16[192,128]{1,0:T(8,128)(2,1)}) custom-call(bf16[384,512]{1,0:T(8,128)(2,1)} %refs_0_.1, bf16[384,512]{1,0:T(8,128)(2,1)} %refs_1_.1, s32[1,256]{1,0:T(1,128)} %bitcast.13, s32[1,1]{1,0:T(1,128)} %bitcast.7.refs_3_, f32[1,256]{1,0:T(1,128)} %bitcast.15, bf16[64,128]{1,0:T(8,128)(2,1)} %refs_5_.1, ...), custom_call_target="tpu_custom_call" | custom-call | flops 201326592 | bytes 837636 | tf_op jit(solution)/shard_map/pallas_call | solution.py:62
  3.8 4.7 %collective-permute-start = (bf16[192,128]{1,0:T(8,128)(2,1)}, bf16[192,128]{1,0:T(8,128)(2,1)S(1)}, u32[]{:S(2)}, u32[]{:S(2)}) collective-permute-start(bf16[192,128]{1,0:T(8,128)(2,1)} %get-tuple-element.16), channel_id=1, source_target_pairs={{0,0},{1,256},{2,8},{3,264},{4,16},{5,272},{6,24},{7,280},{8,64},{... | collective-permute-start | bytes 147464 | tf_op jit(solution)/shard_map/ppermute | solution.py:209
  8.6 1.9 %collective-permute-done = bf16[192,128]{1,0:T(8,128)(2,1)S(1)} collective-permute-done((bf16[192,128]{1,0:T(8,128)(2,1)}, bf16[192,128]{1,0:T(8,128)(2,1)S(1)}, u32[]{:S(2)}, u32[]{:S(2)}) %collective-permute-start) | collective-permute-done | bytes 49184 | tf_op jit(solution)/shard_map/ppermute | solution.py:209
  11.5 20.2 %all-to-all-start = ((bf16[16,192,128]{2,1,0:T(8,128)(2,1)}), bf16[16,192,128]{2,1,0:T(8,128)(2,1)S(1)}, u32[]{:S(2)}, u32[]{:S(2)}) async-start(bf16[16,192,128]{2,1,0:T(8,128)(2,1)} %broadcast_in_dim.18), calls=%async_computation | async-start | bytes 1572864 | tf_op jit(solution)/shard_map/all_to_all | solution.py:49
  31.7 2.6 %collective-permute-start.1 = (bf16[2,256,512]{2,1,0:T(8,128)(2,1)S(1)}, bf16[2,256,512]{2,1,0:T(8,128)(2,1)S(1)}, u32[]{:S(2)}, u32[]{:S(2)}) collective-permute-start(bf16[2,256,512]{2,1,0:T(8,128)(2,1)S(1)} %copy-done.4), channel_id=1, source_target_pairs={{0,8},{8,0},{16,24},{24,16},{32,40},{40,32},{48,56},{56,48},{64,72... | collective-permute-start | bytes 1572872 | tf_op jit(solution)/shard_map/ppermute | solution.py:211
  34.4 5.3 %collective-permute-start.3 = (bf16[2,256,512]{2,1,0:T(8,128)(2,1)S(1)}, bf16[2,256,512]{2,1,0:T(8,128)(2,1)S(1)}, u32[]{:S(2)}, u32[]{:S(2)}) collective-permute-start(bf16[2,256,512]{2,1,0:T(8,128)(2,1)S(1)} %copy-done.4), channel_id=1, source_target_pairs={{0,16},{8,24},{16,0},{24,8},{32,48},{40,56},{48,32},{56,40},{64,80... | collective-permute-start | bytes 1572872 | tf_op jit(solution)/shard_map/ppermute | solution.py:210
  39.7 14.8 %all-to-all-done.refs_0_ = bf16[16,192,128]{2,1,0:T(8,128)(2,1)S(1)} async-done(((bf16[16,192,128]{2,1,0:T(8,128)(2,1)}), bf16[16,192,128]{2,1,0:T(8,128)(2,1)S(1)}, u32[]{:S(2)}, u32[]{:S(2)}) %all-to-all-start) | async-done | bytes 786464 | tf_op jit(solution)/shard_map/all_to_all | solution.py:49
  54.5 1.6 shard_map.120
  56.1 4.3 %all-to-all-start.1 = ((bf16[4,128,768]{2,1,0:T(8,128)(2,1)}), bf16[4,128,768]{2,1,0:T(8,128)(2,1)S(1)}, u32[]{:S(2)}, u32[]{:S(2)}) async-start(bf16[4,128,768]{2,1,0:T(8,128)(2,1)} %bitcast.3), calls=%async_computation.1 | async-start | bytes 1572864 | tf_op jit(solution)/shard_map/all_to_all | solution.py:49
  60.4 4.9 %collective-permute-start.4 = (bf16[2,256,512]{2,1,0:T(8,128)(2,1)S(1)}, bf16[2,256,512]{2,1,0:T(8,128)(2,1)S(1)}, u32[]{:S(2)}, u32[]{:S(2)}) collective-permute-start(bf16[2,256,512]{2,1,0:T(8,128)(2,1)S(1)} %collective-permute-done.3.refs_1_), channel_id=1, source_target_pairs={{0,8},{8,0},{16,24},{24,16},{32,40},{40,32},{48,56},{56,48},{64,72... | collective-permute-start | bytes 1572872 | tf_op jit(solution)/shard_map/ppermute | solution.py:212
  65.4 1.5 collective-permute-done.4.refs_2_
  66.9 1.5 shard_map.121
  69.5 3.5 %all-to-all-start.2 = ((bf16[4,128,768]{2,1,0:T(8,128)(2,1)}), bf16[4,128,768]{2,1,0:T(8,128)(2,1)S(1)}, u32[]{:S(2)}, u32[]{:S(2)}) async-start(bf16[4,128,768]{2,1,0:T(8,128)(2,1)} %bitcast.4), calls=%async_computation.2 | async-start | bytes 1572864 | tf_op jit(solution)/shard_map/all_to_all | solution.py:49
  73.8 7.1 %collective-permute-start.2 = (bf16[128,768]{1,0:T(8,128)(2,1)}, bf16[128,768]{1,0:T(8,128)(2,1)}, u32[]{:S(2)}, u32[]{:S(2)}) collective-permute-start(bf16[128,768]{1,0:T(8,128)(2,1)} %reduce_sum.36), channel_id=1, source_target_pairs={{0,1},{1,0},{2,3},{3,2},{4,5},{5,4},{6,7},{7,6},{8,9},{9,8},{10,11... | collective-permute-start | bytes 589832 | tf_op jit(solution)/shard_map/ppermute | solution.py:227
  81.3 3.2 %collective-permute-done.2.refs_1_ = bf16[128,768]{1,0:T(8,128)(2,1)} collective-permute-done((bf16[128,768]{1,0:T(8,128)(2,1)}, bf16[128,768]{1,0:T(8,128)(2,1)}, u32[]{:S(2)}, u32[]{:S(2)}) %collective-permute-start.2) | collective-permute-done | bytes 196640 | tf_op jit(solution)/shard_map/ppermute | solution.py:227
  84.5 2.0 %shard_map.122 = bf16[4,128,768]{2,1,0:T(8,128)(2,1)} custom-call(bf16[4,128,768]{2,1,0:T(8,128)(2,1)S(1)} %all-to-all-done.1.refs_0_, bf16[128,768]{1,0:T(8,128)(2,1)} %collective-permute-done.2.refs_1_, bf16[4,128,768]{2,1,0:T(8,128)(2,1)S(1)} %all-to-all-done.2.refs_2_.refs_0_), custom_call_target="tpu_custom_call" | custom-call | flops 1966080 | bytes 983040 | tf_op jit(solution)/shard_map/pallas_call | solution.py:62
  86.5 4.2 %all-to-all-start.3 = ((bf16[4,128,768]{2,1,0:T(8,128)(2,1)}), bf16[4,128,768]{2,1,0:T(8,128)(2,1)S(1)}, u32[]{:S(2)}, u32[]{:S(2)}) async-start(bf16[4,128,768]{2,1,0:T(8,128)(2,1)} %shard_map.122), calls=%async_computation.3 | async-start | bytes 1572864 | tf_op jit(solution)/shard_map/all_to_all | solution.py:49
  91.5 7.1 %collective-permute-start.6 = (bf16[128,768]{1,0:T(8,128)(2,1)}, bf16[128,768]{1,0:T(8,128)(2,1)S(1)}, u32[]{:S(2)}, u32[]{:S(2)}) collective-permute-start(bf16[128,768]{1,0:T(8,128)(2,1)} %reduce_sum.37), channel_id=1, source_target_pairs={{0,1},{1,0},{2,3},{3,2},{4,5},{5,4},{6,7},{7,6},{8,9},{9,8},{10,11... | collective-permute-start | bytes 589832 | tf_op jit(solution)/shard_map/ppermute | solution.py:227
  98.7 3.5 %collective-permute-done.6.refs_1_ = bf16[128,768]{1,0:T(8,128)(2,1)S(1)} collective-permute-done((bf16[128,768]{1,0:T(8,128)(2,1)}, bf16[128,768]{1,0:T(8,128)(2,1)S(1)}, u32[]{:S(2)}, u32[]{:S(2)}) %collective-permute-start.6) | collective-permute-done | bytes 196640 | tf_op jit(solution)/shard_map/ppermute | solution.py:227
  104.8 4.2 %all-to-all-start.4 = ((bf16[4,128,768]{2,1,0:T(8,128)(2,1)}), bf16[4,128,768]{2,1,0:T(8,128)(2,1)S(1)}, u32[]{:S(2)}, u32[]{:S(2)}) async-start(bf16[4,128,768]{2,1,0:T(8,128)(2,1)} %shard_map.124), calls=%async_computation.4 | async-start | bytes 1572864 | tf_op jit(solution)/shard_map/all_to_all | solution.py:49
  111.2 1.5 shard_map.123
  114.9 2.5 %all-to-all-done.4 = bf16[4,128,768]{2,1,0:T(8,128)(2,1)S(1)} async-done(((bf16[4,128,768]{2,1,0:T(8,128)(2,1)}), bf16[4,128,768]{2,1,0:T(8,128)(2,1)S(1)}, u32[]{:S(2)}, u32[]{:S(2)}) %all-to-all-start.4) | async-done | bytes 786464 | tf_op jit(solution)/shard_map/all_to_all | solution.py:49
  117.4 1.4 copy-done.1
  118.8 1.6 shard_map.127
  120.4 19.3 %all-to-all-start.5 = ((bf16[16,192,128]{2,1,0:T(8,128)(2,1)}), bf16[16,192,128]{2,1,0:T(8,128)(2,1)}, u32[]{:S(2)}, u32[]{:S(2)}) async-start(bf16[16,192,128]{2,1,0:T(8,128)(2,1)} %shard_map.127), calls=%async_computation.5 | async-start | bytes 1572864 | tf_op jit(solution)/shard_map/all_to_all | solution.py:49
  140.3 5.2 %collective-permute-start.7 = (bf16[2,256,512]{2,1,0:T(8,128)(2,1)S(1)}, bf16[2,256,512]{2,1,0:T(8,128)(2,1)S(1)}, u32[]{:S(2)}, u32[]{:S(2)}) collective-permute-start(bf16[2,256,512]{2,1,0:T(8,128)(2,1)S(1)} %get-tuple-element.23), channel_id=1, source_target_pairs={{0,8},{8,0},{16,24},{24,16},{32,40},{40,32},{48,56},{56,48},{64,72... | collective-permute-start | bytes 1572872 | tf_op jit(solution)/shard_map/ppermute | solution.py:250
  145.6 1.9 %collective-permute-start.5 = (bf16[2,256,512]{2,1,0:T(8,128)(2,1)}, bf16[2,256,512]{2,1,0:T(8,128)(2,1)S(1)}, u32[]{:S(2)}, u32[]{:S(2)}) collective-permute-start(bf16[2,256,512]{2,1,0:T(8,128)(2,1)} %get-tuple-element.21), channel_id=1, source_target_pairs={{0,8},{8,0},{16,24},{24,16},{32,40},{40,32},{48,56},{56,48},{64,72... | collective-permute-start | bytes 1572872 | tf_op jit(solution)/shard_map/ppermute | solution.py:246
  147.7 1.9 %collective-permute-start.8 = (bf16[2,256,512]{2,1,0:T(8,128)(2,1)S(1)}, bf16[2,256,512]{2,1,0:T(8,128)(2,1)S(1)}, u32[]{:S(2)}, u32[]{:S(2)}) collective-permute-start(bf16[2,256,512]{2,1,0:T(8,128)(2,1)S(1)} %add_convert_fusion), channel_id=1, source_target_pairs={{0,16},{8,24},{16,0},{24,8},{32,48},{40,56},{48,32},{56,40},{64,80... | collective-permute-start | bytes 1572872 | tf_op jit(solution)/shard_map/ppermute | solution.py:254
  149.6 10.5 %all-to-all-done.5 = bf16[16,192,128]{2,1,0:T(8,128)(2,1)} async-done(((bf16[16,192,128]{2,1,0:T(8,128)(2,1)}), bf16[16,192,128]{2,1,0:T(8,128)(2,1)}, u32[]{:S(2)}, u32[]{:S(2)}) %all-to-all-start.5) | async-done | bytes 786464 | tf_op jit(solution)/shard_map/all_to_all | solution.py:49
  161.4 6.4 %collective-permute-start.9 = (bf16[192,128]{1,0:T(8,128)(2,1)S(1)}, bf16[192,128]{1,0:T(8,128)(2,1)S(1)}, u32[]{:S(2)}, u32[]{:S(2)}) collective-permute-start(bf16[192,128]{1,0:T(8,128)(2,1)S(1)} %reduce_sum.38), channel_id=1, source_target_pairs={{0,0},{256,1},{8,2},{264,3},{16,4},{272,5},{24,6},{280,7},{64,8},{... | collective-permute-start | bytes 147464 | tf_op jit(solution)/shard_map/ppermute | solution.py:257
  167.8 8.2 %collective-permute-done.8.refs_2_ = bf16[2,256,512]{2,1,0:T(8,128)(2,1)S(1)} collective-permute-done((bf16[2,256,512]{2,1,0:T(8,128)(2,1)S(1)}, bf16[2,256,512]{2,1,0:T(8,128)(2,1)S(1)}, u32[]{:S(2)}, u32[]{:S(2)}) %collective-permute-start.8) | collective-permute-done | bytes 524320 | tf_op jit(solution)/shard_map/ppermute | solution.py:254
  176.0 1.3 shard_map.126
  (39 shorter events, 13.8 us)
Async XLA Ops:
  3.8 27.9 %copy-start.4 = (bf16[2,256,512]{2,1,0:T(8,128)(2,1)S(1)}, bf16[2,256,512]{2,1,0:T(8,128)(2,1)}, u32[]{:S(2)}) copy-start(bf16[2,256,512]{2,1,0:T(8,128)(2,1)} %get-tuple-element.17.refs_1_) | copy-start | bytes 1572868
  3.8 6.6 %collective-permute-start = (bf16[192,128]{1,0:T(8,128)(2,1)}, bf16[192,128]{1,0:T(8,128)(2,1)S(1)}, u32[]{:S(2)}, u32[]{:S(2)}) collective-permute-start(bf16[192,128]{1,0:T(8,128)(2,1)} %get-tuple-element.16), channel_id=1, source_target_pairs={{0,0},{1,256},{2,8},{3,264},{4,16},{5,272},{6,24},{7,280},{8,64},{... | collective-permute-start | bytes 147464 | tf_op jit(solution)/shard_map/ppermute | solution.py:209
  11.5 43.0 %all-to-all-start = ((bf16[16,192,128]{2,1,0:T(8,128)(2,1)}), bf16[16,192,128]{2,1,0:T(8,128)(2,1)S(1)}, u32[]{:S(2)}, u32[]{:S(2)}) async-start(bf16[16,192,128]{2,1,0:T(8,128)(2,1)} %broadcast_in_dim.18), calls=%async_computation | async-start | bytes 1572864 | tf_op jit(solution)/shard_map/all_to_all | solution.py:49
  31.7 8.0 %collective-permute-start.1 = (bf16[2,256,512]{2,1,0:T(8,128)(2,1)S(1)}, bf16[2,256,512]{2,1,0:T(8,128)(2,1)S(1)}, u32[]{:S(2)}, u32[]{:S(2)}) collective-permute-start(bf16[2,256,512]{2,1,0:T(8,128)(2,1)S(1)} %copy-done.4), channel_id=1, source_target_pairs={{0,8},{8,0},{16,24},{24,16},{32,40},{40,32},{48,56},{56,48},{64,72... | collective-permute-start | bytes 1572872 | tf_op jit(solution)/shard_map/ppermute | solution.py:211
  34.4 26.1 %collective-permute-start.3 = (bf16[2,256,512]{2,1,0:T(8,128)(2,1)S(1)}, bf16[2,256,512]{2,1,0:T(8,128)(2,1)S(1)}, u32[]{:S(2)}, u32[]{:S(2)}) collective-permute-start(bf16[2,256,512]{2,1,0:T(8,128)(2,1)S(1)} %copy-done.4), channel_id=1, source_target_pairs={{0,16},{8,24},{16,0},{24,8},{32,48},{40,56},{48,32},{56,40},{64,80... | collective-permute-start | bytes 1572872 | tf_op jit(solution)/shard_map/ppermute | solution.py:210
  39.7 16.4 %copy-start.6 = (bf16[2,256,512]{2,1,0:T(8,128)(2,1)}, bf16[2,256,512]{2,1,0:T(8,128)(2,1)S(1)}, u32[]{:S(2)}) copy-start(bf16[2,256,512]{2,1,0:T(8,128)(2,1)S(1)} %collective-permute-done.1.refs_2_) | copy-start | bytes 1572868
  56.1 13.3 %all-to-all-start.1 = ((bf16[4,128,768]{2,1,0:T(8,128)(2,1)}), bf16[4,128,768]{2,1,0:T(8,128)(2,1)S(1)}, u32[]{:S(2)}, u32[]{:S(2)}) async-start(bf16[4,128,768]{2,1,0:T(8,128)(2,1)} %bitcast.3), calls=%async_computation.1 | async-start | bytes 1572864 | tf_op jit(solution)/shard_map/all_to_all | solution.py:49
  60.4 6.4 %collective-permute-start.4 = (bf16[2,256,512]{2,1,0:T(8,128)(2,1)S(1)}, bf16[2,256,512]{2,1,0:T(8,128)(2,1)S(1)}, u32[]{:S(2)}, u32[]{:S(2)}) collective-permute-start(bf16[2,256,512]{2,1,0:T(8,128)(2,1)S(1)} %collective-permute-done.3.refs_1_), channel_id=1, source_target_pairs={{0,8},{8,0},{16,24},{24,16},{32,40},{40,32},{48,56},{56,48},{64,72... | collective-permute-start | bytes 1572872 | tf_op jit(solution)/shard_map/ppermute | solution.py:212
  69.5 11.8 %all-to-all-start.2 = ((bf16[4,128,768]{2,1,0:T(8,128)(2,1)}), bf16[4,128,768]{2,1,0:T(8,128)(2,1)S(1)}, u32[]{:S(2)}, u32[]{:S(2)}) async-start(bf16[4,128,768]{2,1,0:T(8,128)(2,1)} %bitcast.4), calls=%async_computation.2 | async-start | bytes 1572864 | tf_op jit(solution)/shard_map/all_to_all | solution.py:49
  73.8 10.7 %collective-permute-start.2 = (bf16[128,768]{1,0:T(8,128)(2,1)}, bf16[128,768]{1,0:T(8,128)(2,1)}, u32[]{:S(2)}, u32[]{:S(2)}) collective-permute-start(bf16[128,768]{1,0:T(8,128)(2,1)} %reduce_sum.36), channel_id=1, source_target_pairs={{0,1},{1,0},{2,3},{3,2},{4,5},{5,4},{6,7},{7,6},{8,9},{9,8},{10,11... | collective-permute-start | bytes 589832 | tf_op jit(solution)/shard_map/ppermute | solution.py:227
  86.5 16.3 %all-to-all-start.3 = ((bf16[4,128,768]{2,1,0:T(8,128)(2,1)}), bf16[4,128,768]{2,1,0:T(8,128)(2,1)S(1)}, u32[]{:S(2)}, u32[]{:S(2)}) async-start(bf16[4,128,768]{2,1,0:T(8,128)(2,1)} %shard_map.122), calls=%async_computation.3 | async-start | bytes 1572864 | tf_op jit(solution)/shard_map/all_to_all | solution.py:49
  91.5 10.6 %collective-permute-start.6 = (bf16[128,768]{1,0:T(8,128)(2,1)}, bf16[128,768]{1,0:T(8,128)(2,1)S(1)}, u32[]{:S(2)}, u32[]{:S(2)}) collective-permute-start(bf16[128,768]{1,0:T(8,128)(2,1)} %reduce_sum.37), channel_id=1, source_target_pairs={{0,1},{1,0},{2,3},{3,2},{4,5},{5,4},{6,7},{7,6},{8,9},{9,8},{10,11... | collective-permute-start | bytes 589832 | tf_op jit(solution)/shard_map/ppermute | solution.py:227
  102.2 0.7 copy-start.8
  102.8 0.9 copy-start.9
  104.8 12.6 %all-to-all-start.4 = ((bf16[4,128,768]{2,1,0:T(8,128)(2,1)}), bf16[4,128,768]{2,1,0:T(8,128)(2,1)S(1)}, u32[]{:S(2)}, u32[]{:S(2)}) async-start(bf16[4,128,768]{2,1,0:T(8,128)(2,1)} %shard_map.124), calls=%async_computation.4 | async-start | bytes 1572864 | tf_op jit(solution)/shard_map/all_to_all | solution.py:49
  109.1 1.0 copy-start.5
  110.1 1.0 copy-start.7
  112.7 1.2 copy-start
  113.9 1.0 copy-start.2
  117.4 1.4 copy-start.1
  120.4 39.8 %all-to-all-start.5 = ((bf16[16,192,128]{2,1,0:T(8,128)(2,1)}), bf16[16,192,128]{2,1,0:T(8,128)(2,1)}, u32[]{:S(2)}, u32[]{:S(2)}) async-start(bf16[16,192,128]{2,1,0:T(8,128)(2,1)} %shard_map.127), calls=%async_computation.5 | async-start | bytes 1572864 | tf_op jit(solution)/shard_map/all_to_all | solution.py:49
  140.3 35.7 %copy-start.3 = (f32[2,256,512]{2,1,0:T(8,128)S(1)}, f32[2,256,512]{2,1,0:T(8,128)}, u32[]{:S(2)}) copy-start(f32[2,256,512]{2,1,0:T(8,128)} %copy-done.2) | copy-start | bytes 3145732
  140.3 35.7 %copy-start.10 = (s32[256]{0:T(256)S(1)}, s32[256]{0:T(256)}, u32[]{:S(2)}) copy-start(s32[256]{0:T(256)} %param.10) | copy-start | bytes 3076
  140.3 35.7 %copy-start.11 = (f32[256]{0:T(256)S(1)}, f32[256]{0:T(256)}, u32[]{:S(2)}) copy-start(f32[256]{0:T(256)} %param.12) | copy-start | bytes 3076
  140.3 7.2 %collective-permute-start.7 = (bf16[2,256,512]{2,1,0:T(8,128)(2,1)S(1)}, bf16[2,256,512]{2,1,0:T(8,128)(2,1)S(1)}, u32[]{:S(2)}, u32[]{:S(2)}) collective-permute-start(bf16[2,256,512]{2,1,0:T(8,128)(2,1)S(1)} %get-tuple-element.23), channel_id=1, source_target_pairs={{0,8},{8,0},{16,24},{24,16},{32,40},{40,32},{48,56},{56,48},{64,72... | collective-permute-start | bytes 1572872 | tf_op jit(solution)/shard_map/ppermute | solution.py:250
  145.6 22.2 %collective-permute-start.5 = (bf16[2,256,512]{2,1,0:T(8,128)(2,1)}, bf16[2,256,512]{2,1,0:T(8,128)(2,1)S(1)}, u32[]{:S(2)}, u32[]{:S(2)}) collective-permute-start(bf16[2,256,512]{2,1,0:T(8,128)(2,1)} %get-tuple-element.21), channel_id=1, source_target_pairs={{0,8},{8,0},{16,24},{24,16},{32,40},{40,32},{48,56},{56,48},{64,72... | collective-permute-start | bytes 1572872 | tf_op jit(solution)/shard_map/ppermute | solution.py:246
  147.7 28.3 %collective-permute-start.8 = (bf16[2,256,512]{2,1,0:T(8,128)(2,1)S(1)}, bf16[2,256,512]{2,1,0:T(8,128)(2,1)S(1)}, u32[]{:S(2)}, u32[]{:S(2)}) collective-permute-start(bf16[2,256,512]{2,1,0:T(8,128)(2,1)S(1)} %add_convert_fusion), channel_id=1, source_target_pairs={{0,16},{8,24},{16,0},{24,8},{32,48},{40,56},{48,32},{56,40},{64,80... | collective-permute-start | bytes 1572872 | tf_op jit(solution)/shard_map/ppermute | solution.py:254
  161.4 15.9 %collective-permute-start.9 = (bf16[192,128]{1,0:T(8,128)(2,1)S(1)}, bf16[192,128]{1,0:T(8,128)(2,1)S(1)}, u32[]{:S(2)}, u32[]{:S(2)}) collective-permute-start(bf16[192,128]{1,0:T(8,128)(2,1)S(1)} %reduce_sum.38), channel_id=1, source_target_pairs={{0,0},{256,1},{8,2},{264,3},{16,4},{272,5},{24,6},{280,7},{64,8},{... | collective-permute-start | bytes 147464 | tf_op jit(solution)/shard_map/ppermute | solution.py:257

commit v5 on v4

--- a/solution.py
+++ b/solution.py
@@ -49,7 +49,7 @@
     return lax.all_to_all(x, axis, 0, 0, axis_index_groups=groups)
 
 
-def call(body, outs, flops, *args, after=(), fetch=False):
+def call(body, outs, flops, *args, after=(), fetch=False, grant=12):
     size = sum(a.size * a.dtype.itemsize for a in args)
     vmem, anywhere = pl.BlockSpec(memory_space=pltpu.VMEM), pl.BlockSpec(memory_space=pl.ANY)
     scratch = ()
@@ -65,7 +65,7 @@
         in_specs=[pl.BlockSpec(memory_space=pltpu.HBM) if fetch else vmem] * len(args) + [anywhere] * len(after),
         out_specs=[vmem] * len(outs),
         scratch_shapes=scratch,
-        compiler_params=pltpu.CompilerParams(vmem_limit_bytes=(60 if fetch else 12) * 1024 * 1024),
+        compiler_params=pltpu.CompilerParams(vmem_limit_bytes=grant * 1024 * 1024),
         cost_estimate=pl.CostEstimate(flops=flops, bytes_accessed=size, transcendentals=0),
     )(*args, *after)
 
@@ -86,7 +86,7 @@
 
 
 def rows_body(*refs):
-    sources, (own, block), held, sem = refs[:8], refs[8:10], refs[10:18], refs[18]
+    sources, (own, x, g, block), held, sem = refs[:8], refs[8:12], refs[12:20], refs[20]
     copies = [pltpu.make_async_copy(s, h, sem.at[i]) for i, (s, h) in enumerate(zip(sources, held))]
     for copy in copies:
         copy.start()
@@ -98,32 +98,39 @@
     for i in (2, 3, 4, 0):
         copies[i].wait()
     pick = pick_of(token[...], tokens.shape[0])
-    own[0] = dot(pick, tokens[...], FIRST).astype(BF16)
+    x[...] = dot(pick, tokens[...], FIRST).astype(BF16)
+    own[0] = x[...]
     copies[1].wait()
-    own[1] = (use_of(gate[...], count[...]) * dot(pick, grad_out[...], FIRST)).astype(BF16)
-
-
-def products(part, x0, x1, weights):
-    slots, units = x0.shape[1], weights.shape[2]
-    for which, x in enumerate((x0, x1)):
+    g[...] = (use_of(gate[...], count[...]) * dot(pick, grad_out[...], FIRST)).astype(BF16)
+    own[1] = g[...]
+
+
+def copies_body(block, copies):
+    for i in range(copies.shape[0]):
+        copies[i] = block[...]
+
+
+def products(part, held, weights):
+    slots, units = held[0][0].shape[0], weights.shape[2]
+    for which, pair in enumerate(held):
         for m in range(3):
             part[slots * which : slots * (which + 1), units * m : units * (m + 1)] = dot(
-                x[m // 2], weights[m]
+                pair[m // 2][...], weights[m]
             ).astype(BF16)
 
 
-def first_body(pieces, x0, x1, part, weights):
+def far_products_body(pieces, x0, g0, x1, g1, part, weights):
     rows, cols = pieces.shape[1] // 3, pieces.shape[2]
     for i, (half, place) in enumerate(PIECES):
         for m in range(3):
             weights[m, rows * place : rows * (place + 1), cols * half : cols * (half + 1)] = pieces[
                 i, rows * m : rows * (m + 1)
             ]
-    products(part, x0, x1, weights)
-
-
-def second_body(weights, x0, x1, part):
-    products(part, x0, x1, weights)
+    products(part, ((x0, g0), (x1, g1)), weights)
+
+
+def near_products_body(weights, own, core, part):
+    products(part, [(held.at[0], held.at[1]) for held in (own, core)], weights)
 
 
 def act_body(got, theirs, acts):
@@ -150,23 +157,7 @@
     return dot(acts[:, :units], weights[0], LAST) + dot(acts[:, units : 2 * units], weights[1], LAST)
 
 
-def term(acts, x0, x1, m, units):
-    slots = x0.shape[1]
-    cut = slice(units * m, units * (m + 1))
-    return dot(x0[m // 2], acts[:slots, cut], FIRST) + dot(x1[m // 2], acts[slots:, cut], FIRST)
-
-
-def near_body(acts, x0, x1, weights, mine, send, terms):
-    units, slots = weights.shape[2], x0.shape[1]
-    for which in range(2):
-        out = outputs(acts, weights, which)
-        mine[which] = out[:slots]
-        send[which] = out[slots:].astype(BF16)
-    for m in range(3):
-        terms[:, units * m : units * (m + 1)] = term(acts, x0, x1, m, units)
-
-
-def far_body(acts, weights, mine, send):
+def outputs_body(acts, weights, mine, send):
     slots = mine.shape[1]
     for which in range(2):
         out = outputs(acts, weights, which)
@@ -174,11 +165,34 @@
         send[which] = out[slots:].astype(BF16)
 
 
-def terms_body(acts, x0, x1, terms, pieces):
+def term(acts, held, m):
+    units, slots = acts.shape[1] // 3, held[0][0].shape[0]
+    cut = slice(units * m, units * (m + 1))
+    (a, b) = [held[i][m // 2][...] for i in range(2)]
+    return dot(a, acts[:slots, cut], FIRST) + dot(b, acts[slots:, cut], FIRST)
+
+
+def far_terms_body(acts, x0, g0, x1, g1, terms):
+    units = acts.shape[1] // 3
+    for m in range(3):
+        terms[:, units * m : units * (m + 1)] = term(acts, ((x0, g0), (x1, g1)), m)
+
+
+def near_terms_body(*refs):
+    sources, pieces, held, sem = refs[:4], refs[4], refs[5:9], refs[9]
+    copies = [pltpu.make_async_copy(s, h, sem.at[i]) for i, (s, h) in enumerate(zip(sources, held))]
+    for copy in copies:
+        copy.start()
+    acts, own, core, terms = held
     units = terms.shape[1] // 3
     rows, cols = pieces.shape[1] // 3, pieces.shape[2]
+    for i in range(3):
+        copies[i].wait()
     for m in range(3):
-        total = (terms[:, units * m : units * (m + 1)] + term(acts, x0, x1, m, units)).astype(BF16)
+        total = term(acts, [(ref.at[0], ref.at[1]) for ref in (own, core)], m)
+        if m == 0:
+            copies[3].wait()
+        total = (total + terms[:, units * m : units * (m + 1)]).astype(BF16)
         for i, (half, place) in enumerate(PIECES):
             pieces[i, rows * m : rows * (m + 1)] = total[
                 rows * place : rows * (place + 1), cols * half : cols * (half + 1)
@@ -198,26 +212,34 @@
     units = 2 * cols
     token, gate, count = slot_token[None], slot_gate[None], slot_count[None]
     pick_flops = 4 * slots * tok * feat
-    own, block = call(
+    own_shape = (slots, feat)
+    own, x, g, block = call(
         rows_body,
-        [((2, slots, feat), BF16), ((3 * rows, cols), BF16)],
+        [((2, slots, feat), BF16), (own_shape, BF16), (own_shape, BF16), ((3 * rows, cols), BF16)],
         pick_flops,
         *(tokens, grad_out, token, count, gate, w_gate, w_up, w_down),
         fetch=True,
+        grant=60,
     )
 
     block = lax.ppermute(block, ("wide", "narrow"), SWAP)
-    chip_own = lax.ppermute(own, "wide", OTHER_CHIP)
+    chip_x = lax.ppermute(x, "wide", OTHER_CHIP)
     core_own = lax.ppermute(own, "wide", OTHER_CORE)
-    core_chip = lax.ppermute(chip_own, "wide", OTHER_CORE)
-    pieces = exchange(jnp.broadcast_to(block[None], (len(PIECES),) + block.shape), "wide", OWNERS)
+    (pieces,) = call(
+        copies_body, [((len(PIECES),) + block.shape, BF16)], 0, block, after=(chip_x, core_own)
+    )
+    pieces = exchange(pieces, "wide", OWNERS)
+    chip_g = lax.ppermute(g, "wide", OTHER_CHIP)
+    core_x = lax.ppermute(chip_x, "wide", OTHER_CORE)
+    core_g = lax.ppermute(chip_g, "wide", OTHER_CORE)
+    far = (chip_x, chip_g, core_x, core_g)
 
     flops = 2 * 3 * 2 * slots * feat * units
     wide_part = ((2 * slots, 3 * units), BF16)
-    part_1, weights = call(
-        first_body, [wide_part, ((3, feat, units), BF16)], flops, pieces, own, core_own
-    )
-    (part_2,) = call(second_body, [wide_part], flops, weights, chip_own, core_chip)
+    part_far, weights = call(
+        far_products_body, [wide_part, ((3, feat, units), BF16)], flops, pieces, *far
+    )
+    (part_near,) = call(near_products_body, [wide_part], flops, weights, own, core_own)
     portion = 2 * slots // N_X
     parts = (N_X, portion, 3 * units)
 
@@ -232,27 +254,26 @@
         )
         return exchange(acts, "narrow", ALONG_X).reshape(2 * slots, 3 * units)
 
-    got_1, theirs_1 = narrow_sum(part_1)
-    got_2, theirs_2 = narrow_sum(part_2)
-    acts_1 = activations(got_1, theirs_1, (got_2,))
-    acts_2 = activations(got_2, theirs_2, (acts_1,))
-
-    mine, send, terms = call(
-        near_body,
-        [((2, slots, feat), F32), ((2, slots, feat), BF16), ((feat, 3 * units), F32)],
-        2 * flops,
-        *(acts_1, own, core_own, weights),
-    )
+    got_far, theirs_far = narrow_sum(part_far)
+    got_near, theirs_near = narrow_sum(part_near)
+    acts_far = activations(got_far, theirs_far, (got_near,))
+    acts_near = activations(got_near, theirs_near, (acts_far,))
+
+    out_shapes = [((2, slots, feat), F32), ((2, slots, feat), BF16)]
+    chip, send = call(outputs_body, out_shapes, flops, acts_far, weights)
+    chip = (chip + lax.ppermute(send, "wide", OTHER_CORE).astype(F32)).astype(BF16)
+    chip = lax.ppermute(chip, "wide", OTHER_CHIP)
+    (terms,) = call(far_terms_body, [((feat, 3 * units), F32)], flops, acts_far, *far)
+    (terms,) = call(
+        near_terms_body,
+        [(pieces.shape, BF16)],
+        flops,
+        *(acts_near, own, core_own, terms),
+        fetch=True,
+    )
+    terms = exchange(terms, "wide", OWNERS)
+    mine, send = call(outputs_body, out_shapes, flops, acts_near, weights)
     core = lax.ppermute(send, "wide", OTHER_CORE)
-    far, send = call(
-        far_body, [((2, slots, feat), F32), ((2, slots, feat), BF16)], flops, acts_2, weights
-    )
-    far = (far + lax.ppermute(send, "wide", OTHER_CORE).astype(F32)).astype(BF16)
-    (terms,) = call(
-        terms_body, [(pieces.shape, BF16)], flops, acts_2, chip_own, core_chip, terms
-    )
-    chip = lax.ppermute(far, "wide", OTHER_CHIP)
-    terms = exchange(terms, "wide", OWNERS)
     grads = terms.astype(F32).sum(axis=0).astype(BF16)
     grads = lax.ppermute(grads, ("wide", "narrow"), SWAP_BACK).astype(F32)
     mixed, grad_tokens = call(

time: 180 us -> 191 us (1.061)
  the two profiles are of different devices: /device:TPU:1 before, /device:TPU:104 now
where the time goes in v5:
time: 191 us; the launch traced here: 190 us
  starting transfers between devices  82.2 us (43%)
  waiting for transfers between devices  76.9 us (40%)
  local copies, waits for them, and re-layouts  16 us (8%)
  Pallas kernels  10.4 us (5%)
  other arithmetic  3.04 us (2%)
    all_to_all x6, waiting for transfers between devices, exchange(): return lax.all_to_all(x, axis, 0, 0, axis_index_groups=groups)  39.4 us
    all_to_all x6, starting transfers between devices, exchange(): return lax.all_to_all(x, axis, 0, 0, axis_index_groups=groups)  39.1 us
    unnamed x40, local copies, waits for them, and re-layouts  15.4 us
    ppermute x1, starting transfers between devices, local(): block = lax.ppermute(block, ('wide', 'narrow'), SWAP)  13.6 us
    ppermute x1, waiting for transfers between devices, local(): grads = lax.ppermute(grads, ('wide', 'narrow'), SWAP_BACK).astype(F32)  12.4 us
    ppermute x2, starting transfers between devices, narrow_sum(): return (got, lax.ppermute(sent, 'narrow', OTHER_HALF))  11.6 us
    pallas_call x11, Pallas kernels, call(): pl.pallas_call(inner, out_shape=[jax.ShapeDtypeStruct(shape, kind) for sh...  10.4 us
    ppermute x2, waiting for transfers between devices, narrow_sum(): return (got, lax.ppermute(sent, 'narrow', OTHER_HALF))  10.2 us
  transfers between devices with their start and end apart: 18, of which 13 were waited for; matrix products, arithmetic and copies ran while one was open for 2% of the time, Pallas kernels for 2%

profile of v5, /device:TPU:104, one launch (start us, length us, event | category | flops | bytes accessed | tf_op | source)
XLA Modules:
  0.0 190.2 jit_solution(8740394705500765758)
XLA Ops:
  1.3 2.6 %shard_map.119 = (bf16[2,256,512]{2,1,0:T(8,128)(2,1)}, bf16[256,512]{1,0:T(8,128)(2,1)}, bf16[256,512]{1,0:T(8,128)(2,1)}, bf16[192,128]{1,0:T(8,128)(2,1)}) custom-call(bf16[384,512]{1,0:T(8,128)(2,1)} %refs_0_.1, bf16[384,512]{1,0:T(8,128)(2,1)} %refs_1_.1, s32[1,256]{1,0:T(1,128)} %bitcast.16, s32[1,1]{1,0:T(1,128)} %bitcast.7.refs_3_, ...), custom_call_target="tpu_custom_call" | custom-call | flops 201326592 | bytes 837636 | tf_op jit(solution)/shard_map/pallas_call | solution.py:62
  3.9 1.9 %collective-permute-start.2 = (bf16[2,256,512]{2,1,0:T(8,128)(2,1)}, bf16[2,256,512]{2,1,0:T(8,128)(2,1)S(1)}, u32[]{:S(2)}, u32[]{:S(2)}) collective-permute-start(bf16[2,256,512]{2,1,0:T(8,128)(2,1)} %get-tuple-element.19.refs_1_), channel_id=1, source_target_pairs={{0,8},{8,0},{16,24},{24,16},{32,40},{40,32},{48,56},{56,48},{64,72... | collective-permute-start | bytes 1572872 | tf_op jit(solution)/shard_map/ppermute | solution.py:227
  5.8 1.9 %collective-permute-start.1 = (bf16[256,512]{1,0:T(8,128)(2,1)}, bf16[256,512]{1,0:T(8,128)(2,1)S(1)}, u32[]{:S(2)}, u32[]{:S(2)}) collective-permute-start(bf16[256,512]{1,0:T(8,128)(2,1)} %get-tuple-element.18), channel_id=1, source_target_pairs={{0,16},{8,24},{16,0},{24,8},{32,48},{40,56},{48,32},{56,40},{64,80... | collective-permute-start | bytes 786440 | tf_op jit(solution)/shard_map/ppermute | solution.py:226
  7.7 13.6 %collective-permute-start = (bf16[192,128]{1,0:T(8,128)(2,1)}, bf16[192,128]{1,0:T(8,128)(2,1)S(1)}, u32[]{:S(2)}, u32[]{:S(2)}) collective-permute-start(bf16[192,128]{1,0:T(8,128)(2,1)} %get-tuple-element.17), channel_id=1, source_target_pairs={{0,0},{1,256},{2,8},{3,264},{4,16},{5,272},{6,24},{7,280},{8,64},{... | collective-permute-start | bytes 147464 | tf_op jit(solution)/shard_map/ppermute | solution.py:225
  21.3 2.0 %collective-permute-done.refs_0_ = bf16[192,128]{1,0:T(8,128)(2,1)S(1)} collective-permute-done((bf16[192,128]{1,0:T(8,128)(2,1)}, bf16[192,128]{1,0:T(8,128)(2,1)S(1)}, u32[]{:S(2)}, u32[]{:S(2)}) %collective-permute-start) | collective-permute-done | bytes 49184 | tf_op jit(solution)/shard_map/ppermute | solution.py:225
  24.4 11.9 %all-to-all-start = ((bf16[16,192,128]{2,1,0:T(8,128)(2,1)}), bf16[16,192,128]{2,1,0:T(8,128)(2,1)S(1)}, u32[]{:S(2)}, u32[]{:S(2)}) async-start(bf16[16,192,128]{2,1,0:T(8,128)(2,1)} %shard_map.120), calls=%async_computation | async-start | bytes 1572864 | tf_op jit(solution)/shard_map/all_to_all | solution.py:49
  36.3 2.5 %collective-permute-start.3 = (bf16[256,512]{1,0:T(8,128)(2,1)}, bf16[256,512]{1,0:T(8,128)(2,1)S(1)}, u32[]{:S(2)}, u32[]{:S(2)}) collective-permute-start(bf16[256,512]{1,0:T(8,128)(2,1)} %get-tuple-element.20), channel_id=1, source_target_pairs={{0,16},{8,24},{16,0},{24,8},{32,48},{40,56},{48,32},{56,40},{64,80... | collective-permute-start | bytes 786440 | tf_op jit(solution)/shard_map/ppermute | solution.py:232
  38.9 1.9 %collective-permute-start.4 = (bf16[256,512]{1,0:T(8,128)(2,1)S(1)}, bf16[256,512]{1,0:T(8,128)(2,1)S(1)}, u32[]{:S(2)}, u32[]{:S(2)}) collective-permute-start(bf16[256,512]{1,0:T(8,128)(2,1)S(1)} %collective-permute-done.1.refs_1_), channel_id=1, source_target_pairs={{0,8},{8,0},{16,24},{24,16},{32,40},{40,32},{48,56},{56,48},{64,72... | collective-permute-start | bytes 786440 | tf_op jit(solution)/shard_map/ppermute | solution.py:233
  40.8 8.3 %collective-permute-done.3.refs_2_ = bf16[256,512]{1,0:T(8,128)(2,1)S(1)} collective-permute-done((bf16[256,512]{1,0:T(8,128)(2,1)}, bf16[256,512]{1,0:T(8,128)(2,1)S(1)}, u32[]{:S(2)}, u32[]{:S(2)}) %collective-permute-start.3) | collective-permute-done | bytes 262176 | tf_op jit(solution)/shard_map/ppermute | solution.py:232
  49.1 1.9 %collective-permute-start.5 = (bf16[256,512]{1,0:T(8,128)(2,1)S(1)}, bf16[256,512]{1,0:T(8,128)(2,1)S(1)}, u32[]{:S(2)}, u32[]{:S(2)}) collective-permute-start(bf16[256,512]{1,0:T(8,128)(2,1)S(1)} %collective-permute-done.3.refs_2_), channel_id=1, source_target_pairs={{0,8},{8,0},{16,24},{24,16},{32,40},{40,32},{48,56},{56,48},{64,72... | collective-permute-start | bytes 786440 | tf_op jit(solution)/shard_map/ppermute | solution.py:234
  51.0 1.5 collective-permute-done.5.refs_4_
  53.2 6.4 %all-to-all-done.refs_0_ = bf16[16,192,128]{2,1,0:T(8,128)(2,1)S(1)} async-done(((bf16[16,192,128]{2,1,0:T(8,128)(2,1)}), bf16[16,192,128]{2,1,0:T(8,128)(2,1)S(1)}, u32[]{:S(2)}, u32[]{:S(2)}) %all-to-all-start) | async-done | bytes 786464 | tf_op jit(solution)/shard_map/all_to_all | solution.py:49
  62.1 3.5 %all-to-all-start.2 = ((bf16[4,128,768]{2,1,0:T(8,128)(2,1)}), bf16[4,128,768]{2,1,0:T(8,128)(2,1)S(1)}, u32[]{:S(2)}, u32[]{:S(2)}) async-start(bf16[4,128,768]{2,1,0:T(8,128)(2,1)} %bitcast.15), calls=%async_computation.2 | async-start | bytes 1572864 | tf_op jit(solution)/shard_map/all_to_all | solution.py:49
  67.1 10.3 %all-to-all-done.2.refs_0_ = bf16[4,128,768]{2,1,0:T(8,128)(2,1)S(1)} async-done(((bf16[4,128,768]{2,1,0:T(8,128)(2,1)}), bf16[4,128,768]{2,1,0:T(8,128)(2,1)S(1)}, u32[]{:S(2)}, u32[]{:S(2)}) %all-to-all-start.2) | async-done | bytes 786464 | tf_op jit(solution)/shard_map/all_to_all | solution.py:49
  77.4 3.5 %all-to-all-start.1 = ((bf16[4,128,768]{2,1,0:T(8,128)(2,1)}), bf16[4,128,768]{2,1,0:T(8,128)(2,1)S(1)}, u32[]{:S(2)}, u32[]{:S(2)}) async-start(bf16[4,128,768]{2,1,0:T(8,128)(2,1)} %bitcast.14), calls=%async_computation.1 | async-start | bytes 1572864 | tf_op jit(solution)/shard_map/all_to_all | solution.py:49
  81.7 5.0 %collective-permute-start.7 = (bf16[128,768]{1,0:T(8,128)(2,1)}, bf16[128,768]{1,0:T(8,128)(2,1)}, u32[]{:S(2)}, u32[]{:S(2)}) collective-permute-start(bf16[128,768]{1,0:T(8,128)(2,1)} %reduce_sum.37), channel_id=1, source_target_pairs={{0,1},{1,0},{2,3},{3,2},{4,5},{5,4},{6,7},{7,6},{8,9},{9,8},{10,11... | collective-permute-start | bytes 589832 | tf_op jit(solution)/shard_map/ppermute | solution.py:249
  86.8 5.0 %all-to-all-done.1.refs_2_.refs_0_ = bf16[4,128,768]{2,1,0:T(8,128)(2,1)S(1)} async-done(((bf16[4,128,768]{2,1,0:T(8,128)(2,1)}), bf16[4,128,768]{2,1,0:T(8,128)(2,1)S(1)}, u32[]{:S(2)}, u32[]{:S(2)}) %all-to-all-start.1) | async-done | bytes 786464 | tf_op jit(solution)/shard_map/all_to_all | solution.py:49
  91.8 3.8 %collective-permute-done.7.refs_1_ = bf16[128,768]{1,0:T(8,128)(2,1)} collective-permute-done((bf16[128,768]{1,0:T(8,128)(2,1)}, bf16[128,768]{1,0:T(8,128)(2,1)}, u32[]{:S(2)}, u32[]{:S(2)}) %collective-permute-start.7) | collective-permute-done | bytes 196640 | tf_op jit(solution)/shard_map/ppermute | solution.py:249
  97.6 4.6 %all-to-all-start.3 = ((bf16[4,128,768]{2,1,0:T(8,128)(2,1)}), bf16[4,128,768]{2,1,0:T(8,128)(2,1)S(1)}, u32[]{:S(2)}, u32[]{:S(2)}) async-start(bf16[4,128,768]{2,1,0:T(8,128)(2,1)} %copy-done.3), calls=%async_computation.3 | async-start | bytes 1572864 | tf_op jit(solution)/shard_map/all_to_all | solution.py:49
  103.1 6.5 %collective-permute-start.6 = (bf16[128,768]{1,0:T(8,128)(2,1)}, bf16[128,768]{1,0:T(8,128)(2,1)S(1)}, u32[]{:S(2)}, u32[]{:S(2)}) collective-permute-start(bf16[128,768]{1,0:T(8,128)(2,1)} %reduce_sum.36), channel_id=1, source_target_pairs={{0,1},{1,0},{2,3},{3,2},{4,5},{5,4},{6,7},{7,6},{8,9},{9,8},{10,11... | collective-permute-start | bytes 589832 | tf_op jit(solution)/shard_map/ppermute | solution.py:249
  109.6 6.4 %collective-permute-done.6.refs_1_ = bf16[128,768]{1,0:T(8,128)(2,1)S(1)} collective-permute-done((bf16[128,768]{1,0:T(8,128)(2,1)}, bf16[128,768]{1,0:T(8,128)(2,1)S(1)}, u32[]{:S(2)}, u32[]{:S(2)}) %collective-permute-start.6) | collective-permute-done | bytes 196640 | tf_op jit(solution)/shard_map/ppermute | solution.py:249
  118.7 4.5 %all-to-all-start.4 = ((bf16[4,128,768]{2,1,0:T(8,128)(2,1)}), bf16[4,128,768]{2,1,0:T(8,128)(2,1)S(1)}, u32[]{:S(2)}, u32[]{:S(2)}) async-start(bf16[4,128,768]{2,1,0:T(8,128)(2,1)} %copy-done.5), calls=%async_computation.4 | async-start | bytes 1572864 | tf_op jit(solution)/shard_map/all_to_all | solution.py:49
  126.9 7.2 %all-to-all-done.4 = bf16[4,128,768]{2,1,0:T(8,128)(2,1)S(1)} async-done(((bf16[4,128,768]{2,1,0:T(8,128)(2,1)}), bf16[4,128,768]{2,1,0:T(8,128)(2,1)S(1)}, u32[]{:S(2)}, u32[]{:S(2)}) %all-to-all-start.4) | async-done | bytes 786464 | tf_op jit(solution)/shard_map/all_to_all | solution.py:49
  134.1 1.4 copy-done.1
  138.6 11.0 %all-to-all-start.5 = ((bf16[16,192,128]{2,1,0:T(8,128)(2,1)}), bf16[16,192,128]{2,1,0:T(8,128)(2,1)}, u32[]{:S(2)}, u32[]{:S(2)}) async-start(bf16[16,192,128]{2,1,0:T(8,128)(2,1)} %copy-done.2), calls=%async_computation.5 | async-start | bytes 1572864 | tf_op jit(solution)/shard_map/all_to_all | solution.py:49
  150.2 1.9 %collective-permute-start.9 = (bf16[2,256,512]{2,1,0:T(8,128)(2,1)S(1)}, bf16[2,256,512]{2,1,0:T(8,128)(2,1)S(1)}, u32[]{:S(2)}, u32[]{:S(2)}) collective-permute-start(bf16[2,256,512]{2,1,0:T(8,128)(2,1)S(1)} %get-tuple-element.26), channel_id=1, source_target_pairs={{0,8},{8,0},{16,24},{24,16},{32,40},{40,32},{48,56},{56,48},{64,72... | collective-permute-start | bytes 1572872 | tf_op jit(solution)/shard_map/ppermute | solution.py:264
  152.2 1.9 collective-permute-done.9
  154.2 1.9 %collective-permute-start.10 = (bf16[2,256,512]{2,1,0:T(8,128)(2,1)S(1)}, bf16[2,256,512]{2,1,0:T(8,128)(2,1)S(1)}, u32[]{:S(2)}, u32[]{:S(2)}) collective-permute-start(bf16[2,256,512]{2,1,0:T(8,128)(2,1)S(1)} %add_convert_fusion), channel_id=1, source_target_pairs={{0,16},{8,24},{16,0},{24,8},{32,48},{40,56},{48,32},{56,40},{64,80... | collective-permute-start | bytes 1572872 | tf_op jit(solution)/shard_map/ppermute | solution.py:265
  157.8 2.0 %collective-permute-start.8 = (bf16[2,256,512]{2,1,0:T(8,128)(2,1)S(1)}, bf16[2,256,512]{2,1,0:T(8,128)(2,1)S(1)}, u32[]{:S(2)}, u32[]{:S(2)}) collective-permute-start(bf16[2,256,512]{2,1,0:T(8,128)(2,1)S(1)} %get-tuple-element.24), channel_id=1, source_target_pairs={{0,8},{8,0},{16,24},{24,16},{32,40},{40,32},{48,56},{56,48},{64,72... | collective-permute-start | bytes 1572872 | tf_op jit(solution)/shard_map/ppermute | solution.py:276
  159.8 10.5 %all-to-all-done.5 = bf16[16,192,128]{2,1,0:T(8,128)(2,1)} async-done(((bf16[16,192,128]{2,1,0:T(8,128)(2,1)}), bf16[16,192,128]{2,1,0:T(8,128)(2,1)}, u32[]{:S(2)}, u32[]{:S(2)}) %all-to-all-start.5) | async-done | bytes 786464 | tf_op jit(solution)/shard_map/all_to_all | solution.py:49
  171.5 1.9 %collective-permute-start.11 = (bf16[192,128]{1,0:T(8,128)(2,1)S(1)}, bf16[192,128]{1,0:T(8,128)(2,1)S(1)}, u32[]{:S(2)}, u32[]{:S(2)}) collective-permute-start(bf16[192,128]{1,0:T(8,128)(2,1)S(1)} %reduce_sum.38), channel_id=1, source_target_pairs={{0,0},{256,1},{8,2},{264,3},{16,4},{272,5},{24,6},{280,7},{64,8},{... | collective-permute-start | bytes 147464 | tf_op jit(solution)/shard_map/ppermute | solution.py:278
  177.2 12.4 %collective-permute-done.11 = bf16[192,128]{1,0:T(8,128)(2,1)S(1)} collective-permute-done((bf16[192,128]{1,0:T(8,128)(2,1)S(1)}, bf16[192,128]{1,0:T(8,128)(2,1)S(1)}, u32[]{:S(2)}, u32[]{:S(2)}) %collective-permute-start.11) | collective-permute-done | bytes 49184 | tf_op jit(solution)/shard_map/ppermute | solution.py:278
  (60 shorter events, 26.6 us)
Async XLA Ops:
  3.9 19.5 %collective-permute-start.2 = (bf16[2,256,512]{2,1,0:T(8,128)(2,1)}, bf16[2,256,512]{2,1,0:T(8,128)(2,1)S(1)}, u32[]{:S(2)}, u32[]{:S(2)}) collective-permute-start(bf16[2,256,512]{2,1,0:T(8,128)(2,1)} %get-tuple-element.19.refs_1_), channel_id=1, source_target_pairs={{0,8},{8,0},{16,24},{24,16},{32,40},{40,32},{48,56},{56,48},{64,72... | collective-permute-start | bytes 1572872 | tf_op jit(solution)/shard_map/ppermute | solution.py:227
  5.8 17.6 %collective-permute-start.1 = (bf16[256,512]{1,0:T(8,128)(2,1)}, bf16[256,512]{1,0:T(8,128)(2,1)S(1)}, u32[]{:S(2)}, u32[]{:S(2)}) collective-permute-start(bf16[256,512]{1,0:T(8,128)(2,1)} %get-tuple-element.18), channel_id=1, source_target_pairs={{0,16},{8,24},{16,0},{24,8},{32,48},{40,56},{48,32},{56,40},{64,80... | collective-permute-start | bytes 786440 | tf_op jit(solution)/shard_map/ppermute | solution.py:226
  7.7 15.6 %collective-permute-start = (bf16[192,128]{1,0:T(8,128)(2,1)}, bf16[192,128]{1,0:T(8,128)(2,1)S(1)}, u32[]{:S(2)}, u32[]{:S(2)}) collective-permute-start(bf16[192,128]{1,0:T(8,128)(2,1)} %get-tuple-element.17), channel_id=1, source_target_pairs={{0,0},{1,256},{2,8},{3,264},{4,16},{5,272},{6,24},{7,280},{8,64},{... | collective-permute-start | bytes 147464 | tf_op jit(solution)/shard_map/ppermute | solution.py:225
  24.4 35.2 %all-to-all-start = ((bf16[16,192,128]{2,1,0:T(8,128)(2,1)}), bf16[16,192,128]{2,1,0:T(8,128)(2,1)S(1)}, u32[]{:S(2)}, u32[]{:S(2)}) async-start(bf16[16,192,128]{2,1,0:T(8,128)(2,1)} %shard_map.120), calls=%async_computation | async-start | bytes 1572864 | tf_op jit(solution)/shard_map/all_to_all | solution.py:49
  36.3 29.3 %copy-start.6 = (bf16[2,256,512]{2,1,0:T(8,128)(2,1)S(1)}, bf16[2,256,512]{2,1,0:T(8,128)(2,1)}, u32[]{:S(2)}) copy-start(bf16[2,256,512]{2,1,0:T(8,128)(2,1)} %get-tuple-element.19.refs_1_) | copy-start | bytes 1572868
  36.3 12.8 %collective-permute-start.3 = (bf16[256,512]{1,0:T(8,128)(2,1)}, bf16[256,512]{1,0:T(8,128)(2,1)S(1)}, u32[]{:S(2)}, u32[]{:S(2)}) collective-permute-start(bf16[256,512]{1,0:T(8,128)(2,1)} %get-tuple-element.20), channel_id=1, source_target_pairs={{0,16},{8,24},{16,0},{24,8},{32,48},{40,56},{48,32},{56,40},{64,80... | collective-permute-start | bytes 786440 | tf_op jit(solution)/shard_map/ppermute | solution.py:232
  38.9 12.1 %collective-permute-start.4 = (bf16[256,512]{1,0:T(8,128)(2,1)S(1)}, bf16[256,512]{1,0:T(8,128)(2,1)S(1)}, u32[]{:S(2)}, u32[]{:S(2)}) collective-permute-start(bf16[256,512]{1,0:T(8,128)(2,1)S(1)} %collective-permute-done.1.refs_1_), channel_id=1, source_target_pairs={{0,8},{8,0},{16,24},{24,16},{32,40},{40,32},{48,56},{56,48},{64,72... | collective-permute-start | bytes 786440 | tf_op jit(solution)/shard_map/ppermute | solution.py:233
  49.1 3.4 %collective-permute-start.5 = (bf16[256,512]{1,0:T(8,128)(2,1)S(1)}, bf16[256,512]{1,0:T(8,128)(2,1)S(1)}, u32[]{:S(2)}, u32[]{:S(2)}) collective-permute-start(bf16[256,512]{1,0:T(8,128)(2,1)S(1)} %collective-permute-done.3.refs_2_), channel_id=1, source_target_pairs={{0,8},{8,0},{16,24},{24,16},{32,40},{40,32},{48,56},{56,48},{64,72... | collective-permute-start | bytes 786440 | tf_op jit(solution)/shard_map/ppermute | solution.py:234
  51.0 11.1 %copy-start.10 = (bf16[256,512]{1,0:T(8,128)(2,1)}, bf16[256,512]{1,0:T(8,128)(2,1)S(1)}, u32[]{:S(2)}) copy-start(bf16[256,512]{1,0:T(8,128)(2,1)S(1)} %collective-permute-done.4.refs_3_) | copy-start | bytes 786436
  59.6 1.0 copy-start.13
  61.2 0.9 copy-start.15
  62.1 15.3 %all-to-all-start.2 = ((bf16[4,128,768]{2,1,0:T(8,128)(2,1)}), bf16[4,128,768]{2,1,0:T(8,128)(2,1)S(1)}, u32[]{:S(2)}, u32[]{:S(2)}) async-start(bf16[4,128,768]{2,1,0:T(8,128)(2,1)} %bitcast.15), calls=%async_computation.2 | async-start | bytes 1572864 | tf_op jit(solution)/shard_map/all_to_all | solution.py:49
  77.4 14.4 %all-to-all-start.1 = ((bf16[4,128,768]{2,1,0:T(8,128)(2,1)}), bf16[4,128,768]{2,1,0:T(8,128)(2,1)S(1)}, u32[]{:S(2)}, u32[]{:S(2)}) async-start(bf16[4,128,768]{2,1,0:T(8,128)(2,1)} %bitcast.14), calls=%async_computation.1 | async-start | bytes 1572864 | tf_op jit(solution)/shard_map/all_to_all | solution.py:49
  81.7 13.9 %collective-permute-start.7 = (bf16[128,768]{1,0:T(8,128)(2,1)}, bf16[128,768]{1,0:T(8,128)(2,1)}, u32[]{:S(2)}, u32[]{:S(2)}) collective-permute-start(bf16[128,768]{1,0:T(8,128)(2,1)} %reduce_sum.37), channel_id=1, source_target_pairs={{0,1},{1,0},{2,3},{3,2},{4,5},{5,4},{6,7},{7,6},{8,9},{9,8},{10,11... | collective-permute-start | bytes 589832 | tf_op jit(solution)/shard_map/ppermute | solution.py:249
  97.6 19.1 %all-to-all-start.3 = ((bf16[4,128,768]{2,1,0:T(8,128)(2,1)}), bf16[4,128,768]{2,1,0:T(8,128)(2,1)S(1)}, u32[]{:S(2)}, u32[]{:S(2)}) async-start(bf16[4,128,768]{2,1,0:T(8,128)(2,1)} %copy-done.3), calls=%async_computation.3 | async-start | bytes 1572864 | tf_op jit(solution)/shard_map/all_to_all | solution.py:49
  103.1 13.0 %collective-permute-start.6 = (bf16[128,768]{1,0:T(8,128)(2,1)}, bf16[128,768]{1,0:T(8,128)(2,1)S(1)}, u32[]{:S(2)}, u32[]{:S(2)}) collective-permute-start(bf16[128,768]{1,0:T(8,128)(2,1)} %reduce_sum.36), channel_id=1, source_target_pairs={{0,1},{1,0},{2,3},{3,2},{4,5},{5,4},{6,7},{7,6},{8,9},{9,8},{10,11... | collective-permute-start | bytes 589832 | tf_op jit(solution)/shard_map/ppermute | solution.py:249
  116.7 0.9 copy-start.17
  118.7 15.4 %all-to-all-start.4 = ((bf16[4,128,768]{2,1,0:T(8,128)(2,1)}), bf16[4,128,768]{2,1,0:T(8,128)(2,1)S(1)}, u32[]{:S(2)}, u32[]{:S(2)}) async-start(bf16[4,128,768]{2,1,0:T(8,128)(2,1)} %copy-done.5), calls=%async_computation.4 | async-start | bytes 1572864 | tf_op jit(solution)/shard_map/all_to_all | solution.py:49
  123.2 0.9 copy-start.11
  124.2 0.9 copy-start.14
  125.7 1.2 copy-start
  134.1 1.4 copy-start.1
  135.5 1.0 copy-start.7
  138.6 31.7 %all-to-all-start.5 = ((bf16[16,192,128]{2,1,0:T(8,128)(2,1)}), bf16[16,192,128]{2,1,0:T(8,128)(2,1)}, u32[]{:S(2)}, u32[]{:S(2)}) async-start(bf16[16,192,128]{2,1,0:T(8,128)(2,1)} %copy-done.2), calls=%async_computation.5 | async-start | bytes 1572864 | tf_op jit(solution)/shard_map/all_to_all | solution.py:49
  150.2 3.8 %collective-permute-start.9 = (bf16[2,256,512]{2,1,0:T(8,128)(2,1)S(1)}, bf16[2,256,512]{2,1,0:T(8,128)(2,1)S(1)}, u32[]{:S(2)}, u32[]{:S(2)}) collective-permute-start(bf16[2,256,512]{2,1,0:T(8,128)(2,1)S(1)} %get-tuple-element.26), channel_id=1, source_target_pairs={{0,8},{8,0},{16,24},{24,16},{32,40},{40,32},{48,56},{56,48},{64,72... | collective-permute-start | bytes 1572872 | tf_op jit(solution)/shard_map/ppermute | solution.py:264
  154.2 20.4 %copy-start.18 = (s32[256]{0:T(256)S(1)}, s32[256]{0:T(256)}, u32[]{:S(2)}) copy-start(s32[256]{0:T(256)} %param.10) | copy-start | bytes 3076
  154.2 20.4 %copy-start.19 = (f32[256]{0:T(256)S(1)}, f32[256]{0:T(256)}, u32[]{:S(2)}) copy-start(f32[256]{0:T(256)} %param.12) | copy-start | bytes 3076
  154.2 20.4 %collective-permute-start.10 = (bf16[2,256,512]{2,1,0:T(8,128)(2,1)S(1)}, bf16[2,256,512]{2,1,0:T(8,128)(2,1)S(1)}, u32[]{:S(2)}, u32[]{:S(2)}) collective-permute-start(bf16[2,256,512]{2,1,0:T(8,128)(2,1)S(1)} %add_convert_fusion), channel_id=1, source_target_pairs={{0,16},{8,24},{16,0},{24,8},{32,48},{40,56},{48,32},{56,40},{64,80... | collective-permute-start | bytes 1572872 | tf_op jit(solution)/shard_map/ppermute | solution.py:265
  156.8 1.0 copy-start.8
  157.8 16.9 %collective-permute-start.8 = (bf16[2,256,512]{2,1,0:T(8,128)(2,1)S(1)}, bf16[2,256,512]{2,1,0:T(8,128)(2,1)S(1)}, u32[]{:S(2)}, u32[]{:S(2)}) collective-permute-start(bf16[2,256,512]{2,1,0:T(8,128)(2,1)S(1)} %get-tuple-element.24), channel_id=1, source_target_pairs={{0,8},{8,0},{16,24},{24,16},{32,40},{40,32},{48,56},{56,48},{64,72... | collective-permute-start | bytes 1572872 | tf_op jit(solution)/shard_map/ppermute | solution.py:276
  171.5 18.0 %collective-permute-start.11 = (bf16[192,128]{1,0:T(8,128)(2,1)S(1)}, bf16[192,128]{1,0:T(8,128)(2,1)S(1)}, u32[]{:S(2)}, u32[]{:S(2)}) collective-permute-start(bf16[192,128]{1,0:T(8,128)(2,1)S(1)} %reduce_sum.38), channel_id=1, source_target_pairs={{0,0},{256,1},{8,2},{264,3},{16,4},{272,5},{24,6},{280,7},{64,8},{... | collective-permute-start | bytes 147464 | tf_op jit(solution)/shard_map/ppermute | solution.py:278
  174.7 1.2 copy-start.9
  (6 other events, 4.9 us)

commit v6 on v2

v6 whole, which is shorter than its diff:
```python
import jax
import jax.numpy as jnp
from jax import lax
from jax.experimental import pallas as pl
from jax.experimental.pallas import tpu as pltpu
from jax.sharding import PartitionSpec as P

N_Y, N_Z, N_CORE, N_X = 8, 4, 2, 4
N_WIDE, N_NARROW = N_Y * N_Z * N_CORE, 2 * N_X
F32, BF16 = jnp.float32, jnp.bfloat16
FIRST, LAST, PLAIN = ((0,), (0,)), ((1,), (1,)), ((1,), (0,))


def wide_index(y, z, core):
    return (y * N_Z + z) * N_CORE + core


def swap_pairs():
    pairs = []
    for y in range(N_Y):
        for z in range(N_Z):
            for core in range(N_CORE):
                for n in range(N_NARROW):
                    to = wide_index(y // 2 * 2 + core, z, n % 2)
                    pairs.append((wide_index(y, z, core) * N_NARROW + n, to * N_NARROW + n // 2 * 2 + y % 2))
    return pairs


SWAP = swap_pairs()
SWAP_BACK = [(b, a) for a, b in SWAP]
OTHER_CORE = [(w, w ^ 1) for w in range(N_WIDE)]
OTHER_HALF = [(n, n ^ 1) for n in range(N_NARROW)]
OWNERS = [[wide_index(y, z, core) for y in range(N_Y) for z in range(N_Z)] for core in range(N_CORE)]


def shift_x(by):
    return [(n, (n + 2 * by) % N_NARROW) for n in range(N_NARROW)]


def dot(a, b, dims=PLAIN):
    return lax.dot_general(a, b, (dims, ((), ())), preferred_element_type=F32)


def call(body, outs, flops, where, *args):
    size = sum(a.size * a.dtype.itemsize for a in args)
    count = len(args)

    def inner(where_ref, *refs):
        sources, results = refs[:count], refs[count : count + len(outs)]
        held, sem = refs[count + len(outs) : -1], refs[-1]
        copies = [
            pltpu.make_async_copy(s, h, sem.at[i]) for i, (s, h) in enumerate(zip(sources, held))
        ]
        for copy in copies:
            copy.start()
        here = set()

        def get(i):
            if i not in here:
                here.add(i)
                copies[i].wait()
            return held[i]

        body(where_ref, get, *results)

    return pl.pallas_call(
        inner,
        out_shape=[jax.ShapeDtypeStruct(shape, kind) for shape, kind in outs],
        in_specs=[pl.BlockSpec(memory_space=pltpu.SMEM)]
        + [pl.BlockSpec(memory_space=pl.ANY)] * count,
        out_specs=[pl.BlockSpec(memory_space=pltpu.VMEM)] * len(outs),
        scratch_shapes=[pltpu.VMEM(a.shape, a.dtype) for a in args]
        + [pltpu.SemaphoreType.DMA((count,))],
        compiler_params=pltpu.CompilerParams(vmem_limit_bytes=60 * 1024 * 1024),
        cost_estimate=pl.CostEstimate(flops=flops, bytes_accessed=size, transcendentals=0),
    )(where, *args)


def use_of(gate, count):
    slots = gate.shape[1]
    lane = lax.broadcasted_iota(jnp.int32, (1, slots), 1)
    use = jnp.where(lane < count, gate, 0.0)
    square = lax.broadcasted_iota(jnp.int32, (slots, slots), 0) == lax.broadcasted_iota(
        jnp.int32, (slots, slots), 1
    )
    return jnp.sum(jnp.where(square, use, 0.0), axis=1, keepdims=True)


def pick_of(token, tok):
    slots = token.shape[1]
    return jnp.where(lax.broadcasted_iota(jnp.int32, (tok, slots), 0) == token, 1.0, 0.0).astype(BF16)


def rows_body(where, get, own, block):
    rows = block.shape[0] // 3
    for i in range(3):
        block[rows * i : rows * (i + 1)] = get(5 + i)[...]
    token, count, gate, tokens = get(2), get(3), get(4), get(0)
    pick = pick_of(token[...], tokens.shape[0])
    own[0] = dot(pick, tokens[...], FIRST).astype(BF16)
    own[1] = (use_of(gate[...], count[...]) * dot(pick, get(1)[...], FIRST)).astype(BF16)


def turn(where, step, size):
    return pl.multiple_of(lax.rem(where[0] + step, N_X) * size, size)


def products_body(where, get, sent, kept, both, down):
    pieces = get(0)
    rows, cols = pieces.shape[1] // 3, pieces.shape[2]
    for i in range(pieces.shape[0]):
        y, z = divmod(i, N_Z)
        at = slice((y // 2 * 8 + z * 2 + y % 2) * rows, (y // 2 * 8 + z * 2 + y % 2 + 1) * rows)
        both[at, :cols] = pieces[i, :rows]
        both[at, cols:] = pieces[i, rows : 2 * rows]
        down[at] = pieces[i, 2 * rows :]
    slots, feat = get(1).shape[1:]
    for who in range(2):
        pre, back = 0.0, 0.0
        for step in range(N_X):
            x = get(1 + who * N_X + step)
            at = pl.ds(turn(where, step, feat), feat)
            pre = pre + dot(x[0], both[at])
            back = back + dot(x[1], down[at])
        at = slice(slots * who, slots * (who + 1))
        kept[at, : 2 * cols] = pre
        kept[at, 2 * cols :] = back
        sent[at, : 2 * cols] = pre.astype(BF16)
        sent[at, 2 * cols :] = back.astype(BF16)


def outputs_body(where, get, acts, mine, send):
    kept, theirs, both, down = [get(i) for i in range(4)]
    total = kept[...] + theirs[...].astype(F32)
    units = total.shape[1] // 3
    pre_gate, pre_up, grad_hidden = total[:, :units], total[:, units : 2 * units], total[:, 2 * units :]
    sigma = jax.nn.sigmoid(pre_gate)
    acts[:, :units] = (
        grad_hidden * pre_up * sigma * (1.0 + pre_gate * (1.0 - sigma))
    ).astype(BF16)
    acts[:, units : 2 * units] = (grad_hidden * pre_gate * sigma).astype(BF16)
    acts[:, 2 * units :] = (pre_gate * sigma * pre_up).astype(BF16)
    slots, feat = mine.shape[2:]
    for step in range(N_X):
        at = pl.ds(turn(where, step, feat), feat)
        for which, out in enumerate(
            (dot(acts[:, 2 * units :], down[at], LAST), dot(acts[:, : 2 * units], both[at], LAST))
        ):
            mine[step, which] = out[:slots].astype(BF16)
            send[step, which] = out[slots:].astype(BF16)


def terms_body(where, get, pieces):
    acts = get(0)
    rows, cols = pieces.shape[1] // 3, pieces.shape[2]
    slots = acts.shape[0] // 2
    for step in range(N_X):
        near, core = get(1 + step), get(1 + N_X + step)
        both = dot(near[0], acts[:slots, : 2 * cols], FIRST)
        both = (both + dot(core[0], acts[slots:, : 2 * cols], FIRST)).astype(BF16)
        down = dot(near[1], acts[:slots, 2 * cols :], FIRST)
        down = (down + dot(core[1], acts[slots:, 2 * cols :], FIRST)).astype(BF16)
        first = turn(where, step, 2 * N_Z)
        for i in range(2 * N_Z):
            y, z = divmod(i, N_Z)
            at = slice((z * 2 + y) * rows, (z * 2 + y + 1) * rows)
            pieces[first + i, :rows] = both[at, :cols]
            pieces[first + i, rows : 2 * rows] = both[at, cols:]
            pieces[first + i, 2 * rows :] = down[at]


def sums_body(where, get, *sums):
    for step in range(N_X):
        sums[step][...] = (get(0)[step].astype(F32) + get(1)[step].astype(F32)).astype(BF16)


def tokens_body(where, get, mixed, grad_tokens):
    token, count, gate = get(0), get(1), get(2)
    pick = pick_of(token[...], mixed.shape[0])
    out, back = [sum(get(3 + step)[i].astype(F32) for step in range(N_X)) for i in range(2)]
    mixed[...] = dot(pick, (use_of(gate[...], count[...]) * out).astype(BF16)).astype(BF16)
    grad_tokens[...] = dot(pick, back.astype(BF16)).astype(BF16)


def local(tokens, grad_out, slot_token, slot_count, slot_gate, w_gate, w_up, w_down):
    slots, (tok, feat) = slot_token.shape[0], tokens.shape
    rows, cols = w_gate.shape
    token, gate, count = slot_token[None], slot_gate[None], slot_count[None]
    where = (lax.axis_index("narrow") // 2).astype(jnp.int32)[None]
    pick_flops = 4 * slots * tok * feat
    own, block = call(
        rows_body,
        [((2, slots, feat), BF16), ((3 * rows, cols), BF16)],
        pick_flops,
        where,
        *(tokens, grad_out, token, count, gate, w_gate, w_up, w_down),
    )

    block = lax.ppermute(block, ("wide", "narrow"), SWAP)
    pieces = jnp.broadcast_to(block[None], (len(OWNERS[0]),) + block.shape)
    pieces = lax.all_to_all(pieces, "wide", 0, 0, axis_index_groups=OWNERS)
    near = [own] + [lax.ppermute(own, "narrow", shift_x(-step)) for step in range(1, N_X)]
    core = [lax.ppermute(held, "wide", OTHER_CORE) for held in near]

    flops = 2 * 3 * 2 * slots * N_X * feat * cols
    part = (2 * slots, 3 * cols)
    sent, kept, both, down = call(
        products_body,
        [(part, BF16), (part, F32), ((N_X * feat, 2 * cols), BF16), ((N_X * feat, cols), BF16)],
        flops,
        where,
        *(pieces, *near, *core),
    )
    theirs = lax.ppermute(sent, "narrow", OTHER_HALF)

    every = ((N_X, 2, slots, feat), BF16)
    acts, mine, send = call(
        outputs_body, [(part, BF16), every, every], flops, where, kept, theirs, both, down
    )
    (terms,) = call(terms_body, [(pieces.shape, BF16)], flops, where, acts, *near, *core)

    got = lax.ppermute(send, "wide", OTHER_CORE)
    sums = call(sums_body, [((2, slots, feat), BF16)] * N_X, 0, where, mine, got)
    home = [sums[0]] + [
        lax.ppermute(sums[step], "narrow", shift_x(step)) for step in range(1, N_X)
    ]
    mixed, grad_tokens = call(
        tokens_body, [((tok, feat), BF16)] * 2, pick_flops, where, token, count, gate, *home
    )

    terms = lax.all_to_all(terms, "wide", 0, 0, axis_index_groups=OWNERS)
    grads = terms.astype(F32).sum(axis=0).astype(BF16)
    grads = lax.ppermute(grads, ("wide", "narrow"), SWAP_BACK).astype(F32)
    return mixed, grad_tokens, grads[:rows], grads[rows : 2 * rows], grads[2 * rows :]


def solution(mesh):
    both = P("wide", "narrow")
    in_specs = (both, both, P("wide"), P("wide"), P("wide"), both, both, both)
    return jax.shard_map(
        local, mesh=mesh, in_specs=in_specs, out_specs=(both,) * 5, check_vma=False
    )
```

time: 216 us -> 166 us (0.77)
  the two profiles are of different devices: /device:TPU:40 before, /device:TPU:1 now
where the time goes in v6:
time: 166 us; the launch traced here: 164 us
  starting transfers between devices  74.5 us (45%)
  waiting for transfers between devices  56.5 us (34%)
  Pallas kernels  24.2 us (15%)
  local copies, waits for them, and re-layouts  7.01 us (4%)
    pallas_call x6, Pallas kernels, call(): pl.pallas_call(inner, out_shape=[jax.ShapeDtypeStruct(shape, kind) for sh...  24.2 us
    all_to_all x1, waiting for transfers between devices, local(): terms = lax.all_to_all(terms, 'wide', 0, 0, axis_index_groups=OWNERS)  17.3 us
    all_to_all x1, starting transfers between devices, local(): terms = lax.all_to_all(terms, 'wide', 0, 0, axis_index_groups=OWNERS)  17 us
    ppermute x1, waiting for transfers between devices, local(): theirs = lax.ppermute(sent, 'narrow', OTHER_HALF)  12.8 us
    ppermute x4, starting transfers between devices, local(): core = [lax.ppermute(held, 'wide', OTHER_CORE) for held in near]  12.7 us
    ppermute x3, starting transfers between devices, local(): lax.ppermute(own, 'narrow', shift_x(-step))  10.5 us
    ppermute x3, waiting for transfers between devices, local(): lax.ppermute(own, 'narrow', shift_x(-step))  10.2 us
    all_to_all x1, starting transfers between devices, local(): pieces = lax.all_to_all(pieces, 'wide', 0, 0, axis_index_groups=OWNERS)  10 us
  transfers between devices with their start and end apart: 16, of which 8 were waited for; matrix products, arithmetic and copies ran while one was open for 0% of the time, Pallas kernels for 4%

profile of v6, /device:TPU:1, one launch (start us, length us, event | category | flops | bytes accessed | tf_op | source)
XLA Modules:
  0.0 164.0 jit_solution(10646037918239012069)
XLA Ops:
  1.3 2.5 %shard_map.119 = (bf16[2,256,512]{2,1,0:T(8,128)(2,1)}, bf16[192,128]{1,0:T(8,128)(2,1)}) custom-call(s32[1]{0:T(128)} %bitcast.where_ref, bf16[384,512]{1,0:T(8,128)(2,1)} %refs_0_.1, bf16[384,512]{1,0:T(8,128)(2,1)} %refs_1_.1, s32[1,256]{1,0:T(1,128)} %bitcast.6, s32[1,1]{1,0:T(1,128)} %bitcast.4.refs_3_, f32[1,256]{1,0:T(1,128)} %bitcast.8, ...), custom_call_target="tpu_custom_call" | custom-call | flops 201326592 | bytes 837636 | tf_op jit(solution)/shard_map/pallas_call | solution.py:66
  3.8 4.6 %collective-permute-start = (bf16[192,128]{1,0:T(8,128)(2,1)}, bf16[192,128]{1,0:T(8,128)(2,1)S(1)}, u32[]{:S(2)}, u32[]{:S(2)}) collective-permute-start(bf16[192,128]{1,0:T(8,128)(2,1)} %get-tuple-element.20), channel_id=1, source_target_pairs={{0,0},{1,8},{2,2},{3,10},{4,4},{5,12},{6,6},{7,14},{8,64},{9,72},{... | collective-permute-start | bytes 147464 | tf_op jit(solution)/shard_map/ppermute | solution.py:199
  8.4 9.5 %collective-permute-done = bf16[192,128]{1,0:T(8,128)(2,1)S(1)} collective-permute-done((bf16[192,128]{1,0:T(8,128)(2,1)}, bf16[192,128]{1,0:T(8,128)(2,1)S(1)}, u32[]{:S(2)}, u32[]{:S(2)}) %collective-permute-start) | collective-permute-done | bytes 49184 | tf_op jit(solution)/shard_map/ppermute | solution.py:199
  17.9 1.5 broadcast_in_dim.22
  19.4 10.0 %all-to-all-start = ((bf16[32,192,128]{2,1,0:T(8,128)(2,1)}), bf16[32,192,128]{2,1,0:T(8,128)(2,1)S(1)}, u32[]{:S(2)}, u32[]{:S(2)}) async-start(bf16[32,192,128]{2,1,0:T(8,128)(2,1)} %broadcast_in_dim.22), calls=%async_computation | async-start | bytes 3145728 | tf_op jit(solution)/shard_map/all_to_all | solution.py:201
  29.4 3.1 %collective-permute-start.3 = (bf16[2,256,512]{2,1,0:T(8,128)(2,1)S(1)}, bf16[2,256,512]{2,1,0:T(8,128)(2,1)S(1)}, u32[]{:S(2)}, u32[]{:S(2)}) collective-permute-start(bf16[2,256,512]{2,1,0:T(8,128)(2,1)S(1)} %copy-done.1), channel_id=1, source_target_pairs={{0,2},{1,3},{2,4},{3,5},{4,6},{5,7},{6,0},{7,1},{8,10},{9,11},{10,... | collective-permute-start | bytes 1572872 | tf_op jit(solution)/shard_map/ppermute | solution.py:202
  32.6 4.4 %collective-permute-start.2 = (bf16[2,256,512]{2,1,0:T(8,128)(2,1)S(1)}, bf16[2,256,512]{2,1,0:T(8,128)(2,1)S(1)}, u32[]{:S(2)}, u32[]{:S(2)}) collective-permute-start(bf16[2,256,512]{2,1,0:T(8,128)(2,1)S(1)} %copy-done.1), channel_id=1, source_target_pairs={{0,4},{1,5},{2,6},{3,7},{4,0},{5,1},{6,2},{7,3},{8,12},{9,13},{10,... | collective-permute-start | bytes 1572872 | tf_op jit(solution)/shard_map/ppermute | solution.py:202
  36.9 3.1 %collective-permute-start.1 = (bf16[2,256,512]{2,1,0:T(8,128)(2,1)S(1)}, bf16[2,256,512]{2,1,0:T(8,128)(2,1)S(1)}, u32[]{:S(2)}, u32[]{:S(2)}) collective-permute-start(bf16[2,256,512]{2,1,0:T(8,128)(2,1)S(1)} %copy-done.1), channel_id=1, source_target_pairs={{0,6},{1,7},{2,0},{3,1},{4,2},{5,3},{6,4},{7,5},{8,14},{9,15},{10,... | collective-permute-start | bytes 1572872 | tf_op jit(solution)/shard_map/ppermute | solution.py:202
  40.0 3.5 %collective-permute-start.4 = (bf16[2,256,512]{2,1,0:T(8,128)(2,1)S(1)}, bf16[2,256,512]{2,1,0:T(8,128)(2,1)S(1)}, u32[]{:S(2)}, u32[]{:S(2)}) collective-permute-start(bf16[2,256,512]{2,1,0:T(8,128)(2,1)S(1)} %copy-done.1), channel_id=1, source_target_pairs={{0,8},{8,0},{16,24},{24,16},{32,40},{40,32},{48,56},{56,48},{64,72... | collective-permute-start | bytes 1572872 | tf_op jit(solution)/shard_map/ppermute | solution.py:203
  43.5 1.7 %collective-permute-done.3.refs_4_ = bf16[2,256,512]{2,1,0:T(8,128)(2,1)S(1)} collective-permute-done((bf16[2,256,512]{2,1,0:T(8,128)(2,1)S(1)}, bf16[2,256,512]{2,1,0:T(8,128)(2,1)S(1)}, u32[]{:S(2)}, u32[]{:S(2)}) %collective-permute-start.3) | collective-permute-done | bytes 524320 | tf_op jit(solution)/shard_map/ppermute | solution.py:202
  45.2 3.8 %collective-permute-start.7 = (bf16[2,256,512]{2,1,0:T(8,128)(2,1)S(1)}, bf16[2,256,512]{2,1,0:T(8,128)(2,1)S(1)}, u32[]{:S(2)}, u32[]{:S(2)}) collective-permute-start(bf16[2,256,512]{2,1,0:T(8,128)(2,1)S(1)} %collective-permute-done.3.refs_4_), channel_id=1, source_target_pairs={{0,8},{8,0},{16,24},{24,16},{32,40},{40,32},{48,56},{56,48},{64,72... | collective-permute-start | bytes 1572872 | tf_op jit(solution)/shard_map/ppermute | solution.py:203
  49.0 8.4 %collective-permute-done.2.refs_3_ = bf16[2,256,512]{2,1,0:T(8,128)(2,1)S(1)} collective-permute-done((bf16[2,256,512]{2,1,0:T(8,128)(2,1)S(1)}, bf16[2,256,512]{2,1,0:T(8,128)(2,1)S(1)}, u32[]{:S(2)}, u32[]{:S(2)}) %collective-permute-start.2) | collective-permute-done | bytes 524320 | tf_op jit(solution)/shard_map/ppermute | solution.py:202
  57.5 3.5 %collective-permute-start.6 = (bf16[2,256,512]{2,1,0:T(8,128)(2,1)S(1)}, bf16[2,256,512]{2,1,0:T(8,128)(2,1)S(1)}, u32[]{:S(2)}, u32[]{:S(2)}) collective-permute-start(bf16[2,256,512]{2,1,0:T(8,128)(2,1)S(1)} %collective-permute-done.2.refs_3_), channel_id=1, source_target_pairs={{0,8},{8,0},{16,24},{24,16},{32,40},{40,32},{48,56},{56,48},{64,72... | collective-permute-start | bytes 1572872 | tf_op jit(solution)/shard_map/ppermute | solution.py:203
  61.0 1.9 %collective-permute-start.5 = (bf16[2,256,512]{2,1,0:T(8,128)(2,1)S(1)}, bf16[2,256,512]{2,1,0:T(8,128)(2,1)}, u32[]{:S(2)}, u32[]{:S(2)}) collective-permute-start(bf16[2,256,512]{2,1,0:T(8,128)(2,1)S(1)} %collective-permute-done.1.refs_2_), channel_id=1, source_target_pairs={{0,8},{8,0},{16,24},{24,16},{32,40},{40,32},{48,56},{56,48},{64,72... | collective-permute-start | bytes 1572872 | tf_op jit(solution)/shard_map/ppermute | solution.py:203
  64.0 0.8 copy-done.7
  65.0 2.4 %all-to-all-done.refs_0_ = bf16[32,192,128]{2,1,0:T(8,128)(2,1)S(1)} async-done(((bf16[32,192,128]{2,1,0:T(8,128)(2,1)}), bf16[32,192,128]{2,1,0:T(8,128)(2,1)S(1)}, u32[]{:S(2)}, u32[]{:S(2)}) %all-to-all-start) | async-done | bytes 1572896 | tf_op jit(solution)/shard_map/all_to_all | solution.py:201
  67.4 1.2 copy-done
  68.5 5.2 %shard_map.120 = (bf16[512,384]{1,0:T(8,128)(2,1)}, f32[512,384]{1,0:T(8,128)}, bf16[2048,256]{1,0:T(8,128)(2,1)}, bf16[2048,128]{1,0:T(8,128)(2,1)}) custom-call(s32[1]{0:T(128)} %bitcast.where_ref, bf16[32,192,128]{2,1,0:T(8,128)(2,1)} %copy-done, bf16[2,256,512]{2,1,0:T(8,128)(2,1)} %get-tuple-element.21.refs_1_, bf16[2,256,512]{2,1,0:T(8,128)(2,1)} %copy-done.4, ...), custom_call_target="tpu_custom_call" | custom-call | flops 805306368 | bytes 5767168 | tf_op jit(solution)/shard_map/pallas_call | solution.py:66
  73.7 1.9 %collective-permute-start.8 = (bf16[512,384]{1,0:T(8,128)(2,1)}, bf16[512,384]{1,0:T(8,128)(2,1)S(1)}, u32[]{:S(2)}, u32[]{:S(2)}) collective-permute-start(bf16[512,384]{1,0:T(8,128)(2,1)} %get-tuple-element.23), channel_id=1, source_target_pairs={{0,1},{1,0},{2,3},{3,2},{4,5},{5,4},{6,7},{7,6},{8,9},{9,8},{10,11... | collective-permute-start | bytes 1179656 | tf_op jit(solution)/shard_map/ppermute | solution.py:214
  75.6 12.8 %collective-permute-done.8.refs_1_ = bf16[512,384]{1,0:T(8,128)(2,1)S(1)} collective-permute-done((bf16[512,384]{1,0:T(8,128)(2,1)}, bf16[512,384]{1,0:T(8,128)(2,1)S(1)}, u32[]{:S(2)}, u32[]{:S(2)}) %collective-permute-start.8) | collective-permute-done | bytes 393248 | tf_op jit(solution)/shard_map/ppermute | solution.py:214
  89.2 5.0 %shard_map.121 = (bf16[512,384]{1,0:T(8,128)(2,1)}, bf16[4,2,256,512]{3,2,1,0:T(8,128)(2,1)}, bf16[4,2,256,512]{3,2,1,0:T(8,128)(2,1)}) custom-call(s32[1]{0:T(128)} %bitcast.where_ref, f32[512,384]{1,0:T(8,128)} %get-tuple-element.22.refs_0_, bf16[512,384]{1,0:T(8,128)(2,1)} %copy-done.11, bf16[2048,256]{1,0:T(8,128)(2,1)} %get-tuple-element.24.refs_2_, ...), custom_call_target="tpu_custom_call" | custom-call | flops 805306368 | bytes 2752512 | tf_op jit(solution)/shard_map/pallas_call | solution.py:66
  94.2 4.9 %shard_map.124 = bf16[32,192,128]{2,1,0:T(8,128)(2,1)} custom-call(s32[1]{0:T(128)} %bitcast.where_ref, bf16[512,384]{1,0:T(8,128)(2,1)} %get-tuple-element.34.refs_0_, bf16[2,256,512]{2,1,0:T(8,128)(2,1)} %get-tuple-element.21.refs_1_, bf16[2,256,512]{2,1,0:T(8,128)(2,1)} %copy-done.4, bf16[2,256,512]{2,1,0:T(8,128)(2,1)} %copy-done.3, ...), custom_call_target="tpu_custom_call" | custom-call | flops 805306368 | bytes 4587520 | tf_op jit(solution)/shard_map/pallas_call | solution.py:66
  99.1 17.0 %all-to-all-start.1 = ((bf16[32,192,128]{2,1,0:T(8,128)(2,1)}), bf16[32,192,128]{2,1,0:T(8,128)(2,1)S(1)}, u32[]{:S(2)}, u32[]{:S(2)}) async-start(bf16[32,192,128]{2,1,0:T(8,128)(2,1)} %shard_map.124), calls=%async_computation.1 | async-start | bytes 3145728 | tf_op jit(solution)/shard_map/all_to_all | solution.py:231
  116.1 2.7 %collective-permute-start.9 = (bf16[4,2,256,512]{3,2,1,0:T(8,128)(2,1)}, bf16[4,2,256,512]{3,2,1,0:T(8,128)(2,1)}, u32[]{:S(2)}, u32[]{:S(2)}) collective-permute-start(bf16[4,2,256,512]{3,2,1,0:T(8,128)(2,1)} %get-tuple-element.27), channel_id=1, source_target_pairs={{0,8},{8,0},{16,24},{24,16},{32,40},{40,32},{48,56},{56,48},{64,72... | collective-permute-start | bytes 6291464 | tf_op jit(solution)/shard_map/ppermute | solution.py:222
  118.9 4.1 %collective-permute-done.9.refs_1_ = bf16[4,2,256,512]{3,2,1,0:T(8,128)(2,1)} collective-permute-done((bf16[4,2,256,512]{3,2,1,0:T(8,128)(2,1)}, bf16[4,2,256,512]{3,2,1,0:T(8,128)(2,1)}, u32[]{:S(2)}, u32[]{:S(2)}) %collective-permute-start.9) | collective-permute-done | bytes 2097184 | tf_op jit(solution)/shard_map/ppermute | solution.py:222
  123.0 3.7 %shard_map.122 = (bf16[2,256,512]{2,1,0:T(8,128)(2,1)}, bf16[2,256,512]{2,1,0:T(8,128)(2,1)}, bf16[2,256,512]{2,1,0:T(8,128)(2,1)}, bf16[2,256,512]{2,1,0:T(8,128)(2,1)}) custom-call(s32[1]{0:T(128)} %bitcast.where_ref, bf16[4,2,256,512]{3,2,1,0:T(8,128)(2,1)} %get-tuple-element.26.refs_0_, bf16[4,2,256,512]{3,2,1,0:T(8,128)(2,1)} %collective-permute-done.9.refs_1_), custom_call_target="tpu_custom_call" | custom-call | bytes 4194304 | tf_op jit(solution)/shard_map/pallas_call | solution.py:66
  126.7 3.4 %collective-permute-start.10 = (bf16[2,256,512]{2,1,0:T(8,128)(2,1)}, bf16[2,256,512]{2,1,0:T(8,128)(2,1)S(1)}, u32[]{:S(2)}, u32[]{:S(2)}) collective-permute-start(bf16[2,256,512]{2,1,0:T(8,128)(2,1)} %get-tuple-element.29), channel_id=1, source_target_pairs={{0,2},{1,3},{2,4},{3,5},{4,6},{5,7},{6,0},{7,1},{8,10},{9,11},{10,... | collective-permute-start | bytes 1572872 | tf_op jit(solution)/shard_map/ppermute | solution.py:225
  130.1 3.3 %collective-permute-start.11 = (bf16[2,256,512]{2,1,0:T(8,128)(2,1)}, bf16[2,256,512]{2,1,0:T(8,128)(2,1)S(1)}, u32[]{:S(2)}, u32[]{:S(2)}) collective-permute-start(bf16[2,256,512]{2,1,0:T(8,128)(2,1)} %get-tuple-element.30), channel_id=1, source_target_pairs={{0,4},{1,5},{2,6},{3,7},{4,0},{5,1},{6,2},{7,3},{8,12},{9,13},{10,... | collective-permute-start | bytes 1572872 | tf_op jit(solution)/shard_map/ppermute | solution.py:225
  133.5 3.2 %collective-permute-start.12 = (bf16[2,256,512]{2,1,0:T(8,128)(2,1)}, bf16[2,256,512]{2,1,0:T(8,128)(2,1)S(1)}, u32[]{:S(2)}, u32[]{:S(2)}) collective-permute-start(bf16[2,256,512]{2,1,0:T(8,128)(2,1)} %get-tuple-element.31), channel_id=1, source_target_pairs={{0,6},{1,7},{2,0},{3,1},{4,2},{5,3},{6,4},{7,5},{8,14},{9,15},{10,... | collective-permute-start | bytes 1572872 | tf_op jit(solution)/shard_map/ppermute | solution.py:225
  136.7 17.3 %all-to-all-done.1 = bf16[32,192,128]{2,1,0:T(8,128)(2,1)S(1)} async-done(((bf16[32,192,128]{2,1,0:T(8,128)(2,1)}), bf16[32,192,128]{2,1,0:T(8,128)(2,1)S(1)}, u32[]{:S(2)}, u32[]{:S(2)}) %all-to-all-start.1) | async-done | bytes 1572896 | tf_op jit(solution)/shard_map/all_to_all | solution.py:231
  154.3 5.0 %collective-permute-start.13 = (bf16[192,128]{1,0:T(8,128)(2,1)S(1)}, bf16[192,128]{1,0:T(8,128)(2,1)S(1)}, u32[]{:S(2)}, u32[]{:S(2)}) collective-permute-start(bf16[192,128]{1,0:T(8,128)(2,1)S(1)} %reduce_sum.12), channel_id=1, source_target_pairs={{0,0},{8,1},{2,2},{10,3},{4,4},{12,5},{6,6},{14,7},{64,8},{72,9},{... | collective-permute-start | bytes 147464 | tf_op jit(solution)/shard_map/ppermute | solution.py:233
  160.5 2.9 %shard_map.123 = (bf16[384,512]{1,0:T(8,128)(2,1)}, bf16[384,512]{1,0:T(8,128)(2,1)}) custom-call(s32[1]{0:T(128)} %bitcast.where_ref, s32[1,256]{1,0:T(1,128)} %bitcast.7, s32[1,1]{1,0:T(1,128)} %bitcast.5.refs_1_, f32[1,256]{1,0:T(1,128)} %bitcast.9, bf16[2,256,512]{2,1,0:T(8,128)(2,1)} %get-tuple-element.28.refs_3_, bf16[2,256,512]{2,1,0:T(8,128)(2,1)} %copy-done.8, ...), custom_call_target="tpu_custom_call" | custom-call | flops 201326592 | bytes 2099204 | tf_op jit(solution)/shard_map/pallas_call | solution.py:66
  (33 shorter events, 4.0 us)
Async XLA Ops:
  3.8 14.1 %collective-permute-start = (bf16[192,128]{1,0:T(8,128)(2,1)}, bf16[192,128]{1,0:T(8,128)(2,1)S(1)}, u32[]{:S(2)}, u32[]{:S(2)}) collective-permute-start(bf16[192,128]{1,0:T(8,128)(2,1)} %get-tuple-element.20), channel_id=1, source_target_pairs={{0,0},{1,8},{2,2},{3,10},{4,4},{5,12},{6,6},{7,14},{8,64},{9,72},{... | collective-permute-start | bytes 147464 | tf_op jit(solution)/shard_map/ppermute | solution.py:199
  19.4 10.0 %copy-start.1 = (bf16[2,256,512]{2,1,0:T(8,128)(2,1)S(1)}, bf16[2,256,512]{2,1,0:T(8,128)(2,1)}, u32[]{:S(2)}) copy-start(bf16[2,256,512]{2,1,0:T(8,128)(2,1)} %get-tuple-element.21.refs_1_) | copy-start | bytes 1572868
  19.4 48.0 %all-to-all-start = ((bf16[32,192,128]{2,1,0:T(8,128)(2,1)}), bf16[32,192,128]{2,1,0:T(8,128)(2,1)S(1)}, u32[]{:S(2)}, u32[]{:S(2)}) async-start(bf16[32,192,128]{2,1,0:T(8,128)(2,1)} %broadcast_in_dim.22), calls=%async_computation | async-start | bytes 3145728 | tf_op jit(solution)/shard_map/all_to_all | solution.py:201
  29.4 15.8 %collective-permute-start.3 = (bf16[2,256,512]{2,1,0:T(8,128)(2,1)S(1)}, bf16[2,256,512]{2,1,0:T(8,128)(2,1)S(1)}, u32[]{:S(2)}, u32[]{:S(2)}) collective-permute-start(bf16[2,256,512]{2,1,0:T(8,128)(2,1)S(1)} %copy-done.1), channel_id=1, source_target_pairs={{0,2},{1,3},{2,4},{3,5},{4,6},{5,7},{6,0},{7,1},{8,10},{9,11},{10,... | collective-permute-start | bytes 1572872 | tf_op jit(solution)/shard_map/ppermute | solution.py:202
  32.6 24.9 %collective-permute-start.2 = (bf16[2,256,512]{2,1,0:T(8,128)(2,1)S(1)}, bf16[2,256,512]{2,1,0:T(8,128)(2,1)S(1)}, u32[]{:S(2)}, u32[]{:S(2)}) collective-permute-start(bf16[2,256,512]{2,1,0:T(8,128)(2,1)S(1)} %copy-done.1), channel_id=1, source_target_pairs={{0,4},{1,5},{2,6},{3,7},{4,0},{5,1},{6,2},{7,3},{8,12},{9,13},{10,... | collective-permute-start | bytes 1572872 | tf_op jit(solution)/shard_map/ppermute | solution.py:202
  36.9 24.1 %collective-permute-start.1 = (bf16[2,256,512]{2,1,0:T(8,128)(2,1)S(1)}, bf16[2,256,512]{2,1,0:T(8,128)(2,1)S(1)}, u32[]{:S(2)}, u32[]{:S(2)}) collective-permute-start(bf16[2,256,512]{2,1,0:T(8,128)(2,1)S(1)} %copy-done.1), channel_id=1, source_target_pairs={{0,6},{1,7},{2,0},{3,1},{4,2},{5,3},{6,4},{7,5},{8,14},{9,15},{10,... | collective-permute-start | bytes 1572872 | tf_op jit(solution)/shard_map/ppermute | solution.py:202
  40.0 23.0 %collective-permute-start.4 = (bf16[2,256,512]{2,1,0:T(8,128)(2,1)S(1)}, bf16[2,256,512]{2,1,0:T(8,128)(2,1)S(1)}, u32[]{:S(2)}, u32[]{:S(2)}) collective-permute-start(bf16[2,256,512]{2,1,0:T(8,128)(2,1)S(1)} %copy-done.1), channel_id=1, source_target_pairs={{0,8},{8,0},{16,24},{24,16},{32,40},{40,32},{48,56},{56,48},{64,72... | collective-permute-start | bytes 1572872 | tf_op jit(solution)/shard_map/ppermute | solution.py:203
  45.2 22.1 %copy-start.2 = (bf16[2,256,512]{2,1,0:T(8,128)(2,1)}, bf16[2,256,512]{2,1,0:T(8,128)(2,1)S(1)}, u32[]{:S(2)}) copy-start(bf16[2,256,512]{2,1,0:T(8,128)(2,1)S(1)} %collective-permute-done.3.refs_4_) | copy-start | bytes 1572868
  45.2 17.7 %collective-permute-start.7 = (bf16[2,256,512]{2,1,0:T(8,128)(2,1)S(1)}, bf16[2,256,512]{2,1,0:T(8,128)(2,1)S(1)}, u32[]{:S(2)}, u32[]{:S(2)}) collective-permute-start(bf16[2,256,512]{2,1,0:T(8,128)(2,1)S(1)} %collective-permute-done.3.refs_4_), channel_id=1, source_target_pairs={{0,8},{8,0},{16,24},{24,16},{32,40},{40,32},{48,56},{56,48},{64,72... | collective-permute-start | bytes 1572872 | tf_op jit(solution)/shard_map/ppermute | solution.py:203
  57.5 9.9 %copy-start.3 = (bf16[2,256,512]{2,1,0:T(8,128)(2,1)}, bf16[2,256,512]{2,1,0:T(8,128)(2,1)S(1)}, u32[]{:S(2)}) copy-start(bf16[2,256,512]{2,1,0:T(8,128)(2,1)S(1)} %collective-permute-done.2.refs_3_) | copy-start | bytes 1572868
  57.5 5.5 %collective-permute-start.6 = (bf16[2,256,512]{2,1,0:T(8,128)(2,1)S(1)}, bf16[2,256,512]{2,1,0:T(8,128)(2,1)S(1)}, u32[]{:S(2)}, u32[]{:S(2)}) collective-permute-start(bf16[2,256,512]{2,1,0:T(8,128)(2,1)S(1)} %collective-permute-done.2.refs_3_), channel_id=1, source_target_pairs={{0,8},{8,0},{16,24},{24,16},{32,40},{40,32},{48,56},{56,48},{64,72... | collective-permute-start | bytes 1572872 | tf_op jit(solution)/shard_map/ppermute | solution.py:203
  61.0 2.0 %copy-start.4 = (bf16[2,256,512]{2,1,0:T(8,128)(2,1)}, bf16[2,256,512]{2,1,0:T(8,128)(2,1)S(1)}, u32[]{:S(2)}) copy-start(bf16[2,256,512]{2,1,0:T(8,128)(2,1)S(1)} %collective-permute-done.1.refs_2_) | copy-start | bytes 1572868
  61.0 3.9 %collective-permute-start.5 = (bf16[2,256,512]{2,1,0:T(8,128)(2,1)S(1)}, bf16[2,256,512]{2,1,0:T(8,128)(2,1)}, u32[]{:S(2)}, u32[]{:S(2)}) collective-permute-start(bf16[2,256,512]{2,1,0:T(8,128)(2,1)S(1)} %collective-permute-done.1.refs_2_), channel_id=1, source_target_pairs={{0,8},{8,0},{16,24},{24,16},{32,40},{40,32},{48,56},{56,48},{64,72... | collective-permute-start | bytes 1572872 | tf_op jit(solution)/shard_map/ppermute | solution.py:203
  63.0 0.8 copy-start.5
  63.0 1.0 copy-start.6
  64.0 0.8 copy-start.7
  67.4 1.2 copy-start
  73.7 14.7 %collective-permute-start.8 = (bf16[512,384]{1,0:T(8,128)(2,1)}, bf16[512,384]{1,0:T(8,128)(2,1)S(1)}, u32[]{:S(2)}, u32[]{:S(2)}) collective-permute-start(bf16[512,384]{1,0:T(8,128)(2,1)} %get-tuple-element.23), channel_id=1, source_target_pairs={{0,1},{1,0},{2,3},{3,2},{4,5},{5,4},{6,7},{7,6},{8,9},{9,8},{10,11... | collective-permute-start | bytes 1179656 | tf_op jit(solution)/shard_map/ppermute | solution.py:214
  88.4 0.7 copy-start.11
  99.1 54.9 %all-to-all-start.1 = ((bf16[32,192,128]{2,1,0:T(8,128)(2,1)}), bf16[32,192,128]{2,1,0:T(8,128)(2,1)S(1)}, u32[]{:S(2)}, u32[]{:S(2)}) async-start(bf16[32,192,128]{2,1,0:T(8,128)(2,1)} %shard_map.124), calls=%async_computation.1 | async-start | bytes 3145728 | tf_op jit(solution)/shard_map/all_to_all | solution.py:231
  116.1 6.8 %collective-permute-start.9 = (bf16[4,2,256,512]{3,2,1,0:T(8,128)(2,1)}, bf16[4,2,256,512]{3,2,1,0:T(8,128)(2,1)}, u32[]{:S(2)}, u32[]{:S(2)}) collective-permute-start(bf16[4,2,256,512]{3,2,1,0:T(8,128)(2,1)} %get-tuple-element.27), channel_id=1, source_target_pairs={{0,8},{8,0},{16,24},{24,16},{32,40},{40,32},{48,56},{56,48},{64,72... | collective-permute-start | bytes 6291464 | tf_op jit(solution)/shard_map/ppermute | solution.py:222
  126.7 32.6 %collective-permute-start.10 = (bf16[2,256,512]{2,1,0:T(8,128)(2,1)}, bf16[2,256,512]{2,1,0:T(8,128)(2,1)S(1)}, u32[]{:S(2)}, u32[]{:S(2)}) collective-permute-start(bf16[2,256,512]{2,1,0:T(8,128)(2,1)} %get-tuple-element.29), channel_id=1, source_target_pairs={{0,2},{1,3},{2,4},{3,5},{4,6},{5,7},{6,0},{7,1},{8,10},{9,11},{10,... | collective-permute-start | bytes 1572872 | tf_op jit(solution)/shard_map/ppermute | solution.py:225
  130.1 29.1 %collective-permute-start.11 = (bf16[2,256,512]{2,1,0:T(8,128)(2,1)}, bf16[2,256,512]{2,1,0:T(8,128)(2,1)S(1)}, u32[]{:S(2)}, u32[]{:S(2)}) collective-permute-start(bf16[2,256,512]{2,1,0:T(8,128)(2,1)} %get-tuple-element.30), channel_id=1, source_target_pairs={{0,4},{1,5},{2,6},{3,7},{4,0},{5,1},{6,2},{7,3},{8,12},{9,13},{10,... | collective-permute-start | bytes 1572872 | tf_op jit(solution)/shard_map/ppermute | solution.py:225
  133.5 25.8 %collective-permute-start.12 = (bf16[2,256,512]{2,1,0:T(8,128)(2,1)}, bf16[2,256,512]{2,1,0:T(8,128)(2,1)S(1)}, u32[]{:S(2)}, u32[]{:S(2)}) collective-permute-start(bf16[2,256,512]{2,1,0:T(8,128)(2,1)} %get-tuple-element.31), channel_id=1, source_target_pairs={{0,6},{1,7},{2,0},{3,1},{4,2},{5,3},{6,4},{7,5},{8,14},{9,15},{10,... | collective-permute-start | bytes 1572872 | tf_op jit(solution)/shard_map/ppermute | solution.py:225
  154.3 9.1 %collective-permute-start.13 = (bf16[192,128]{1,0:T(8,128)(2,1)S(1)}, bf16[192,128]{1,0:T(8,128)(2,1)S(1)}, u32[]{:S(2)}, u32[]{:S(2)}) collective-permute-start(bf16[192,128]{1,0:T(8,128)(2,1)S(1)} %reduce_sum.12), channel_id=1, source_target_pairs={{0,0},{8,1},{2,2},{10,3},{4,4},{12,5},{6,6},{14,7},{64,8},{72,9},{... | collective-permute-start | bytes 147464 | tf_op jit(solution)/shard_map/ppermute | solution.py:233
  159.3 0.8 copy-start.8
  159.3 1.0 copy-start.9
  159.3 1.2 copy-start.10

commit v7 on v6

v7 whole, which is shorter than its diff:
```python
import jax
import jax.numpy as jnp
from jax import lax
from jax.experimental import pallas as pl
from jax.experimental.pallas import tpu as pltpu
from jax.sharding import PartitionSpec as P

N_Y, N_Z, N_CORE, N_X = 8, 4, 2, 4
N_WIDE, N_NARROW = N_Y * N_Z * N_CORE, 2 * N_X
F32, BF16 = jnp.float32, jnp.bfloat16
FIRST, LAST, PLAIN = ((0,), (0,)), ((1,), (1,)), ((1,), (0,))


def wide_index(y, z, core):
    return (y * N_Z + z) * N_CORE + core


def swap_pairs():
    pairs = []
    for y in range(N_Y):
        for z in range(N_Z):
            for core in range(N_CORE):
                for n in range(N_NARROW):
                    to = wide_index(y // 2 * 2 + core, z, n % 2)
                    pairs.append((wide_index(y, z, core) * N_NARROW + n, to * N_NARROW + n // 2 * 2 + y % 2))
    return pairs


SWAP = swap_pairs()
SWAP_BACK = [(b, a) for a, b in SWAP]
OTHER_CORE = [(w, w ^ 1) for w in range(N_WIDE)]
OTHER_HALF = [(n, n ^ 1) for n in range(N_NARROW)]
OWNERS = [[wide_index(y, z, core) for y in range(N_Y) for z in range(N_Z)] for core in range(N_CORE)]


def shift_x(by):
    return [(n, (n + 2 * by) % N_NARROW) for n in range(N_NARROW)]


def dot(a, b, dims=PLAIN):
    return lax.dot_general(a, b, (dims, ((), ())), preferred_element_type=F32)


def call(body, outs, flops, where, *args):
    size = sum(a.size * a.dtype.itemsize for a in args)
    count, results = len(args), len(outs)
    most = N_X * results

    def inner(where_ref, *refs):
        sources, targets = refs[:count], refs[count : count + results]
        held, made = refs[count + results : -2 - results], refs[-2 - results : -2]
        sem, out_sem = refs[-2:]
        copies = [
            pltpu.make_async_copy(s, h, sem.at[i]) for i, (s, h) in enumerate(zip(sources, held))
        ]
        for copy in copies:
            copy.start()
        here, leaving = set(), []

        def get(i):
            if i not in here:
                here.add(i)
                copies[i].wait()
            return held[i]

        def put(i, at=slice(None)):
            copy = pltpu.make_async_copy(made[i].at[at], targets[i].at[at], out_sem.at[len(leaving)])
            copy.start()
            leaving.append(copy)
            whole.discard(i)

        whole = set(range(results))
        body(where_ref, get, put, *made)
        for i in sorted(whole):
            put(i)
        for i in range(count):
            get(i)
        for copy in leaving:
            copy.wait()

    shapes = [jax.ShapeDtypeStruct(shape, kind) for shape, kind in outs]
    return pl.pallas_call(
        inner,
        out_shape=shapes,
        in_specs=[pl.BlockSpec(memory_space=pltpu.SMEM)]
        + [pl.BlockSpec(memory_space=pl.ANY)] * count,
        out_specs=[pl.BlockSpec(memory_space=pl.ANY)] * results,
        scratch_shapes=[pltpu.VMEM(a.shape, a.dtype) for a in (*args, *shapes)]
        + [pltpu.SemaphoreType.DMA((count,)), pltpu.SemaphoreType.DMA((most,))],
        compiler_params=pltpu.CompilerParams(vmem_limit_bytes=60 * 1024 * 1024),
        cost_estimate=pl.CostEstimate(flops=flops, bytes_accessed=size, transcendentals=0),
    )(where, *args)


def use_of(gate, count):
    slots = gate.shape[1]
    lane = lax.broadcasted_iota(jnp.int32, (1, slots), 1)
    use = jnp.where(lane < count, gate, 0.0)
    square = lax.broadcasted_iota(jnp.int32, (slots, slots), 0) == lax.broadcasted_iota(
        jnp.int32, (slots, slots), 1
    )
    return jnp.sum(jnp.where(square, use, 0.0), axis=1, keepdims=True)


def pick_of(token, tok):
    slots = token.shape[1]
    return jnp.where(lax.broadcasted_iota(jnp.int32, (tok, slots), 0) == token, 1.0, 0.0).astype(BF16)


def block_body(where, get, put, block):
    rows = block.shape[0] // 3
    for i in range(3):
        block[rows * i : rows * (i + 1)] = get(i)[...]


def rows_body(where, get, put, own):
    token, count, gate, tokens = get(2), get(3), get(4), get(0)
    pick = pick_of(token[...], tokens.shape[0])
    own[0] = dot(pick, tokens[...], FIRST).astype(BF16)
    put(0, pl.ds(0, 1))
    own[1] = (use_of(gate[...], count[...]) * dot(pick, get(1)[...], FIRST)).astype(BF16)
    put(0, pl.ds(1, 1))


def turned_body(where, get, put, *turned):
    slots = get(0).shape[1]
    for step in range(N_X):
        for who in range(2):
            for which in range(2):
                turned[step][which, :, slots * who : slots * (who + 1)] = get(who * N_X + step)[which].T
        put(step)


def turn(where, step, size):
    return pl.multiple_of(lax.rem(where[0] + step, N_X) * size, size)


def assemble(pieces, both, down):
    rows, cols = pieces.shape[1] // 3, pieces.shape[2]
    for i in range(pieces.shape[0]):
        y, z = divmod(i, N_Z)
        place = y // 2 * 8 + z * 2 + y % 2
        at = slice(place * rows, (place + 1) * rows)
        both[at, :cols] = pieces[i, :rows]
        both[at, cols:] = pieces[i, rows : 2 * rows]
        down[at] = pieces[i, 2 * rows :]


def products_body(where, get, put, part, both, down):
    assemble(get(0), both, down)
    put(1)
    put(2)
    cols = down.shape[1]
    slots, feat = get(1).shape[1:]
    for who in range(2):
        pre, back = 0.0, 0.0
        for step in range(N_X):
            x = get(1 + who * N_X + step)
            at = pl.ds(turn(where, step, feat), feat)
            pre = pre + dot(x[0], both[at])
            back = back + dot(x[1], down[at])
        at = slice(slots * who, slots * (who + 1))
        part[at, : 2 * cols] = pre.astype(BF16)
        part[at, 2 * cols :] = back.astype(BF16)
        put(0, pl.ds(slots * who, slots))


def terms_body(where, get, put, pieces, acts):
    total = get(0)[...].astype(F32) + get(1)[...].astype(F32)
    units = total.shape[1] // 3
    pre_gate, pre_up, grad_hidden = total[:, :units], total[:, units : 2 * units], total[:, 2 * units :]
    sigma = jax.nn.sigmoid(pre_gate)
    acts[:, :units] = (
        grad_hidden * pre_up * sigma * (1.0 + pre_gate * (1.0 - sigma))
    ).astype(BF16)
    acts[:, units : 2 * units] = (grad_hidden * pre_gate * sigma).astype(BF16)
    acts[:, 2 * units :] = (pre_gate * sigma * pre_up).astype(BF16)
    put(1)
    rows = pieces.shape[1] // 3
    for step in range(N_X):
        turned = get(2 + step)
        both = dot(turned[0], acts[:, : 2 * units]).astype(BF16)
        down = dot(turned[1], acts[:, 2 * units :]).astype(BF16)
        first = turn(where, step, 2 * N_Z)
        for i in range(2 * N_Z):
            y, z = divmod(i, N_Z)
            at = slice((z * 2 + y) * rows, (z * 2 + y + 1) * rows)
            pieces[first + i, :rows] = both[at, :units]
            pieces[first + i, rows : 2 * rows] = both[at, units:]
            pieces[first + i, 2 * rows :] = down[at]
        put(0, pl.ds(first, 2 * N_Z))


def outputs_body(where, get, put, send, mine):
    acts, both, down = [get(i) for i in range(3)]
    units = acts.shape[1] // 3
    slots, feat = mine.shape[2:]
    for step in (2, 1, 3, 0):
        at = pl.ds(turn(where, step, feat), feat)
        for which, out in enumerate(
            (dot(acts[:, 2 * units :], down[at], LAST), dot(acts[:, : 2 * units], both[at], LAST))
        ):
            mine[step, which] = out[:slots].astype(BF16)
            send[step, which] = out[slots:].astype(BF16)
        put(0, pl.ds(step, 1))
        put(1, pl.ds(step, 1))


def tokens_body(where, get, put, mixed, grad_tokens):
    token, count, gate = get(0), get(1), get(2)
    pick = pick_of(token[...], mixed.shape[0])
    out, back = [sum(get(3 + step)[i].astype(F32) for step in range(N_X)) for i in range(2)]
    mixed[...] = dot(pick, (use_of(gate[...], count[...]) * out).astype(BF16)).astype(BF16)
    put(0)
    grad_tokens[...] = dot(pick, back.astype(BF16)).astype(BF16)


def local(tokens, grad_out, slot_token, slot_count, slot_gate, w_gate, w_up, w_down):
    slots, (tok, feat) = slot_token.shape[0], tokens.shape
    rows, cols = w_gate.shape
    token, gate, count = slot_token[None], slot_gate[None], slot_count[None]
    where = (lax.axis_index("narrow") // 2).astype(jnp.int32)[None]
    pick_flops = 4 * slots * tok * feat

    (block,) = call(block_body, [((3 * rows, cols), BF16)], 0, where, w_gate, w_up, w_down)
    block = lax.ppermute(block, ("wide", "narrow"), SWAP)
    pieces = jnp.broadcast_to(block[None], (len(OWNERS[0]),) + block.shape)
    pieces = lax.all_to_all(pieces, "wide", 0, 0, axis_index_groups=OWNERS)
    (own,) = call(
        rows_body,
        [((2, slots, feat), BF16)],
        pick_flops,
        where,
        *(tokens, grad_out, token, count, gate),
    )
    near = [own] + [lax.ppermute(own, "narrow", shift_x(-step)) for step in range(1, N_X)]
    core = [lax.ppermute(held, "wide", OTHER_CORE) for held in near]
    turned = call(
        turned_body, [((2, feat, 2 * slots), BF16)] * N_X, pick_flops, where, *near, *core
    )

    flops = 2 * 3 * 2 * slots * N_X * feat * cols
    part = ((2 * slots, 3 * cols), BF16)
    sent, both, down = call(
        products_body,
        [part, ((N_X * feat, 2 * cols), BF16), ((N_X * feat, cols), BF16)],
        flops,
        where,
        *(pieces, *near, *core),
    )
    theirs = lax.ppermute(sent, "narrow", OTHER_HALF)
    terms, acts = call(
        terms_body,
        [(pieces.shape, BF16), part],
        flops,
        where,
        *(sent, theirs, *turned),
    )

    terms = lax.all_to_all(terms, "wide", 0, 0, axis_index_groups=OWNERS)
    grads = terms.astype(F32).sum(axis=0).astype(BF16)
    grads = lax.ppermute(grads, ("wide", "narrow"), SWAP_BACK).astype(F32)

    every = ((N_X, 2, slots, feat), BF16)
    send, mine = call(outputs_body, [every, every], flops, where, acts, both, down)
    got = lax.ppermute(send, "wide", OTHER_CORE)
    sums = [(mine[step].astype(F32) + got[step].astype(F32)).astype(BF16) for step in range(N_X)]
    home = [sums[0]] + [
        lax.ppermute(sums[step], "narrow", shift_x(step)) for step in range(1, N_X)
    ]
    mixed, grad_tokens = call(
        tokens_body, [((tok, feat), BF16)] * 2, pick_flops, where, token, count, gate, *home
    )
    return mixed, grad_tokens, grads[:rows], grads[rows : 2 * rows], grads[2 * rows :]


def solution(mesh):
    both = P("wide", "narrow")
    in_specs = (both, both, P("wide"), P("wide"), P("wide"), both, both, both)
    return jax.shard_map(
        local, mesh=mesh, in_specs=in_specs, out_specs=(both,) * 5, check_vma=False
    )
```

time: 166 us -> 162 us (0.976)
  waiting for transfers between devices: 56.5 us -> 50.3 us
  other arithmetic: 0.22 us -> 3.35 us
  starting transfers between devices: 74.5 us -> 76.3 us
    ppermute x1, waiting for transfers between devices: 12.8 us -> 8.3 us  [local(): theirs = lax.ppermute(sent, 'narrow', OTHER_HALF)]
    convert_element_type x0 -> x1, other arithmetic: none -> 3.12 us  [local(): (mine[step].astype(F32) + got[step].astype(F32)).astype(BF16)]
    ppermute x3, waiting for transfers between devices: 0.01 us -> 3.08 us  [local(): lax.ppermute(sums[step], 'narrow', shift_x(step))]
    all_to_all x1, waiting for transfers between devices: 2.42 us -> 0.01 us  [local(): pieces = lax.all_to_all(pieces, 'wide', 0, 0, axis_index_groups=OWNERS)]
    all_to_all x1, waiting for transfers between devices: 17.3 us -> 14.9 us  [local(): terms = lax.all_to_all(terms, 'wide', 0, 0, axis_index_groups=OWNERS)]
    unnamed x24 -> x20, local copies, waits for them, and re-layouts: 4.85 us -> 3.74 us
    pallas_call x6 -> x7, Pallas kernels: 24.2 us -> 23.8 us  [call(): pl.pallas_call(inner, out_shape=shapes, in_specs=[pl.BlockSpec(memory_spa...]
  transfers between devices with their start and end apart: 16 -> 16, of which waited for: 8 -> 8; matrix products, arithmetic and copies ran while one was open for 0% -> 2% of each run, Pallas kernels for 4% -> 8%
where the time goes in v7:
time: 162 us; the launch traced here: 161 us
  starting transfers between devices  76.3 us (47%)
  waiting for transfers between devices  50.3 us (31%)
  Pallas kernels  23.8 us (15%)
  local copies, waits for them, and re-layouts  5.93 us (4%)
  other arithmetic  3.35 us (2%)
    pallas_call x7, Pallas kernels, call(): pl.pallas_call(inner, out_shape=shapes, in_specs=[pl.BlockSpec(memory_spa...  23.8 us
    all_to_all x1, starting transfers between devices, local(): terms = lax.all_to_all(terms, 'wide', 0, 0, axis_index_groups=OWNERS)  18.6 us
    all_to_all x1, waiting for transfers between devices, local(): terms = lax.all_to_all(terms, 'wide', 0, 0, axis_index_groups=OWNERS)  14.9 us
    ppermute x4, starting transfers between devices, local(): core = [lax.ppermute(held, 'wide', OTHER_CORE) for held in near]  12.7 us
    ppermute x3, starting transfers between devices, local(): lax.ppermute(own, 'narrow', shift_x(-step))  10.5 us
    ppermute x3, waiting for transfers between devices, local(): lax.ppermute(own, 'narrow', shift_x(-step))  10.4 us
    all_to_all x1, starting transfers between devices, local(): pieces = lax.all_to_all(pieces, 'wide', 0, 0, axis_index_groups=OWNERS)  9.89 us
    ppermute x1, waiting for transfers between devices, local(): block = lax.ppermute(block, ('wide', 'narrow'), SWAP)  9.46 us
  transfers between devices with their start and end apart: 16, of which 8 were waited for; matrix products, arithmetic and copies ran while one was open for 2% of the time, Pallas kernels for 8%

profile of v7, /device:TPU:1, one launch (start us, length us, event | category | flops | bytes accessed | tf_op | source)
XLA Modules:
  0.0 161.3 jit_solution(680859348104927695)
XLA Ops:
  0.6 1.4 shard_map.119
  2.1 4.6 %collective-permute-start = (bf16[192,128]{1,0:T(8,128)(2,1)}, bf16[192,128]{1,0:T(8,128)(2,1)S(1)}, u32[]{:S(2)}, u32[]{:S(2)}) collective-permute-start(bf16[192,128]{1,0:T(8,128)(2,1)} %shard_map.119), channel_id=1, source_target_pairs={{0,0},{1,8},{2,2},{3,10},{4,4},{5,12},{6,6},{7,14},{8,64},{9,72},{... | collective-permute-start | bytes 147464 | tf_op jit(solution)/shard_map/ppermute | solution.py:226
  6.7 9.5 %collective-permute-done = bf16[192,128]{1,0:T(8,128)(2,1)S(1)} collective-permute-done((bf16[192,128]{1,0:T(8,128)(2,1)}, bf16[192,128]{1,0:T(8,128)(2,1)S(1)}, u32[]{:S(2)}, u32[]{:S(2)}) %collective-permute-start) | collective-permute-done | bytes 49184 | tf_op jit(solution)/shard_map/ppermute | solution.py:226
  16.1 1.5 broadcast_in_dim.22
  17.7 9.9 %all-to-all-start = ((bf16[32,192,128]{2,1,0:T(8,128)(2,1)}), bf16[32,192,128]{2,1,0:T(8,128)(2,1)S(1)}, u32[]{:S(2)}, u32[]{:S(2)}) async-start(bf16[32,192,128]{2,1,0:T(8,128)(2,1)} %broadcast_in_dim.22), calls=%async_computation | async-start | bytes 3145728 | tf_op jit(solution)/shard_map/all_to_all | solution.py:228
  28.2 2.4 %shard_map.120.refs_1_.refs_0_ = bf16[2,256,512]{2,1,0:T(8,128)(2,1)} custom-call(s32[1]{0:T(128)} %bitcast.where_ref, bf16[384,512]{1,0:T(8,128)(2,1)} %refs_0_.3, bf16[384,512]{1,0:T(8,128)(2,1)} %refs_1_.3, s32[1,256]{1,0:T(1,128)} %bitcast.14, s32[1,1]{1,0:T(1,128)} %bitcast.12.refs_3_, f32[1,256]{1,0:T(1,128)} %bitcast.16), custom_call_target="tpu_custom_call" | custom-call | flops 201326592 | bytes 788484 | tf_op jit(solution)/shard_map/pallas_call | solution.py:82
  30.7 3.1 %collective-permute-start.3 = (bf16[2,256,512]{2,1,0:T(8,128)(2,1)}, bf16[2,256,512]{2,1,0:T(8,128)(2,1)S(1)}, u32[]{:S(2)}, u32[]{:S(2)}) collective-permute-start(bf16[2,256,512]{2,1,0:T(8,128)(2,1)} %shard_map.120.refs_1_.refs_0_), channel_id=1, source_target_pairs={{0,2},{1,3},{2,4},{3,5},{4,6},{5,7},{6,0},{7,1},{8,10},{9,11},{10,... | collective-permute-start | bytes 1572872 | tf_op jit(solution)/shard_map/ppermute | solution.py:236
  33.8 4.4 %collective-permute-start.2 = (bf16[2,256,512]{2,1,0:T(8,128)(2,1)}, bf16[2,256,512]{2,1,0:T(8,128)(2,1)S(1)}, u32[]{:S(2)}, u32[]{:S(2)}) collective-permute-start(bf16[2,256,512]{2,1,0:T(8,128)(2,1)} %shard_map.120.refs_1_.refs_0_), channel_id=1, source_target_pairs={{0,4},{1,5},{2,6},{3,7},{4,0},{5,1},{6,2},{7,3},{8,12},{9,13},{10,... | collective-permute-start | bytes 1572872 | tf_op jit(solution)/shard_map/ppermute | solution.py:236
  38.1 3.1 %collective-permute-start.1 = (bf16[2,256,512]{2,1,0:T(8,128)(2,1)}, bf16[2,256,512]{2,1,0:T(8,128)(2,1)S(1)}, u32[]{:S(2)}, u32[]{:S(2)}) collective-permute-start(bf16[2,256,512]{2,1,0:T(8,128)(2,1)} %shard_map.120.refs_1_.refs_0_), channel_id=1, source_target_pairs={{0,6},{1,7},{2,0},{3,1},{4,2},{5,3},{6,4},{7,5},{8,14},{9,15},{10,... | collective-permute-start | bytes 1572872 | tf_op jit(solution)/shard_map/ppermute | solution.py:236
  41.2 3.5 %collective-permute-start.4 = (bf16[2,256,512]{2,1,0:T(8,128)(2,1)}, bf16[2,256,512]{2,1,0:T(8,128)(2,1)S(1)}, u32[]{:S(2)}, u32[]{:S(2)}) collective-permute-start(bf16[2,256,512]{2,1,0:T(8,128)(2,1)} %shard_map.120.refs_1_.refs_0_), channel_id=1, source_target_pairs={{0,8},{8,0},{16,24},{24,16},{32,40},{40,32},{48,56},{56,48},{64,72... | collective-permute-start | bytes 1572872 | tf_op jit(solution)/shard_map/ppermute | solution.py:237
  44.7 1.9 %collective-permute-done.3.refs_4_.refs_3_ = bf16[2,256,512]{2,1,0:T(8,128)(2,1)S(1)} collective-permute-done((bf16[2,256,512]{2,1,0:T(8,128)(2,1)}, bf16[2,256,512]{2,1,0:T(8,128)(2,1)S(1)}, u32[]{:S(2)}, u32[]{:S(2)}) %collective-permute-start.3) | collective-permute-done | bytes 524320 | tf_op jit(solution)/shard_map/ppermute | solution.py:236
  46.7 3.8 %collective-permute-start.7 = (bf16[2,256,512]{2,1,0:T(8,128)(2,1)S(1)}, bf16[2,256,512]{2,1,0:T(8,128)(2,1)S(1)}, u32[]{:S(2)}, u32[]{:S(2)}) collective-permute-start(bf16[2,256,512]{2,1,0:T(8,128)(2,1)S(1)} %collective-permute-done.3.refs_4_.refs_3_), channel_id=1, source_target_pairs={{0,8},{8,0},{16,24},{24,16},{32,40},{40,32},{48,56},{56,48},{64,72... | collective-permute-start | bytes 1572872 | tf_op jit(solution)/shard_map/ppermute | solution.py:237
  50.5 8.4 %collective-permute-done.2.refs_3_.refs_2_ = bf16[2,256,512]{2,1,0:T(8,128)(2,1)S(1)} collective-permute-done((bf16[2,256,512]{2,1,0:T(8,128)(2,1)}, bf16[2,256,512]{2,1,0:T(8,128)(2,1)S(1)}, u32[]{:S(2)}, u32[]{:S(2)}) %collective-permute-start.2) | collective-permute-done | bytes 524320 | tf_op jit(solution)/shard_map/ppermute | solution.py:236
  58.9 3.5 %collective-permute-start.6 = (bf16[2,256,512]{2,1,0:T(8,128)(2,1)S(1)}, bf16[2,256,512]{2,1,0:T(8,128)(2,1)S(1)}, u32[]{:S(2)}, u32[]{:S(2)}) collective-permute-start(bf16[2,256,512]{2,1,0:T(8,128)(2,1)S(1)} %collective-permute-done.2.refs_3_.refs_2_), channel_id=1, source_target_pairs={{0,8},{8,0},{16,24},{24,16},{32,40},{40,32},{48,56},{56,48},{64,72... | collective-permute-start | bytes 1572872 | tf_op jit(solution)/shard_map/ppermute | solution.py:237
  62.5 1.9 %collective-permute-start.5 = (bf16[2,256,512]{2,1,0:T(8,128)(2,1)S(1)}, bf16[2,256,512]{2,1,0:T(8,128)(2,1)}, u32[]{:S(2)}, u32[]{:S(2)}) collective-permute-start(bf16[2,256,512]{2,1,0:T(8,128)(2,1)S(1)} %collective-permute-done.1.refs_2_.refs_1_), channel_id=1, source_target_pairs={{0,8},{8,0},{16,24},{24,16},{32,40},{40,32},{48,56},{56,48},{64,72... | collective-permute-start | bytes 1572872 | tf_op jit(solution)/shard_map/ppermute | solution.py:237
  67.6 4.6 %shard_map.121 = (bf16[512,384]{1,0:T(8,128)(2,1)}, bf16[2048,256]{1,0:T(8,128)(2,1)}, bf16[2048,128]{1,0:T(8,128)(2,1)}) custom-call(s32[1]{0:T(128)} %bitcast.where_ref, bf16[32,192,128]{2,1,0:T(8,128)(2,1)} %copy-done, bf16[2,256,512]{2,1,0:T(8,128)(2,1)} %shard_map.120.refs_1_.refs_0_, bf16[2,256,512]{2,1,0:T(8,128)(2,1)} %copy-done.3, ...), custom_call_target="tpu_custom_call" | custom-call | flops 805306368 | bytes 5767168 | tf_op jit(solution)/shard_map/pallas_call | solution.py:82
  72.2 3.1 %collective-permute-start.8 = (bf16[512,384]{1,0:T(8,128)(2,1)}, bf16[512,384]{1,0:T(8,128)(2,1)S(1)}, u32[]{:S(2)}, u32[]{:S(2)}) collective-permute-start(bf16[512,384]{1,0:T(8,128)(2,1)} %get-tuple-element.18.refs_0_), channel_id=1, source_target_pairs={{0,1},{1,0},{2,3},{3,2},{4,5},{5,4},{6,7},{7,6},{8,9},{9,8},{10,11... | collective-permute-start | bytes 1179656 | tf_op jit(solution)/shard_map/ppermute | solution.py:251
  75.3 4.2 %shard_map.122 = (bf16[2,512,512]{2,1,0:T(8,128)(2,1)}, bf16[2,512,512]{2,1,0:T(8,128)(2,1)}, bf16[2,512,512]{2,1,0:T(8,128)(2,1)}, bf16[2,512,512]{2,1,0:T(8,128)(2,1)}) custom-call(s32[1]{0:T(128)} %bitcast.where_ref, bf16[2,256,512]{2,1,0:T(8,128)(2,1)} %shard_map.120.refs_1_.refs_0_, bf16[2,256,512]{2,1,0:T(8,128)(2,1)} %copy-done.3, ...), custom_call_target="tpu_custom_call" | custom-call | flops 201326592 | bytes 4194304 | tf_op jit(solution)/shard_map/pallas_call | solution.py:82
  79.5 8.3 %collective-permute-done.8.refs_1_ = bf16[512,384]{1,0:T(8,128)(2,1)S(1)} collective-permute-done((bf16[512,384]{1,0:T(8,128)(2,1)}, bf16[512,384]{1,0:T(8,128)(2,1)S(1)}, u32[]{:S(2)}, u32[]{:S(2)}) %collective-permute-start.8) | collective-permute-done | bytes 393248 | tf_op jit(solution)/shard_map/ppermute | solution.py:251
  88.5 4.1 %shard_map.123 = (bf16[32,192,128]{2,1,0:T(8,128)(2,1)}, bf16[512,384]{1,0:T(8,128)(2,1)}) custom-call(s32[1]{0:T(128)} %bitcast.where_ref, bf16[512,384]{1,0:T(8,128)(2,1)} %get-tuple-element.18.refs_0_, bf16[512,384]{1,0:T(8,128)(2,1)} %copy-done.9, bf16[2,512,512]{2,1,0:T(8,128)(2,1)} %get-tuple-element.19.refs_2_, ...), custom_call_target="tpu_custom_call" | custom-call | flops 805306368 | bytes 4980736 | tf_op jit(solution)/shard_map/pallas_call | solution.py:82
  92.7 18.6 %all-to-all-start.1 = ((bf16[32,192,128]{2,1,0:T(8,128)(2,1)}), bf16[32,192,128]{2,1,0:T(8,128)(2,1)S(1)}, u32[]{:S(2)}, u32[]{:S(2)}) async-start(bf16[32,192,128]{2,1,0:T(8,128)(2,1)} %get-tuple-element.30), calls=%async_computation.1 | async-start | bytes 3145728 | tf_op jit(solution)/shard_map/all_to_all | solution.py:260
  111.2 4.0 %shard_map.124 = (bf16[4,2,256,512]{3,2,1,0:T(8,128)(2,1)}, bf16[4,2,256,512]{3,2,1,0:T(8,128)(2,1)}) custom-call(s32[1]{0:T(128)} %bitcast.where_ref, bf16[512,384]{1,0:T(8,128)(2,1)} %get-tuple-element.23.refs_0_, bf16[2048,256]{1,0:T(8,128)(2,1)} %get-tuple-element.24.refs_1_, bf16[2048,128]{1,0:T(8,128)(2,1)} %get-tuple-element.25.refs_2_), custom_call_target="tpu_custom_call" | custom-call | flops 805306368 | bytes 1966080 | tf_op jit(solution)/shard_map/pallas_call | solution.py:82
  115.3 2.7 %collective-permute-start.9 = (bf16[4,2,256,512]{3,2,1,0:T(8,128)(2,1)}, bf16[4,2,256,512]{3,2,1,0:T(8,128)(2,1)S(1)}, u32[]{:S(2)}, u32[]{:S(2)}) collective-permute-start(bf16[4,2,256,512]{3,2,1,0:T(8,128)(2,1)} %get-tuple-element.27), channel_id=1, source_target_pairs={{0,8},{8,0},{16,24},{24,16},{32,40},{40,32},{48,56},{56,48},{64,72... | collective-permute-start | bytes 6291464 | tf_op jit(solution)/shard_map/ppermute | solution.py:266
  118.0 4.0 %collective-permute-done.9 = bf16[4,2,256,512]{3,2,1,0:T(8,128)(2,1)S(1)} collective-permute-done((bf16[4,2,256,512]{3,2,1,0:T(8,128)(2,1)}, bf16[4,2,256,512]{3,2,1,0:T(8,128)(2,1)S(1)}, u32[]{:S(2)}, u32[]{:S(2)}) %collective-permute-start.9) | collective-permute-done | bytes 2097184 | tf_op jit(solution)/shard_map/ppermute | solution.py:266
  122.0 3.1 %fusion.3 = (bf16[2,256,512]{2,1,0:T(8,128)(2,1)}, bf16[2,256,512]{2,1,0:T(8,128)(2,1)}, bf16[2,256,512]{2,1,0:T(8,128)(2,1)S(1)}, bf16[2,256,512]{2,1,0:T(8,128)(2,1)}) fusion(bf16[4,2,256,512]{3,2,1,0:T(8,128)(2,1)S(1)} %collective-permute-done.9, bf16[4,2,256,512]{3,2,1,0:T(8,128)(2,1)} %get-tuple-element.26), kind=kLoop, calls=%fused_computation.7 | loop fusion | flops 4194304 | bytes 6291456 | tf_op jit(solution)/shard_map/convert_element_type | solution.py:267
  125.1 3.7 %collective-permute-start.12 = (bf16[2,256,512]{2,1,0:T(8,128)(2,1)}, bf16[2,256,512]{2,1,0:T(8,128)(2,1)S(1)}, u32[]{:S(2)}, u32[]{:S(2)}) collective-permute-start(bf16[2,256,512]{2,1,0:T(8,128)(2,1)} %get-tuple-element.31), channel_id=1, source_target_pairs={{0,6},{1,7},{2,0},{3,1},{4,2},{5,3},{6,4},{7,5},{8,14},{9,15},{10,... | collective-permute-start | bytes 1572872 | tf_op jit(solution)/shard_map/ppermute | solution.py:269
  128.8 3.4 %collective-permute-start.11 = (bf16[2,256,512]{2,1,0:T(8,128)(2,1)}, bf16[2,256,512]{2,1,0:T(8,128)(2,1)S(1)}, u32[]{:S(2)}, u32[]{:S(2)}) collective-permute-start(bf16[2,256,512]{2,1,0:T(8,128)(2,1)} %get-tuple-element.32), channel_id=1, source_target_pairs={{0,4},{1,5},{2,6},{3,7},{4,0},{5,1},{6,2},{7,3},{8,12},{9,13},{10,... | collective-permute-start | bytes 1572872 | tf_op jit(solution)/shard_map/ppermute | solution.py:269
  132.3 1.9 %collective-permute-start.10 = (bf16[2,256,512]{2,1,0:T(8,128)(2,1)S(1)}, bf16[2,256,512]{2,1,0:T(8,128)(2,1)}, u32[]{:S(2)}, u32[]{:S(2)}) collective-permute-start(bf16[2,256,512]{2,1,0:T(8,128)(2,1)S(1)} %get-tuple-element.33), channel_id=1, source_target_pairs={{0,2},{1,3},{2,4},{3,5},{4,6},{5,7},{6,0},{7,1},{8,10},{9,11},{10,... | collective-permute-start | bytes 1572872 | tf_op jit(solution)/shard_map/ppermute | solution.py:269
  134.2 14.9 %all-to-all-done.1 = bf16[32,192,128]{2,1,0:T(8,128)(2,1)S(1)} async-done(((bf16[32,192,128]{2,1,0:T(8,128)(2,1)}), bf16[32,192,128]{2,1,0:T(8,128)(2,1)S(1)}, u32[]{:S(2)}, u32[]{:S(2)}) %all-to-all-start.1) | async-done | bytes 1572896 | tf_op jit(solution)/shard_map/all_to_all | solution.py:260
  149.3 5.2 %collective-permute-start.13 = (bf16[192,128]{1,0:T(8,128)(2,1)S(1)}, bf16[192,128]{1,0:T(8,128)(2,1)S(1)}, u32[]{:S(2)}, u32[]{:S(2)}) collective-permute-start(bf16[192,128]{1,0:T(8,128)(2,1)S(1)} %reduce_sum.12), channel_id=1, source_target_pairs={{0,0},{8,1},{2,2},{10,3},{4,4},{12,5},{6,6},{14,7},{64,8},{72,9},{... | collective-permute-start | bytes 147464 | tf_op jit(solution)/shard_map/ppermute | solution.py:262
  154.5 3.1 %collective-permute-done.10.refs_4_ = bf16[2,256,512]{2,1,0:T(8,128)(2,1)} collective-permute-done((bf16[2,256,512]{2,1,0:T(8,128)(2,1)S(1)}, bf16[2,256,512]{2,1,0:T(8,128)(2,1)}, u32[]{:S(2)}, u32[]{:S(2)}) %collective-permute-start.10) | collective-permute-done | bytes 524320 | tf_op jit(solution)/shard_map/ppermute | solution.py:269
  157.6 3.0 %shard_map.125 = (bf16[384,512]{1,0:T(8,128)(2,1)}, bf16[384,512]{1,0:T(8,128)(2,1)}) custom-call(s32[1]{0:T(128)} %bitcast.where_ref, s32[1,256]{1,0:T(1,128)} %bitcast.15, s32[1,1]{1,0:T(1,128)} %bitcast.13.refs_1_, f32[1,256]{1,0:T(1,128)} %bitcast.17, bf16[2,256,512]{2,1,0:T(8,128)(2,1)} %get-tuple-element.34.refs_3_, ...), custom_call_target="tpu_custom_call" | custom-call | flops 201326592 | bytes 2099204 | tf_op jit(solution)/shard_map/pallas_call | solution.py:82
  (31 shorter events, 4.8 us)
Async XLA Ops:
  2.1 14.1 %collective-permute-start = (bf16[192,128]{1,0:T(8,128)(2,1)}, bf16[192,128]{1,0:T(8,128)(2,1)S(1)}, u32[]{:S(2)}, u32[]{:S(2)}) collective-permute-start(bf16[192,128]{1,0:T(8,128)(2,1)} %shard_map.119), channel_id=1, source_target_pairs={{0,0},{1,8},{2,2},{3,10},{4,4},{5,12},{6,6},{7,14},{8,64},{9,72},{... | collective-permute-start | bytes 147464 | tf_op jit(solution)/shard_map/ppermute | solution.py:226
  17.7 48.7 %all-to-all-start = ((bf16[32,192,128]{2,1,0:T(8,128)(2,1)}), bf16[32,192,128]{2,1,0:T(8,128)(2,1)S(1)}, u32[]{:S(2)}, u32[]{:S(2)}) async-start(bf16[32,192,128]{2,1,0:T(8,128)(2,1)} %broadcast_in_dim.22), calls=%async_computation | async-start | bytes 3145728 | tf_op jit(solution)/shard_map/all_to_all | solution.py:228
  30.7 16.0 %collective-permute-start.3 = (bf16[2,256,512]{2,1,0:T(8,128)(2,1)}, bf16[2,256,512]{2,1,0:T(8,128)(2,1)S(1)}, u32[]{:S(2)}, u32[]{:S(2)}) collective-permute-start(bf16[2,256,512]{2,1,0:T(8,128)(2,1)} %shard_map.120.refs_1_.refs_0_), channel_id=1, source_target_pairs={{0,2},{1,3},{2,4},{3,5},{4,6},{5,7},{6,0},{7,1},{8,10},{9,11},{10,... | collective-permute-start | bytes 1572872 | tf_op jit(solution)/shard_map/ppermute | solution.py:236
  33.8 25.1 %collective-permute-start.2 = (bf16[2,256,512]{2,1,0:T(8,128)(2,1)}, bf16[2,256,512]{2,1,0:T(8,128)(2,1)S(1)}, u32[]{:S(2)}, u32[]{:S(2)}) collective-permute-start(bf16[2,256,512]{2,1,0:T(8,128)(2,1)} %shard_map.120.refs_1_.refs_0_), channel_id=1, source_target_pairs={{0,4},{1,5},{2,6},{3,7},{4,0},{5,1},{6,2},{7,3},{8,12},{9,13},{10,... | collective-permute-start | bytes 1572872 | tf_op jit(solution)/shard_map/ppermute | solution.py:236
  38.1 24.3 %collective-permute-start.1 = (bf16[2,256,512]{2,1,0:T(8,128)(2,1)}, bf16[2,256,512]{2,1,0:T(8,128)(2,1)S(1)}, u32[]{:S(2)}, u32[]{:S(2)}) collective-permute-start(bf16[2,256,512]{2,1,0:T(8,128)(2,1)} %shard_map.120.refs_1_.refs_0_), channel_id=1, source_target_pairs={{0,6},{1,7},{2,0},{3,1},{4,2},{5,3},{6,4},{7,5},{8,14},{9,15},{10,... | collective-permute-start | bytes 1572872 | tf_op jit(solution)/shard_map/ppermute | solution.py:236
  41.2 23.2 %collective-permute-start.4 = (bf16[2,256,512]{2,1,0:T(8,128)(2,1)}, bf16[2,256,512]{2,1,0:T(8,128)(2,1)S(1)}, u32[]{:S(2)}, u32[]{:S(2)}) collective-permute-start(bf16[2,256,512]{2,1,0:T(8,128)(2,1)} %shard_map.120.refs_1_.refs_0_), channel_id=1, source_target_pairs={{0,8},{8,0},{16,24},{24,16},{32,40},{40,32},{48,56},{56,48},{64,72... | collective-permute-start | bytes 1572872 | tf_op jit(solution)/shard_map/ppermute | solution.py:237
  46.7 19.7 %copy-start.1 = (bf16[2,256,512]{2,1,0:T(8,128)(2,1)}, bf16[2,256,512]{2,1,0:T(8,128)(2,1)S(1)}, u32[]{:S(2)}) copy-start(bf16[2,256,512]{2,1,0:T(8,128)(2,1)S(1)} %collective-permute-done.3.refs_4_.refs_3_) | copy-start | bytes 1572868
  46.7 17.7 %collective-permute-start.7 = (bf16[2,256,512]{2,1,0:T(8,128)(2,1)S(1)}, bf16[2,256,512]{2,1,0:T(8,128)(2,1)S(1)}, u32[]{:S(2)}, u32[]{:S(2)}) collective-permute-start(bf16[2,256,512]{2,1,0:T(8,128)(2,1)S(1)} %collective-permute-done.3.refs_4_.refs_3_), channel_id=1, source_target_pairs={{0,8},{8,0},{16,24},{24,16},{32,40},{40,32},{48,56},{56,48},{64,72... | collective-permute-start | bytes 1572872 | tf_op jit(solution)/shard_map/ppermute | solution.py:237
  58.9 7.5 %copy-start.2 = (bf16[2,256,512]{2,1,0:T(8,128)(2,1)}, bf16[2,256,512]{2,1,0:T(8,128)(2,1)S(1)}, u32[]{:S(2)}) copy-start(bf16[2,256,512]{2,1,0:T(8,128)(2,1)S(1)} %collective-permute-done.2.refs_3_.refs_2_) | copy-start | bytes 1572868
  58.9 5.5 %collective-permute-start.6 = (bf16[2,256,512]{2,1,0:T(8,128)(2,1)S(1)}, bf16[2,256,512]{2,1,0:T(8,128)(2,1)S(1)}, u32[]{:S(2)}, u32[]{:S(2)}) collective-permute-start(bf16[2,256,512]{2,1,0:T(8,128)(2,1)S(1)} %collective-permute-done.2.refs_3_.refs_2_), channel_id=1, source_target_pairs={{0,8},{8,0},{16,24},{24,16},{32,40},{40,32},{48,56},{56,48},{64,72... | collective-permute-start | bytes 1572872 | tf_op jit(solution)/shard_map/ppermute | solution.py:237
  62.4 4.0 %copy-start.3 = (bf16[2,256,512]{2,1,0:T(8,128)(2,1)}, bf16[2,256,512]{2,1,0:T(8,128)(2,1)S(1)}, u32[]{:S(2)}) copy-start(bf16[2,256,512]{2,1,0:T(8,128)(2,1)S(1)} %collective-permute-done.1.refs_2_.refs_1_) | copy-start | bytes 1572868
  62.5 3.9 %collective-permute-start.5 = (bf16[2,256,512]{2,1,0:T(8,128)(2,1)S(1)}, bf16[2,256,512]{2,1,0:T(8,128)(2,1)}, u32[]{:S(2)}, u32[]{:S(2)}) collective-permute-start(bf16[2,256,512]{2,1,0:T(8,128)(2,1)S(1)} %collective-permute-done.1.refs_2_.refs_1_), channel_id=1, source_target_pairs={{0,8},{8,0},{16,24},{24,16},{32,40},{40,32},{48,56},{56,48},{64,72... | collective-permute-start | bytes 1572872 | tf_op jit(solution)/shard_map/ppermute | solution.py:237
  64.4 0.8 copy-start.4
  64.4 1.0 copy-start.5
  65.4 0.8 copy-start.6
  66.4 1.2 copy-start
  72.2 15.6 %collective-permute-start.8 = (bf16[512,384]{1,0:T(8,128)(2,1)}, bf16[512,384]{1,0:T(8,128)(2,1)S(1)}, u32[]{:S(2)}, u32[]{:S(2)}) collective-permute-start(bf16[512,384]{1,0:T(8,128)(2,1)} %get-tuple-element.18.refs_0_), channel_id=1, source_target_pairs={{0,1},{1,0},{2,3},{3,2},{4,5},{5,4},{6,7},{7,6},{8,9},{9,8},{10,11... | collective-permute-start | bytes 1179656 | tf_op jit(solution)/shard_map/ppermute | solution.py:251
  87.8 0.7 copy-start.9
  92.7 56.5 %all-to-all-start.1 = ((bf16[32,192,128]{2,1,0:T(8,128)(2,1)}), bf16[32,192,128]{2,1,0:T(8,128)(2,1)S(1)}, u32[]{:S(2)}, u32[]{:S(2)}) async-start(bf16[32,192,128]{2,1,0:T(8,128)(2,1)} %get-tuple-element.30), calls=%async_computation.1 | async-start | bytes 3145728 | tf_op jit(solution)/shard_map/all_to_all | solution.py:260
  115.3 6.7 %collective-permute-start.9 = (bf16[4,2,256,512]{3,2,1,0:T(8,128)(2,1)}, bf16[4,2,256,512]{3,2,1,0:T(8,128)(2,1)S(1)}, u32[]{:S(2)}, u32[]{:S(2)}) collective-permute-start(bf16[4,2,256,512]{3,2,1,0:T(8,128)(2,1)} %get-tuple-element.27), channel_id=1, source_target_pairs={{0,8},{8,0},{16,24},{24,16},{32,40},{40,32},{48,56},{56,48},{64,72... | collective-permute-start | bytes 6291464 | tf_op jit(solution)/shard_map/ppermute | solution.py:266
  125.1 29.4 %collective-permute-start.12 = (bf16[2,256,512]{2,1,0:T(8,128)(2,1)}, bf16[2,256,512]{2,1,0:T(8,128)(2,1)S(1)}, u32[]{:S(2)}, u32[]{:S(2)}) collective-permute-start(bf16[2,256,512]{2,1,0:T(8,128)(2,1)} %get-tuple-element.31), channel_id=1, source_target_pairs={{0,6},{1,7},{2,0},{3,1},{4,2},{5,3},{6,4},{7,5},{8,14},{9,15},{10,... | collective-permute-start | bytes 1572872 | tf_op jit(solution)/shard_map/ppermute | solution.py:269
  128.8 25.7 %collective-permute-start.11 = (bf16[2,256,512]{2,1,0:T(8,128)(2,1)}, bf16[2,256,512]{2,1,0:T(8,128)(2,1)S(1)}, u32[]{:S(2)}, u32[]{:S(2)}) collective-permute-start(bf16[2,256,512]{2,1,0:T(8,128)(2,1)} %get-tuple-element.32), channel_id=1, source_target_pairs={{0,4},{1,5},{2,6},{3,7},{4,0},{5,1},{6,2},{7,3},{8,12},{9,13},{10,... | collective-permute-start | bytes 1572872 | tf_op jit(solution)/shard_map/ppermute | solution.py:269
  132.3 25.4 %collective-permute-start.10 = (bf16[2,256,512]{2,1,0:T(8,128)(2,1)S(1)}, bf16[2,256,512]{2,1,0:T(8,128)(2,1)}, u32[]{:S(2)}, u32[]{:S(2)}) collective-permute-start(bf16[2,256,512]{2,1,0:T(8,128)(2,1)S(1)} %get-tuple-element.33), channel_id=1, source_target_pairs={{0,2},{1,3},{2,4},{3,5},{4,6},{5,7},{6,0},{7,1},{8,10},{9,11},{10,... | collective-permute-start | bytes 1572872 | tf_op jit(solution)/shard_map/ppermute | solution.py:269
  149.3 11.3 %collective-permute-start.13 = (bf16[192,128]{1,0:T(8,128)(2,1)S(1)}, bf16[192,128]{1,0:T(8,128)(2,1)S(1)}, u32[]{:S(2)}, u32[]{:S(2)}) collective-permute-start(bf16[192,128]{1,0:T(8,128)(2,1)S(1)} %reduce_sum.12), channel_id=1, source_target_pairs={{0,0},{8,1},{2,2},{10,3},{4,4},{12,5},{6,6},{14,7},{64,8},{72,9},{... | collective-permute-start | bytes 147464 | tf_op jit(solution)/shard_map/ppermute | solution.py:262
  154.5 3.1 %copy-start.7 = (bf16[2,256,512]{2,1,0:T(8,128)(2,1)}, bf16[2,256,512]{2,1,0:T(8,128)(2,1)S(1)}, u32[]{:S(2)}) copy-start(bf16[2,256,512]{2,1,0:T(8,128)(2,1)S(1)} %collective-permute-done.12.refs_6_) | copy-start | bytes 1572868
  154.5 3.1 %copy-start.8 = (bf16[2,256,512]{2,1,0:T(8,128)(2,1)}, bf16[2,256,512]{2,1,0:T(8,128)(2,1)S(1)}, u32[]{:S(2)}) copy-start(bf16[2,256,512]{2,1,0:T(8,128)(2,1)S(1)} %collective-permute-done.11.refs_5_) | copy-start | bytes 1572868

commit v8 on v7

--- a/solution.py
+++ b/solution.py
@@ -41,15 +41,15 @@
     return lax.dot_general(a, b, (dims, ((), ())), preferred_element_type=F32)
 
 
-def call(body, outs, flops, where, *args):
+def call(body, outs, flops, where, *args, after=(), grant=60):
     size = sum(a.size * a.dtype.itemsize for a in args)
     count, results = len(args), len(outs)
     most = N_X * results
 
     def inner(where_ref, *refs):
-        sources, targets = refs[:count], refs[count : count + results]
-        held, made = refs[count + results : -2 - results], refs[-2 - results : -2]
-        sem, out_sem = refs[-2:]
+        sources, refs = refs[:count], refs[count + len(after) :]
+        targets, held = refs[:results], refs[results : results + count]
+        made, (sem, out_sem) = refs[results + count : -2], refs[-2:]
         copies = [
             pltpu.make_async_copy(s, h, sem.at[i]) for i, (s, h) in enumerate(zip(sources, held))
         ]
@@ -83,13 +83,13 @@
         inner,
         out_shape=shapes,
         in_specs=[pl.BlockSpec(memory_space=pltpu.SMEM)]
-        + [pl.BlockSpec(memory_space=pl.ANY)] * count,
+        + [pl.BlockSpec(memory_space=pl.ANY)] * (count + len(after)),
         out_specs=[pl.BlockSpec(memory_space=pl.ANY)] * results,
         scratch_shapes=[pltpu.VMEM(a.shape, a.dtype) for a in (*args, *shapes)]
         + [pltpu.SemaphoreType.DMA((count,)), pltpu.SemaphoreType.DMA((most,))],
-        compiler_params=pltpu.CompilerParams(vmem_limit_bytes=60 * 1024 * 1024),
+        compiler_params=pltpu.CompilerParams(vmem_limit_bytes=grant * 1024 * 1024),
         cost_estimate=pl.CostEstimate(flops=flops, bytes_accessed=size, transcendentals=0),
-    )(where, *args)
+    )(where, *args, *after)
 
 
 def use_of(gate, count):
@@ -135,37 +135,32 @@
     return pl.multiple_of(lax.rem(where[0] + step, N_X) * size, size)
 
 
-def assemble(pieces, both, down):
+def products_body(where, get, put, part, weights):
+    pieces = get(0)
     rows, cols = pieces.shape[1] // 3, pieces.shape[2]
     for i in range(pieces.shape[0]):
         y, z = divmod(i, N_Z)
         place = y // 2 * 8 + z * 2 + y % 2
-        at = slice(place * rows, (place + 1) * rows)
-        both[at, :cols] = pieces[i, :rows]
-        both[at, cols:] = pieces[i, rows : 2 * rows]
-        down[at] = pieces[i, 2 * rows :]
-
-
-def products_body(where, get, put, part, both, down):
-    assemble(get(0), both, down)
+        for m in range(3):
+            weights[place * rows : (place + 1) * rows, cols * m : cols * (m + 1)] = pieces[
+                i, rows * m : rows * (m + 1)
+            ]
     put(1)
-    put(2)
-    cols = down.shape[1]
     slots, feat = get(1).shape[1:]
     for who in range(2):
         pre, back = 0.0, 0.0
         for step in range(N_X):
             x = get(1 + who * N_X + step)
             at = pl.ds(turn(where, step, feat), feat)
-            pre = pre + dot(x[0], both[at])
-            back = back + dot(x[1], down[at])
+            pre = pre + dot(x[0], weights[at, : 2 * cols])
+            back = back + dot(x[1], weights[at, 2 * cols :])
         at = slice(slots * who, slots * (who + 1))
         part[at, : 2 * cols] = pre.astype(BF16)
         part[at, 2 * cols :] = back.astype(BF16)
         put(0, pl.ds(slots * who, slots))
 
 
-def terms_body(where, get, put, pieces, acts):
+def terms_body(where, get, put, pieces, acts, send):
     total = get(0)[...].astype(F32) + get(1)[...].astype(F32)
     units = total.shape[1] // 3
     pre_gate, pre_up, grad_hidden = total[:, :units], total[:, units : 2 * units], total[:, 2 * units :]
@@ -175,7 +170,9 @@
     ).astype(BF16)
     acts[:, units : 2 * units] = (grad_hidden * pre_gate * sigma).astype(BF16)
     acts[:, 2 * units :] = (pre_gate * sigma * pre_up).astype(BF16)
+    send[...] = acts[send.shape[0] :]
     put(1)
+    put(2)
     rows = pieces.shape[1] // 3
     for step in range(N_X):
         turned = get(2 + step)
@@ -191,19 +188,19 @@
         put(0, pl.ds(first, 2 * N_Z))
 
 
-def outputs_body(where, get, put, send, mine):
-    acts, both, down = [get(i) for i in range(3)]
-    units = acts.shape[1] // 3
-    slots, feat = mine.shape[2:]
-    for step in (2, 1, 3, 0):
+def outputs_body(where, get, put, *outs):
+    slots, feat = outs[0].shape[1:]
+    cols = get(1).shape[1] // 3
+    for step in (2, 3, 1, 0):
         at = pl.ds(turn(where, step, feat), feat)
-        for which, out in enumerate(
-            (dot(acts[:, 2 * units :], down[at], LAST), dot(acts[:, : 2 * units], both[at], LAST))
-        ):
-            mine[step, which] = out[:slots].astype(BF16)
-            send[step, which] = out[slots:].astype(BF16)
-        put(0, pl.ds(step, 1))
-        put(1, pl.ds(step, 1))
+        out, back = 0.0, 0.0
+        for who in range(2):
+            acts, weights = get(2 * who), get(2 * who + 1)
+            out = out + dot(acts[:slots, 2 * cols :], weights[at, 2 * cols :], LAST)
+            back = back + dot(acts[:slots, : 2 * cols], weights[at, : 2 * cols], LAST)
+        outs[step][0] = out.astype(BF16)
+        outs[step][1] = back.astype(BF16)
+        put(step)
 
 
 def tokens_body(where, get, put, mixed, grad_tokens):
@@ -233,7 +230,8 @@
         where,
         *(tokens, grad_out, token, count, gate),
     )
-    near = [own] + [lax.ppermute(own, "narrow", shift_x(-step)) for step in range(1, N_X)]
+    near = {step: lax.ppermute(own, "narrow", shift_x(-step)) for step in (1, 3, 2)}
+    near = [own] + [near[step] for step in range(1, N_X)]
     core = [lax.ppermute(held, "wide", OTHER_CORE) for held in near]
     turned = call(
         turned_body, [((2, feat, 2 * slots), BF16)] * N_X, pick_flops, where, *near, *core
@@ -241,17 +239,17 @@
 
     flops = 2 * 3 * 2 * slots * N_X * feat * cols
     part = ((2 * slots, 3 * cols), BF16)
-    sent, both, down = call(
+    sent, weights = call(
         products_body,
-        [part, ((N_X * feat, 2 * cols), BF16), ((N_X * feat, cols), BF16)],
+        [part, ((N_X * feat, 3 * cols), BF16)],
         flops,
         where,
         *(pieces, *near, *core),
     )
     theirs = lax.ppermute(sent, "narrow", OTHER_HALF)
-    terms, acts = call(
+    terms, acts, send = call(
         terms_body,
-        [(pieces.shape, BF16), part],
+        [(pieces.shape, BF16), part, ((slots, 3 * cols), BF16)],
         flops,
         where,
         *(sent, theirs, *turned),
@@ -261,13 +259,17 @@
     grads = terms.astype(F32).sum(axis=0).astype(BF16)
     grads = lax.ppermute(grads, ("wide", "narrow"), SWAP_BACK).astype(F32)
 
-    every = ((N_X, 2, slots, feat), BF16)
-    send, mine = call(outputs_body, [every, every], flops, where, acts, both, down)
     got = lax.ppermute(send, "wide", OTHER_CORE)
-    sums = [(mine[step].astype(F32) + got[step].astype(F32)).astype(BF16) for step in range(N_X)]
-    home = [sums[0]] + [
-        lax.ppermute(sums[step], "narrow", shift_x(step)) for step in range(1, N_X)
-    ]
+    core_weights = lax.ppermute(weights, "wide", OTHER_CORE)
+    outs = call(
+        outputs_body,
+        [((2, slots, feat), BF16)] * N_X,
+        flops,
+        where,
+        *(acts, weights, got, core_weights),
+    )
+    home = {step: lax.ppermute(outs[step], "narrow", shift_x(step)) for step in (1, 3, 2)}
+    home = [outs[0]] + [home[step] for step in range(1, N_X)]
     mixed, grad_tokens = call(
         tokens_body, [((tok, feat), BF16)] * 2, pick_flops, where, token, count, gate, *home
     )

time: 162 us -> 161 us (level)
  waiting for transfers between devices: 50.3 us -> 46.1 us
  starting transfers between devices: 76.3 us -> 79.7 us
  other arithmetic: 3.35 us -> 0.22 us
  local copies, waits for them, and re-layouts: 5.93 us -> 8.16 us
    ppermute x3 -> x4, starting transfers between devices: 9.05 us -> 12.7 us  [the longest x3 9.98 us: local(): lax.ppermute(outs[step], 'narrow', shift_x(step))]
    convert_element_type x1 -> x0, other arithmetic: 3.12 us -> none  [local(): (mine[step].astype(F32) + got[step].astype(F32)).astype(BF16)]
    ppermute x3 -> x4, waiting for transfers between devices: 3.08 us -> 0.01 us  [the longest x3 0.01 us: local(): lax.ppermute(outs[step], 'narrow', shift_x(step))]
    ppermute x1, waiting for transfers between devices: 3.97 us -> 1.41 us  [local(): got = lax.ppermute(send, 'wide', OTHER_CORE)]
    unnamed x20 -> x30, local copies, waits for them, and re-layouts: 3.74 us -> 5.98 us
  transfers between devices with their start and end apart: 16 -> 17, of which waited for: 8 -> 7; matrix products, arithmetic and copies ran while one was open for 2% -> 0% of each run, Pallas kernels for 8% -> 9%
where the time goes in v8:
time: 161 us; the launch traced here: 160 us
  starting transfers between devices  79.7 us (50%)
  waiting for transfers between devices  46.1 us (29%)
  Pallas kernels  24.1 us (15%)
  local copies, waits for them, and re-layouts  8.16 us (5%)
  between operations  1.66 us (1%)
    pallas_call x7, Pallas kernels, call(): pl.pallas_call(inner, out_shape=shapes, in_specs=[pl.BlockSpec(memory_spa...  24.1 us
    all_to_all x1, starting transfers between devices, local(): terms = lax.all_to_all(terms, 'wide', 0, 0, axis_index_groups=OWNERS)  18.7 us
    all_to_all x1, waiting for transfers between devices, local(): terms = lax.all_to_all(terms, 'wide', 0, 0, axis_index_groups=OWNERS)  16.3 us
    ppermute x4, starting transfers between devices, local(): core = [lax.ppermute(held, 'wide', OTHER_CORE) for held in near]  12.7 us
    ppermute x3, starting transfers between devices, local(): lax.ppermute(own, 'narrow', shift_x(-step))  10.5 us
    ppermute x3, waiting for transfers between devices, local(): lax.ppermute(own, 'narrow', shift_x(-step))  10.4 us
    ppermute x3, starting transfers between devices, local(): lax.ppermute(outs[step], 'narrow', shift_x(step))  9.98 us
    all_to_all x1, starting transfers between devices, local(): pieces = lax.all_to_all(pieces, 'wide', 0, 0, axis_index_groups=OWNERS)  9.89 us
  transfers between devices with their start and end apart: 17, of which 7 were waited for; matrix products, arithmetic and copies ran while one was open for 0% of the time, Pallas kernels for 9%

profile of v8, /device:TPU:1, one launch (start us, length us, event | category | flops | bytes accessed | tf_op | source)
XLA Modules:
  0.0 159.9 jit_solution(205985258181596629)
XLA Ops:
  0.6 1.4 shard_map.119
  2.1 4.6 %collective-permute-start = (bf16[192,128]{1,0:T(8,128)(2,1)}, bf16[192,128]{1,0:T(8,128)(2,1)S(1)}, u32[]{:S(2)}, u32[]{:S(2)}) collective-permute-start(bf16[192,128]{1,0:T(8,128)(2,1)} %shard_map.119), channel_id=1, source_target_pairs={{0,0},{1,8},{2,2},{3,10},{4,4},{5,12},{6,6},{7,14},{8,64},{9,72},{... | collective-permute-start | bytes 147464 | tf_op jit(solution)/shard_map/ppermute | solution.py:223
  6.7 9.5 %collective-permute-done = bf16[192,128]{1,0:T(8,128)(2,1)S(1)} collective-permute-done((bf16[192,128]{1,0:T(8,128)(2,1)}, bf16[192,128]{1,0:T(8,128)(2,1)S(1)}, u32[]{:S(2)}, u32[]{:S(2)}) %collective-permute-start) | collective-permute-done | bytes 49184 | tf_op jit(solution)/shard_map/ppermute | solution.py:223
  16.1 1.5 broadcast_in_dim.22
  17.7 9.9 %all-to-all-start = ((bf16[32,192,128]{2,1,0:T(8,128)(2,1)}), bf16[32,192,128]{2,1,0:T(8,128)(2,1)S(1)}, u32[]{:S(2)}, u32[]{:S(2)}) async-start(bf16[32,192,128]{2,1,0:T(8,128)(2,1)} %broadcast_in_dim.22), calls=%async_computation | async-start | bytes 3145728 | tf_op jit(solution)/shard_map/all_to_all | solution.py:225
  28.2 2.4 %shard_map.120.refs_1_.refs_0_ = bf16[2,256,512]{2,1,0:T(8,128)(2,1)} custom-call(s32[1]{0:T(128)} %bitcast.where_ref, bf16[384,512]{1,0:T(8,128)(2,1)} %refs_0_.3, bf16[384,512]{1,0:T(8,128)(2,1)} %refs_1_.3, s32[1,256]{1,0:T(1,128)} %bitcast.6, s32[1,1]{1,0:T(1,128)} %bitcast.4.refs_3_, f32[1,256]{1,0:T(1,128)} %bitcast.8), custom_call_target="tpu_custom_call" | custom-call | flops 201326592 | bytes 788484 | tf_op jit(solution)/shard_map/pallas_call | solution.py:82
  30.6 3.1 %collective-permute-start.3 = (bf16[2,256,512]{2,1,0:T(8,128)(2,1)}, bf16[2,256,512]{2,1,0:T(8,128)(2,1)S(1)}, u32[]{:S(2)}, u32[]{:S(2)}) collective-permute-start(bf16[2,256,512]{2,1,0:T(8,128)(2,1)} %shard_map.120.refs_1_.refs_0_), channel_id=1, source_target_pairs={{0,2},{1,3},{2,4},{3,5},{4,6},{5,7},{6,0},{7,1},{8,10},{9,11},{10,... | collective-permute-start | bytes 1572872 | tf_op jit(solution)/shard_map/ppermute | solution.py:233
  33.8 4.4 %collective-permute-start.2 = (bf16[2,256,512]{2,1,0:T(8,128)(2,1)}, bf16[2,256,512]{2,1,0:T(8,128)(2,1)S(1)}, u32[]{:S(2)}, u32[]{:S(2)}) collective-permute-start(bf16[2,256,512]{2,1,0:T(8,128)(2,1)} %shard_map.120.refs_1_.refs_0_), channel_id=1, source_target_pairs={{0,4},{1,5},{2,6},{3,7},{4,0},{5,1},{6,2},{7,3},{8,12},{9,13},{10,... | collective-permute-start | bytes 1572872 | tf_op jit(solution)/shard_map/ppermute | solution.py:233
  38.1 3.1 %collective-permute-start.1 = (bf16[2,256,512]{2,1,0:T(8,128)(2,1)}, bf16[2,256,512]{2,1,0:T(8,128)(2,1)S(1)}, u32[]{:S(2)}, u32[]{:S(2)}) collective-permute-start(bf16[2,256,512]{2,1,0:T(8,128)(2,1)} %shard_map.120.refs_1_.refs_0_), channel_id=1, source_target_pairs={{0,6},{1,7},{2,0},{3,1},{4,2},{5,3},{6,4},{7,5},{8,14},{9,15},{10,... | collective-permute-start | bytes 1572872 | tf_op jit(solution)/shard_map/ppermute | solution.py:233
  41.2 3.5 %collective-permute-start.4 = (bf16[2,256,512]{2,1,0:T(8,128)(2,1)}, bf16[2,256,512]{2,1,0:T(8,128)(2,1)S(1)}, u32[]{:S(2)}, u32[]{:S(2)}) collective-permute-start(bf16[2,256,512]{2,1,0:T(8,128)(2,1)} %shard_map.120.refs_1_.refs_0_), channel_id=1, source_target_pairs={{0,8},{8,0},{16,24},{24,16},{32,40},{40,32},{48,56},{56,48},{64,72... | collective-permute-start | bytes 1572872 | tf_op jit(solution)/shard_map/ppermute | solution.py:235
  44.7 1.9 %collective-permute-done.3.refs_4_.refs_3_ = bf16[2,256,512]{2,1,0:T(8,128)(2,1)S(1)} collective-permute-done((bf16[2,256,512]{2,1,0:T(8,128)(2,1)}, bf16[2,256,512]{2,1,0:T(8,128)(2,1)S(1)}, u32[]{:S(2)}, u32[]{:S(2)}) %collective-permute-start.3) | collective-permute-done | bytes 524320 | tf_op jit(solution)/shard_map/ppermute | solution.py:233
  46.7 3.8 %collective-permute-start.7 = (bf16[2,256,512]{2,1,0:T(8,128)(2,1)S(1)}, bf16[2,256,512]{2,1,0:T(8,128)(2,1)S(1)}, u32[]{:S(2)}, u32[]{:S(2)}) collective-permute-start(bf16[2,256,512]{2,1,0:T(8,128)(2,1)S(1)} %collective-permute-done.3.refs_4_.refs_3_), channel_id=1, source_target_pairs={{0,8},{8,0},{16,24},{24,16},{32,40},{40,32},{48,56},{56,48},{64,72... | collective-permute-start | bytes 1572872 | tf_op jit(solution)/shard_map/ppermute | solution.py:235
  50.4 8.4 %collective-permute-done.2.refs_3_.refs_2_ = bf16[2,256,512]{2,1,0:T(8,128)(2,1)S(1)} collective-permute-done((bf16[2,256,512]{2,1,0:T(8,128)(2,1)}, bf16[2,256,512]{2,1,0:T(8,128)(2,1)S(1)}, u32[]{:S(2)}, u32[]{:S(2)}) %collective-permute-start.2) | collective-permute-done | bytes 524320 | tf_op jit(solution)/shard_map/ppermute | solution.py:233
  58.9 3.5 %collective-permute-start.6 = (bf16[2,256,512]{2,1,0:T(8,128)(2,1)S(1)}, bf16[2,256,512]{2,1,0:T(8,128)(2,1)S(1)}, u32[]{:S(2)}, u32[]{:S(2)}) collective-permute-start(bf16[2,256,512]{2,1,0:T(8,128)(2,1)S(1)} %collective-permute-done.2.refs_3_.refs_2_), channel_id=1, source_target_pairs={{0,8},{8,0},{16,24},{24,16},{32,40},{40,32},{48,56},{56,48},{64,72... | collective-permute-start | bytes 1572872 | tf_op jit(solution)/shard_map/ppermute | solution.py:235
  62.4 1.9 %collective-permute-start.5 = (bf16[2,256,512]{2,1,0:T(8,128)(2,1)S(1)}, bf16[2,256,512]{2,1,0:T(8,128)(2,1)}, u32[]{:S(2)}, u32[]{:S(2)}) collective-permute-start(bf16[2,256,512]{2,1,0:T(8,128)(2,1)S(1)} %collective-permute-done.1.refs_2_.refs_1_), channel_id=1, source_target_pairs={{0,8},{8,0},{16,24},{24,16},{32,40},{40,32},{48,56},{56,48},{64,72... | collective-permute-start | bytes 1572872 | tf_op jit(solution)/shard_map/ppermute | solution.py:235
  67.5 4.6 %shard_map.121 = (bf16[512,384]{1,0:T(8,128)(2,1)}, bf16[2048,384]{1,0:T(8,128)(2,1)}) custom-call(s32[1]{0:T(128)} %bitcast.where_ref, bf16[32,192,128]{2,1,0:T(8,128)(2,1)} %copy-done, bf16[2,256,512]{2,1,0:T(8,128)(2,1)} %shard_map.120.refs_1_.refs_0_, bf16[2,256,512]{2,1,0:T(8,128)(2,1)} %copy-done.3, bf16[2,256,512]{2,1,0:T(8,128)(2,1)} %copy-done.2, ...), custom_call_target="tpu_custom_call" | custom-call | flops 805306368 | bytes 5767168 | tf_op jit(solution)/shard_map/pallas_call | solution.py:82
  72.2 3.1 %collective-permute-start.8 = (bf16[512,384]{1,0:T(8,128)(2,1)}, bf16[512,384]{1,0:T(8,128)(2,1)S(1)}, u32[]{:S(2)}, u32[]{:S(2)}) collective-permute-start(bf16[512,384]{1,0:T(8,128)(2,1)} %get-tuple-element.20.refs_0_), channel_id=1, source_target_pairs={{0,1},{1,0},{2,3},{3,2},{4,5},{5,4},{6,7},{7,6},{8,9},{9,8},{10,11... | collective-permute-start | bytes 1179656 | tf_op jit(solution)/shard_map/ppermute | solution.py:249
  75.3 4.2 %shard_map.122 = (bf16[2,512,512]{2,1,0:T(8,128)(2,1)}, bf16[2,512,512]{2,1,0:T(8,128)(2,1)}, bf16[2,512,512]{2,1,0:T(8,128)(2,1)}, bf16[2,512,512]{2,1,0:T(8,128)(2,1)}) custom-call(s32[1]{0:T(128)} %bitcast.where_ref, bf16[2,256,512]{2,1,0:T(8,128)(2,1)} %shard_map.120.refs_1_.refs_0_, bf16[2,256,512]{2,1,0:T(8,128)(2,1)} %copy-done.3, ...), custom_call_target="tpu_custom_call" | custom-call | flops 201326592 | bytes 4194304 | tf_op jit(solution)/shard_map/pallas_call | solution.py:82
  79.5 8.3 %collective-permute-done.8.refs_1_ = bf16[512,384]{1,0:T(8,128)(2,1)S(1)} collective-permute-done((bf16[512,384]{1,0:T(8,128)(2,1)}, bf16[512,384]{1,0:T(8,128)(2,1)S(1)}, u32[]{:S(2)}, u32[]{:S(2)}) %collective-permute-start.8) | collective-permute-done | bytes 393248 | tf_op jit(solution)/shard_map/ppermute | solution.py:249
  88.5 4.2 %shard_map.123 = (bf16[32,192,128]{2,1,0:T(8,128)(2,1)}, bf16[512,384]{1,0:T(8,128)(2,1)}, bf16[256,384]{1,0:T(8,128)(2,1)}) custom-call(s32[1]{0:T(128)} %bitcast.where_ref, bf16[512,384]{1,0:T(8,128)(2,1)} %get-tuple-element.20.refs_0_, bf16[512,384]{1,0:T(8,128)(2,1)} %copy-done.12, bf16[2,512,512]{2,1,0:T(8,128)(2,1)} %get-tuple-element.21.refs_2_, ...), custom_call_target="tpu_custom_call" | custom-call | flops 805306368 | bytes 4980736 | tf_op jit(solution)/shard_map/pallas_call | solution.py:82
  92.7 18.7 %all-to-all-start.1 = ((bf16[32,192,128]{2,1,0:T(8,128)(2,1)}), bf16[32,192,128]{2,1,0:T(8,128)(2,1)S(1)}, u32[]{:S(2)}, u32[]{:S(2)}) async-start(bf16[32,192,128]{2,1,0:T(8,128)(2,1)} %get-tuple-element.34), calls=%async_computation.1 | async-start | bytes 3145728 | tf_op jit(solution)/shard_map/all_to_all | solution.py:258
  111.4 2.7 %collective-permute-start.10 = (bf16[2048,384]{1,0:T(8,128)(2,1)S(1)}, bf16[2048,384]{1,0:T(8,128)(2,1)S(1)}, u32[]{:S(2)}, u32[]{:S(2)}) collective-permute-start(bf16[2048,384]{1,0:T(8,128)(2,1)S(1)} %copy-done.7), channel_id=1, source_target_pairs={{0,8},{8,0},{16,24},{24,16},{32,40},{40,32},{48,56},{56,48},{64,72... | collective-permute-start | bytes 4718600 | tf_op jit(solution)/shard_map/ppermute | solution.py:263
  114.1 1.9 %collective-permute-start.9 = (bf16[256,384]{1,0:T(8,128)(2,1)S(1)}, bf16[256,384]{1,0:T(8,128)(2,1)S(1)}, u32[]{:S(2)}, u32[]{:S(2)}) collective-permute-start(bf16[256,384]{1,0:T(8,128)(2,1)S(1)} %copy-done.14), channel_id=1, source_target_pairs={{0,8},{8,0},{16,24},{24,16},{32,40},{40,32},{48,56},{56,48},{64,72... | collective-permute-start | bytes 589832 | tf_op jit(solution)/shard_map/ppermute | solution.py:262
  116.1 1.4 collective-permute-done.9.refs_2_
  117.5 1.2 copy-done.8
  118.7 4.3 %shard_map.124 = (bf16[2,256,512]{2,1,0:T(8,128)(2,1)}, bf16[2,256,512]{2,1,0:T(8,128)(2,1)}, bf16[2,256,512]{2,1,0:T(8,128)(2,1)}, bf16[2,256,512]{2,1,0:T(8,128)(2,1)}) custom-call(s32[1]{0:T(128)} %bitcast.where_ref, bf16[512,384]{1,0:T(8,128)(2,1)} %get-tuple-element.25.refs_0_, bf16[2048,384]{1,0:T(8,128)(2,1)} %get-tuple-element.26.refs_1_, ...), custom_call_target="tpu_custom_call" | custom-call | flops 805306368 | bytes 3735552 | tf_op jit(solution)/shard_map/pallas_call | solution.py:82
  122.9 3.4 %collective-permute-start.11 = (bf16[2,256,512]{2,1,0:T(8,128)(2,1)}, bf16[2,256,512]{2,1,0:T(8,128)(2,1)S(1)}, u32[]{:S(2)}, u32[]{:S(2)}) collective-permute-start(bf16[2,256,512]{2,1,0:T(8,128)(2,1)} %get-tuple-element.29), channel_id=1, source_target_pairs={{0,2},{1,3},{2,4},{3,5},{4,6},{5,7},{6,0},{7,1},{8,10},{9,11},{10,... | collective-permute-start | bytes 1572872 | tf_op jit(solution)/shard_map/ppermute | solution.py:271
  126.3 3.4 %collective-permute-start.12 = (bf16[2,256,512]{2,1,0:T(8,128)(2,1)}, bf16[2,256,512]{2,1,0:T(8,128)(2,1)S(1)}, u32[]{:S(2)}, u32[]{:S(2)}) collective-permute-start(bf16[2,256,512]{2,1,0:T(8,128)(2,1)} %get-tuple-element.30), channel_id=1, source_target_pairs={{0,4},{1,5},{2,6},{3,7},{4,0},{5,1},{6,2},{7,3},{8,12},{9,13},{10,... | collective-permute-start | bytes 1572872 | tf_op jit(solution)/shard_map/ppermute | solution.py:271
  129.7 3.2 %collective-permute-start.13 = (bf16[2,256,512]{2,1,0:T(8,128)(2,1)}, bf16[2,256,512]{2,1,0:T(8,128)(2,1)S(1)}, u32[]{:S(2)}, u32[]{:S(2)}) collective-permute-start(bf16[2,256,512]{2,1,0:T(8,128)(2,1)} %get-tuple-element.31), channel_id=1, source_target_pairs={{0,6},{1,7},{2,0},{3,1},{4,2},{5,3},{6,4},{7,5},{8,14},{9,15},{10,... | collective-permute-start | bytes 1572872 | tf_op jit(solution)/shard_map/ppermute | solution.py:271
  133.0 16.3 %all-to-all-done.1 = bf16[32,192,128]{2,1,0:T(8,128)(2,1)S(1)} async-done(((bf16[32,192,128]{2,1,0:T(8,128)(2,1)}), bf16[32,192,128]{2,1,0:T(8,128)(2,1)S(1)}, u32[]{:S(2)}, u32[]{:S(2)}) %all-to-all-start.1) | async-done | bytes 1572896 | tf_op jit(solution)/shard_map/all_to_all | solution.py:258
  149.5 5.6 %collective-permute-start.14 = (bf16[192,128]{1,0:T(8,128)(2,1)S(1)}, bf16[192,128]{1,0:T(8,128)(2,1)S(1)}, u32[]{:S(2)}, u32[]{:S(2)}) collective-permute-start(bf16[192,128]{1,0:T(8,128)(2,1)S(1)} %reduce_sum.12), channel_id=1, source_target_pairs={{0,0},{8,1},{2,2},{10,3},{4,4},{12,5},{6,6},{14,7},{64,8},{72,9},{... | collective-permute-start | bytes 147464 | tf_op jit(solution)/shard_map/ppermute | solution.py:260
  156.3 3.0 %shard_map.125 = (bf16[384,512]{1,0:T(8,128)(2,1)}, bf16[384,512]{1,0:T(8,128)(2,1)}) custom-call(s32[1]{0:T(128)} %bitcast.where_ref, s32[1,256]{1,0:T(1,128)} %bitcast.7, s32[1,1]{1,0:T(1,128)} %bitcast.5.refs_1_, f32[1,256]{1,0:T(1,128)} %bitcast.9, bf16[2,256,512]{2,1,0:T(8,128)(2,1)} %get-tuple-element.28.refs_3_, bf16[2,256,512]{2,1,0:T(8,128)(2,1)} %copy-done.9, ...), custom_call_target="tpu_custom_call" | custom-call | flops 201326592 | bytes 2099204 | tf_op jit(solution)/shard_map/pallas_call | solution.py:82
  (42 shorter events, 5.9 us)
Async XLA Ops:
  2.1 14.1 %collective-permute-start = (bf16[192,128]{1,0:T(8,128)(2,1)}, bf16[192,128]{1,0:T(8,128)(2,1)S(1)}, u32[]{:S(2)}, u32[]{:S(2)}) collective-permute-start(bf16[192,128]{1,0:T(8,128)(2,1)} %shard_map.119), channel_id=1, source_target_pairs={{0,0},{1,8},{2,2},{3,10},{4,4},{5,12},{6,6},{7,14},{8,64},{9,72},{... | collective-permute-start | bytes 147464 | tf_op jit(solution)/shard_map/ppermute | solution.py:223
  17.7 48.7 %all-to-all-start = ((bf16[32,192,128]{2,1,0:T(8,128)(2,1)}), bf16[32,192,128]{2,1,0:T(8,128)(2,1)S(1)}, u32[]{:S(2)}, u32[]{:S(2)}) async-start(bf16[32,192,128]{2,1,0:T(8,128)(2,1)} %broadcast_in_dim.22), calls=%async_computation | async-start | bytes 3145728 | tf_op jit(solution)/shard_map/all_to_all | solution.py:225
  30.6 16.0 %collective-permute-start.3 = (bf16[2,256,512]{2,1,0:T(8,128)(2,1)}, bf16[2,256,512]{2,1,0:T(8,128)(2,1)S(1)}, u32[]{:S(2)}, u32[]{:S(2)}) collective-permute-start(bf16[2,256,512]{2,1,0:T(8,128)(2,1)} %shard_map.120.refs_1_.refs_0_), channel_id=1, source_target_pairs={{0,2},{1,3},{2,4},{3,5},{4,6},{5,7},{6,0},{7,1},{8,10},{9,11},{10,... | collective-permute-start | bytes 1572872 | tf_op jit(solution)/shard_map/ppermute | solution.py:233
  33.8 25.1 %collective-permute-start.2 = (bf16[2,256,512]{2,1,0:T(8,128)(2,1)}, bf16[2,256,512]{2,1,0:T(8,128)(2,1)S(1)}, u32[]{:S(2)}, u32[]{:S(2)}) collective-permute-start(bf16[2,256,512]{2,1,0:T(8,128)(2,1)} %shard_map.120.refs_1_.refs_0_), channel_id=1, source_target_pairs={{0,4},{1,5},{2,6},{3,7},{4,0},{5,1},{6,2},{7,3},{8,12},{9,13},{10,... | collective-permute-start | bytes 1572872 | tf_op jit(solution)/shard_map/ppermute | solution.py:233
  38.1 24.3 %collective-permute-start.1 = (bf16[2,256,512]{2,1,0:T(8,128)(2,1)}, bf16[2,256,512]{2,1,0:T(8,128)(2,1)S(1)}, u32[]{:S(2)}, u32[]{:S(2)}) collective-permute-start(bf16[2,256,512]{2,1,0:T(8,128)(2,1)} %shard_map.120.refs_1_.refs_0_), channel_id=1, source_target_pairs={{0,6},{1,7},{2,0},{3,1},{4,2},{5,3},{6,4},{7,5},{8,14},{9,15},{10,... | collective-permute-start | bytes 1572872 | tf_op jit(solution)/shard_map/ppermute | solution.py:233
  41.2 23.2 %collective-permute-start.4 = (bf16[2,256,512]{2,1,0:T(8,128)(2,1)}, bf16[2,256,512]{2,1,0:T(8,128)(2,1)S(1)}, u32[]{:S(2)}, u32[]{:S(2)}) collective-permute-start(bf16[2,256,512]{2,1,0:T(8,128)(2,1)} %shard_map.120.refs_1_.refs_0_), channel_id=1, source_target_pairs={{0,8},{8,0},{16,24},{24,16},{32,40},{40,32},{48,56},{56,48},{64,72... | collective-permute-start | bytes 1572872 | tf_op jit(solution)/shard_map/ppermute | solution.py:235
  46.6 19.7 %copy-start.1 = (bf16[2,256,512]{2,1,0:T(8,128)(2,1)}, bf16[2,256,512]{2,1,0:T(8,128)(2,1)S(1)}, u32[]{:S(2)}) copy-start(bf16[2,256,512]{2,1,0:T(8,128)(2,1)S(1)} %collective-permute-done.3.refs_4_.refs_3_) | copy-start | bytes 1572868
  46.7 17.7 %collective-permute-start.7 = (bf16[2,256,512]{2,1,0:T(8,128)(2,1)S(1)}, bf16[2,256,512]{2,1,0:T(8,128)(2,1)S(1)}, u32[]{:S(2)}, u32[]{:S(2)}) collective-permute-start(bf16[2,256,512]{2,1,0:T(8,128)(2,1)S(1)} %collective-permute-done.3.refs_4_.refs_3_), channel_id=1, source_target_pairs={{0,8},{8,0},{16,24},{24,16},{32,40},{40,32},{48,56},{56,48},{64,72... | collective-permute-start | bytes 1572872 | tf_op jit(solution)/shard_map/ppermute | solution.py:235
  58.9 7.5 %copy-start.2 = (bf16[2,256,512]{2,1,0:T(8,128)(2,1)}, bf16[2,256,512]{2,1,0:T(8,128)(2,1)S(1)}, u32[]{:S(2)}) copy-start(bf16[2,256,512]{2,1,0:T(8,128)(2,1)S(1)} %collective-permute-done.2.refs_3_.refs_2_) | copy-start | bytes 1572868
  58.9 5.5 %collective-permute-start.6 = (bf16[2,256,512]{2,1,0:T(8,128)(2,1)S(1)}, bf16[2,256,512]{2,1,0:T(8,128)(2,1)S(1)}, u32[]{:S(2)}, u32[]{:S(2)}) collective-permute-start(bf16[2,256,512]{2,1,0:T(8,128)(2,1)S(1)} %collective-permute-done.2.refs_3_.refs_2_), channel_id=1, source_target_pairs={{0,8},{8,0},{16,24},{24,16},{32,40},{40,32},{48,56},{56,48},{64,72... | collective-permute-start | bytes 1572872 | tf_op jit(solution)/shard_map/ppermute | solution.py:235
  62.4 4.0 %copy-start.3 = (bf16[2,256,512]{2,1,0:T(8,128)(2,1)}, bf16[2,256,512]{2,1,0:T(8,128)(2,1)S(1)}, u32[]{:S(2)}) copy-start(bf16[2,256,512]{2,1,0:T(8,128)(2,1)S(1)} %collective-permute-done.1.refs_2_.refs_1_) | copy-start | bytes 1572868
  62.4 3.9 %collective-permute-start.5 = (bf16[2,256,512]{2,1,0:T(8,128)(2,1)S(1)}, bf16[2,256,512]{2,1,0:T(8,128)(2,1)}, u32[]{:S(2)}, u32[]{:S(2)}) collective-permute-start(bf16[2,256,512]{2,1,0:T(8,128)(2,1)S(1)} %collective-permute-done.1.refs_2_.refs_1_), channel_id=1, source_target_pairs={{0,8},{8,0},{16,24},{24,16},{32,40},{40,32},{48,56},{56,48},{64,72... | collective-permute-start | bytes 1572872 | tf_op jit(solution)/shard_map/ppermute | solution.py:235
  64.4 0.8 copy-start.4
  64.4 1.0 copy-start.5
  65.4 0.8 copy-start.6
  66.4 1.2 copy-start
  72.2 15.6 %collective-permute-start.8 = (bf16[512,384]{1,0:T(8,128)(2,1)}, bf16[512,384]{1,0:T(8,128)(2,1)S(1)}, u32[]{:S(2)}, u32[]{:S(2)}) collective-permute-start(bf16[512,384]{1,0:T(8,128)(2,1)} %get-tuple-element.20.refs_0_), channel_id=1, source_target_pairs={{0,1},{1,0},{2,3},{3,2},{4,5},{5,4},{6,7},{7,6},{8,9},{9,8},{10,11... | collective-permute-start | bytes 1179656 | tf_op jit(solution)/shard_map/ppermute | solution.py:249
  87.8 0.7 copy-start.12
  92.7 18.7 %copy-start.7 = (bf16[2048,384]{1,0:T(8,128)(2,1)S(1)}, bf16[2048,384]{1,0:T(8,128)(2,1)}, u32[]{:S(2)}) copy-start(bf16[2048,384]{1,0:T(8,128)(2,1)} %get-tuple-element.26.refs_1_) | copy-start | bytes 4718596
  92.7 21.4 %copy-start.14 = (bf16[256,384]{1,0:T(8,128)(2,1)S(1)}, bf16[256,384]{1,0:T(8,128)(2,1)}, u32[]{:S(2)}) copy-start(bf16[256,384]{1,0:T(8,128)(2,1)} %get-tuple-element.27) | copy-start | bytes 589828
  92.7 56.6 %all-to-all-start.1 = ((bf16[32,192,128]{2,1,0:T(8,128)(2,1)}), bf16[32,192,128]{2,1,0:T(8,128)(2,1)S(1)}, u32[]{:S(2)}, u32[]{:S(2)}) async-start(bf16[32,192,128]{2,1,0:T(8,128)(2,1)} %get-tuple-element.34), calls=%async_computation.1 | async-start | bytes 3145728 | tf_op jit(solution)/shard_map/all_to_all | solution.py:258
  111.4 6.1 %collective-permute-start.10 = (bf16[2048,384]{1,0:T(8,128)(2,1)S(1)}, bf16[2048,384]{1,0:T(8,128)(2,1)S(1)}, u32[]{:S(2)}, u32[]{:S(2)}) collective-permute-start(bf16[2048,384]{1,0:T(8,128)(2,1)S(1)} %copy-done.7), channel_id=1, source_target_pairs={{0,8},{8,0},{16,24},{24,16},{32,40},{40,32},{48,56},{56,48},{64,72... | collective-permute-start | bytes 4718600 | tf_op jit(solution)/shard_map/ppermute | solution.py:263
  114.1 3.3 %collective-permute-start.9 = (bf16[256,384]{1,0:T(8,128)(2,1)S(1)}, bf16[256,384]{1,0:T(8,128)(2,1)S(1)}, u32[]{:S(2)}, u32[]{:S(2)}) collective-permute-start(bf16[256,384]{1,0:T(8,128)(2,1)S(1)} %copy-done.14), channel_id=1, source_target_pairs={{0,8},{8,0},{16,24},{24,16},{32,40},{40,32},{48,56},{56,48},{64,72... | collective-permute-start | bytes 589832 | tf_op jit(solution)/shard_map/ppermute | solution.py:262
  117.5 1.2 copy-start.13
  117.5 1.2 copy-start.8
  122.9 32.1 %collective-permute-start.11 = (bf16[2,256,512]{2,1,0:T(8,128)(2,1)}, bf16[2,256,512]{2,1,0:T(8,128)(2,1)S(1)}, u32[]{:S(2)}, u32[]{:S(2)}) collective-permute-start(bf16[2,256,512]{2,1,0:T(8,128)(2,1)} %get-tuple-element.29), channel_id=1, source_target_pairs={{0,2},{1,3},{2,4},{3,5},{4,6},{5,7},{6,0},{7,1},{8,10},{9,11},{10,... | collective-permute-start | bytes 1572872 | tf_op jit(solution)/shard_map/ppermute | solution.py:271
  126.3 28.7 %collective-permute-start.12 = (bf16[2,256,512]{2,1,0:T(8,128)(2,1)}, bf16[2,256,512]{2,1,0:T(8,128)(2,1)S(1)}, u32[]{:S(2)}, u32[]{:S(2)}) collective-permute-start(bf16[2,256,512]{2,1,0:T(8,128)(2,1)} %get-tuple-element.30), channel_id=1, source_target_pairs={{0,4},{1,5},{2,6},{3,7},{4,0},{5,1},{6,2},{7,3},{8,12},{9,13},{10,... | collective-permute-start | bytes 1572872 | tf_op jit(solution)/shard_map/ppermute | solution.py:271
  129.7 25.4 %collective-permute-start.13 = (bf16[2,256,512]{2,1,0:T(8,128)(2,1)}, bf16[2,256,512]{2,1,0:T(8,128)(2,1)S(1)}, u32[]{:S(2)}, u32[]{:S(2)}) collective-permute-start(bf16[2,256,512]{2,1,0:T(8,128)(2,1)} %get-tuple-element.31), channel_id=1, source_target_pairs={{0,6},{1,7},{2,0},{3,1},{4,2},{5,3},{6,4},{7,5},{8,14},{9,15},{10,... | collective-permute-start | bytes 1572872 | tf_op jit(solution)/shard_map/ppermute | solution.py:271
  149.5 9.8 %collective-permute-start.14 = (bf16[192,128]{1,0:T(8,128)(2,1)S(1)}, bf16[192,128]{1,0:T(8,128)(2,1)S(1)}, u32[]{:S(2)}, u32[]{:S(2)}) collective-permute-start(bf16[192,128]{1,0:T(8,128)(2,1)S(1)} %reduce_sum.12), channel_id=1, source_target_pairs={{0,0},{8,1},{2,2},{10,3},{4,4},{12,5},{6,6},{14,7},{64,8},{72,9},{... | collective-permute-start | bytes 147464 | tf_op jit(solution)/shard_map/ppermute | solution.py:260
  155.1 0.8 copy-start.9
  155.1 1.0 copy-start.10
  155.1 1.1 copy-start.11

commit v9 on v8

--- a/solution.py
+++ b/solution.py
@@ -5,6 +5,7 @@
 from jax.experimental.pallas import tpu as pltpu
 from jax.sharding import PartitionSpec as P
 
+TERMS = 2 * 10**10
 N_Y, N_Z, N_CORE, N_X = 8, 4, 2, 4
 N_WIDE, N_NARROW = N_Y * N_Z * N_CORE, 2 * N_X
 F32, BF16 = jnp.float32, jnp.bfloat16
@@ -41,29 +42,45 @@
     return lax.dot_general(a, b, (dims, ((), ())), preferred_element_type=F32)
 
 
-def call(body, outs, flops, where, *args, after=(), grant=60):
-    size = sum(a.size * a.dtype.itemsize for a in args)
-    count, results = len(args), len(outs)
+def turn(where, step, size):
+    return pl.multiple_of(lax.rem(where[0] + step, N_X) * size, size)
+
+
+def call(body, outs, flops, where, *args, after=(), grant=60, direct=False, keep=False):
+    entries = [a if isinstance(a, list) else [a] for a in args]
+    flat = [a for entry in entries for a in entry]
+    size = sum(a.size * a.dtype.itemsize for a in flat)
+    count, results = len(flat), len(outs)
     most = N_X * results
+
+    def shape_of(entry):
+        first, rows, *rest = entry[0].shape if len(entry) > 1 else (0, 0)
+        return (first, rows * len(entry), *rest) if len(entry) > 1 else entry[0].shape
 
     def inner(where_ref, *refs):
         sources, refs = refs[:count], refs[count + len(after) :]
-        targets, held = refs[:results], refs[results : results + count]
-        made, (sem, out_sem) = refs[results + count : -2], refs[-2:]
-        copies = [
-            pltpu.make_async_copy(s, h, sem.at[i]) for i, (s, h) in enumerate(zip(sources, held))
-        ]
-        for copy in copies:
-            copy.start()
-        here, leaving = set(), []
+        targets, held = refs[:results], refs[results:-2]
+        made, (sem, out_sem) = (targets if keep else held[len(held) - results :]), refs[-2:]
+        copies = []
+        for entry, h in zip(() if direct else entries, held):
+            copies.append([])
+            for i, a in enumerate(entry):
+                n = sum(len(c) for c in copies)
+                to = h if len(entry) == 1 else h.at[:, pl.ds(a.shape[1] * i, a.shape[1])]
+                copies[-1].append(pltpu.make_async_copy(sources[n], to, sem.at[n]))
+                copies[-1][-1].start()
+        here, leaving = set(range(len(entries)) if direct else ()), []
 
         def get(i):
             if i not in here:
                 here.add(i)
-                copies[i].wait()
-            return held[i]
+                for copy in copies[i]:
+                    copy.wait()
+            return sources[i] if direct else held[i]
 
         def put(i, at=slice(None)):
+            if keep:
+                return
             copy = pltpu.make_async_copy(made[i].at[at], targets[i].at[at], out_sem.at[len(leaving)])
             copy.start()
             leaving.append(copy)
@@ -73,7 +90,7 @@
         body(where_ref, get, put, *made)
         for i in sorted(whole):
             put(i)
-        for i in range(count):
+        for i in range(len(entries)):
             get(i)
         for copy in leaving:
             copy.wait()
@@ -83,13 +100,15 @@
         inner,
         out_shape=shapes,
         in_specs=[pl.BlockSpec(memory_space=pltpu.SMEM)]
-        + [pl.BlockSpec(memory_space=pl.ANY)] * (count + len(after)),
-        out_specs=[pl.BlockSpec(memory_space=pl.ANY)] * results,
-        scratch_shapes=[pltpu.VMEM(a.shape, a.dtype) for a in (*args, *shapes)]
+        + [pl.BlockSpec(memory_space=pltpu.VMEM if direct else pl.ANY)] * count
+        + [pl.BlockSpec(memory_space=pl.ANY)] * len(after),
+        out_specs=[pl.BlockSpec(memory_space=pltpu.VMEM if keep else pl.ANY)] * results,
+        scratch_shapes=[pltpu.VMEM(shape_of(entry), entry[0].dtype) for entry in entries if not direct]
+        + [pltpu.VMEM(a.shape, a.dtype) for a in shapes if not keep]
         + [pltpu.SemaphoreType.DMA((count,)), pltpu.SemaphoreType.DMA((most,))],
         compiler_params=pltpu.CompilerParams(vmem_limit_bytes=grant * 1024 * 1024),
         cost_estimate=pl.CostEstimate(flops=flops, bytes_accessed=size, transcendentals=0),
-    )(where, *args, *after)
+    )(where, *flat, *after)
 
 
 def use_of(gate, count):
@@ -105,12 +124,6 @@
 def pick_of(token, tok):
     slots = token.shape[1]
     return jnp.where(lax.broadcasted_iota(jnp.int32, (tok, slots), 0) == token, 1.0, 0.0).astype(BF16)
-
-
-def block_body(where, get, put, block):
-    rows = block.shape[0] // 3
-    for i in range(3):
-        block[rows * i : rows * (i + 1)] = get(i)[...]
 
 
 def rows_body(where, get, put, own):
@@ -129,10 +142,6 @@
             for which in range(2):
                 turned[step][which, :, slots * who : slots * (who + 1)] = get(who * N_X + step)[which].T
         put(step)
-
-
-def turn(where, step, size):
-    return pl.multiple_of(lax.rem(where[0] + step, N_X) * size, size)
 
 
 def products_body(where, get, put, part, weights):
@@ -146,18 +155,15 @@
                 i, rows * m : rows * (m + 1)
             ]
     put(1)
-    slots, feat = get(1).shape[1:]
-    for who in range(2):
-        pre, back = 0.0, 0.0
-        for step in range(N_X):
-            x = get(1 + who * N_X + step)
-            at = pl.ds(turn(where, step, feat), feat)
-            pre = pre + dot(x[0], weights[at, : 2 * cols])
-            back = back + dot(x[1], weights[at, 2 * cols :])
-        at = slice(slots * who, slots * (who + 1))
-        part[at, : 2 * cols] = pre.astype(BF16)
-        part[at, 2 * cols :] = back.astype(BF16)
-        put(0, pl.ds(slots * who, slots))
+    feat = get(1).shape[2]
+    pre, back = 0.0, 0.0
+    for step in range(N_X):
+        x = get(1 + step)
+        at = pl.ds(turn(where, step, feat), feat)
+        pre = pre + dot(x[0], weights[at, : 2 * cols])
+        back = back + dot(x[1], weights[at, 2 * cols :])
+    part[:, : 2 * cols] = pre.astype(BF16)
+    part[:, 2 * cols :] = back.astype(BF16)
 
 
 def terms_body(where, get, put, pieces, acts, send):
@@ -205,9 +211,9 @@
 
 def tokens_body(where, get, put, mixed, grad_tokens):
     token, count, gate = get(0), get(1), get(2)
-    pick = pick_of(token[...], mixed.shape[0])
+    pick, use = pick_of(token[...], mixed.shape[0]), use_of(gate[...], count[...])
     out, back = [sum(get(3 + step)[i].astype(F32) for step in range(N_X)) for i in range(2)]
-    mixed[...] = dot(pick, (use_of(gate[...], count[...]) * out).astype(BF16)).astype(BF16)
+    mixed[...] = dot(pick, (use * out).astype(BF16)).astype(BF16)
     put(0)
     grad_tokens[...] = dot(pick, back.astype(BF16)).astype(BF16)
 
@@ -219,7 +225,7 @@
     where = (lax.axis_index("narrow") // 2).astype(jnp.int32)[None]
     pick_flops = 4 * slots * tok * feat
 
-    (block,) = call(block_body, [((3 * rows, cols), BF16)], 0, where, w_gate, w_up, w_down)
+    block = jnp.concatenate((w_gate, w_up, w_down), axis=0)
     block = lax.ppermute(block, ("wide", "narrow"), SWAP)
     pieces = jnp.broadcast_to(block[None], (len(OWNERS[0]),) + block.shape)
     pieces = lax.all_to_all(pieces, "wide", 0, 0, axis_index_groups=OWNERS)
@@ -234,7 +240,7 @@
     near = [own] + [near[step] for step in range(1, N_X)]
     core = [lax.ppermute(held, "wide", OTHER_CORE) for held in near]
     turned = call(
-        turned_body, [((2, feat, 2 * slots), BF16)] * N_X, pick_flops, where, *near, *core
+        turned_body, [((2, feat, 2 * slots), BF16)] * N_X, pick_flops, where, *near, *core, grant=12, keep=True
     )
 
     flops = 2 * 3 * 2 * slots * N_X * feat * cols
@@ -244,23 +250,27 @@
         [part, ((N_X * feat, 3 * cols), BF16)],
         flops,
         where,
-        *(pieces, *near, *core),
+        *(pieces, *([a, b] for a, b in zip(near, core))),
     )
     theirs = lax.ppermute(sent, "narrow", OTHER_HALF)
     terms, acts, send = call(
         terms_body,
         [(pieces.shape, BF16), part, ((slots, 3 * cols), BF16)],
-        flops,
+        TERMS,
         where,
         *(sent, theirs, *turned),
-    )
+        grant=12,
+        direct=True,
+    )
+
+    core_weights = lax.ppermute(weights, "wide", OTHER_CORE)
+    terms, core_weights = lax.optimization_barrier((terms, core_weights))
 
     terms = lax.all_to_all(terms, "wide", 0, 0, axis_index_groups=OWNERS)
     grads = terms.astype(F32).sum(axis=0).astype(BF16)
     grads = lax.ppermute(grads, ("wide", "narrow"), SWAP_BACK).astype(F32)
 
     got = lax.ppermute(send, "wide", OTHER_CORE)
-    core_weights = lax.ppermute(weights, "wide", OTHER_CORE)
     outs = call(
         outputs_body,
         [((2, slots, feat), BF16)] * N_X,
@@ -271,7 +281,13 @@
     home = {step: lax.ppermute(outs[step], "narrow", shift_x(step)) for step in (1, 3, 2)}
     home = [outs[0]] + [home[step] for step in range(1, N_X)]
     mixed, grad_tokens = call(
-        tokens_body, [((tok, feat), BF16)] * 2, pick_flops, where, token, count, gate, *home
+        tokens_body,
+        [((tok, feat), BF16)] * 2,
+        pick_flops,
+        where,
+        *(token, count, gate, *home),
+        grant=12,
+        direct=True,
     )
     return mixed, grad_tokens, grads[:rows], grads[rows : 2 * rows], grads[2 * rows :]
 

time: 161 us -> 161 us (level)
  the two profiles are of different devices: /device:TPU:1 before, /device:TPU:24 now
where the time goes in v9:
time: 161 us; the launch traced here: 160 us
  starting transfers between devices  79.7 us (50%)
  waiting for transfers between devices  46.8 us (29%)
  Pallas kernels  18 us (11%)
  local copies, waits for them, and re-layouts  10.9 us (7%)
  other arithmetic  2.39 us (1%)
  between operations  1.7 us (1%)
    all_to_all x1, waiting for transfers between devices, local(): terms = lax.all_to_all(terms, 'wide', 0, 0, axis_index_groups=OWNERS)  18.9 us
    pallas_call x6, Pallas kernels, call(): pl.pallas_call(inner, out_shape=shapes, in_specs=[pl.BlockSpec(memory_spa...  18 us
    all_to_all x1, starting transfers between devices, local(): terms = lax.all_to_all(terms, 'wide', 0, 0, axis_index_groups=OWNERS)  17.6 us
    ppermute x3, waiting for transfers between devices, local(): lax.ppermute(own, 'narrow', shift_x(-step))  13.7 us
    ppermute x3, starting transfers between devices, local(): lax.ppermute(own, 'narrow', shift_x(-step))  11.5 us
    ppermute x1, starting transfers between devices, local(): block = lax.ppermute(block, ('wide', 'narrow'), SWAP)  10.8 us
    ppermute x3, starting transfers between devices, local(): lax.ppermute(outs[step], 'narrow', shift_x(step))  10.8 us
    all_to_all x1, starting transfers between devices, local(): pieces = lax.all_to_all(pieces, 'wide', 0, 0, axis_index_groups=OWNERS)  10.4 us
  transfers between devices with their start and end apart: 17, of which 9 were waited for; matrix products, arithmetic and copies ran while one was open for 1% of the time, Pallas kernels for 9%

profile of v9, /device:TPU:24, one launch (start us, length us, event | category | flops | bytes accessed | tf_op | source)
XLA Modules:
  0.0 159.6 jit_solution(14029222022550665758)
XLA Ops:
  1.4 10.8 %collective-permute-start = (bf16[192,128]{1,0:T(8,128)(2,1)S(1)}, bf16[192,128]{1,0:T(8,128)(2,1)S(1)}, u32[]{:S(2)}, u32[]{:S(2)}) collective-permute-start(bf16[192,128]{1,0:T(8,128)(2,1)S(1)} %pad_maximum_fusion), channel_id=1, source_target_pairs={{0,0},{1,8},{2,2},{3,10},{4,4},{5,12},{6,6},{7,14},{8,64},{9,72},{... | collective-permute-start | bytes 147464 | tf_op jit(solution)/shard_map/ppermute | solution.py:229
  12.2 1.7 %collective-permute-done = bf16[192,128]{1,0:T(8,128)(2,1)S(1)} collective-permute-done((bf16[192,128]{1,0:T(8,128)(2,1)S(1)}, bf16[192,128]{1,0:T(8,128)(2,1)S(1)}, u32[]{:S(2)}, u32[]{:S(2)}) %collective-permute-start) | collective-permute-done | bytes 49184 | tf_op jit(solution)/shard_map/ppermute | solution.py:229
  13.9 1.5 broadcast_in_dim.22
  15.4 10.4 %all-to-all-start = ((bf16[32,192,128]{2,1,0:T(8,128)(2,1)}), bf16[32,192,128]{2,1,0:T(8,128)(2,1)}, u32[]{:S(2)}, u32[]{:S(2)}) async-start(bf16[32,192,128]{2,1,0:T(8,128)(2,1)} %broadcast_in_dim.22), calls=%async_computation | async-start | bytes 3145728 | tf_op jit(solution)/shard_map/all_to_all | solution.py:231
  26.5 2.4 %shard_map.119.refs_1_.refs_0_ = bf16[2,256,512]{2,1,0:T(8,128)(2,1)} custom-call(s32[1]{0:T(128)} %bitcast.where_ref, bf16[384,512]{1,0:T(8,128)(2,1)} %refs_0_.1, bf16[384,512]{1,0:T(8,128)(2,1)} %refs_1_.1, s32[1,256]{1,0:T(1,128)} %bitcast.6, s32[1,1]{1,0:T(1,128)} %bitcast.4.refs_3_, f32[1,256]{1,0:T(1,128)} %bitcast.8), custom_call_target="tpu_custom_call" | custom-call | flops 201326592 | bytes 788484 | tf_op jit(solution)/shard_map/pallas_call | solution.py:99
  28.9 3.5 %collective-permute-start.6 = (bf16[2,256,512]{2,1,0:T(8,128)(2,1)}, bf16[2,256,512]{2,1,0:T(8,128)(2,1)S(1)}, u32[]{:S(2)}, u32[]{:S(2)}) collective-permute-start(bf16[2,256,512]{2,1,0:T(8,128)(2,1)} %shard_map.119.refs_1_.refs_0_), channel_id=1, source_target_pairs={{0,2},{1,3},{2,4},{3,5},{4,6},{5,7},{6,0},{7,1},{8,10},{9,11},{10,... | collective-permute-start | bytes 1572872 | tf_op jit(solution)/shard_map/ppermute | solution.py:239
  32.4 4.6 %collective-permute-start.4 = (bf16[2,256,512]{2,1,0:T(8,128)(2,1)}, bf16[2,256,512]{2,1,0:T(8,128)(2,1)S(1)}, u32[]{:S(2)}, u32[]{:S(2)}) collective-permute-start(bf16[2,256,512]{2,1,0:T(8,128)(2,1)} %shard_map.119.refs_1_.refs_0_), channel_id=1, source_target_pairs={{0,4},{1,5},{2,6},{3,7},{4,0},{5,1},{6,2},{7,3},{8,12},{9,13},{10,... | collective-permute-start | bytes 1572872 | tf_op jit(solution)/shard_map/ppermute | solution.py:239
  37.1 3.3 %collective-permute-start.2 = (bf16[2,256,512]{2,1,0:T(8,128)(2,1)}, bf16[2,256,512]{2,1,0:T(8,128)(2,1)S(1)}, u32[]{:S(2)}, u32[]{:S(2)}) collective-permute-start(bf16[2,256,512]{2,1,0:T(8,128)(2,1)} %shard_map.119.refs_1_.refs_0_), channel_id=1, source_target_pairs={{0,6},{1,7},{2,0},{3,1},{4,2},{5,3},{6,4},{7,5},{8,14},{9,15},{10,... | collective-permute-start | bytes 1572872 | tf_op jit(solution)/shard_map/ppermute | solution.py:239
  40.4 1.9 %collective-permute-start.1 = (bf16[2,256,512]{2,1,0:T(8,128)(2,1)}, bf16[2,256,512]{2,1,0:T(8,128)(2,1)S(1)}, u32[]{:S(2)}, u32[]{:S(2)}) collective-permute-start(bf16[2,256,512]{2,1,0:T(8,128)(2,1)} %shard_map.119.refs_1_.refs_0_), channel_id=1, source_target_pairs={{0,8},{8,0},{16,24},{24,16},{32,40},{40,32},{48,56},{56,48},{64,72... | collective-permute-start | bytes 1572872 | tf_op jit(solution)/shard_map/ppermute | solution.py:241
  42.4 3.9 %collective-permute-done.6.refs_7_.refs_3_ = bf16[2,256,512]{2,1,0:T(8,128)(2,1)S(1)} collective-permute-done((bf16[2,256,512]{2,1,0:T(8,128)(2,1)}, bf16[2,256,512]{2,1,0:T(8,128)(2,1)S(1)}, u32[]{:S(2)}, u32[]{:S(2)}) %collective-permute-start.6) | collective-permute-done | bytes 524320 | tf_op jit(solution)/shard_map/ppermute | solution.py:239
  46.2 1.9 %collective-permute-start.7 = (bf16[2,256,512]{2,1,0:T(8,128)(2,1)S(1)}, bf16[2,256,512]{2,1,0:T(8,128)(2,1)S(1)}, u32[]{:S(2)}, u32[]{:S(2)}) collective-permute-start(bf16[2,256,512]{2,1,0:T(8,128)(2,1)S(1)} %collective-permute-done.6.refs_7_.refs_3_), channel_id=1, source_target_pairs={{0,8},{8,0},{16,24},{24,16},{32,40},{40,32},{48,56},{56,48},{64,72... | collective-permute-start | bytes 1572872 | tf_op jit(solution)/shard_map/ppermute | solution.py:241
  48.1 9.8 %collective-permute-done.4.refs_5_.refs_2_ = bf16[2,256,512]{2,1,0:T(8,128)(2,1)S(1)} collective-permute-done((bf16[2,256,512]{2,1,0:T(8,128)(2,1)}, bf16[2,256,512]{2,1,0:T(8,128)(2,1)S(1)}, u32[]{:S(2)}, u32[]{:S(2)}) %collective-permute-start.4) | collective-permute-done | bytes 524320 | tf_op jit(solution)/shard_map/ppermute | solution.py:239
  58.0 1.9 %collective-permute-start.5 = (bf16[2,256,512]{2,1,0:T(8,128)(2,1)S(1)}, bf16[2,256,512]{2,1,0:T(8,128)(2,1)S(1)}, u32[]{:S(2)}, u32[]{:S(2)}) collective-permute-start(bf16[2,256,512]{2,1,0:T(8,128)(2,1)S(1)} %collective-permute-done.4.refs_5_.refs_2_), channel_id=1, source_target_pairs={{0,8},{8,0},{16,24},{24,16},{32,40},{40,32},{48,56},{56,48},{64,72... | collective-permute-start | bytes 1572872 | tf_op jit(solution)/shard_map/ppermute | solution.py:241
  59.9 2.4 %collective-permute-start.3 = (bf16[2,256,512]{2,1,0:T(8,128)(2,1)S(1)}, bf16[2,256,512]{2,1,0:T(8,128)(2,1)}, u32[]{:S(2)}, u32[]{:S(2)}) collective-permute-start(bf16[2,256,512]{2,1,0:T(8,128)(2,1)S(1)} %collective-permute-done.2.refs_3_.refs_1_), channel_id=1, source_target_pairs={{0,8},{8,0},{16,24},{24,16},{32,40},{40,32},{48,56},{56,48},{64,72... | collective-permute-start | bytes 1572872 | tf_op jit(solution)/shard_map/ppermute | solution.py:241
  64.3 4.3 %shard_map.120 = (bf16[512,384]{1,0:T(8,128)(2,1)}, bf16[2048,384]{1,0:T(8,128)(2,1)}) custom-call(s32[1]{0:T(128)} %bitcast.where_ref, bf16[32,192,128]{2,1,0:T(8,128)(2,1)} %all-to-all-done.refs_0_, bf16[2,256,512]{2,1,0:T(8,128)(2,1)} %shard_map.119.refs_1_.refs_0_, bf16[2,256,512]{2,1,0:T(8,128)(2,1)} %copy-done.7, bf16[2,256,512]{2,1,0:T(8,128)(2,1)} %copy-done.5, ...), custom_call_target="tpu_custom_call" | custom-call | flops 805306368 | bytes 5767168 | tf_op jit(solution)/shard_map/pallas_call | solution.py:99
  68.7 4.1 %collective-permute-start.8 = (bf16[512,384]{1,0:T(8,128)(2,1)}, bf16[512,384]{1,0:T(8,128)(2,1)S(1)}, u32[]{:S(2)}, u32[]{:S(2)}) collective-permute-start(bf16[512,384]{1,0:T(8,128)(2,1)} %get-tuple-element.22.refs_0_), channel_id=1, source_target_pairs={{0,1},{1,0},{2,3},{3,2},{4,5},{5,4},{6,7},{7,6},{8,9},{9,8},{10,11... | collective-permute-start | bytes 1179656 | tf_op jit(solution)/shard_map/ppermute | solution.py:255
  78.0 2.5 %shard_map.121 = (bf16[2,512,512]{2,1,0:T(8,128)(2,1)S(1)}, bf16[2,512,512]{2,1,0:T(8,128)(2,1)S(1)}, bf16[2,512,512]{2,1,0:T(8,128)(2,1)S(1)}, bf16[2,512,512]{2,1,0:T(8,128)(2,1)S(1)}) custom-call(s32[1]{0:T(128)} %bitcast.where_ref, bf16[2,256,512]{2,1,0:T(8,128)(2,1)S(1)} %copy-done, bf16[2,256,512]{2,1,0:T(8,128)(2,1)S(1)} %copy-done.6, ...), custom_call_target="tpu_custom_call" | custom-call | flops 201326592 | bytes 4194304 | tf_op jit(solution)/shard_map/pallas_call | solution.py:99
  80.5 1.9 %collective-permute-start.10 = (bf16[2048,384]{1,0:T(8,128)(2,1)S(1)}, bf16[2048,384]{1,0:T(8,128)(2,1)S(1)}, u32[]{:S(2)}, u32[]{:S(2)}) collective-permute-start(bf16[2048,384]{1,0:T(8,128)(2,1)S(1)} %copy-done.18), channel_id=1, source_target_pairs={{0,8},{8,0},{16,24},{24,16},{32,40},{40,32},{48,56},{56,48},{64,72... | collective-permute-start | bytes 4718600 | tf_op jit(solution)/shard_map/ppermute | solution.py:266
  82.4 3.5 %collective-permute-done.8.refs_1_ = bf16[512,384]{1,0:T(8,128)(2,1)S(1)} collective-permute-done((bf16[512,384]{1,0:T(8,128)(2,1)}, bf16[512,384]{1,0:T(8,128)(2,1)S(1)}, u32[]{:S(2)}, u32[]{:S(2)}) %collective-permute-start.8) | collective-permute-done | bytes 393248 | tf_op jit(solution)/shard_map/ppermute | solution.py:255
  85.9 3.0 %shard_map.122 = (bf16[32,192,128]{2,1,0:T(8,128)(2,1)}, bf16[512,384]{1,0:T(8,128)(2,1)S(1)}, bf16[256,384]{1,0:T(8,128)(2,1)S(1)}) custom-call(s32[1]{0:T(128)} %bitcast.where_ref, bf16[512,384]{1,0:T(8,128)(2,1)S(1)} %copy-done.17, bf16[512,384]{1,0:T(8,128)(2,1)S(1)} %collective-permute-done.8.refs_1_, ...), custom_call_target="tpu_custom_call" | custom-call | flops 20000000000 | bytes 4980736 | tf_op jit(solution)/shard_map/pallas_call | solution.py:99
  90.9 17.6 %all-to-all-start.1 = ((bf16[32,192,128]{2,1,0:T(8,128)(2,1)}), bf16[32,192,128]{2,1,0:T(8,128)(2,1)}, u32[]{:S(2)}, u32[]{:S(2)}) async-start(bf16[32,192,128]{2,1,0:T(8,128)(2,1)} %get-tuple-element.38), calls=%async_computation.1 | async-start | bytes 3145728 | tf_op jit(solution)/shard_map/all_to_all | solution.py:269
  108.5 1.9 %collective-permute-start.9 = (bf16[256,384]{1,0:T(8,128)(2,1)S(1)}, bf16[256,384]{1,0:T(8,128)(2,1)S(1)}, u32[]{:S(2)}, u32[]{:S(2)}) collective-permute-start(bf16[256,384]{1,0:T(8,128)(2,1)S(1)} %get-tuple-element.29), channel_id=1, source_target_pairs={{0,8},{8,0},{16,24},{24,16},{32,40},{40,32},{48,56},{56,48},{64,72... | collective-permute-start | bytes 589832 | tf_op jit(solution)/shard_map/ppermute | solution.py:273
  110.4 1.4 collective-permute-done.9.refs_2_
  112.5 4.3 %shard_map.123 = (bf16[2,256,512]{2,1,0:T(8,128)(2,1)}, bf16[2,256,512]{2,1,0:T(8,128)(2,1)}, bf16[2,256,512]{2,1,0:T(8,128)(2,1)}, bf16[2,256,512]{2,1,0:T(8,128)(2,1)}) custom-call(s32[1]{0:T(128)} %bitcast.where_ref, bf16[512,384]{1,0:T(8,128)(2,1)} %copy-done.14, bf16[2048,384]{1,0:T(8,128)(2,1)} %get-tuple-element.28.refs_1_, ...), custom_call_target="tpu_custom_call" | custom-call | flops 805306368 | bytes 3735552 | tf_op jit(solution)/shard_map/pallas_call | solution.py:99
  116.8 3.6 %collective-permute-start.11 = (bf16[2,256,512]{2,1,0:T(8,128)(2,1)}, bf16[2,256,512]{2,1,0:T(8,128)(2,1)S(1)}, u32[]{:S(2)}, u32[]{:S(2)}) collective-permute-start(bf16[2,256,512]{2,1,0:T(8,128)(2,1)} %get-tuple-element.33), channel_id=1, source_target_pairs={{0,2},{1,3},{2,4},{3,5},{4,6},{5,7},{6,0},{7,1},{8,10},{9,11},{10,... | collective-permute-start | bytes 1572872 | tf_op jit(solution)/shard_map/ppermute | solution.py:281
  120.4 3.6 %collective-permute-start.12 = (bf16[2,256,512]{2,1,0:T(8,128)(2,1)}, bf16[2,256,512]{2,1,0:T(8,128)(2,1)S(1)}, u32[]{:S(2)}, u32[]{:S(2)}) collective-permute-start(bf16[2,256,512]{2,1,0:T(8,128)(2,1)} %get-tuple-element.34), channel_id=1, source_target_pairs={{0,4},{1,5},{2,6},{3,7},{4,0},{5,1},{6,2},{7,3},{8,12},{9,13},{10,... | collective-permute-start | bytes 1572872 | tf_op jit(solution)/shard_map/ppermute | solution.py:281
  124.1 3.5 %collective-permute-start.13 = (bf16[2,256,512]{2,1,0:T(8,128)(2,1)}, bf16[2,256,512]{2,1,0:T(8,128)(2,1)S(1)}, u32[]{:S(2)}, u32[]{:S(2)}) collective-permute-start(bf16[2,256,512]{2,1,0:T(8,128)(2,1)} %get-tuple-element.35), channel_id=1, source_target_pairs={{0,6},{1,7},{2,0},{3,1},{4,2},{5,3},{6,4},{7,5},{8,14},{9,15},{10,... | collective-permute-start | bytes 1572872 | tf_op jit(solution)/shard_map/ppermute | solution.py:281
  127.6 18.9 %all-to-all-done.1 = bf16[32,192,128]{2,1,0:T(8,128)(2,1)} async-done(((bf16[32,192,128]{2,1,0:T(8,128)(2,1)}), bf16[32,192,128]{2,1,0:T(8,128)(2,1)}, u32[]{:S(2)}, u32[]{:S(2)}) %all-to-all-start.1) | async-done | bytes 1572896 | tf_op jit(solution)/shard_map/all_to_all | solution.py:269
  146.5 1.6 %reduce_sum.12 = bf16[192,128]{1,0:T(8,128)(2,1)S(1)} reduce(bf16[32,192,128]{2,1,0:T(8,128)(2,1)} %all-to-all-done.1, bf16[]{:T(256)} %constant.20.clone.1), dimensions={0}, to_apply=%region_0.1 | reduce | flops 761856 | bytes 1622018 | tf_op jit(solution)/shard_map/reduce_sum | solution.py:270
  148.1 2.6 %collective-permute-start.14 = (bf16[192,128]{1,0:T(8,128)(2,1)S(1)}, bf16[192,128]{1,0:T(8,128)(2,1)S(1)}, u32[]{:S(2)}, u32[]{:S(2)}) collective-permute-start(bf16[192,128]{1,0:T(8,128)(2,1)S(1)} %reduce_sum.12), channel_id=1, source_target_pairs={{0,0},{8,1},{2,2},{10,3},{4,4},{12,5},{6,6},{14,7},{64,8},{72,9},{... | collective-permute-start | bytes 147464 | tf_op jit(solution)/shard_map/ppermute | solution.py:271
  150.8 1.5 shard_map.124
  152.4 6.5 %collective-permute-done.14 = bf16[192,128]{1,0:T(8,128)(2,1)S(1)} collective-permute-done((bf16[192,128]{1,0:T(8,128)(2,1)S(1)}, bf16[192,128]{1,0:T(8,128)(2,1)S(1)}, u32[]{:S(2)}, u32[]{:S(2)}) %collective-permute-start.14) | collective-permute-done | bytes 49184 | tf_op jit(solution)/shard_map/ppermute | solution.py:271
  (54 shorter events, 11.2 us)
Async XLA Ops:
  1.4 12.5 %collective-permute-start = (bf16[192,128]{1,0:T(8,128)(2,1)S(1)}, bf16[192,128]{1,0:T(8,128)(2,1)S(1)}, u32[]{:S(2)}, u32[]{:S(2)}) collective-permute-start(bf16[192,128]{1,0:T(8,128)(2,1)S(1)} %pad_maximum_fusion), channel_id=1, source_target_pairs={{0,0},{1,8},{2,2},{3,10},{4,4},{5,12},{6,6},{7,14},{8,64},{9,72},{... | collective-permute-start | bytes 147464 | tf_op jit(solution)/shard_map/ppermute | solution.py:229
  15.4 48.9 %all-to-all-start = ((bf16[32,192,128]{2,1,0:T(8,128)(2,1)}), bf16[32,192,128]{2,1,0:T(8,128)(2,1)}, u32[]{:S(2)}, u32[]{:S(2)}) async-start(bf16[32,192,128]{2,1,0:T(8,128)(2,1)} %broadcast_in_dim.22), calls=%async_computation | async-start | bytes 3145728 | tf_op jit(solution)/shard_map/all_to_all | solution.py:231
  28.9 43.9 %copy-start = (bf16[2,256,512]{2,1,0:T(8,128)(2,1)S(1)}, bf16[2,256,512]{2,1,0:T(8,128)(2,1)}, u32[]{:S(2)}) copy-start(bf16[2,256,512]{2,1,0:T(8,128)(2,1)} %shard_map.119.refs_1_.refs_0_) | copy-start | bytes 1572868
  28.9 17.3 %collective-permute-start.6 = (bf16[2,256,512]{2,1,0:T(8,128)(2,1)}, bf16[2,256,512]{2,1,0:T(8,128)(2,1)S(1)}, u32[]{:S(2)}, u32[]{:S(2)}) collective-permute-start(bf16[2,256,512]{2,1,0:T(8,128)(2,1)} %shard_map.119.refs_1_.refs_0_), channel_id=1, source_target_pairs={{0,2},{1,3},{2,4},{3,5},{4,6},{5,7},{6,0},{7,1},{8,10},{9,11},{10,... | collective-permute-start | bytes 1572872 | tf_op jit(solution)/shard_map/ppermute | solution.py:239
  32.4 25.5 %collective-permute-start.4 = (bf16[2,256,512]{2,1,0:T(8,128)(2,1)}, bf16[2,256,512]{2,1,0:T(8,128)(2,1)S(1)}, u32[]{:S(2)}, u32[]{:S(2)}) collective-permute-start(bf16[2,256,512]{2,1,0:T(8,128)(2,1)} %shard_map.119.refs_1_.refs_0_), channel_id=1, source_target_pairs={{0,4},{1,5},{2,6},{3,7},{4,0},{5,1},{6,2},{7,3},{8,12},{9,13},{10,... | collective-permute-start | bytes 1572872 | tf_op jit(solution)/shard_map/ppermute | solution.py:239
  37.1 22.8 %collective-permute-start.2 = (bf16[2,256,512]{2,1,0:T(8,128)(2,1)}, bf16[2,256,512]{2,1,0:T(8,128)(2,1)S(1)}, u32[]{:S(2)}, u32[]{:S(2)}) collective-permute-start(bf16[2,256,512]{2,1,0:T(8,128)(2,1)} %shard_map.119.refs_1_.refs_0_), channel_id=1, source_target_pairs={{0,6},{1,7},{2,0},{3,1},{4,2},{5,3},{6,4},{7,5},{8,14},{9,15},{10,... | collective-permute-start | bytes 1572872 | tf_op jit(solution)/shard_map/ppermute | solution.py:239
  40.4 21.9 %collective-permute-start.1 = (bf16[2,256,512]{2,1,0:T(8,128)(2,1)}, bf16[2,256,512]{2,1,0:T(8,128)(2,1)S(1)}, u32[]{:S(2)}, u32[]{:S(2)}) collective-permute-start(bf16[2,256,512]{2,1,0:T(8,128)(2,1)} %shard_map.119.refs_1_.refs_0_), channel_id=1, source_target_pairs={{0,8},{8,0},{16,24},{24,16},{32,40},{40,32},{48,56},{56,48},{64,72... | collective-permute-start | bytes 1572872 | tf_op jit(solution)/shard_map/ppermute | solution.py:241
  46.2 18.1 %copy-start.1 = (bf16[2,256,512]{2,1,0:T(8,128)(2,1)}, bf16[2,256,512]{2,1,0:T(8,128)(2,1)S(1)}, u32[]{:S(2)}) copy-start(bf16[2,256,512]{2,1,0:T(8,128)(2,1)S(1)} %collective-permute-done.6.refs_7_.refs_3_) | copy-start | bytes 1572868
  46.2 16.1 %collective-permute-start.7 = (bf16[2,256,512]{2,1,0:T(8,128)(2,1)S(1)}, bf16[2,256,512]{2,1,0:T(8,128)(2,1)S(1)}, u32[]{:S(2)}, u32[]{:S(2)}) collective-permute-start(bf16[2,256,512]{2,1,0:T(8,128)(2,1)S(1)} %collective-permute-done.6.refs_7_.refs_3_), channel_id=1, source_target_pairs={{0,8},{8,0},{16,24},{24,16},{32,40},{40,32},{48,56},{56,48},{64,72... | collective-permute-start | bytes 1572872 | tf_op jit(solution)/shard_map/ppermute | solution.py:241
  58.0 6.3 %copy-start.3 = (bf16[2,256,512]{2,1,0:T(8,128)(2,1)}, bf16[2,256,512]{2,1,0:T(8,128)(2,1)S(1)}, u32[]{:S(2)}) copy-start(bf16[2,256,512]{2,1,0:T(8,128)(2,1)S(1)} %collective-permute-done.4.refs_5_.refs_2_) | copy-start | bytes 1572868
  58.0 4.4 %collective-permute-start.5 = (bf16[2,256,512]{2,1,0:T(8,128)(2,1)S(1)}, bf16[2,256,512]{2,1,0:T(8,128)(2,1)S(1)}, u32[]{:S(2)}, u32[]{:S(2)}) collective-permute-start(bf16[2,256,512]{2,1,0:T(8,128)(2,1)S(1)} %collective-permute-done.4.refs_5_.refs_2_), channel_id=1, source_target_pairs={{0,8},{8,0},{16,24},{24,16},{32,40},{40,32},{48,56},{56,48},{64,72... | collective-permute-start | bytes 1572872 | tf_op jit(solution)/shard_map/ppermute | solution.py:241
  59.9 4.4 %copy-start.5 = (bf16[2,256,512]{2,1,0:T(8,128)(2,1)}, bf16[2,256,512]{2,1,0:T(8,128)(2,1)S(1)}, u32[]{:S(2)}) copy-start(bf16[2,256,512]{2,1,0:T(8,128)(2,1)S(1)} %collective-permute-done.2.refs_3_.refs_1_) | copy-start | bytes 1572868
  59.9 4.1 %collective-permute-start.3 = (bf16[2,256,512]{2,1,0:T(8,128)(2,1)S(1)}, bf16[2,256,512]{2,1,0:T(8,128)(2,1)}, u32[]{:S(2)}, u32[]{:S(2)}) collective-permute-start(bf16[2,256,512]{2,1,0:T(8,128)(2,1)S(1)} %collective-permute-done.2.refs_3_.refs_1_), channel_id=1, source_target_pairs={{0,8},{8,0},{16,24},{24,16},{32,40},{40,32},{48,56},{56,48},{64,72... | collective-permute-start | bytes 1572872 | tf_op jit(solution)/shard_map/ppermute | solution.py:241
  62.3 2.0 %copy-start.7 = (bf16[2,256,512]{2,1,0:T(8,128)(2,1)}, bf16[2,256,512]{2,1,0:T(8,128)(2,1)S(1)}, u32[]{:S(2)}) copy-start(bf16[2,256,512]{2,1,0:T(8,128)(2,1)S(1)} %collective-permute-done.1.refs_2_.refs_4_) | copy-start | bytes 1572868
  62.4 2.0 %copy-start.9 = (bf16[2,256,512]{2,1,0:T(8,128)(2,1)}, bf16[2,256,512]{2,1,0:T(8,128)(2,1)S(1)}, u32[]{:S(2)}) copy-start(bf16[2,256,512]{2,1,0:T(8,128)(2,1)S(1)} %collective-permute-done.7.refs_8_.refs_7_) | copy-start | bytes 1572868
  64.3 8.4 %copy-start.12 = (bf16[2,256,512]{2,1,0:T(8,128)(2,1)S(1)}, bf16[2,256,512]{2,1,0:T(8,128)(2,1)}, u32[]{:S(2)}) copy-start(bf16[2,256,512]{2,1,0:T(8,128)(2,1)} %copy-done.11) | copy-start | bytes 1572868
  68.7 17.2 %collective-permute-start.8 = (bf16[512,384]{1,0:T(8,128)(2,1)}, bf16[512,384]{1,0:T(8,128)(2,1)S(1)}, u32[]{:S(2)}, u32[]{:S(2)}) collective-permute-start(bf16[512,384]{1,0:T(8,128)(2,1)} %get-tuple-element.22.refs_0_), channel_id=1, source_target_pairs={{0,1},{1,0},{2,3},{3,2},{4,5},{5,4},{6,7},{7,6},{8,9},{9,8},{10,11... | collective-permute-start | bytes 1179656 | tf_op jit(solution)/shard_map/ppermute | solution.py:255
  72.8 1.0 copy-start.2
  73.8 1.0 copy-start.4
  78.0 2.5 %copy-start.18 = (bf16[2048,384]{1,0:T(8,128)(2,1)S(1)}, bf16[2048,384]{1,0:T(8,128)(2,1)}, u32[]{:S(2)}) copy-start(bf16[2048,384]{1,0:T(8,128)(2,1)} %get-tuple-element.28.refs_1_) | copy-start | bytes 4718596
  78.0 7.9 %copy-start.17 = (bf16[512,384]{1,0:T(8,128)(2,1)S(1)}, bf16[512,384]{1,0:T(8,128)(2,1)}, u32[]{:S(2)}) copy-start(bf16[512,384]{1,0:T(8,128)(2,1)} %get-tuple-element.22.refs_0_) | copy-start | bytes 1179652
  80.5 9.2 %collective-permute-start.10 = (bf16[2048,384]{1,0:T(8,128)(2,1)S(1)}, bf16[2048,384]{1,0:T(8,128)(2,1)S(1)}, u32[]{:S(2)}, u32[]{:S(2)}) collective-permute-start(bf16[2048,384]{1,0:T(8,128)(2,1)S(1)} %copy-done.18), channel_id=1, source_target_pairs={{0,8},{8,0},{16,24},{24,16},{32,40},{40,32},{48,56},{56,48},{64,72... | collective-permute-start | bytes 4718600 | tf_op jit(solution)/shard_map/ppermute | solution.py:266
  89.7 1.2 copy-start.19
  90.9 55.6 %all-to-all-start.1 = ((bf16[32,192,128]{2,1,0:T(8,128)(2,1)}), bf16[32,192,128]{2,1,0:T(8,128)(2,1)}, u32[]{:S(2)}, u32[]{:S(2)}) async-start(bf16[32,192,128]{2,1,0:T(8,128)(2,1)} %get-tuple-element.38), calls=%async_computation.1 | async-start | bytes 3145728 | tf_op jit(solution)/shard_map/all_to_all | solution.py:269
  108.5 3.3 %collective-permute-start.9 = (bf16[256,384]{1,0:T(8,128)(2,1)S(1)}, bf16[256,384]{1,0:T(8,128)(2,1)S(1)}, u32[]{:S(2)}, u32[]{:S(2)}) collective-permute-start(bf16[256,384]{1,0:T(8,128)(2,1)S(1)} %get-tuple-element.29), channel_id=1, source_target_pairs={{0,8},{8,0},{16,24},{24,16},{32,40},{40,32},{48,56},{56,48},{64,72... | collective-permute-start | bytes 589832 | tf_op jit(solution)/shard_map/ppermute | solution.py:273
  116.8 34.0 %copy-start.13 = (bf16[2,256,512]{2,1,0:T(8,128)(2,1)S(1)}, bf16[2,256,512]{2,1,0:T(8,128)(2,1)}, u32[]{:S(2)}) copy-start(bf16[2,256,512]{2,1,0:T(8,128)(2,1)} %get-tuple-element.32.refs_3_) | copy-start | bytes 1572868
  116.8 34.0 %copy-start.15 = (s32[256]{0:T(256)S(1)}, s32[256]{0:T(256)}, u32[]{:S(2)}) copy-start(s32[256]{0:T(256)} %param.10) | copy-start | bytes 3076
  116.8 34.0 %copy-start.16 = (f32[256]{0:T(256)S(1)}, f32[256]{0:T(256)}, u32[]{:S(2)}) copy-start(f32[256]{0:T(256)} %param.12) | copy-start | bytes 3076
  116.8 34.0 %collective-permute-start.11 = (bf16[2,256,512]{2,1,0:T(8,128)(2,1)}, bf16[2,256,512]{2,1,0:T(8,128)(2,1)S(1)}, u32[]{:S(2)}, u32[]{:S(2)}) collective-permute-start(bf16[2,256,512]{2,1,0:T(8,128)(2,1)} %get-tuple-element.33), channel_id=1, source_target_pairs={{0,2},{1,3},{2,4},{3,5},{4,6},{5,7},{6,0},{7,1},{8,10},{9,11},{10,... | collective-permute-start | bytes 1572872 | tf_op jit(solution)/shard_map/ppermute | solution.py:281
  120.4 30.4 %collective-permute-start.12 = (bf16[2,256,512]{2,1,0:T(8,128)(2,1)}, bf16[2,256,512]{2,1,0:T(8,128)(2,1)S(1)}, u32[]{:S(2)}, u32[]{:S(2)}) collective-permute-start(bf16[2,256,512]{2,1,0:T(8,128)(2,1)} %get-tuple-element.34), channel_id=1, source_target_pairs={{0,4},{1,5},{2,6},{3,7},{4,0},{5,1},{6,2},{7,3},{8,12},{9,13},{10,... | collective-permute-start | bytes 1572872 | tf_op jit(solution)/shard_map/ppermute | solution.py:281
  124.1 26.7 %collective-permute-start.13 = (bf16[2,256,512]{2,1,0:T(8,128)(2,1)}, bf16[2,256,512]{2,1,0:T(8,128)(2,1)S(1)}, u32[]{:S(2)}, u32[]{:S(2)}) collective-permute-start(bf16[2,256,512]{2,1,0:T(8,128)(2,1)} %get-tuple-element.35), channel_id=1, source_target_pairs={{0,6},{1,7},{2,0},{3,1},{4,2},{5,3},{6,4},{7,5},{8,14},{9,15},{10,... | collective-permute-start | bytes 1572872 | tf_op jit(solution)/shard_map/ppermute | solution.py:281
  148.1 10.8 %collective-permute-start.14 = (bf16[192,128]{1,0:T(8,128)(2,1)S(1)}, bf16[192,128]{1,0:T(8,128)(2,1)S(1)}, u32[]{:S(2)}, u32[]{:S(2)}) collective-permute-start(bf16[192,128]{1,0:T(8,128)(2,1)S(1)} %reduce_sum.12), channel_id=1, source_target_pairs={{0,0},{8,1},{2,2},{10,3},{4,4},{12,5},{6,6},{14,7},{64,8},{72,9},{... | collective-permute-start | bytes 147464 | tf_op jit(solution)/shard_map/ppermute | solution.py:271
  (6 other events, 5.4 us)

commit v10 on v9

--- a/solution.py
+++ b/solution.py
@@ -5,7 +5,7 @@
 from jax.experimental.pallas import tpu as pltpu
 from jax.sharding import PartitionSpec as P
 
-TERMS = 2 * 10**10
+TURN = 2 * 10**10
 N_Y, N_Z, N_CORE, N_X = 8, 4, 2, 4
 N_WIDE, N_NARROW = N_Y * N_Z * N_CORE, 2 * N_X
 F32, BF16 = jnp.float32, jnp.bfloat16
@@ -240,7 +240,7 @@
     near = [own] + [near[step] for step in range(1, N_X)]
     core = [lax.ppermute(held, "wide", OTHER_CORE) for held in near]
     turned = call(
-        turned_body, [((2, feat, 2 * slots), BF16)] * N_X, pick_flops, where, *near, *core, grant=12, keep=True
+        turned_body, [((2, feat, 2 * slots), BF16)] * N_X, TURN, where, *near, *core, grant=12, keep=True
     )
 
     flops = 2 * 3 * 2 * slots * N_X * feat * cols
@@ -253,18 +253,18 @@
         *(pieces, *([a, b] for a, b in zip(near, core))),
     )
     theirs = lax.ppermute(sent, "narrow", OTHER_HALF)
+    core_weights = lax.ppermute(weights, "wide", OTHER_CORE)
+    theirs, core_weights = lax.optimization_barrier((theirs, core_weights))
     terms, acts, send = call(
         terms_body,
         [(pieces.shape, BF16), part, ((slots, 3 * cols), BF16)],
-        TERMS,
+        flops,
         where,
         *(sent, theirs, *turned),
         grant=12,
         direct=True,
     )
 
-    core_weights = lax.ppermute(weights, "wide", OTHER_CORE)
-    terms, core_weights = lax.optimization_barrier((terms, core_weights))
 
     terms = lax.all_to_all(terms, "wide", 0, 0, axis_index_groups=OWNERS)
     grads = terms.astype(F32).sum(axis=0).astype(BF16)
@@ -286,8 +286,6 @@
         pick_flops,
         where,
         *(token, count, gate, *home),
-        grant=12,
-        direct=True,
     )
     return mixed, grad_tokens, grads[:rows], grads[rows : 2 * rows], grads[2 * rows :]
 

time: 161 us -> 158 us (0.981)
  the two profiles are of different devices: /device:TPU:24 before, /device:TPU:1 now
where the time goes in v10:
time: 158 us; the launch traced here: 157 us
  starting transfers between devices  80.2 us (51%)
  waiting for transfers between devices  43.6 us (28%)
  Pallas kernels  19.3 us (12%)
  local copies, waits for them, and re-layouts  10.8 us (7%)
  between operations  1.69 us (1%)
    all_to_all x1, waiting for transfers between devices, local(): terms = lax.all_to_all(terms, 'wide', 0, 0, axis_index_groups=OWNERS)  19.3 us
    pallas_call x6, Pallas kernels, call(): pl.pallas_call(inner, out_shape=shapes, in_specs=[pl.BlockSpec(memory_spa...  19.3 us
    all_to_all x1, starting transfers between devices, local(): terms = lax.all_to_all(terms, 'wide', 0, 0, axis_index_groups=OWNERS)  18.2 us
    ppermute x4, starting transfers between devices, local(): core = [lax.ppermute(held, 'wide', OTHER_CORE) for held in near]  12.1 us
    ppermute x3, waiting for transfers between devices, local(): lax.ppermute(own, 'narrow', shift_x(-step))  11.1 us
    ppermute x3, starting transfers between devices, local(): lax.ppermute(own, 'narrow', shift_x(-step))  10.7 us
    all_to_all x1, starting transfers between devices, local(): pieces = lax.all_to_all(pieces, 'wide', 0, 0, axis_index_groups=OWNERS)  10 us
    ppermute x3, starting transfers between devices, local(): lax.ppermute(outs[step], 'narrow', shift_x(step))  9.8 us
  transfers between devices with their start and end apart: 17, of which 7 were waited for; matrix products, arithmetic and copies ran while one was open for 0% of the time, Pallas kernels for 8%

profile of v10, /device:TPU:1, one launch (start us, length us, event | category | flops | bytes accessed | tf_op | source)
XLA Modules:
  0.0 156.6 jit_solution(14771392663328071199)
XLA Ops:
  1.4 4.6 %collective-permute-start = (bf16[192,128]{1,0:T(8,128)(2,1)S(1)}, bf16[192,128]{1,0:T(8,128)(2,1)S(1)}, u32[]{:S(2)}, u32[]{:S(2)}) collective-permute-start(bf16[192,128]{1,0:T(8,128)(2,1)S(1)} %pad_maximum_fusion), channel_id=1, source_target_pairs={{0,0},{1,8},{2,2},{3,10},{4,4},{5,12},{6,6},{7,14},{8,64},{9,72},{... | collective-permute-start | bytes 147464 | tf_op jit(solution)/shard_map/ppermute | solution.py:229
  6.0 9.2 %collective-permute-done = bf16[192,128]{1,0:T(8,128)(2,1)S(1)} collective-permute-done((bf16[192,128]{1,0:T(8,128)(2,1)S(1)}, bf16[192,128]{1,0:T(8,128)(2,1)S(1)}, u32[]{:S(2)}, u32[]{:S(2)}) %collective-permute-start) | collective-permute-done | bytes 49184 | tf_op jit(solution)/shard_map/ppermute | solution.py:229
  15.2 1.5 broadcast_in_dim.22
  16.8 10.0 %all-to-all-start = ((bf16[32,192,128]{2,1,0:T(8,128)(2,1)}), bf16[32,192,128]{2,1,0:T(8,128)(2,1)}, u32[]{:S(2)}, u32[]{:S(2)}) async-start(bf16[32,192,128]{2,1,0:T(8,128)(2,1)} %broadcast_in_dim.22), calls=%async_computation | async-start | bytes 3145728 | tf_op jit(solution)/shard_map/all_to_all | solution.py:231
  27.4 2.4 %shard_map.119.refs_1_.refs_0_ = bf16[2,256,512]{2,1,0:T(8,128)(2,1)} custom-call(s32[1]{0:T(128)} %bitcast.where_ref, bf16[384,512]{1,0:T(8,128)(2,1)} %refs_0_.1, bf16[384,512]{1,0:T(8,128)(2,1)} %refs_1_.1, s32[1,256]{1,0:T(1,128)} %bitcast.6, s32[1,1]{1,0:T(1,128)} %bitcast.4.refs_3_, f32[1,256]{1,0:T(1,128)} %bitcast.8), custom_call_target="tpu_custom_call" | custom-call | flops 201326592 | bytes 788484 | tf_op jit(solution)/shard_map/pallas_call | solution.py:99
  29.8 3.3 %collective-permute-start.6 = (bf16[2,256,512]{2,1,0:T(8,128)(2,1)}, bf16[2,256,512]{2,1,0:T(8,128)(2,1)S(1)}, u32[]{:S(2)}, u32[]{:S(2)}) collective-permute-start(bf16[2,256,512]{2,1,0:T(8,128)(2,1)} %shard_map.119.refs_1_.refs_0_), channel_id=1, source_target_pairs={{0,2},{1,3},{2,4},{3,5},{4,6},{5,7},{6,0},{7,1},{8,10},{9,11},{10,... | collective-permute-start | bytes 1572872 | tf_op jit(solution)/shard_map/ppermute | solution.py:239
  33.1 4.4 %collective-permute-start.4 = (bf16[2,256,512]{2,1,0:T(8,128)(2,1)}, bf16[2,256,512]{2,1,0:T(8,128)(2,1)S(1)}, u32[]{:S(2)}, u32[]{:S(2)}) collective-permute-start(bf16[2,256,512]{2,1,0:T(8,128)(2,1)} %shard_map.119.refs_1_.refs_0_), channel_id=1, source_target_pairs={{0,4},{1,5},{2,6},{3,7},{4,0},{5,1},{6,2},{7,3},{8,12},{9,13},{10,... | collective-permute-start | bytes 1572872 | tf_op jit(solution)/shard_map/ppermute | solution.py:239
  37.5 3.1 %collective-permute-start.2 = (bf16[2,256,512]{2,1,0:T(8,128)(2,1)}, bf16[2,256,512]{2,1,0:T(8,128)(2,1)S(1)}, u32[]{:S(2)}, u32[]{:S(2)}) collective-permute-start(bf16[2,256,512]{2,1,0:T(8,128)(2,1)} %shard_map.119.refs_1_.refs_0_), channel_id=1, source_target_pairs={{0,6},{1,7},{2,0},{3,1},{4,2},{5,3},{6,4},{7,5},{8,14},{9,15},{10,... | collective-permute-start | bytes 1572872 | tf_op jit(solution)/shard_map/ppermute | solution.py:239
  40.5 3.4 %collective-permute-start.1 = (bf16[2,256,512]{2,1,0:T(8,128)(2,1)}, bf16[2,256,512]{2,1,0:T(8,128)(2,1)S(1)}, u32[]{:S(2)}, u32[]{:S(2)}) collective-permute-start(bf16[2,256,512]{2,1,0:T(8,128)(2,1)} %shard_map.119.refs_1_.refs_0_), channel_id=1, source_target_pairs={{0,8},{8,0},{16,24},{24,16},{32,40},{40,32},{48,56},{56,48},{64,72... | collective-permute-start | bytes 1572872 | tf_op jit(solution)/shard_map/ppermute | solution.py:241
  43.9 2.3 %collective-permute-done.6.refs_7_.refs_3_ = bf16[2,256,512]{2,1,0:T(8,128)(2,1)S(1)} collective-permute-done((bf16[2,256,512]{2,1,0:T(8,128)(2,1)}, bf16[2,256,512]{2,1,0:T(8,128)(2,1)S(1)}, u32[]{:S(2)}, u32[]{:S(2)}) %collective-permute-start.6) | collective-permute-done | bytes 524320 | tf_op jit(solution)/shard_map/ppermute | solution.py:239
  46.2 3.4 %collective-permute-start.7 = (bf16[2,256,512]{2,1,0:T(8,128)(2,1)S(1)}, bf16[2,256,512]{2,1,0:T(8,128)(2,1)S(1)}, u32[]{:S(2)}, u32[]{:S(2)}) collective-permute-start(bf16[2,256,512]{2,1,0:T(8,128)(2,1)S(1)} %collective-permute-done.6.refs_7_.refs_3_), channel_id=1, source_target_pairs={{0,8},{8,0},{16,24},{24,16},{32,40},{40,32},{48,56},{56,48},{64,72... | collective-permute-start | bytes 1572872 | tf_op jit(solution)/shard_map/ppermute | solution.py:241
  49.7 8.8 %collective-permute-done.4.refs_5_.refs_2_ = bf16[2,256,512]{2,1,0:T(8,128)(2,1)S(1)} collective-permute-done((bf16[2,256,512]{2,1,0:T(8,128)(2,1)}, bf16[2,256,512]{2,1,0:T(8,128)(2,1)S(1)}, u32[]{:S(2)}, u32[]{:S(2)}) %collective-permute-start.4) | collective-permute-done | bytes 524320 | tf_op jit(solution)/shard_map/ppermute | solution.py:239
  58.4 3.3 %collective-permute-start.5 = (bf16[2,256,512]{2,1,0:T(8,128)(2,1)S(1)}, bf16[2,256,512]{2,1,0:T(8,128)(2,1)S(1)}, u32[]{:S(2)}, u32[]{:S(2)}) collective-permute-start(bf16[2,256,512]{2,1,0:T(8,128)(2,1)S(1)} %collective-permute-done.4.refs_5_.refs_2_), channel_id=1, source_target_pairs={{0,8},{8,0},{16,24},{24,16},{32,40},{40,32},{48,56},{56,48},{64,72... | collective-permute-start | bytes 1572872 | tf_op jit(solution)/shard_map/ppermute | solution.py:241
  61.8 1.9 %collective-permute-start.3 = (bf16[2,256,512]{2,1,0:T(8,128)(2,1)S(1)}, bf16[2,256,512]{2,1,0:T(8,128)(2,1)}, u32[]{:S(2)}, u32[]{:S(2)}) collective-permute-start(bf16[2,256,512]{2,1,0:T(8,128)(2,1)S(1)} %collective-permute-done.2.refs_3_.refs_1_), channel_id=1, source_target_pairs={{0,8},{8,0},{16,24},{24,16},{32,40},{40,32},{48,56},{56,48},{64,72... | collective-permute-start | bytes 1572872 | tf_op jit(solution)/shard_map/ppermute | solution.py:241
  64.6 1.1 collective-permute-done.3.refs_4_.refs_5_
  65.8 4.3 %shard_map.120 = (bf16[512,384]{1,0:T(8,128)(2,1)}, bf16[2048,384]{1,0:T(8,128)(2,1)}) custom-call(s32[1]{0:T(128)} %bitcast.where_ref, bf16[32,192,128]{2,1,0:T(8,128)(2,1)} %all-to-all-done.refs_0_, bf16[2,256,512]{2,1,0:T(8,128)(2,1)} %shard_map.119.refs_1_.refs_0_, bf16[2,256,512]{2,1,0:T(8,128)(2,1)} %copy-done.7, bf16[2,256,512]{2,1,0:T(8,128)(2,1)} %copy-done.5, ...), custom_call_target="tpu_custom_call" | custom-call | flops 805306368 | bytes 5767168 | tf_op jit(solution)/shard_map/pallas_call | solution.py:99
  70.1 3.1 %collective-permute-start.8 = (bf16[512,384]{1,0:T(8,128)(2,1)}, bf16[512,384]{1,0:T(8,128)(2,1)S(1)}, u32[]{:S(2)}, u32[]{:S(2)}) collective-permute-start(bf16[512,384]{1,0:T(8,128)(2,1)} %get-tuple-element.22.refs_0_), channel_id=1, source_target_pairs={{0,1},{1,0},{2,3},{3,2},{4,5},{5,4},{6,7},{7,6},{8,9},{9,8},{10,11... | collective-permute-start | bytes 1179656 | tf_op jit(solution)/shard_map/ppermute | solution.py:255
  73.2 3.3 %collective-permute-start.9 = (bf16[2048,384]{1,0:T(8,128)(2,1)}, bf16[2048,384]{1,0:T(8,128)(2,1)S(1)}, u32[]{:S(2)}, u32[]{:S(2)}) collective-permute-start(bf16[2048,384]{1,0:T(8,128)(2,1)} %get-tuple-element.23.refs_1_), channel_id=1, source_target_pairs={{0,8},{8,0},{16,24},{24,16},{32,40},{40,32},{48,56},{56,48},{64,72... | collective-permute-start | bytes 4718600 | tf_op jit(solution)/shard_map/ppermute | solution.py:256
  78.6 1.0 copy-done.6
  81.7 2.4 %shard_map.121 = (bf16[2,512,512]{2,1,0:T(8,128)(2,1)S(1)}, bf16[2,512,512]{2,1,0:T(8,128)(2,1)S(1)}, bf16[2,512,512]{2,1,0:T(8,128)(2,1)S(1)}, bf16[2,512,512]{2,1,0:T(8,128)(2,1)S(1)}) custom-call(s32[1]{0:T(128)} %bitcast.where_ref, bf16[2,256,512]{2,1,0:T(8,128)(2,1)S(1)} %copy-done, bf16[2,256,512]{2,1,0:T(8,128)(2,1)S(1)} %copy-done.6, ...), custom_call_target="tpu_custom_call" | custom-call | flops 20000000000 | bytes 4194304 | tf_op jit(solution)/shard_map/pallas_call | solution.py:99
  84.1 1.8 %collective-permute-done.8.refs_1_ = bf16[512,384]{1,0:T(8,128)(2,1)S(1)} collective-permute-done((bf16[512,384]{1,0:T(8,128)(2,1)}, bf16[512,384]{1,0:T(8,128)(2,1)S(1)}, u32[]{:S(2)}, u32[]{:S(2)}) %collective-permute-start.8) | collective-permute-done | bytes 393248 | tf_op jit(solution)/shard_map/ppermute | solution.py:255
  85.9 3.0 %shard_map.122 = (bf16[32,192,128]{2,1,0:T(8,128)(2,1)}, bf16[512,384]{1,0:T(8,128)(2,1)S(1)}, bf16[256,384]{1,0:T(8,128)(2,1)S(1)}) custom-call(s32[1]{0:T(128)} %bitcast.where_ref, bf16[512,384]{1,0:T(8,128)(2,1)S(1)} %copy-done.13, bf16[512,384]{1,0:T(8,128)(2,1)S(1)} %collective-permute-done.8.refs_1_, ...), custom_call_target="tpu_custom_call" | custom-call | flops 805306368 | bytes 4980736 | tf_op jit(solution)/shard_map/pallas_call | solution.py:99
  89.7 18.2 %all-to-all-start.1 = ((bf16[32,192,128]{2,1,0:T(8,128)(2,1)}), bf16[32,192,128]{2,1,0:T(8,128)(2,1)S(1)}, u32[]{:S(2)}, u32[]{:S(2)}) async-start(bf16[32,192,128]{2,1,0:T(8,128)(2,1)} %get-tuple-element.38), calls=%async_computation.1 | async-start | bytes 3145728 | tf_op jit(solution)/shard_map/all_to_all | solution.py:269
  107.9 2.7 %collective-permute-start.10 = (bf16[256,384]{1,0:T(8,128)(2,1)S(1)}, bf16[256,384]{1,0:T(8,128)(2,1)S(1)}, u32[]{:S(2)}, u32[]{:S(2)}) collective-permute-start(bf16[256,384]{1,0:T(8,128)(2,1)S(1)} %get-tuple-element.30), channel_id=1, source_target_pairs={{0,8},{8,0},{16,24},{24,16},{32,40},{40,32},{48,56},{56,48},{64,72... | collective-permute-start | bytes 589832 | tf_op jit(solution)/shard_map/ppermute | solution.py:273
  110.6 1.0 collective-permute-done.10.refs_2_
  112.4 4.3 %shard_map.123 = (bf16[2,256,512]{2,1,0:T(8,128)(2,1)}, bf16[2,256,512]{2,1,0:T(8,128)(2,1)}, bf16[2,256,512]{2,1,0:T(8,128)(2,1)}, bf16[2,256,512]{2,1,0:T(8,128)(2,1)}) custom-call(s32[1]{0:T(128)} %bitcast.where_ref, bf16[512,384]{1,0:T(8,128)(2,1)} %copy-done.14, bf16[2048,384]{1,0:T(8,128)(2,1)} %get-tuple-element.23.refs_1_, ...), custom_call_target="tpu_custom_call" | custom-call | flops 805306368 | bytes 3735552 | tf_op jit(solution)/shard_map/pallas_call | solution.py:99
  116.7 3.2 %collective-permute-start.11 = (bf16[2,256,512]{2,1,0:T(8,128)(2,1)}, bf16[2,256,512]{2,1,0:T(8,128)(2,1)S(1)}, u32[]{:S(2)}, u32[]{:S(2)}) collective-permute-start(bf16[2,256,512]{2,1,0:T(8,128)(2,1)} %get-tuple-element.33), channel_id=1, source_target_pairs={{0,2},{1,3},{2,4},{3,5},{4,6},{5,7},{6,0},{7,1},{8,10},{9,11},{10,... | collective-permute-start | bytes 1572872 | tf_op jit(solution)/shard_map/ppermute | solution.py:281
  119.9 3.4 %collective-permute-start.12 = (bf16[2,256,512]{2,1,0:T(8,128)(2,1)}, bf16[2,256,512]{2,1,0:T(8,128)(2,1)S(1)}, u32[]{:S(2)}, u32[]{:S(2)}) collective-permute-start(bf16[2,256,512]{2,1,0:T(8,128)(2,1)} %get-tuple-element.34), channel_id=1, source_target_pairs={{0,4},{1,5},{2,6},{3,7},{4,0},{5,1},{6,2},{7,3},{8,12},{9,13},{10,... | collective-permute-start | bytes 1572872 | tf_op jit(solution)/shard_map/ppermute | solution.py:281
  123.3 3.2 %collective-permute-start.13 = (bf16[2,256,512]{2,1,0:T(8,128)(2,1)}, bf16[2,256,512]{2,1,0:T(8,128)(2,1)S(1)}, u32[]{:S(2)}, u32[]{:S(2)}) collective-permute-start(bf16[2,256,512]{2,1,0:T(8,128)(2,1)} %get-tuple-element.35), channel_id=1, source_target_pairs={{0,6},{1,7},{2,0},{3,1},{4,2},{5,3},{6,4},{7,5},{8,14},{9,15},{10,... | collective-permute-start | bytes 1572872 | tf_op jit(solution)/shard_map/ppermute | solution.py:281
  126.5 19.3 %all-to-all-done.1 = bf16[32,192,128]{2,1,0:T(8,128)(2,1)S(1)} async-done(((bf16[32,192,128]{2,1,0:T(8,128)(2,1)}), bf16[32,192,128]{2,1,0:T(8,128)(2,1)S(1)}, u32[]{:S(2)}, u32[]{:S(2)}) %all-to-all-start.1) | async-done | bytes 1572896 | tf_op jit(solution)/shard_map/all_to_all | solution.py:269
  146.1 5.8 %collective-permute-start.14 = (bf16[192,128]{1,0:T(8,128)(2,1)S(1)}, bf16[192,128]{1,0:T(8,128)(2,1)S(1)}, u32[]{:S(2)}, u32[]{:S(2)}) collective-permute-start(bf16[192,128]{1,0:T(8,128)(2,1)S(1)} %reduce_sum.12), channel_id=1, source_target_pairs={{0,0},{8,1},{2,2},{10,3},{4,4},{12,5},{6,6},{14,7},{64,8},{72,9},{... | collective-permute-start | bytes 147464 | tf_op jit(solution)/shard_map/ppermute | solution.py:271
  153.1 2.9 %shard_map.124 = (bf16[384,512]{1,0:T(8,128)(2,1)}, bf16[384,512]{1,0:T(8,128)(2,1)}) custom-call(s32[1]{0:T(128)} %bitcast.where_ref, s32[1,256]{1,0:T(1,128)} %bitcast.7, s32[1,1]{1,0:T(1,128)} %bitcast.5.refs_1_, f32[1,256]{1,0:T(1,128)} %bitcast.9, bf16[2,256,512]{2,1,0:T(8,128)(2,1)} %get-tuple-element.32.refs_3_, bf16[2,256,512]{2,1,0:T(8,128)(2,1)} %copy-done.16, ...), custom_call_target="tpu_custom_call" | custom-call | flops 201326592 | bytes 2099204 | tf_op jit(solution)/shard_map/pallas_call | solution.py:99
  (52 shorter events, 9.2 us)
Async XLA Ops:
  1.4 13.8 %collective-permute-start = (bf16[192,128]{1,0:T(8,128)(2,1)S(1)}, bf16[192,128]{1,0:T(8,128)(2,1)S(1)}, u32[]{:S(2)}, u32[]{:S(2)}) collective-permute-start(bf16[192,128]{1,0:T(8,128)(2,1)S(1)} %pad_maximum_fusion), channel_id=1, source_target_pairs={{0,0},{1,8},{2,2},{3,10},{4,4},{5,12},{6,6},{7,14},{8,64},{9,72},{... | collective-permute-start | bytes 147464 | tf_op jit(solution)/shard_map/ppermute | solution.py:229
  16.8 49.0 %all-to-all-start = ((bf16[32,192,128]{2,1,0:T(8,128)(2,1)}), bf16[32,192,128]{2,1,0:T(8,128)(2,1)}, u32[]{:S(2)}, u32[]{:S(2)}) async-start(bf16[32,192,128]{2,1,0:T(8,128)(2,1)} %broadcast_in_dim.22), calls=%async_computation | async-start | bytes 3145728 | tf_op jit(solution)/shard_map/all_to_all | solution.py:231
  29.8 46.6 %copy-start = (bf16[2,256,512]{2,1,0:T(8,128)(2,1)S(1)}, bf16[2,256,512]{2,1,0:T(8,128)(2,1)}, u32[]{:S(2)}) copy-start(bf16[2,256,512]{2,1,0:T(8,128)(2,1)} %shard_map.119.refs_1_.refs_0_) | copy-start | bytes 1572868
  29.8 16.4 %collective-permute-start.6 = (bf16[2,256,512]{2,1,0:T(8,128)(2,1)}, bf16[2,256,512]{2,1,0:T(8,128)(2,1)S(1)}, u32[]{:S(2)}, u32[]{:S(2)}) collective-permute-start(bf16[2,256,512]{2,1,0:T(8,128)(2,1)} %shard_map.119.refs_1_.refs_0_), channel_id=1, source_target_pairs={{0,2},{1,3},{2,4},{3,5},{4,6},{5,7},{6,0},{7,1},{8,10},{9,11},{10,... | collective-permute-start | bytes 1572872 | tf_op jit(solution)/shard_map/ppermute | solution.py:239
  33.1 25.3 %collective-permute-start.4 = (bf16[2,256,512]{2,1,0:T(8,128)(2,1)}, bf16[2,256,512]{2,1,0:T(8,128)(2,1)S(1)}, u32[]{:S(2)}, u32[]{:S(2)}) collective-permute-start(bf16[2,256,512]{2,1,0:T(8,128)(2,1)} %shard_map.119.refs_1_.refs_0_), channel_id=1, source_target_pairs={{0,4},{1,5},{2,6},{3,7},{4,0},{5,1},{6,2},{7,3},{8,12},{9,13},{10,... | collective-permute-start | bytes 1572872 | tf_op jit(solution)/shard_map/ppermute | solution.py:239
  37.5 24.3 %collective-permute-start.2 = (bf16[2,256,512]{2,1,0:T(8,128)(2,1)}, bf16[2,256,512]{2,1,0:T(8,128)(2,1)S(1)}, u32[]{:S(2)}, u32[]{:S(2)}) collective-permute-start(bf16[2,256,512]{2,1,0:T(8,128)(2,1)} %shard_map.119.refs_1_.refs_0_), channel_id=1, source_target_pairs={{0,6},{1,7},{2,0},{3,1},{4,2},{5,3},{6,4},{7,5},{8,14},{9,15},{10,... | collective-permute-start | bytes 1572872 | tf_op jit(solution)/shard_map/ppermute | solution.py:239
  40.5 23.2 %collective-permute-start.1 = (bf16[2,256,512]{2,1,0:T(8,128)(2,1)}, bf16[2,256,512]{2,1,0:T(8,128)(2,1)S(1)}, u32[]{:S(2)}, u32[]{:S(2)}) collective-permute-start(bf16[2,256,512]{2,1,0:T(8,128)(2,1)} %shard_map.119.refs_1_.refs_0_), channel_id=1, source_target_pairs={{0,8},{8,0},{16,24},{24,16},{32,40},{40,32},{48,56},{56,48},{64,72... | collective-permute-start | bytes 1572872 | tf_op jit(solution)/shard_map/ppermute | solution.py:241
  46.2 19.5 %copy-start.1 = (bf16[2,256,512]{2,1,0:T(8,128)(2,1)}, bf16[2,256,512]{2,1,0:T(8,128)(2,1)S(1)}, u32[]{:S(2)}) copy-start(bf16[2,256,512]{2,1,0:T(8,128)(2,1)S(1)} %collective-permute-done.6.refs_7_.refs_3_) | copy-start | bytes 1572868
  46.2 17.5 %collective-permute-start.7 = (bf16[2,256,512]{2,1,0:T(8,128)(2,1)S(1)}, bf16[2,256,512]{2,1,0:T(8,128)(2,1)S(1)}, u32[]{:S(2)}, u32[]{:S(2)}) collective-permute-start(bf16[2,256,512]{2,1,0:T(8,128)(2,1)S(1)} %collective-permute-done.6.refs_7_.refs_3_), channel_id=1, source_target_pairs={{0,8},{8,0},{16,24},{24,16},{32,40},{40,32},{48,56},{56,48},{64,72... | collective-permute-start | bytes 1572872 | tf_op jit(solution)/shard_map/ppermute | solution.py:241
  58.4 7.3 %copy-start.3 = (bf16[2,256,512]{2,1,0:T(8,128)(2,1)}, bf16[2,256,512]{2,1,0:T(8,128)(2,1)S(1)}, u32[]{:S(2)}) copy-start(bf16[2,256,512]{2,1,0:T(8,128)(2,1)S(1)} %collective-permute-done.4.refs_5_.refs_2_) | copy-start | bytes 1572868
  58.4 5.3 %collective-permute-start.5 = (bf16[2,256,512]{2,1,0:T(8,128)(2,1)S(1)}, bf16[2,256,512]{2,1,0:T(8,128)(2,1)S(1)}, u32[]{:S(2)}, u32[]{:S(2)}) collective-permute-start(bf16[2,256,512]{2,1,0:T(8,128)(2,1)S(1)} %collective-permute-done.4.refs_5_.refs_2_), channel_id=1, source_target_pairs={{0,8},{8,0},{16,24},{24,16},{32,40},{40,32},{48,56},{56,48},{64,72... | collective-permute-start | bytes 1572872 | tf_op jit(solution)/shard_map/ppermute | solution.py:241
  61.8 4.0 %copy-start.5 = (bf16[2,256,512]{2,1,0:T(8,128)(2,1)}, bf16[2,256,512]{2,1,0:T(8,128)(2,1)S(1)}, u32[]{:S(2)}) copy-start(bf16[2,256,512]{2,1,0:T(8,128)(2,1)S(1)} %collective-permute-done.2.refs_3_.refs_1_) | copy-start | bytes 1572868
  61.8 3.9 %collective-permute-start.3 = (bf16[2,256,512]{2,1,0:T(8,128)(2,1)S(1)}, bf16[2,256,512]{2,1,0:T(8,128)(2,1)}, u32[]{:S(2)}, u32[]{:S(2)}) collective-permute-start(bf16[2,256,512]{2,1,0:T(8,128)(2,1)S(1)} %collective-permute-done.2.refs_3_.refs_1_), channel_id=1, source_target_pairs={{0,8},{8,0},{16,24},{24,16},{32,40},{40,32},{48,56},{56,48},{64,72... | collective-permute-start | bytes 1572872 | tf_op jit(solution)/shard_map/ppermute | solution.py:241
  63.7 2.0 %copy-start.7 = (bf16[2,256,512]{2,1,0:T(8,128)(2,1)}, bf16[2,256,512]{2,1,0:T(8,128)(2,1)S(1)}, u32[]{:S(2)}) copy-start(bf16[2,256,512]{2,1,0:T(8,128)(2,1)S(1)} %collective-permute-done.1.refs_2_.refs_4_) | copy-start | bytes 1572868
  63.7 2.0 %copy-start.9 = (bf16[2,256,512]{2,1,0:T(8,128)(2,1)}, bf16[2,256,512]{2,1,0:T(8,128)(2,1)S(1)}, u32[]{:S(2)}) copy-start(bf16[2,256,512]{2,1,0:T(8,128)(2,1)S(1)} %collective-permute-done.7.refs_8_.refs_7_) | copy-start | bytes 1572868
  65.8 10.7 %copy-start.12 = (bf16[2,256,512]{2,1,0:T(8,128)(2,1)S(1)}, bf16[2,256,512]{2,1,0:T(8,128)(2,1)}, u32[]{:S(2)}) copy-start(bf16[2,256,512]{2,1,0:T(8,128)(2,1)} %copy-done.11) | copy-start | bytes 1572868
  70.1 15.8 %collective-permute-start.8 = (bf16[512,384]{1,0:T(8,128)(2,1)}, bf16[512,384]{1,0:T(8,128)(2,1)S(1)}, u32[]{:S(2)}, u32[]{:S(2)}) collective-permute-start(bf16[512,384]{1,0:T(8,128)(2,1)} %get-tuple-element.22.refs_0_), channel_id=1, source_target_pairs={{0,1},{1,0},{2,3},{3,2},{4,5},{5,4},{6,7},{7,6},{8,9},{9,8},{10,11... | collective-permute-start | bytes 1179656 | tf_op jit(solution)/shard_map/ppermute | solution.py:255
  73.2 12.8 %collective-permute-start.9 = (bf16[2048,384]{1,0:T(8,128)(2,1)}, bf16[2048,384]{1,0:T(8,128)(2,1)S(1)}, u32[]{:S(2)}, u32[]{:S(2)}) collective-permute-start(bf16[2048,384]{1,0:T(8,128)(2,1)} %get-tuple-element.23.refs_1_), channel_id=1, source_target_pairs={{0,8},{8,0},{16,24},{24,16},{32,40},{40,32},{48,56},{56,48},{64,72... | collective-permute-start | bytes 4718600 | tf_op jit(solution)/shard_map/ppermute | solution.py:256
  76.5 1.0 copy-start.2
  77.5 1.0 copy-start.4
  78.6 1.0 copy-start.6
  79.6 1.0 copy-start.8
  80.6 1.0 copy-start.10
  81.7 4.2 %copy-start.13 = (bf16[512,384]{1,0:T(8,128)(2,1)S(1)}, bf16[512,384]{1,0:T(8,128)(2,1)}, u32[]{:S(2)}) copy-start(bf16[512,384]{1,0:T(8,128)(2,1)} %get-tuple-element.22.refs_0_) | copy-start | bytes 1179652
  85.9 3.0 %copy-start.15 = (bf16[2048,384]{1,0:T(8,128)(2,1)}, bf16[2048,384]{1,0:T(8,128)(2,1)S(1)}, u32[]{:S(2)}) copy-start(bf16[2048,384]{1,0:T(8,128)(2,1)S(1)} %collective-permute-done.9.refs_3_) | copy-start | bytes 4718596
  89.7 56.2 %all-to-all-start.1 = ((bf16[32,192,128]{2,1,0:T(8,128)(2,1)}), bf16[32,192,128]{2,1,0:T(8,128)(2,1)S(1)}, u32[]{:S(2)}, u32[]{:S(2)}) async-start(bf16[32,192,128]{2,1,0:T(8,128)(2,1)} %get-tuple-element.38), calls=%async_computation.1 | async-start | bytes 3145728 | tf_op jit(solution)/shard_map/all_to_all | solution.py:269
  107.9 3.8 %collective-permute-start.10 = (bf16[256,384]{1,0:T(8,128)(2,1)S(1)}, bf16[256,384]{1,0:T(8,128)(2,1)S(1)}, u32[]{:S(2)}, u32[]{:S(2)}) collective-permute-start(bf16[256,384]{1,0:T(8,128)(2,1)S(1)} %get-tuple-element.30), channel_id=1, source_target_pairs={{0,8},{8,0},{16,24},{24,16},{32,40},{40,32},{48,56},{56,48},{64,72... | collective-permute-start | bytes 589832 | tf_op jit(solution)/shard_map/ppermute | solution.py:273
  116.7 35.2 %collective-permute-start.11 = (bf16[2,256,512]{2,1,0:T(8,128)(2,1)}, bf16[2,256,512]{2,1,0:T(8,128)(2,1)S(1)}, u32[]{:S(2)}, u32[]{:S(2)}) collective-permute-start(bf16[2,256,512]{2,1,0:T(8,128)(2,1)} %get-tuple-element.33), channel_id=1, source_target_pairs={{0,2},{1,3},{2,4},{3,5},{4,6},{5,7},{6,0},{7,1},{8,10},{9,11},{10,... | collective-permute-start | bytes 1572872 | tf_op jit(solution)/shard_map/ppermute | solution.py:281
  119.9 32.0 %collective-permute-start.12 = (bf16[2,256,512]{2,1,0:T(8,128)(2,1)}, bf16[2,256,512]{2,1,0:T(8,128)(2,1)S(1)}, u32[]{:S(2)}, u32[]{:S(2)}) collective-permute-start(bf16[2,256,512]{2,1,0:T(8,128)(2,1)} %get-tuple-element.34), channel_id=1, source_target_pairs={{0,4},{1,5},{2,6},{3,7},{4,0},{5,1},{6,2},{7,3},{8,12},{9,13},{10,... | collective-permute-start | bytes 1572872 | tf_op jit(solution)/shard_map/ppermute | solution.py:281
  123.3 28.6 %collective-permute-start.13 = (bf16[2,256,512]{2,1,0:T(8,128)(2,1)}, bf16[2,256,512]{2,1,0:T(8,128)(2,1)S(1)}, u32[]{:S(2)}, u32[]{:S(2)}) collective-permute-start(bf16[2,256,512]{2,1,0:T(8,128)(2,1)} %get-tuple-element.35), channel_id=1, source_target_pairs={{0,6},{1,7},{2,0},{3,1},{4,2},{5,3},{6,4},{7,5},{8,14},{9,15},{10,... | collective-permute-start | bytes 1572872 | tf_op jit(solution)/shard_map/ppermute | solution.py:281
  146.1 9.9 %collective-permute-start.14 = (bf16[192,128]{1,0:T(8,128)(2,1)S(1)}, bf16[192,128]{1,0:T(8,128)(2,1)S(1)}, u32[]{:S(2)}, u32[]{:S(2)}) collective-permute-start(bf16[192,128]{1,0:T(8,128)(2,1)S(1)} %reduce_sum.12), channel_id=1, source_target_pairs={{0,0},{8,1},{2,2},{10,3},{4,4},{12,5},{6,6},{14,7},{64,8},{72,9},{... | collective-permute-start | bytes 147464 | tf_op jit(solution)/shard_map/ppermute | solution.py:271
  151.9 1.1 copy-start.18
  (5 other events, 4.0 us)

commit v11 on v10

--- a/solution.py
+++ b/solution.py
@@ -227,8 +227,6 @@
 
     block = jnp.concatenate((w_gate, w_up, w_down), axis=0)
     block = lax.ppermute(block, ("wide", "narrow"), SWAP)
-    pieces = jnp.broadcast_to(block[None], (len(OWNERS[0]),) + block.shape)
-    pieces = lax.all_to_all(pieces, "wide", 0, 0, axis_index_groups=OWNERS)
     (own,) = call(
         rows_body,
         [((2, slots, feat), BF16)],
@@ -236,6 +234,9 @@
         where,
         *(tokens, grad_out, token, count, gate),
     )
+    block, own = lax.optimization_barrier((block, own))
+    pieces = jnp.broadcast_to(block[None], (len(OWNERS[0]),) + block.shape)
+    pieces = lax.all_to_all(pieces, "wide", 0, 0, axis_index_groups=OWNERS)
     near = {step: lax.ppermute(own, "narrow", shift_x(-step)) for step in (1, 3, 2)}
     near = [own] + [near[step] for step in range(1, N_X)]
     core = [lax.ppermute(held, "wide", OTHER_CORE) for held in near]

time: 158 us -> 157 us (level); the launches traced: 157 us -> 154 us
  waiting for transfers between devices: 43.6 us -> 35.4 us
  starting transfers between devices: 80.2 us -> 84.8 us
    ppermute x3, waiting for transfers between devices: 11.1 us -> 7.43 us  [local(): lax.ppermute(own, 'narrow', shift_x(-step))]
    ppermute x4, starting transfers between devices: 12.1 us -> 15.5 us  [local(): core = [lax.ppermute(held, 'wide', OTHER_CORE) for held in near]]
    ppermute x1, waiting for transfers between devices: 9.25 us -> 6.16 us  [local(): block = lax.ppermute(block, ('wide', 'narrow'), SWAP)]
    ppermute x1, starting transfers between devices: 3.27 us -> 6.11 us  [local(): core_weights = lax.ppermute(weights, 'wide', OTHER_CORE)]
    ppermute x1, waiting for transfers between devices: 1.84 us -> 0.01 us  [local(): theirs = lax.ppermute(sent, 'narrow', OTHER_HALF)]
    unnamed x40 -> x42, local copies, waits for them, and re-layouts: 8.63 us -> 9.47 us
where the time goes in v11:
time: 157 us; the launch traced here: 154 us
  starting transfers between devices  84.8 us (54%)
  waiting for transfers between devices  35.4 us (23%)
  Pallas kernels  19.3 us (12%)
  local copies, waits for them, and re-layouts  11.6 us (7%)
  between operations  1.7 us (1%)
    all_to_all x1, waiting for transfers between devices, local(): terms = lax.all_to_all(terms, 'wide', 0, 0, axis_index_groups=OWNERS)  19.4 us
    pallas_call x6, Pallas kernels, call(): pl.pallas_call(inner, out_shape=shapes, in_specs=[pl.BlockSpec(memory_spa...  19.3 us
    all_to_all x1, starting transfers between devices, local(): terms = lax.all_to_all(terms, 'wide', 0, 0, axis_index_groups=OWNERS)  18.3 us
    ppermute x4, starting transfers between devices, local(): core = [lax.ppermute(held, 'wide', OTHER_CORE) for held in near]  15.5 us
    all_to_all x1, starting transfers between devices, local(): pieces = lax.all_to_all(pieces, 'wide', 0, 0, axis_index_groups=OWNERS)  10.7 us
    ppermute x3, starting transfers between devices, local(): lax.ppermute(own, 'narrow', shift_x(-step))  10.7 us
    ppermute x3, starting transfers between devices, local(): lax.ppermute(outs[step], 'narrow', shift_x(step))  9.78 us
    unnamed x42, local copies, waits for them, and re-layouts  9.47 us
  transfers between devices with their start and end apart: 17, of which 7 were waited for; matrix products, arithmetic and copies ran while one was open for 0% of the time, Pallas kernels for 8%

profile of v11, /device:TPU:1, one launch (start us, length us, event | category | flops | bytes accessed | tf_op | source)
XLA Modules:
  0.0 153.9 jit_solution(7824131467014143843)
XLA Ops:
  1.4 4.6 %collective-permute-start = (bf16[192,128]{1,0:T(8,128)(2,1)S(1)}, bf16[192,128]{1,0:T(8,128)(2,1)S(1)}, u32[]{:S(2)}, u32[]{:S(2)}) collective-permute-start(bf16[192,128]{1,0:T(8,128)(2,1)S(1)} %pad_maximum_fusion), channel_id=1, source_target_pairs={{0,0},{1,8},{2,2},{3,10},{4,4},{5,12},{6,6},{7,14},{8,64},{9,72},{... | collective-permute-start | bytes 147464 | tf_op jit(solution)/shard_map/ppermute | solution.py:229
  6.6 2.4 %shard_map.119.refs_1_.refs_0_ = bf16[2,256,512]{2,1,0:T(8,128)(2,1)} custom-call(s32[1]{0:T(128)} %bitcast.where_ref, bf16[384,512]{1,0:T(8,128)(2,1)} %refs_0_.1, bf16[384,512]{1,0:T(8,128)(2,1)} %refs_1_.1, s32[1,256]{1,0:T(1,128)} %bitcast.6, s32[1,1]{1,0:T(1,128)} %bitcast.4.refs_3_, f32[1,256]{1,0:T(1,128)} %bitcast.8), custom_call_target="tpu_custom_call" | custom-call | flops 201326592 | bytes 788484 | tf_op jit(solution)/shard_map/pallas_call | solution.py:99
  9.1 6.2 %collective-permute-done = bf16[192,128]{1,0:T(8,128)(2,1)S(1)} collective-permute-done((bf16[192,128]{1,0:T(8,128)(2,1)S(1)}, bf16[192,128]{1,0:T(8,128)(2,1)S(1)}, u32[]{:S(2)}, u32[]{:S(2)}) %collective-permute-start) | collective-permute-done | bytes 49184 | tf_op jit(solution)/shard_map/ppermute | solution.py:229
  15.2 1.5 broadcast_in_dim.22
  16.8 10.7 %all-to-all-start = ((bf16[32,192,128]{2,1,0:T(8,128)(2,1)}), bf16[32,192,128]{2,1,0:T(8,128)(2,1)}, u32[]{:S(2)}, u32[]{:S(2)}) async-start(bf16[32,192,128]{2,1,0:T(8,128)(2,1)} %broadcast_in_dim.22), calls=%async_computation | async-start | bytes 3145728 | tf_op jit(solution)/shard_map/all_to_all | solution.py:239
  27.5 3.3 %collective-permute-start.6 = (bf16[2,256,512]{2,1,0:T(8,128)(2,1)S(1)}, bf16[2,256,512]{2,1,0:T(8,128)(2,1)S(1)}, u32[]{:S(2)}, u32[]{:S(2)}) collective-permute-start(bf16[2,256,512]{2,1,0:T(8,128)(2,1)S(1)} %copy-done), channel_id=1, source_target_pairs={{0,2},{1,3},{2,4},{3,5},{4,6},{5,7},{6,0},{7,1},{8,10},{9,11},{10,... | collective-permute-start | bytes 1572872 | tf_op jit(solution)/shard_map/ppermute | solution.py:240
  30.7 4.4 %collective-permute-start.4 = (bf16[2,256,512]{2,1,0:T(8,128)(2,1)S(1)}, bf16[2,256,512]{2,1,0:T(8,128)(2,1)S(1)}, u32[]{:S(2)}, u32[]{:S(2)}) collective-permute-start(bf16[2,256,512]{2,1,0:T(8,128)(2,1)S(1)} %copy-done), channel_id=1, source_target_pairs={{0,4},{1,5},{2,6},{3,7},{4,0},{5,1},{6,2},{7,3},{8,12},{9,13},{10,... | collective-permute-start | bytes 1572872 | tf_op jit(solution)/shard_map/ppermute | solution.py:240
  35.1 3.1 %collective-permute-start.2 = (bf16[2,256,512]{2,1,0:T(8,128)(2,1)S(1)}, bf16[2,256,512]{2,1,0:T(8,128)(2,1)S(1)}, u32[]{:S(2)}, u32[]{:S(2)}) collective-permute-start(bf16[2,256,512]{2,1,0:T(8,128)(2,1)S(1)} %copy-done), channel_id=1, source_target_pairs={{0,6},{1,7},{2,0},{3,1},{4,2},{5,3},{6,4},{7,5},{8,14},{9,15},{10,... | collective-permute-start | bytes 1572872 | tf_op jit(solution)/shard_map/ppermute | solution.py:240
  38.2 4.2 %collective-permute-start.1 = (bf16[2,256,512]{2,1,0:T(8,128)(2,1)S(1)}, bf16[2,256,512]{2,1,0:T(8,128)(2,1)S(1)}, u32[]{:S(2)}, u32[]{:S(2)}) collective-permute-start(bf16[2,256,512]{2,1,0:T(8,128)(2,1)S(1)} %copy-done), channel_id=1, source_target_pairs={{0,8},{8,0},{16,24},{24,16},{32,40},{40,32},{48,56},{56,48},{64,72... | collective-permute-start | bytes 1572872 | tf_op jit(solution)/shard_map/ppermute | solution.py:242
  42.8 5.2 %collective-permute-start.7 = (bf16[2,256,512]{2,1,0:T(8,128)(2,1)S(1)}, bf16[2,256,512]{2,1,0:T(8,128)(2,1)S(1)}, u32[]{:S(2)}, u32[]{:S(2)}) collective-permute-start(bf16[2,256,512]{2,1,0:T(8,128)(2,1)S(1)} %collective-permute-done.6.refs_7_.refs_3_), channel_id=1, source_target_pairs={{0,8},{8,0},{16,24},{24,16},{32,40},{40,32},{48,56},{56,48},{64,72... | collective-permute-start | bytes 1572872 | tf_op jit(solution)/shard_map/ppermute | solution.py:242
  47.9 7.0 %collective-permute-done.4.refs_5_.refs_2_ = bf16[2,256,512]{2,1,0:T(8,128)(2,1)S(1)} collective-permute-done((bf16[2,256,512]{2,1,0:T(8,128)(2,1)S(1)}, bf16[2,256,512]{2,1,0:T(8,128)(2,1)S(1)}, u32[]{:S(2)}, u32[]{:S(2)}) %collective-permute-start.4) | collective-permute-done | bytes 524320 | tf_op jit(solution)/shard_map/ppermute | solution.py:240
  55.0 4.2 %collective-permute-start.5 = (bf16[2,256,512]{2,1,0:T(8,128)(2,1)S(1)}, bf16[2,256,512]{2,1,0:T(8,128)(2,1)S(1)}, u32[]{:S(2)}, u32[]{:S(2)}) collective-permute-start(bf16[2,256,512]{2,1,0:T(8,128)(2,1)S(1)} %collective-permute-done.4.refs_5_.refs_2_), channel_id=1, source_target_pairs={{0,8},{8,0},{16,24},{24,16},{32,40},{40,32},{48,56},{56,48},{64,72... | collective-permute-start | bytes 1572872 | tf_op jit(solution)/shard_map/ppermute | solution.py:242
  59.2 1.9 %collective-permute-start.3 = (bf16[2,256,512]{2,1,0:T(8,128)(2,1)S(1)}, bf16[2,256,512]{2,1,0:T(8,128)(2,1)}, u32[]{:S(2)}, u32[]{:S(2)}) collective-permute-start(bf16[2,256,512]{2,1,0:T(8,128)(2,1)S(1)} %collective-permute-done.2.refs_3_.refs_1_), channel_id=1, source_target_pairs={{0,8},{8,0},{16,24},{24,16},{32,40},{40,32},{48,56},{56,48},{64,72... | collective-permute-start | bytes 1572872 | tf_op jit(solution)/shard_map/ppermute | solution.py:242
  63.1 1.1 all-to-all-done.refs_0_
  64.2 4.3 %shard_map.120 = (bf16[512,384]{1,0:T(8,128)(2,1)}, bf16[2048,384]{1,0:T(8,128)(2,1)}) custom-call(s32[1]{0:T(128)} %bitcast.where_ref, bf16[32,192,128]{2,1,0:T(8,128)(2,1)} %all-to-all-done.refs_0_, bf16[2,256,512]{2,1,0:T(8,128)(2,1)} %shard_map.119.refs_1_.refs_0_, bf16[2,256,512]{2,1,0:T(8,128)(2,1)} %copy-done.8, bf16[2,256,512]{2,1,0:T(8,128)(2,1)} %copy-done.6, ...), custom_call_target="tpu_custom_call" | custom-call | flops 805306368 | bytes 5767168 | tf_op jit(solution)/shard_map/pallas_call | solution.py:99
  68.5 1.9 %collective-permute-start.8 = (bf16[512,384]{1,0:T(8,128)(2,1)}, bf16[512,384]{1,0:T(8,128)(2,1)S(1)}, u32[]{:S(2)}, u32[]{:S(2)}) collective-permute-start(bf16[512,384]{1,0:T(8,128)(2,1)} %get-tuple-element.26.refs_0_), channel_id=1, source_target_pairs={{0,1},{1,0},{2,3},{3,2},{4,5},{5,4},{6,7},{7,6},{8,9},{9,8},{10,11... | collective-permute-start | bytes 1179656 | tf_op jit(solution)/shard_map/ppermute | solution.py:256
  70.5 6.1 %collective-permute-start.9 = (bf16[2048,384]{1,0:T(8,128)(2,1)}, bf16[2048,384]{1,0:T(8,128)(2,1)S(1)}, u32[]{:S(2)}, u32[]{:S(2)}) collective-permute-start(bf16[2048,384]{1,0:T(8,128)(2,1)} %get-tuple-element.27.refs_1_), channel_id=1, source_target_pairs={{0,8},{8,0},{16,24},{24,16},{32,40},{40,32},{48,56},{56,48},{64,72... | collective-permute-start | bytes 4718600 | tf_op jit(solution)/shard_map/ppermute | solution.py:257
  77.6 1.0 copy-done.5
  79.7 1.0 copy-done.9
  80.8 2.4 %shard_map.121 = (bf16[2,512,512]{2,1,0:T(8,128)(2,1)S(1)}, bf16[2,512,512]{2,1,0:T(8,128)(2,1)S(1)}, bf16[2,512,512]{2,1,0:T(8,128)(2,1)S(1)}, bf16[2,512,512]{2,1,0:T(8,128)(2,1)S(1)}) custom-call(s32[1]{0:T(128)} %bitcast.where_ref, bf16[2,256,512]{2,1,0:T(8,128)(2,1)S(1)} %copy-done.1, bf16[2,256,512]{2,1,0:T(8,128)(2,1)S(1)} %copy-done.7, ...), custom_call_target="tpu_custom_call" | custom-call | flops 20000000000 | bytes 4194304 | tf_op jit(solution)/shard_map/pallas_call | solution.py:99
  83.2 1.1 copy-done.16
  84.3 3.0 %shard_map.122 = (bf16[32,192,128]{2,1,0:T(8,128)(2,1)}, bf16[512,384]{1,0:T(8,128)(2,1)S(1)}, bf16[256,384]{1,0:T(8,128)(2,1)S(1)}) custom-call(s32[1]{0:T(128)} %bitcast.where_ref, bf16[512,384]{1,0:T(8,128)(2,1)S(1)} %copy-done.14, bf16[512,384]{1,0:T(8,128)(2,1)S(1)} %collective-permute-done.8.refs_1_, ...), custom_call_target="tpu_custom_call" | custom-call | flops 805306368 | bytes 4980736 | tf_op jit(solution)/shard_map/pallas_call | solution.py:99
  88.1 18.3 %all-to-all-start.1 = ((bf16[32,192,128]{2,1,0:T(8,128)(2,1)}), bf16[32,192,128]{2,1,0:T(8,128)(2,1)S(1)}, u32[]{:S(2)}, u32[]{:S(2)}) async-start(bf16[32,192,128]{2,1,0:T(8,128)(2,1)} %get-tuple-element.42), calls=%async_computation.1 | async-start | bytes 3145728 | tf_op jit(solution)/shard_map/all_to_all | solution.py:270
  106.4 2.7 %collective-permute-start.10 = (bf16[256,384]{1,0:T(8,128)(2,1)S(1)}, bf16[256,384]{1,0:T(8,128)(2,1)S(1)}, u32[]{:S(2)}, u32[]{:S(2)}) collective-permute-start(bf16[256,384]{1,0:T(8,128)(2,1)S(1)} %get-tuple-element.34), channel_id=1, source_target_pairs={{0,8},{8,0},{16,24},{24,16},{32,40},{40,32},{48,56},{56,48},{64,72... | collective-permute-start | bytes 589832 | tf_op jit(solution)/shard_map/ppermute | solution.py:274
  109.1 1.0 collective-permute-done.10.refs_2_
  110.8 4.3 %shard_map.123 = (bf16[2,256,512]{2,1,0:T(8,128)(2,1)}, bf16[2,256,512]{2,1,0:T(8,128)(2,1)}, bf16[2,256,512]{2,1,0:T(8,128)(2,1)}, bf16[2,256,512]{2,1,0:T(8,128)(2,1)}) custom-call(s32[1]{0:T(128)} %bitcast.where_ref, bf16[512,384]{1,0:T(8,128)(2,1)} %copy-done.15, bf16[2048,384]{1,0:T(8,128)(2,1)} %get-tuple-element.27.refs_1_, ...), custom_call_target="tpu_custom_call" | custom-call | flops 805306368 | bytes 3735552 | tf_op jit(solution)/shard_map/pallas_call | solution.py:99
  115.2 3.2 %collective-permute-start.11 = (bf16[2,256,512]{2,1,0:T(8,128)(2,1)}, bf16[2,256,512]{2,1,0:T(8,128)(2,1)S(1)}, u32[]{:S(2)}, u32[]{:S(2)}) collective-permute-start(bf16[2,256,512]{2,1,0:T(8,128)(2,1)} %get-tuple-element.37), channel_id=1, source_target_pairs={{0,2},{1,3},{2,4},{3,5},{4,6},{5,7},{6,0},{7,1},{8,10},{9,11},{10,... | collective-permute-start | bytes 1572872 | tf_op jit(solution)/shard_map/ppermute | solution.py:282
  118.4 3.3 %collective-permute-start.12 = (bf16[2,256,512]{2,1,0:T(8,128)(2,1)}, bf16[2,256,512]{2,1,0:T(8,128)(2,1)S(1)}, u32[]{:S(2)}, u32[]{:S(2)}) collective-permute-start(bf16[2,256,512]{2,1,0:T(8,128)(2,1)} %get-tuple-element.38), channel_id=1, source_target_pairs={{0,4},{1,5},{2,6},{3,7},{4,0},{5,1},{6,2},{7,3},{8,12},{9,13},{10,... | collective-permute-start | bytes 1572872 | tf_op jit(solution)/shard_map/ppermute | solution.py:282
  121.8 3.2 %collective-permute-start.13 = (bf16[2,256,512]{2,1,0:T(8,128)(2,1)}, bf16[2,256,512]{2,1,0:T(8,128)(2,1)S(1)}, u32[]{:S(2)}, u32[]{:S(2)}) collective-permute-start(bf16[2,256,512]{2,1,0:T(8,128)(2,1)} %get-tuple-element.39), channel_id=1, source_target_pairs={{0,6},{1,7},{2,0},{3,1},{4,2},{5,3},{6,4},{7,5},{8,14},{9,15},{10,... | collective-permute-start | bytes 1572872 | tf_op jit(solution)/shard_map/ppermute | solution.py:282
  125.0 19.4 %all-to-all-done.1 = bf16[32,192,128]{2,1,0:T(8,128)(2,1)S(1)} async-done(((bf16[32,192,128]{2,1,0:T(8,128)(2,1)}), bf16[32,192,128]{2,1,0:T(8,128)(2,1)S(1)}, u32[]{:S(2)}, u32[]{:S(2)}) %all-to-all-start.1) | async-done | bytes 1572896 | tf_op jit(solution)/shard_map/all_to_all | solution.py:270
  144.6 4.6 %collective-permute-start.14 = (bf16[192,128]{1,0:T(8,128)(2,1)S(1)}, bf16[192,128]{1,0:T(8,128)(2,1)S(1)}, u32[]{:S(2)}, u32[]{:S(2)}) collective-permute-start(bf16[192,128]{1,0:T(8,128)(2,1)S(1)} %reduce_sum.12), channel_id=1, source_target_pairs={{0,0},{8,1},{2,2},{10,3},{4,4},{12,5},{6,6},{14,7},{64,8},{72,9},{... | collective-permute-start | bytes 147464 | tf_op jit(solution)/shard_map/ppermute | solution.py:272
  150.3 2.9 %shard_map.124 = (bf16[384,512]{1,0:T(8,128)(2,1)}, bf16[384,512]{1,0:T(8,128)(2,1)}) custom-call(s32[1]{0:T(128)} %bitcast.where_ref, s32[1,256]{1,0:T(1,128)} %bitcast.7, s32[1,1]{1,0:T(1,128)} %bitcast.5.refs_1_, f32[1,256]{1,0:T(1,128)} %bitcast.9, bf16[2,256,512]{2,1,0:T(8,128)(2,1)} %get-tuple-element.36.refs_3_, bf16[2,256,512]{2,1,0:T(8,128)(2,1)} %copy-done.17, ...), custom_call_target="tpu_custom_call" | custom-call | flops 201326592 | bytes 2099204 | tf_op jit(solution)/shard_map/pallas_call | solution.py:99
  (54 shorter events, 8.6 us)
Async XLA Ops:
  1.4 13.8 %collective-permute-start = (bf16[192,128]{1,0:T(8,128)(2,1)S(1)}, bf16[192,128]{1,0:T(8,128)(2,1)S(1)}, u32[]{:S(2)}, u32[]{:S(2)}) collective-permute-start(bf16[192,128]{1,0:T(8,128)(2,1)S(1)} %pad_maximum_fusion), channel_id=1, source_target_pairs={{0,0},{1,8},{2,2},{3,10},{4,4},{5,12},{6,6},{7,14},{8,64},{9,72},{... | collective-permute-start | bytes 147464 | tf_op jit(solution)/shard_map/ppermute | solution.py:229
  16.8 10.7 %copy-start = (bf16[2,256,512]{2,1,0:T(8,128)(2,1)S(1)}, bf16[2,256,512]{2,1,0:T(8,128)(2,1)}, u32[]{:S(2)}) copy-start(bf16[2,256,512]{2,1,0:T(8,128)(2,1)} %shard_map.119.refs_1_.refs_0_) | copy-start | bytes 1572868
  16.8 47.4 %all-to-all-start = ((bf16[32,192,128]{2,1,0:T(8,128)(2,1)}), bf16[32,192,128]{2,1,0:T(8,128)(2,1)}, u32[]{:S(2)}, u32[]{:S(2)}) async-start(bf16[32,192,128]{2,1,0:T(8,128)(2,1)} %broadcast_in_dim.22), calls=%async_computation | async-start | bytes 3145728 | tf_op jit(solution)/shard_map/all_to_all | solution.py:239
  27.4 49.1 %copy-start.1 = (bf16[2,256,512]{2,1,0:T(8,128)(2,1)S(1)}, bf16[2,256,512]{2,1,0:T(8,128)(2,1)}, u32[]{:S(2)}) copy-start(bf16[2,256,512]{2,1,0:T(8,128)(2,1)} %shard_map.119.refs_1_.refs_0_) | copy-start | bytes 1572868
  27.5 15.3 %collective-permute-start.6 = (bf16[2,256,512]{2,1,0:T(8,128)(2,1)S(1)}, bf16[2,256,512]{2,1,0:T(8,128)(2,1)S(1)}, u32[]{:S(2)}, u32[]{:S(2)}) collective-permute-start(bf16[2,256,512]{2,1,0:T(8,128)(2,1)S(1)} %copy-done), channel_id=1, source_target_pairs={{0,2},{1,3},{2,4},{3,5},{4,6},{5,7},{6,0},{7,1},{8,10},{9,11},{10,... | collective-permute-start | bytes 1572872 | tf_op jit(solution)/shard_map/ppermute | solution.py:240
  30.7 24.3 %collective-permute-start.4 = (bf16[2,256,512]{2,1,0:T(8,128)(2,1)S(1)}, bf16[2,256,512]{2,1,0:T(8,128)(2,1)S(1)}, u32[]{:S(2)}, u32[]{:S(2)}) collective-permute-start(bf16[2,256,512]{2,1,0:T(8,128)(2,1)S(1)} %copy-done), channel_id=1, source_target_pairs={{0,4},{1,5},{2,6},{3,7},{4,0},{5,1},{6,2},{7,3},{8,12},{9,13},{10,... | collective-permute-start | bytes 1572872 | tf_op jit(solution)/shard_map/ppermute | solution.py:240
  35.1 24.1 %collective-permute-start.2 = (bf16[2,256,512]{2,1,0:T(8,128)(2,1)S(1)}, bf16[2,256,512]{2,1,0:T(8,128)(2,1)S(1)}, u32[]{:S(2)}, u32[]{:S(2)}) collective-permute-start(bf16[2,256,512]{2,1,0:T(8,128)(2,1)S(1)} %copy-done), channel_id=1, source_target_pairs={{0,6},{1,7},{2,0},{3,1},{4,2},{5,3},{6,4},{7,5},{8,14},{9,15},{10,... | collective-permute-start | bytes 1572872 | tf_op jit(solution)/shard_map/ppermute | solution.py:240
  38.2 23.0 %collective-permute-start.1 = (bf16[2,256,512]{2,1,0:T(8,128)(2,1)S(1)}, bf16[2,256,512]{2,1,0:T(8,128)(2,1)S(1)}, u32[]{:S(2)}, u32[]{:S(2)}) collective-permute-start(bf16[2,256,512]{2,1,0:T(8,128)(2,1)S(1)} %copy-done), channel_id=1, source_target_pairs={{0,8},{8,0},{16,24},{24,16},{32,40},{40,32},{48,56},{56,48},{64,72... | collective-permute-start | bytes 1572872 | tf_op jit(solution)/shard_map/ppermute | solution.py:242
  42.8 21.4 %copy-start.2 = (bf16[2,256,512]{2,1,0:T(8,128)(2,1)}, bf16[2,256,512]{2,1,0:T(8,128)(2,1)S(1)}, u32[]{:S(2)}) copy-start(bf16[2,256,512]{2,1,0:T(8,128)(2,1)S(1)} %collective-permute-done.6.refs_7_.refs_3_) | copy-start | bytes 1572868
  42.8 18.4 %collective-permute-start.7 = (bf16[2,256,512]{2,1,0:T(8,128)(2,1)S(1)}, bf16[2,256,512]{2,1,0:T(8,128)(2,1)S(1)}, u32[]{:S(2)}, u32[]{:S(2)}) collective-permute-start(bf16[2,256,512]{2,1,0:T(8,128)(2,1)S(1)} %collective-permute-done.6.refs_7_.refs_3_), channel_id=1, source_target_pairs={{0,8},{8,0},{16,24},{24,16},{32,40},{40,32},{48,56},{56,48},{64,72... | collective-permute-start | bytes 1572872 | tf_op jit(solution)/shard_map/ppermute | solution.py:242
  55.0 9.2 %copy-start.4 = (bf16[2,256,512]{2,1,0:T(8,128)(2,1)}, bf16[2,256,512]{2,1,0:T(8,128)(2,1)S(1)}, u32[]{:S(2)}) copy-start(bf16[2,256,512]{2,1,0:T(8,128)(2,1)S(1)} %collective-permute-done.4.refs_5_.refs_2_) | copy-start | bytes 1572868
  55.0 6.2 %collective-permute-start.5 = (bf16[2,256,512]{2,1,0:T(8,128)(2,1)S(1)}, bf16[2,256,512]{2,1,0:T(8,128)(2,1)S(1)}, u32[]{:S(2)}, u32[]{:S(2)}) collective-permute-start(bf16[2,256,512]{2,1,0:T(8,128)(2,1)S(1)} %collective-permute-done.4.refs_5_.refs_2_), channel_id=1, source_target_pairs={{0,8},{8,0},{16,24},{24,16},{32,40},{40,32},{48,56},{56,48},{64,72... | collective-permute-start | bytes 1572872 | tf_op jit(solution)/shard_map/ppermute | solution.py:242
  59.2 5.0 %copy-start.6 = (bf16[2,256,512]{2,1,0:T(8,128)(2,1)}, bf16[2,256,512]{2,1,0:T(8,128)(2,1)S(1)}, u32[]{:S(2)}) copy-start(bf16[2,256,512]{2,1,0:T(8,128)(2,1)S(1)} %collective-permute-done.2.refs_3_.refs_1_) | copy-start | bytes 1572868
  59.2 3.9 %collective-permute-start.3 = (bf16[2,256,512]{2,1,0:T(8,128)(2,1)S(1)}, bf16[2,256,512]{2,1,0:T(8,128)(2,1)}, u32[]{:S(2)}, u32[]{:S(2)}) collective-permute-start(bf16[2,256,512]{2,1,0:T(8,128)(2,1)S(1)} %collective-permute-done.2.refs_3_.refs_1_), channel_id=1, source_target_pairs={{0,8},{8,0},{16,24},{24,16},{32,40},{40,32},{48,56},{56,48},{64,72... | collective-permute-start | bytes 1572872 | tf_op jit(solution)/shard_map/ppermute | solution.py:242
  61.1 3.1 %copy-start.8 = (bf16[2,256,512]{2,1,0:T(8,128)(2,1)}, bf16[2,256,512]{2,1,0:T(8,128)(2,1)S(1)}, u32[]{:S(2)}) copy-start(bf16[2,256,512]{2,1,0:T(8,128)(2,1)S(1)} %collective-permute-done.1.refs_2_.refs_4_) | copy-start | bytes 1572868
  63.1 13.5 %copy-start.11 = (bf16[2,256,512]{2,1,0:T(8,128)(2,1)S(1)}, bf16[2,256,512]{2,1,0:T(8,128)(2,1)}, u32[]{:S(2)}) copy-start(bf16[2,256,512]{2,1,0:T(8,128)(2,1)} %copy-done.10) | copy-start | bytes 1572868
  64.2 12.4 %copy-start.13 = (bf16[2,256,512]{2,1,0:T(8,128)(2,1)S(1)}, bf16[2,256,512]{2,1,0:T(8,128)(2,1)}, u32[]{:S(2)}) copy-start(bf16[2,256,512]{2,1,0:T(8,128)(2,1)} %copy-done.12) | copy-start | bytes 1572868
  68.5 14.6 %collective-permute-start.8 = (bf16[512,384]{1,0:T(8,128)(2,1)}, bf16[512,384]{1,0:T(8,128)(2,1)S(1)}, u32[]{:S(2)}, u32[]{:S(2)}) collective-permute-start(bf16[512,384]{1,0:T(8,128)(2,1)} %get-tuple-element.26.refs_0_), channel_id=1, source_target_pairs={{0,1},{1,0},{2,3},{3,2},{4,5},{5,4},{6,7},{7,6},{8,9},{9,8},{10,11... | collective-permute-start | bytes 1179656 | tf_op jit(solution)/shard_map/ppermute | solution.py:256
  70.5 12.7 %collective-permute-start.9 = (bf16[2048,384]{1,0:T(8,128)(2,1)}, bf16[2048,384]{1,0:T(8,128)(2,1)S(1)}, u32[]{:S(2)}, u32[]{:S(2)}) collective-permute-start(bf16[2048,384]{1,0:T(8,128)(2,1)} %get-tuple-element.27.refs_1_), channel_id=1, source_target_pairs={{0,8},{8,0},{16,24},{24,16},{32,40},{40,32},{48,56},{56,48},{64,72... | collective-permute-start | bytes 4718600 | tf_op jit(solution)/shard_map/ppermute | solution.py:257
  76.6 1.0 copy-start.3
  77.6 1.0 copy-start.5
  78.7 1.0 copy-start.7
  79.7 1.0 copy-start.9
  80.8 3.6 %copy-start.14 = (bf16[512,384]{1,0:T(8,128)(2,1)S(1)}, bf16[512,384]{1,0:T(8,128)(2,1)}, u32[]{:S(2)}) copy-start(bf16[512,384]{1,0:T(8,128)(2,1)} %get-tuple-element.26.refs_0_) | copy-start | bytes 1179652
  83.2 1.1 copy-start.16
  88.1 56.3 %all-to-all-start.1 = ((bf16[32,192,128]{2,1,0:T(8,128)(2,1)}), bf16[32,192,128]{2,1,0:T(8,128)(2,1)S(1)}, u32[]{:S(2)}, u32[]{:S(2)}) async-start(bf16[32,192,128]{2,1,0:T(8,128)(2,1)} %get-tuple-element.42), calls=%async_computation.1 | async-start | bytes 3145728 | tf_op jit(solution)/shard_map/all_to_all | solution.py:270
  106.4 3.7 %collective-permute-start.10 = (bf16[256,384]{1,0:T(8,128)(2,1)S(1)}, bf16[256,384]{1,0:T(8,128)(2,1)S(1)}, u32[]{:S(2)}, u32[]{:S(2)}) collective-permute-start(bf16[256,384]{1,0:T(8,128)(2,1)S(1)} %get-tuple-element.34), channel_id=1, source_target_pairs={{0,8},{8,0},{16,24},{24,16},{32,40},{40,32},{48,56},{56,48},{64,72... | collective-permute-start | bytes 589832 | tf_op jit(solution)/shard_map/ppermute | solution.py:274
  115.2 34.0 %collective-permute-start.11 = (bf16[2,256,512]{2,1,0:T(8,128)(2,1)}, bf16[2,256,512]{2,1,0:T(8,128)(2,1)S(1)}, u32[]{:S(2)}, u32[]{:S(2)}) collective-permute-start(bf16[2,256,512]{2,1,0:T(8,128)(2,1)} %get-tuple-element.37), channel_id=1, source_target_pairs={{0,2},{1,3},{2,4},{3,5},{4,6},{5,7},{6,0},{7,1},{8,10},{9,11},{10,... | collective-permute-start | bytes 1572872 | tf_op jit(solution)/shard_map/ppermute | solution.py:282
  118.4 30.7 %collective-permute-start.12 = (bf16[2,256,512]{2,1,0:T(8,128)(2,1)}, bf16[2,256,512]{2,1,0:T(8,128)(2,1)S(1)}, u32[]{:S(2)}, u32[]{:S(2)}) collective-permute-start(bf16[2,256,512]{2,1,0:T(8,128)(2,1)} %get-tuple-element.38), channel_id=1, source_target_pairs={{0,4},{1,5},{2,6},{3,7},{4,0},{5,1},{6,2},{7,3},{8,12},{9,13},{10,... | collective-permute-start | bytes 1572872 | tf_op jit(solution)/shard_map/ppermute | solution.py:282
  121.8 27.4 %collective-permute-start.13 = (bf16[2,256,512]{2,1,0:T(8,128)(2,1)}, bf16[2,256,512]{2,1,0:T(8,128)(2,1)S(1)}, u32[]{:S(2)}, u32[]{:S(2)}) collective-permute-start(bf16[2,256,512]{2,1,0:T(8,128)(2,1)} %get-tuple-element.39), channel_id=1, source_target_pairs={{0,6},{1,7},{2,0},{3,1},{4,2},{5,3},{6,4},{7,5},{8,14},{9,15},{10,... | collective-permute-start | bytes 1572872 | tf_op jit(solution)/shard_map/ppermute | solution.py:282
  144.6 8.7 %collective-permute-start.14 = (bf16[192,128]{1,0:T(8,128)(2,1)S(1)}, bf16[192,128]{1,0:T(8,128)(2,1)S(1)}, u32[]{:S(2)}, u32[]{:S(2)}) collective-permute-start(bf16[192,128]{1,0:T(8,128)(2,1)S(1)} %reduce_sum.12), channel_id=1, source_target_pairs={{0,0},{8,1},{2,2},{10,3},{4,4},{12,5},{6,6},{14,7},{64,8},{72,9},{... | collective-permute-start | bytes 147464 | tf_op jit(solution)/shard_map/ppermute | solution.py:272
  149.2 1.1 copy-start.19
  (6 other events, 4.8 us)

commit v12 on v11

--- a/solution.py
+++ b/solution.py
@@ -166,7 +166,7 @@
     part[:, 2 * cols :] = back.astype(BF16)
 
 
-def terms_body(where, get, put, pieces, acts, send):
+def acts_body(where, get, put, acts, send):
     total = get(0)[...].astype(F32) + get(1)[...].astype(F32)
     units = total.shape[1] // 3
     pre_gate, pre_up, grad_hidden = total[:, :units], total[:, units : 2 * units], total[:, 2 * units :]
@@ -177,11 +177,13 @@
     acts[:, units : 2 * units] = (grad_hidden * pre_gate * sigma).astype(BF16)
     acts[:, 2 * units :] = (pre_gate * sigma * pre_up).astype(BF16)
     send[...] = acts[send.shape[0] :]
-    put(1)
-    put(2)
-    rows = pieces.shape[1] // 3
+
+
+def terms_body(where, get, put, pieces):
+    acts = get(0)
+    rows, units = pieces.shape[1] // 3, pieces.shape[2]
     for step in range(N_X):
-        turned = get(2 + step)
+        turned = get(1 + step)
         both = dot(turned[0], acts[:, : 2 * units]).astype(BF16)
         down = dot(turned[1], acts[:, 2 * units :]).astype(BF16)
         first = turn(where, step, 2 * N_Z)
@@ -256,16 +258,19 @@
     theirs = lax.ppermute(sent, "narrow", OTHER_HALF)
     core_weights = lax.ppermute(weights, "wide", OTHER_CORE)
     theirs, core_weights = lax.optimization_barrier((theirs, core_weights))
-    terms, acts, send = call(
-        terms_body,
-        [(pieces.shape, BF16), part, ((slots, 3 * cols), BF16)],
-        flops,
-        where,
-        *(sent, theirs, *turned),
+    acts, send = call(
+        acts_body,
+        [part, ((slots, 3 * cols), BF16)],
+        20 * 2 * slots * 3 * cols,
+        where,
+        *(sent, theirs),
         grant=12,
         direct=True,
-    )
-
+        keep=True,
+    )
+    (terms,) = call(
+        terms_body, [(pieces.shape, BF16)], flops, where, acts, *turned, grant=12, direct=True
+    )
 
     terms = lax.all_to_all(terms, "wide", 0, 0, axis_index_groups=OWNERS)
     grads = terms.astype(F32).sum(axis=0).astype(BF16)

time: 157 us -> 157 us (level)
  starting transfers between devices: 84.8 us -> 90.4 us
  waiting for transfers between devices: 35.4 us -> 31.7 us
    ppermute x4, starting transfers between devices: 15.5 us -> 23.2 us  [local(): core = [lax.ppermute(held, 'wide', OTHER_CORE) for held in near]]
    ppermute x3, waiting for transfers between devices: 7.43 us -> 2.71 us  [local(): lax.ppermute(own, 'narrow', shift_x(-step))]
    ppermute x1, starting transfers between devices: 6.11 us -> 4.3 us  [local(): core_weights = lax.ppermute(weights, 'wide', OTHER_CORE)]
    ppermute x1, waiting for transfers between devices: 0.01 us -> 1.62 us  [local(): theirs = lax.ppermute(sent, 'narrow', OTHER_HALF)]
    pallas_call x6 -> x7, Pallas kernels: 19.3 us -> 19.3 us  [call(): pl.pallas_call(inner, out_shape=shapes, in_specs=[pl.BlockSpec(memory_spa...]
  transfers between devices with their start and end apart: 17 -> 17, of which waited for: 7 -> 6; matrix products, arithmetic and copies ran while one was open for 0% -> 0% of each run, Pallas kernels for 8% -> 8%
where the time goes in v12:
time: 157 us; the launch traced here: 155 us
  starting transfers between devices  90.4 us (58%)
  waiting for transfers between devices  31.7 us (20%)
  Pallas kernels  19.3 us (12%)
  local copies, waits for them, and re-layouts  10.5 us (7%)
  between operations  1.71 us (1%)
    ppermute x4, starting transfers between devices, local(): core = [lax.ppermute(held, 'wide', OTHER_CORE) for held in near]  23.2 us
    all_to_all x1, waiting for transfers between devices, local(): terms = lax.all_to_all(terms, 'wide', 0, 0, axis_index_groups=OWNERS)  20.1 us
    all_to_all x1, starting transfers between devices, local(): terms = lax.all_to_all(terms, 'wide', 0, 0, axis_index_groups=OWNERS)  19.4 us
    pallas_call x7, Pallas kernels, call(): pl.pallas_call(inner, out_shape=shapes, in_specs=[pl.BlockSpec(memory_spa...  19.3 us
    all_to_all x1, starting transfers between devices, local(): pieces = lax.all_to_all(pieces, 'wide', 0, 0, axis_index_groups=OWNERS)  10.7 us
    ppermute x3, starting transfers between devices, local(): lax.ppermute(own, 'narrow', shift_x(-step))  9.46 us
    ppermute x3, starting transfers between devices, local(): lax.ppermute(outs[step], 'narrow', shift_x(step))  9.09 us
    unnamed x42, local copies, waits for them, and re-layouts  8.32 us
  transfers between devices with their start and end apart: 17, of which 6 were waited for; matrix products, arithmetic and copies ran while one was open for 0% of the time, Pallas kernels for 8%

profile of v12, /device:TPU:1, one launch (start us, length us, event | category | flops | bytes accessed | tf_op | source)
XLA Modules:
  0.0 154.5 jit_solution(11233245248579371862)
XLA Ops:
  1.4 4.6 %collective-permute-start = (bf16[192,128]{1,0:T(8,128)(2,1)S(1)}, bf16[192,128]{1,0:T(8,128)(2,1)S(1)}, u32[]{:S(2)}, u32[]{:S(2)}) collective-permute-start(bf16[192,128]{1,0:T(8,128)(2,1)S(1)} %pad_maximum_fusion), channel_id=1, source_target_pairs={{0,0},{1,8},{2,2},{3,10},{4,4},{5,12},{6,6},{7,14},{8,64},{9,72},{... | collective-permute-start | bytes 147464 | tf_op jit(solution)/shard_map/ppermute | solution.py:231
  6.6 2.4 %shard_map.119.refs_1_.refs_0_ = bf16[2,256,512]{2,1,0:T(8,128)(2,1)} custom-call(s32[1]{0:T(128)} %bitcast.where_ref, bf16[384,512]{1,0:T(8,128)(2,1)} %refs_0_.1, bf16[384,512]{1,0:T(8,128)(2,1)} %refs_1_.1, s32[1,256]{1,0:T(1,128)} %bitcast.6, s32[1,1]{1,0:T(1,128)} %bitcast.4.refs_3_, f32[1,256]{1,0:T(1,128)} %bitcast.8), custom_call_target="tpu_custom_call" | custom-call | flops 201326592 | bytes 788484 | tf_op jit(solution)/shard_map/pallas_call | solution.py:99
  9.1 6.2 %collective-permute-done = bf16[192,128]{1,0:T(8,128)(2,1)S(1)} collective-permute-done((bf16[192,128]{1,0:T(8,128)(2,1)S(1)}, bf16[192,128]{1,0:T(8,128)(2,1)S(1)}, u32[]{:S(2)}, u32[]{:S(2)}) %collective-permute-start) | collective-permute-done | bytes 49184 | tf_op jit(solution)/shard_map/ppermute | solution.py:231
  15.2 1.5 broadcast_in_dim.22
  16.8 10.7 %all-to-all-start = ((bf16[32,192,128]{2,1,0:T(8,128)(2,1)}), bf16[32,192,128]{2,1,0:T(8,128)(2,1)}, u32[]{:S(2)}, u32[]{:S(2)}) async-start(bf16[32,192,128]{2,1,0:T(8,128)(2,1)} %broadcast_in_dim.22), calls=%async_computation | async-start | bytes 3145728 | tf_op jit(solution)/shard_map/all_to_all | solution.py:241
  27.5 4.5 %collective-permute-start.2 = (bf16[2,256,512]{2,1,0:T(8,128)(2,1)S(1)}, bf16[2,256,512]{2,1,0:T(8,128)(2,1)S(1)}, u32[]{:S(2)}, u32[]{:S(2)}) collective-permute-start(bf16[2,256,512]{2,1,0:T(8,128)(2,1)S(1)} %copy-done), channel_id=1, source_target_pairs={{0,6},{1,7},{2,0},{3,1},{4,2},{5,3},{6,4},{7,5},{8,14},{9,15},{10,... | collective-permute-start | bytes 1572872 | tf_op jit(solution)/shard_map/ppermute | solution.py:242
  32.0 2.4 %collective-permute-start.4 = (bf16[2,256,512]{2,1,0:T(8,128)(2,1)S(1)}, bf16[2,256,512]{2,1,0:T(8,128)(2,1)S(1)}, u32[]{:S(2)}, u32[]{:S(2)}) collective-permute-start(bf16[2,256,512]{2,1,0:T(8,128)(2,1)S(1)} %copy-done), channel_id=1, source_target_pairs={{0,4},{1,5},{2,6},{3,7},{4,0},{5,1},{6,2},{7,3},{8,12},{9,13},{10,... | collective-permute-start | bytes 1572872 | tf_op jit(solution)/shard_map/ppermute | solution.py:242
  34.4 2.5 %collective-permute-start.6 = (bf16[2,256,512]{2,1,0:T(8,128)(2,1)S(1)}, bf16[2,256,512]{2,1,0:T(8,128)(2,1)S(1)}, u32[]{:S(2)}, u32[]{:S(2)}) collective-permute-start(bf16[2,256,512]{2,1,0:T(8,128)(2,1)S(1)} %copy-done), channel_id=1, source_target_pairs={{0,2},{1,3},{2,4},{3,5},{4,6},{5,7},{6,0},{7,1},{8,10},{9,11},{10,... | collective-permute-start | bytes 1572872 | tf_op jit(solution)/shard_map/ppermute | solution.py:242
  36.9 4.2 %collective-permute-start.1 = (bf16[2,256,512]{2,1,0:T(8,128)(2,1)S(1)}, bf16[2,256,512]{2,1,0:T(8,128)(2,1)S(1)}, u32[]{:S(2)}, u32[]{:S(2)}) collective-permute-start(bf16[2,256,512]{2,1,0:T(8,128)(2,1)S(1)} %copy-done), channel_id=1, source_target_pairs={{0,8},{8,0},{16,24},{24,16},{32,40},{40,32},{48,56},{56,48},{64,72... | collective-permute-start | bytes 1572872 | tf_op jit(solution)/shard_map/ppermute | solution.py:244
  41.2 1.4 collective-permute-done.2.refs_3_.refs_1_
  42.5 14.7 %collective-permute-start.3 = (bf16[2,256,512]{2,1,0:T(8,128)(2,1)S(1)}, bf16[2,256,512]{2,1,0:T(8,128)(2,1)S(1)}, u32[]{:S(2)}, u32[]{:S(2)}) collective-permute-start(bf16[2,256,512]{2,1,0:T(8,128)(2,1)S(1)} %collective-permute-done.2.refs_3_.refs_1_), channel_id=1, source_target_pairs={{0,8},{8,0},{16,24},{24,16},{32,40},{40,32},{48,56},{56,48},{64,72... | collective-permute-start | bytes 1572872 | tf_op jit(solution)/shard_map/ppermute | solution.py:244
  57.3 1.9 %collective-permute-start.5 = (bf16[2,256,512]{2,1,0:T(8,128)(2,1)S(1)}, bf16[2,256,512]{2,1,0:T(8,128)(2,1)S(1)}, u32[]{:S(2)}, u32[]{:S(2)}) collective-permute-start(bf16[2,256,512]{2,1,0:T(8,128)(2,1)S(1)} %collective-permute-done.4.refs_5_.refs_2_), channel_id=1, source_target_pairs={{0,8},{8,0},{16,24},{24,16},{32,40},{40,32},{48,56},{56,48},{64,72... | collective-permute-start | bytes 1572872 | tf_op jit(solution)/shard_map/ppermute | solution.py:244
  59.2 1.3 collective-permute-done.6.refs_7_.refs_3_
  60.6 2.3 %collective-permute-start.7 = (bf16[2,256,512]{2,1,0:T(8,128)(2,1)S(1)}, bf16[2,256,512]{2,1,0:T(8,128)(2,1)}, u32[]{:S(2)}, u32[]{:S(2)}) collective-permute-start(bf16[2,256,512]{2,1,0:T(8,128)(2,1)S(1)} %collective-permute-done.6.refs_7_.refs_3_), channel_id=1, source_target_pairs={{0,8},{8,0},{16,24},{24,16},{32,40},{40,32},{48,56},{56,48},{64,72... | collective-permute-start | bytes 1572872 | tf_op jit(solution)/shard_map/ppermute | solution.py:244
  64.6 5.1 %shard_map.120 = (bf16[512,384]{1,0:T(8,128)(2,1)}, bf16[2048,384]{1,0:T(8,128)(2,1)}) custom-call(s32[1]{0:T(128)} %bitcast.where_ref, bf16[32,192,128]{2,1,0:T(8,128)(2,1)} %all-to-all-done.refs_0_, bf16[2,256,512]{2,1,0:T(8,128)(2,1)} %shard_map.119.refs_1_.refs_0_, bf16[2,256,512]{2,1,0:T(8,128)(2,1)} %copy-done.9, bf16[2,256,512]{2,1,0:T(8,128)(2,1)} %copy-done.3, ...), custom_call_target="tpu_custom_call" | custom-call | flops 805306368 | bytes 5767168 | tf_op jit(solution)/shard_map/pallas_call | solution.py:99
  69.7 2.5 %collective-permute-start.8 = (bf16[512,384]{1,0:T(8,128)(2,1)}, bf16[512,384]{1,0:T(8,128)(2,1)S(1)}, u32[]{:S(2)}, u32[]{:S(2)}) collective-permute-start(bf16[512,384]{1,0:T(8,128)(2,1)} %get-tuple-element.25.refs_0_), channel_id=1, source_target_pairs={{0,1},{1,0},{2,3},{3,2},{4,5},{5,4},{6,7},{7,6},{8,9},{9,8},{10,11... | collective-permute-start | bytes 1179656 | tf_op jit(solution)/shard_map/ppermute | solution.py:258
  72.3 4.3 %collective-permute-start.9 = (bf16[2048,384]{1,0:T(8,128)(2,1)}, bf16[2048,384]{1,0:T(8,128)(2,1)S(1)}, u32[]{:S(2)}, u32[]{:S(2)}) collective-permute-start(bf16[2048,384]{1,0:T(8,128)(2,1)} %get-tuple-element.26.refs_1_), channel_id=1, source_target_pairs={{0,8},{8,0},{16,24},{24,16},{32,40},{40,32},{48,56},{56,48},{64,72... | collective-permute-start | bytes 4718600 | tf_op jit(solution)/shard_map/ppermute | solution.py:259
  78.7 1.0 copy-done.8
  79.7 1.0 copy-done.10
  80.8 2.0 %shard_map.124 = (bf16[2,512,512]{2,1,0:T(8,128)(2,1)S(1)}, bf16[2,512,512]{2,1,0:T(8,128)(2,1)S(1)}, bf16[2,512,512]{2,1,0:T(8,128)(2,1)S(1)}, bf16[2,512,512]{2,1,0:T(8,128)(2,1)S(1)}) custom-call(s32[1]{0:T(128)} %bitcast.where_ref, bf16[2,256,512]{2,1,0:T(8,128)(2,1)S(1)} %copy-done.1, bf16[2,256,512]{2,1,0:T(8,128)(2,1)S(1)} %copy-done.4, ...), custom_call_target="tpu_custom_call" | custom-call | flops 20000000000 | bytes 4194304 | tf_op jit(solution)/shard_map/pallas_call | solution.py:99
  82.8 1.6 %collective-permute-done.8.refs_1_ = bf16[512,384]{1,0:T(8,128)(2,1)S(1)} collective-permute-done((bf16[512,384]{1,0:T(8,128)(2,1)}, bf16[512,384]{1,0:T(8,128)(2,1)S(1)}, u32[]{:S(2)}, u32[]{:S(2)}) %collective-permute-start.8) | collective-permute-done | bytes 393248 | tf_op jit(solution)/shard_map/ppermute | solution.py:258
  85.6 2.1 %shard_map.125 = bf16[32,192,128]{2,1,0:T(8,128)(2,1)} custom-call(s32[1]{0:T(128)} %bitcast.where_ref, bf16[512,384]{1,0:T(8,128)(2,1)S(1)} %get-tuple-element.28.refs_0_, bf16[2,512,512]{2,1,0:T(8,128)(2,1)S(1)} %get-tuple-element.37.refs_1_, bf16[2,512,512]{2,1,0:T(8,128)(2,1)S(1)} %get-tuple-element.38.refs_2_, ...), custom_call_target="tpu_custom_call" | custom-call | flops 805306368 | bytes 4587520 | tf_op jit(solution)/shard_map/pallas_call | solution.py:99
  87.7 19.4 %all-to-all-start.1 = ((bf16[32,192,128]{2,1,0:T(8,128)(2,1)}), bf16[32,192,128]{2,1,0:T(8,128)(2,1)S(1)}, u32[]{:S(2)}, u32[]{:S(2)}) async-start(bf16[32,192,128]{2,1,0:T(8,128)(2,1)} %shard_map.125), calls=%async_computation.1 | async-start | bytes 3145728 | tf_op jit(solution)/shard_map/all_to_all | solution.py:275
  107.1 2.7 %collective-permute-start.10 = (bf16[256,384]{1,0:T(8,128)(2,1)S(1)}, bf16[256,384]{1,0:T(8,128)(2,1)S(1)}, u32[]{:S(2)}, u32[]{:S(2)}) collective-permute-start(bf16[256,384]{1,0:T(8,128)(2,1)S(1)} %get-tuple-element.29), channel_id=1, source_target_pairs={{0,8},{8,0},{16,24},{24,16},{32,40},{40,32},{48,56},{56,48},{64,72... | collective-permute-start | bytes 589832 | tf_op jit(solution)/shard_map/ppermute | solution.py:279
  109.7 1.0 collective-permute-done.10.refs_2_
  111.5 4.3 %shard_map.122 = (bf16[2,256,512]{2,1,0:T(8,128)(2,1)}, bf16[2,256,512]{2,1,0:T(8,128)(2,1)}, bf16[2,256,512]{2,1,0:T(8,128)(2,1)}, bf16[2,256,512]{2,1,0:T(8,128)(2,1)}) custom-call(s32[1]{0:T(128)} %bitcast.where_ref, bf16[512,384]{1,0:T(8,128)(2,1)} %copy-done.2, bf16[2048,384]{1,0:T(8,128)(2,1)} %get-tuple-element.26.refs_1_, ...), custom_call_target="tpu_custom_call" | custom-call | flops 805306368 | bytes 3735552 | tf_op jit(solution)/shard_map/pallas_call | solution.py:99
  115.8 1.9 %collective-permute-start.11 = (bf16[2,256,512]{2,1,0:T(8,128)(2,1)}, bf16[2,256,512]{2,1,0:T(8,128)(2,1)S(1)}, u32[]{:S(2)}, u32[]{:S(2)}) collective-permute-start(bf16[2,256,512]{2,1,0:T(8,128)(2,1)} %get-tuple-element.32), channel_id=1, source_target_pairs={{0,2},{1,3},{2,4},{3,5},{4,6},{5,7},{6,0},{7,1},{8,10},{9,11},{10,... | collective-permute-start | bytes 1572872 | tf_op jit(solution)/shard_map/ppermute | solution.py:287
  117.7 5.3 %collective-permute-start.12 = (bf16[2,256,512]{2,1,0:T(8,128)(2,1)}, bf16[2,256,512]{2,1,0:T(8,128)(2,1)S(1)}, u32[]{:S(2)}, u32[]{:S(2)}) collective-permute-start(bf16[2,256,512]{2,1,0:T(8,128)(2,1)} %get-tuple-element.33), channel_id=1, source_target_pairs={{0,4},{1,5},{2,6},{3,7},{4,0},{5,1},{6,2},{7,3},{8,12},{9,13},{10,... | collective-permute-start | bytes 1572872 | tf_op jit(solution)/shard_map/ppermute | solution.py:287
  123.0 1.9 %collective-permute-start.13 = (bf16[2,256,512]{2,1,0:T(8,128)(2,1)}, bf16[2,256,512]{2,1,0:T(8,128)(2,1)S(1)}, u32[]{:S(2)}, u32[]{:S(2)}) collective-permute-start(bf16[2,256,512]{2,1,0:T(8,128)(2,1)} %get-tuple-element.34), channel_id=1, source_target_pairs={{0,6},{1,7},{2,0},{3,1},{4,2},{5,3},{6,4},{7,5},{8,14},{9,15},{10,... | collective-permute-start | bytes 1572872 | tf_op jit(solution)/shard_map/ppermute | solution.py:287
  124.9 20.1 %all-to-all-done.1 = bf16[32,192,128]{2,1,0:T(8,128)(2,1)S(1)} async-done(((bf16[32,192,128]{2,1,0:T(8,128)(2,1)}), bf16[32,192,128]{2,1,0:T(8,128)(2,1)S(1)}, u32[]{:S(2)}, u32[]{:S(2)}) %all-to-all-start.1) | async-done | bytes 1572896 | tf_op jit(solution)/shard_map/all_to_all | solution.py:275
  145.2 4.5 %collective-permute-start.14 = (bf16[192,128]{1,0:T(8,128)(2,1)S(1)}, bf16[192,128]{1,0:T(8,128)(2,1)S(1)}, u32[]{:S(2)}, u32[]{:S(2)}) collective-permute-start(bf16[192,128]{1,0:T(8,128)(2,1)S(1)} %reduce_sum.12), channel_id=1, source_target_pairs={{0,0},{8,1},{2,2},{10,3},{4,4},{12,5},{6,6},{14,7},{64,8},{72,9},{... | collective-permute-start | bytes 147464 | tf_op jit(solution)/shard_map/ppermute | solution.py:277
  150.9 2.9 %shard_map.123 = (bf16[384,512]{1,0:T(8,128)(2,1)}, bf16[384,512]{1,0:T(8,128)(2,1)}) custom-call(s32[1]{0:T(128)} %bitcast.where_ref, s32[1,256]{1,0:T(1,128)} %bitcast.7, s32[1,1]{1,0:T(1,128)} %bitcast.5.refs_1_, f32[1,256]{1,0:T(1,128)} %bitcast.9, bf16[2,256,512]{2,1,0:T(8,128)(2,1)} %get-tuple-element.31.refs_3_, bf16[2,256,512]{2,1,0:T(8,128)(2,1)} %copy-done.17, ...), custom_call_target="tpu_custom_call" | custom-call | flops 201326592 | bytes 2099204 | tf_op jit(solution)/shard_map/pallas_call | solution.py:99
  (55 shorter events, 8.3 us)
Async XLA Ops:
  1.4 13.8 %collective-permute-start = (bf16[192,128]{1,0:T(8,128)(2,1)S(1)}, bf16[192,128]{1,0:T(8,128)(2,1)S(1)}, u32[]{:S(2)}, u32[]{:S(2)}) collective-permute-start(bf16[192,128]{1,0:T(8,128)(2,1)S(1)} %pad_maximum_fusion), channel_id=1, source_target_pairs={{0,0},{1,8},{2,2},{3,10},{4,4},{5,12},{6,6},{7,14},{8,64},{9,72},{... | collective-permute-start | bytes 147464 | tf_op jit(solution)/shard_map/ppermute | solution.py:231
  16.8 10.7 %copy-start = (bf16[2,256,512]{2,1,0:T(8,128)(2,1)S(1)}, bf16[2,256,512]{2,1,0:T(8,128)(2,1)}, u32[]{:S(2)}) copy-start(bf16[2,256,512]{2,1,0:T(8,128)(2,1)} %shard_map.119.refs_1_.refs_0_) | copy-start | bytes 1572868
  16.8 47.8 %all-to-all-start = ((bf16[32,192,128]{2,1,0:T(8,128)(2,1)}), bf16[32,192,128]{2,1,0:T(8,128)(2,1)}, u32[]{:S(2)}, u32[]{:S(2)}) async-start(bf16[32,192,128]{2,1,0:T(8,128)(2,1)} %broadcast_in_dim.22), calls=%async_computation | async-start | bytes 3145728 | tf_op jit(solution)/shard_map/all_to_all | solution.py:241
  27.4 49.1 %copy-start.1 = (bf16[2,256,512]{2,1,0:T(8,128)(2,1)S(1)}, bf16[2,256,512]{2,1,0:T(8,128)(2,1)}, u32[]{:S(2)}) copy-start(bf16[2,256,512]{2,1,0:T(8,128)(2,1)} %shard_map.119.refs_1_.refs_0_) | copy-start | bytes 1572868
  27.5 15.1 %collective-permute-start.2 = (bf16[2,256,512]{2,1,0:T(8,128)(2,1)S(1)}, bf16[2,256,512]{2,1,0:T(8,128)(2,1)S(1)}, u32[]{:S(2)}, u32[]{:S(2)}) collective-permute-start(bf16[2,256,512]{2,1,0:T(8,128)(2,1)S(1)} %copy-done), channel_id=1, source_target_pairs={{0,6},{1,7},{2,0},{3,1},{4,2},{5,3},{6,4},{7,5},{8,14},{9,15},{10,... | collective-permute-start | bytes 1572872 | tf_op jit(solution)/shard_map/ppermute | solution.py:242
  32.0 25.3 %collective-permute-start.4 = (bf16[2,256,512]{2,1,0:T(8,128)(2,1)S(1)}, bf16[2,256,512]{2,1,0:T(8,128)(2,1)S(1)}, u32[]{:S(2)}, u32[]{:S(2)}) collective-permute-start(bf16[2,256,512]{2,1,0:T(8,128)(2,1)S(1)} %copy-done), channel_id=1, source_target_pairs={{0,4},{1,5},{2,6},{3,7},{4,0},{5,1},{6,2},{7,3},{8,12},{9,13},{10,... | collective-permute-start | bytes 1572872 | tf_op jit(solution)/shard_map/ppermute | solution.py:242
  34.4 26.1 %collective-permute-start.6 = (bf16[2,256,512]{2,1,0:T(8,128)(2,1)S(1)}, bf16[2,256,512]{2,1,0:T(8,128)(2,1)S(1)}, u32[]{:S(2)}, u32[]{:S(2)}) collective-permute-start(bf16[2,256,512]{2,1,0:T(8,128)(2,1)S(1)} %copy-done), channel_id=1, source_target_pairs={{0,2},{1,3},{2,4},{3,5},{4,6},{5,7},{6,0},{7,1},{8,10},{9,11},{10,... | collective-permute-start | bytes 1572872 | tf_op jit(solution)/shard_map/ppermute | solution.py:242
  36.9 25.9 %collective-permute-start.1 = (bf16[2,256,512]{2,1,0:T(8,128)(2,1)S(1)}, bf16[2,256,512]{2,1,0:T(8,128)(2,1)S(1)}, u32[]{:S(2)}, u32[]{:S(2)}) collective-permute-start(bf16[2,256,512]{2,1,0:T(8,128)(2,1)S(1)} %copy-done), channel_id=1, source_target_pairs={{0,8},{8,0},{16,24},{24,16},{32,40},{40,32},{48,56},{56,48},{64,72... | collective-permute-start | bytes 1572872 | tf_op jit(solution)/shard_map/ppermute | solution.py:244
  42.5 22.0 %copy-start.3 = (bf16[2,256,512]{2,1,0:T(8,128)(2,1)}, bf16[2,256,512]{2,1,0:T(8,128)(2,1)S(1)}, u32[]{:S(2)}) copy-start(bf16[2,256,512]{2,1,0:T(8,128)(2,1)S(1)} %collective-permute-done.2.refs_3_.refs_1_) | copy-start | bytes 1572868
  42.5 20.4 %collective-permute-start.3 = (bf16[2,256,512]{2,1,0:T(8,128)(2,1)S(1)}, bf16[2,256,512]{2,1,0:T(8,128)(2,1)S(1)}, u32[]{:S(2)}, u32[]{:S(2)}) collective-permute-start(bf16[2,256,512]{2,1,0:T(8,128)(2,1)S(1)} %collective-permute-done.2.refs_3_.refs_1_), channel_id=1, source_target_pairs={{0,8},{8,0},{16,24},{24,16},{32,40},{40,32},{48,56},{56,48},{64,72... | collective-permute-start | bytes 1572872 | tf_op jit(solution)/shard_map/ppermute | solution.py:244
  57.3 7.3 %copy-start.5 = (bf16[2,256,512]{2,1,0:T(8,128)(2,1)}, bf16[2,256,512]{2,1,0:T(8,128)(2,1)S(1)}, u32[]{:S(2)}) copy-start(bf16[2,256,512]{2,1,0:T(8,128)(2,1)S(1)} %collective-permute-done.4.refs_5_.refs_2_) | copy-start | bytes 1572868
  57.3 5.6 %collective-permute-start.5 = (bf16[2,256,512]{2,1,0:T(8,128)(2,1)S(1)}, bf16[2,256,512]{2,1,0:T(8,128)(2,1)S(1)}, u32[]{:S(2)}, u32[]{:S(2)}) collective-permute-start(bf16[2,256,512]{2,1,0:T(8,128)(2,1)S(1)} %collective-permute-done.4.refs_5_.refs_2_), channel_id=1, source_target_pairs={{0,8},{8,0},{16,24},{24,16},{32,40},{40,32},{48,56},{56,48},{64,72... | collective-permute-start | bytes 1572872 | tf_op jit(solution)/shard_map/ppermute | solution.py:244
  60.6 4.0 %copy-start.7 = (bf16[2,256,512]{2,1,0:T(8,128)(2,1)}, bf16[2,256,512]{2,1,0:T(8,128)(2,1)S(1)}, u32[]{:S(2)}) copy-start(bf16[2,256,512]{2,1,0:T(8,128)(2,1)S(1)} %collective-permute-done.6.refs_7_.refs_3_) | copy-start | bytes 1572868
  60.6 4.0 %collective-permute-start.7 = (bf16[2,256,512]{2,1,0:T(8,128)(2,1)S(1)}, bf16[2,256,512]{2,1,0:T(8,128)(2,1)}, u32[]{:S(2)}, u32[]{:S(2)}) collective-permute-start(bf16[2,256,512]{2,1,0:T(8,128)(2,1)S(1)} %collective-permute-done.6.refs_7_.refs_3_), channel_id=1, source_target_pairs={{0,8},{8,0},{16,24},{24,16},{32,40},{40,32},{48,56},{56,48},{64,72... | collective-permute-start | bytes 1572872 | tf_op jit(solution)/shard_map/ppermute | solution.py:244
  62.9 1.7 %copy-start.9 = (bf16[2,256,512]{2,1,0:T(8,128)(2,1)}, bf16[2,256,512]{2,1,0:T(8,128)(2,1)S(1)}, u32[]{:S(2)}) copy-start(bf16[2,256,512]{2,1,0:T(8,128)(2,1)S(1)} %collective-permute-done.1.refs_2_.refs_4_) | copy-start | bytes 1572868
  64.5 12.0 %copy-start.12 = (bf16[2,256,512]{2,1,0:T(8,128)(2,1)S(1)}, bf16[2,256,512]{2,1,0:T(8,128)(2,1)}, u32[]{:S(2)}) copy-start(bf16[2,256,512]{2,1,0:T(8,128)(2,1)} %copy-done.11) | copy-start | bytes 1572868
  64.6 12.0 %copy-start.14 = (bf16[2,256,512]{2,1,0:T(8,128)(2,1)S(1)}, bf16[2,256,512]{2,1,0:T(8,128)(2,1)}, u32[]{:S(2)}) copy-start(bf16[2,256,512]{2,1,0:T(8,128)(2,1)} %copy-done.13) | copy-start | bytes 1572868
  69.7 14.7 %collective-permute-start.8 = (bf16[512,384]{1,0:T(8,128)(2,1)}, bf16[512,384]{1,0:T(8,128)(2,1)S(1)}, u32[]{:S(2)}, u32[]{:S(2)}) collective-permute-start(bf16[512,384]{1,0:T(8,128)(2,1)} %get-tuple-element.25.refs_0_), channel_id=1, source_target_pairs={{0,1},{1,0},{2,3},{3,2},{4,5},{5,4},{6,7},{7,6},{8,9},{9,8},{10,11... | collective-permute-start | bytes 1179656 | tf_op jit(solution)/shard_map/ppermute | solution.py:258
  72.3 12.1 %collective-permute-start.9 = (bf16[2048,384]{1,0:T(8,128)(2,1)}, bf16[2048,384]{1,0:T(8,128)(2,1)S(1)}, u32[]{:S(2)}, u32[]{:S(2)}) collective-permute-start(bf16[2048,384]{1,0:T(8,128)(2,1)} %get-tuple-element.26.refs_1_), channel_id=1, source_target_pairs={{0,8},{8,0},{16,24},{24,16},{32,40},{40,32},{48,56},{56,48},{64,72... | collective-permute-start | bytes 4718600 | tf_op jit(solution)/shard_map/ppermute | solution.py:259
  76.6 1.0 copy-start.4
  77.6 1.0 copy-start.6
  78.7 1.0 copy-start.8
  80.8 3.6 %copy-start.15 = (bf16[512,384]{1,0:T(8,128)(2,1)S(1)}, bf16[512,384]{1,0:T(8,128)(2,1)}, u32[]{:S(2)}) copy-start(bf16[512,384]{1,0:T(8,128)(2,1)} %get-tuple-element.25.refs_0_) | copy-start | bytes 1179652
  84.4 1.2 copy-start.16
  85.6 2.1 %copy-start.2 = (bf16[512,384]{1,0:T(8,128)(2,1)}, bf16[512,384]{1,0:T(8,128)(2,1)S(1)}, u32[]{:S(2)}) copy-start(bf16[512,384]{1,0:T(8,128)(2,1)S(1)} %get-tuple-element.28.refs_0_) | copy-start | bytes 1179652
  87.7 57.4 %all-to-all-start.1 = ((bf16[32,192,128]{2,1,0:T(8,128)(2,1)}), bf16[32,192,128]{2,1,0:T(8,128)(2,1)S(1)}, u32[]{:S(2)}, u32[]{:S(2)}) async-start(bf16[32,192,128]{2,1,0:T(8,128)(2,1)} %shard_map.125), calls=%async_computation.1 | async-start | bytes 3145728 | tf_op jit(solution)/shard_map/all_to_all | solution.py:275
  107.1 3.7 %collective-permute-start.10 = (bf16[256,384]{1,0:T(8,128)(2,1)S(1)}, bf16[256,384]{1,0:T(8,128)(2,1)S(1)}, u32[]{:S(2)}, u32[]{:S(2)}) collective-permute-start(bf16[256,384]{1,0:T(8,128)(2,1)S(1)} %get-tuple-element.29), channel_id=1, source_target_pairs={{0,8},{8,0},{16,24},{24,16},{32,40},{40,32},{48,56},{56,48},{64,72... | collective-permute-start | bytes 589832 | tf_op jit(solution)/shard_map/ppermute | solution.py:279
  115.8 34.0 %collective-permute-start.11 = (bf16[2,256,512]{2,1,0:T(8,128)(2,1)}, bf16[2,256,512]{2,1,0:T(8,128)(2,1)S(1)}, u32[]{:S(2)}, u32[]{:S(2)}) collective-permute-start(bf16[2,256,512]{2,1,0:T(8,128)(2,1)} %get-tuple-element.32), channel_id=1, source_target_pairs={{0,2},{1,3},{2,4},{3,5},{4,6},{5,7},{6,0},{7,1},{8,10},{9,11},{10,... | collective-permute-start | bytes 1572872 | tf_op jit(solution)/shard_map/ppermute | solution.py:287
  117.7 32.1 %collective-permute-start.12 = (bf16[2,256,512]{2,1,0:T(8,128)(2,1)}, bf16[2,256,512]{2,1,0:T(8,128)(2,1)S(1)}, u32[]{:S(2)}, u32[]{:S(2)}) collective-permute-start(bf16[2,256,512]{2,1,0:T(8,128)(2,1)} %get-tuple-element.33), channel_id=1, source_target_pairs={{0,4},{1,5},{2,6},{3,7},{4,0},{5,1},{6,2},{7,3},{8,12},{9,13},{10,... | collective-permute-start | bytes 1572872 | tf_op jit(solution)/shard_map/ppermute | solution.py:287
  123.0 26.8 %collective-permute-start.13 = (bf16[2,256,512]{2,1,0:T(8,128)(2,1)}, bf16[2,256,512]{2,1,0:T(8,128)(2,1)S(1)}, u32[]{:S(2)}, u32[]{:S(2)}) collective-permute-start(bf16[2,256,512]{2,1,0:T(8,128)(2,1)} %get-tuple-element.34), channel_id=1, source_target_pairs={{0,6},{1,7},{2,0},{3,1},{4,2},{5,3},{6,4},{7,5},{8,14},{9,15},{10,... | collective-permute-start | bytes 1572872 | tf_op jit(solution)/shard_map/ppermute | solution.py:287
  145.2 8.6 %collective-permute-start.14 = (bf16[192,128]{1,0:T(8,128)(2,1)S(1)}, bf16[192,128]{1,0:T(8,128)(2,1)S(1)}, u32[]{:S(2)}, u32[]{:S(2)}) collective-permute-start(bf16[192,128]{1,0:T(8,128)(2,1)S(1)} %reduce_sum.12), channel_id=1, source_target_pairs={{0,0},{8,1},{2,2},{10,3},{4,4},{12,5},{6,6},{14,7},{64,8},{72,9},{... | collective-permute-start | bytes 147464 | tf_op jit(solution)/shard_map/ppermute | solution.py:277
  149.8 1.1 copy-start.19
  (6 other events, 5.1 us)

commit v13 on v11

--- a/solution.py
+++ b/solution.py
@@ -157,13 +157,15 @@
     put(1)
     feat = get(1).shape[2]
     pre, back = 0.0, 0.0
-    for step in range(N_X):
-        x = get(1 + step)
-        at = pl.ds(turn(where, step, feat), feat)
-        pre = pre + dot(x[0], weights[at, : 2 * cols])
-        back = back + dot(x[1], weights[at, 2 * cols :])
+    spans = [pl.ds(turn(where, step, feat), feat) for step in range(N_X)]
+    for step, at in enumerate(spans):
+        pre = pre + dot(get(1 + step)[0], weights[at, : 2 * cols])
     part[:, : 2 * cols] = pre.astype(BF16)
+    put(0, (slice(None), pl.ds(0, 2 * cols)))
+    for step, at in enumerate(spans):
+        back = back + dot(get(1 + step)[1], weights[at, 2 * cols :])
     part[:, 2 * cols :] = back.astype(BF16)
+    put(0, (slice(None), pl.ds(2 * cols, cols)))
 
 
 def terms_body(where, get, put, pieces, acts, send):

time: 157 us -> 157 us (level)
  no operation moved by 1% of the time
where the time goes in v13:
time: 157 us; the launch traced here: 155 us
  starting transfers between devices  84.8 us (54%)
  waiting for transfers between devices  35.5 us (23%)
  Pallas kernels  20 us (13%)
  local copies, waits for them, and re-layouts  11.6 us (7%)
  between operations  1.7 us (1%)
    pallas_call x6, Pallas kernels, call(): pl.pallas_call(inner, out_shape=shapes, in_specs=[pl.BlockSpec(memory_spa...  20 us
    all_to_all x1, waiting for transfers between devices, local(): terms = lax.all_to_all(terms, 'wide', 0, 0, axis_index_groups=OWNERS)  19.4 us
    all_to_all x1, starting transfers between devices, local(): terms = lax.all_to_all(terms, 'wide', 0, 0, axis_index_groups=OWNERS)  18.3 us
    ppermute x4, starting transfers between devices, local(): core = [lax.ppermute(held, 'wide', OTHER_CORE) for held in near]  15.5 us
    all_to_all x1, starting transfers between devices, local(): pieces = lax.all_to_all(pieces, 'wide', 0, 0, axis_index_groups=OWNERS)  10.7 us
    ppermute x3, starting transfers between devices, local(): lax.ppermute(own, 'narrow', shift_x(-step))  10.7 us
    ppermute x3, starting transfers between devices, local(): lax.ppermute(outs[step], 'narrow', shift_x(step))  9.78 us
    unnamed x42, local copies, waits for them, and re-layouts  9.47 us
  transfers between devices with their start and end apart: 17, of which 7 were waited for; matrix products, arithmetic and copies ran while one was open for 0% of the time, Pallas kernels for 8%

profile of v13, /device:TPU:1, one launch (start us, length us, event | category | flops | bytes accessed | tf_op | source)
XLA Modules:
  0.0 154.6 jit_solution(11470038992880758725)
XLA Ops:
  1.4 4.6 %collective-permute-start = (bf16[192,128]{1,0:T(8,128)(2,1)S(1)}, bf16[192,128]{1,0:T(8,128)(2,1)S(1)}, u32[]{:S(2)}, u32[]{:S(2)}) collective-permute-start(bf16[192,128]{1,0:T(8,128)(2,1)S(1)} %pad_maximum_fusion), channel_id=1, source_target_pairs={{0,0},{1,8},{2,2},{3,10},{4,4},{5,12},{6,6},{7,14},{8,64},{9,72},{... | collective-permute-start | bytes 147464 | tf_op jit(solution)/shard_map/ppermute | solution.py:231
  6.6 2.4 %shard_map.119.refs_1_.refs_0_ = bf16[2,256,512]{2,1,0:T(8,128)(2,1)} custom-call(s32[1]{0:T(128)} %bitcast.where_ref, bf16[384,512]{1,0:T(8,128)(2,1)} %refs_0_.1, bf16[384,512]{1,0:T(8,128)(2,1)} %refs_1_.1, s32[1,256]{1,0:T(1,128)} %bitcast.6, s32[1,1]{1,0:T(1,128)} %bitcast.4.refs_3_, f32[1,256]{1,0:T(1,128)} %bitcast.8), custom_call_target="tpu_custom_call" | custom-call | flops 201326592 | bytes 788484 | tf_op jit(solution)/shard_map/pallas_call | solution.py:99
  9.1 6.2 %collective-permute-done = bf16[192,128]{1,0:T(8,128)(2,1)S(1)} collective-permute-done((bf16[192,128]{1,0:T(8,128)(2,1)S(1)}, bf16[192,128]{1,0:T(8,128)(2,1)S(1)}, u32[]{:S(2)}, u32[]{:S(2)}) %collective-permute-start) | collective-permute-done | bytes 49184 | tf_op jit(solution)/shard_map/ppermute | solution.py:231
  15.2 1.5 broadcast_in_dim.22
  16.8 10.7 %all-to-all-start = ((bf16[32,192,128]{2,1,0:T(8,128)(2,1)}), bf16[32,192,128]{2,1,0:T(8,128)(2,1)}, u32[]{:S(2)}, u32[]{:S(2)}) async-start(bf16[32,192,128]{2,1,0:T(8,128)(2,1)} %broadcast_in_dim.22), calls=%async_computation | async-start | bytes 3145728 | tf_op jit(solution)/shard_map/all_to_all | solution.py:241
  27.5 3.3 %collective-permute-start.6 = (bf16[2,256,512]{2,1,0:T(8,128)(2,1)S(1)}, bf16[2,256,512]{2,1,0:T(8,128)(2,1)S(1)}, u32[]{:S(2)}, u32[]{:S(2)}) collective-permute-start(bf16[2,256,512]{2,1,0:T(8,128)(2,1)S(1)} %copy-done), channel_id=1, source_target_pairs={{0,2},{1,3},{2,4},{3,5},{4,6},{5,7},{6,0},{7,1},{8,10},{9,11},{10,... | collective-permute-start | bytes 1572872 | tf_op jit(solution)/shard_map/ppermute | solution.py:242
  30.7 4.4 %collective-permute-start.4 = (bf16[2,256,512]{2,1,0:T(8,128)(2,1)S(1)}, bf16[2,256,512]{2,1,0:T(8,128)(2,1)S(1)}, u32[]{:S(2)}, u32[]{:S(2)}) collective-permute-start(bf16[2,256,512]{2,1,0:T(8,128)(2,1)S(1)} %copy-done), channel_id=1, source_target_pairs={{0,4},{1,5},{2,6},{3,7},{4,0},{5,1},{6,2},{7,3},{8,12},{9,13},{10,... | collective-permute-start | bytes 1572872 | tf_op jit(solution)/shard_map/ppermute | solution.py:242
  35.1 3.1 %collective-permute-start.2 = (bf16[2,256,512]{2,1,0:T(8,128)(2,1)S(1)}, bf16[2,256,512]{2,1,0:T(8,128)(2,1)S(1)}, u32[]{:S(2)}, u32[]{:S(2)}) collective-permute-start(bf16[2,256,512]{2,1,0:T(8,128)(2,1)S(1)} %copy-done), channel_id=1, source_target_pairs={{0,6},{1,7},{2,0},{3,1},{4,2},{5,3},{6,4},{7,5},{8,14},{9,15},{10,... | collective-permute-start | bytes 1572872 | tf_op jit(solution)/shard_map/ppermute | solution.py:242
  38.2 4.2 %collective-permute-start.1 = (bf16[2,256,512]{2,1,0:T(8,128)(2,1)S(1)}, bf16[2,256,512]{2,1,0:T(8,128)(2,1)S(1)}, u32[]{:S(2)}, u32[]{:S(2)}) collective-permute-start(bf16[2,256,512]{2,1,0:T(8,128)(2,1)S(1)} %copy-done), channel_id=1, source_target_pairs={{0,8},{8,0},{16,24},{24,16},{32,40},{40,32},{48,56},{56,48},{64,72... | collective-permute-start | bytes 1572872 | tf_op jit(solution)/shard_map/ppermute | solution.py:244
  42.8 5.2 %collective-permute-start.7 = (bf16[2,256,512]{2,1,0:T(8,128)(2,1)S(1)}, bf16[2,256,512]{2,1,0:T(8,128)(2,1)S(1)}, u32[]{:S(2)}, u32[]{:S(2)}) collective-permute-start(bf16[2,256,512]{2,1,0:T(8,128)(2,1)S(1)} %collective-permute-done.6.refs_7_.refs_3_), channel_id=1, source_target_pairs={{0,8},{8,0},{16,24},{24,16},{32,40},{40,32},{48,56},{56,48},{64,72... | collective-permute-start | bytes 1572872 | tf_op jit(solution)/shard_map/ppermute | solution.py:244
  47.9 7.0 %collective-permute-done.4.refs_5_.refs_2_ = bf16[2,256,512]{2,1,0:T(8,128)(2,1)S(1)} collective-permute-done((bf16[2,256,512]{2,1,0:T(8,128)(2,1)S(1)}, bf16[2,256,512]{2,1,0:T(8,128)(2,1)S(1)}, u32[]{:S(2)}, u32[]{:S(2)}) %collective-permute-start.4) | collective-permute-done | bytes 524320 | tf_op jit(solution)/shard_map/ppermute | solution.py:242
  55.0 4.2 %collective-permute-start.5 = (bf16[2,256,512]{2,1,0:T(8,128)(2,1)S(1)}, bf16[2,256,512]{2,1,0:T(8,128)(2,1)S(1)}, u32[]{:S(2)}, u32[]{:S(2)}) collective-permute-start(bf16[2,256,512]{2,1,0:T(8,128)(2,1)S(1)} %collective-permute-done.4.refs_5_.refs_2_), channel_id=1, source_target_pairs={{0,8},{8,0},{16,24},{24,16},{32,40},{40,32},{48,56},{56,48},{64,72... | collective-permute-start | bytes 1572872 | tf_op jit(solution)/shard_map/ppermute | solution.py:244
  59.2 1.9 %collective-permute-start.3 = (bf16[2,256,512]{2,1,0:T(8,128)(2,1)S(1)}, bf16[2,256,512]{2,1,0:T(8,128)(2,1)}, u32[]{:S(2)}, u32[]{:S(2)}) collective-permute-start(bf16[2,256,512]{2,1,0:T(8,128)(2,1)S(1)} %collective-permute-done.2.refs_3_.refs_1_), channel_id=1, source_target_pairs={{0,8},{8,0},{16,24},{24,16},{32,40},{40,32},{48,56},{56,48},{64,72... | collective-permute-start | bytes 1572872 | tf_op jit(solution)/shard_map/ppermute | solution.py:244
  63.1 1.1 all-to-all-done.refs_0_
  64.2 5.0 %shard_map.120 = (bf16[512,384]{1,0:T(8,128)(2,1)}, bf16[2048,384]{1,0:T(8,128)(2,1)}) custom-call(s32[1]{0:T(128)} %bitcast.where_ref, bf16[32,192,128]{2,1,0:T(8,128)(2,1)} %all-to-all-done.refs_0_, bf16[2,256,512]{2,1,0:T(8,128)(2,1)} %shard_map.119.refs_1_.refs_0_, bf16[2,256,512]{2,1,0:T(8,128)(2,1)} %copy-done.8, bf16[2,256,512]{2,1,0:T(8,128)(2,1)} %copy-done.6, ...), custom_call_target="tpu_custom_call" | custom-call | flops 805306368 | bytes 5767168 | tf_op jit(solution)/shard_map/pallas_call | solution.py:99
  69.2 1.9 %collective-permute-start.8 = (bf16[512,384]{1,0:T(8,128)(2,1)}, bf16[512,384]{1,0:T(8,128)(2,1)S(1)}, u32[]{:S(2)}, u32[]{:S(2)}) collective-permute-start(bf16[512,384]{1,0:T(8,128)(2,1)} %get-tuple-element.26.refs_0_), channel_id=1, source_target_pairs={{0,1},{1,0},{2,3},{3,2},{4,5},{5,4},{6,7},{7,6},{8,9},{9,8},{10,11... | collective-permute-start | bytes 1179656 | tf_op jit(solution)/shard_map/ppermute | solution.py:258
  71.1 6.1 %collective-permute-start.9 = (bf16[2048,384]{1,0:T(8,128)(2,1)}, bf16[2048,384]{1,0:T(8,128)(2,1)S(1)}, u32[]{:S(2)}, u32[]{:S(2)}) collective-permute-start(bf16[2048,384]{1,0:T(8,128)(2,1)} %get-tuple-element.27.refs_1_), channel_id=1, source_target_pairs={{0,8},{8,0},{16,24},{24,16},{32,40},{40,32},{48,56},{56,48},{64,72... | collective-permute-start | bytes 4718600 | tf_op jit(solution)/shard_map/ppermute | solution.py:259
  78.3 1.0 copy-done.5
  79.4 1.0 copy-done.7
  81.4 2.4 %shard_map.121 = (bf16[2,512,512]{2,1,0:T(8,128)(2,1)S(1)}, bf16[2,512,512]{2,1,0:T(8,128)(2,1)S(1)}, bf16[2,512,512]{2,1,0:T(8,128)(2,1)S(1)}, bf16[2,512,512]{2,1,0:T(8,128)(2,1)S(1)}) custom-call(s32[1]{0:T(128)} %bitcast.where_ref, bf16[2,256,512]{2,1,0:T(8,128)(2,1)S(1)} %copy-done.1, bf16[2,256,512]{2,1,0:T(8,128)(2,1)S(1)} %copy-done.7, ...), custom_call_target="tpu_custom_call" | custom-call | flops 20000000000 | bytes 4194304 | tf_op jit(solution)/shard_map/pallas_call | solution.py:99
  83.9 1.1 copy-done.16
  85.0 3.0 %shard_map.122 = (bf16[32,192,128]{2,1,0:T(8,128)(2,1)}, bf16[512,384]{1,0:T(8,128)(2,1)S(1)}, bf16[256,384]{1,0:T(8,128)(2,1)S(1)}) custom-call(s32[1]{0:T(128)} %bitcast.where_ref, bf16[512,384]{1,0:T(8,128)(2,1)S(1)} %copy-done.14, bf16[512,384]{1,0:T(8,128)(2,1)S(1)} %collective-permute-done.8.refs_1_, ...), custom_call_target="tpu_custom_call" | custom-call | flops 805306368 | bytes 4980736 | tf_op jit(solution)/shard_map/pallas_call | solution.py:99
  88.7 18.3 %all-to-all-start.1 = ((bf16[32,192,128]{2,1,0:T(8,128)(2,1)}), bf16[32,192,128]{2,1,0:T(8,128)(2,1)S(1)}, u32[]{:S(2)}, u32[]{:S(2)}) async-start(bf16[32,192,128]{2,1,0:T(8,128)(2,1)} %get-tuple-element.42), calls=%async_computation.1 | async-start | bytes 3145728 | tf_op jit(solution)/shard_map/all_to_all | solution.py:272
  107.1 2.7 %collective-permute-start.10 = (bf16[256,384]{1,0:T(8,128)(2,1)S(1)}, bf16[256,384]{1,0:T(8,128)(2,1)S(1)}, u32[]{:S(2)}, u32[]{:S(2)}) collective-permute-start(bf16[256,384]{1,0:T(8,128)(2,1)S(1)} %get-tuple-element.34), channel_id=1, source_target_pairs={{0,8},{8,0},{16,24},{24,16},{32,40},{40,32},{48,56},{56,48},{64,72... | collective-permute-start | bytes 589832 | tf_op jit(solution)/shard_map/ppermute | solution.py:276
  109.8 1.0 collective-permute-done.10.refs_2_
  111.5 4.3 %shard_map.123 = (bf16[2,256,512]{2,1,0:T(8,128)(2,1)}, bf16[2,256,512]{2,1,0:T(8,128)(2,1)}, bf16[2,256,512]{2,1,0:T(8,128)(2,1)}, bf16[2,256,512]{2,1,0:T(8,128)(2,1)}) custom-call(s32[1]{0:T(128)} %bitcast.where_ref, bf16[512,384]{1,0:T(8,128)(2,1)} %copy-done.15, bf16[2048,384]{1,0:T(8,128)(2,1)} %get-tuple-element.27.refs_1_, ...), custom_call_target="tpu_custom_call" | custom-call | flops 805306368 | bytes 3735552 | tf_op jit(solution)/shard_map/pallas_call | solution.py:99
  115.8 3.2 %collective-permute-start.11 = (bf16[2,256,512]{2,1,0:T(8,128)(2,1)}, bf16[2,256,512]{2,1,0:T(8,128)(2,1)S(1)}, u32[]{:S(2)}, u32[]{:S(2)}) collective-permute-start(bf16[2,256,512]{2,1,0:T(8,128)(2,1)} %get-tuple-element.37), channel_id=1, source_target_pairs={{0,2},{1,3},{2,4},{3,5},{4,6},{5,7},{6,0},{7,1},{8,10},{9,11},{10,... | collective-permute-start | bytes 1572872 | tf_op jit(solution)/shard_map/ppermute | solution.py:284
  119.1 3.3 %collective-permute-start.12 = (bf16[2,256,512]{2,1,0:T(8,128)(2,1)}, bf16[2,256,512]{2,1,0:T(8,128)(2,1)S(1)}, u32[]{:S(2)}, u32[]{:S(2)}) collective-permute-start(bf16[2,256,512]{2,1,0:T(8,128)(2,1)} %get-tuple-element.38), channel_id=1, source_target_pairs={{0,4},{1,5},{2,6},{3,7},{4,0},{5,1},{6,2},{7,3},{8,12},{9,13},{10,... | collective-permute-start | bytes 1572872 | tf_op jit(solution)/shard_map/ppermute | solution.py:284
  122.4 3.2 %collective-permute-start.13 = (bf16[2,256,512]{2,1,0:T(8,128)(2,1)}, bf16[2,256,512]{2,1,0:T(8,128)(2,1)S(1)}, u32[]{:S(2)}, u32[]{:S(2)}) collective-permute-start(bf16[2,256,512]{2,1,0:T(8,128)(2,1)} %get-tuple-element.39), channel_id=1, source_target_pairs={{0,6},{1,7},{2,0},{3,1},{4,2},{5,3},{6,4},{7,5},{8,14},{9,15},{10,... | collective-permute-start | bytes 1572872 | tf_op jit(solution)/shard_map/ppermute | solution.py:284
  125.7 19.4 %all-to-all-done.1 = bf16[32,192,128]{2,1,0:T(8,128)(2,1)S(1)} async-done(((bf16[32,192,128]{2,1,0:T(8,128)(2,1)}), bf16[32,192,128]{2,1,0:T(8,128)(2,1)S(1)}, u32[]{:S(2)}, u32[]{:S(2)}) %all-to-all-start.1) | async-done | bytes 1572896 | tf_op jit(solution)/shard_map/all_to_all | solution.py:272
  145.3 4.6 %collective-permute-start.14 = (bf16[192,128]{1,0:T(8,128)(2,1)S(1)}, bf16[192,128]{1,0:T(8,128)(2,1)S(1)}, u32[]{:S(2)}, u32[]{:S(2)}) collective-permute-start(bf16[192,128]{1,0:T(8,128)(2,1)S(1)} %reduce_sum.12), channel_id=1, source_target_pairs={{0,0},{8,1},{2,2},{10,3},{4,4},{12,5},{6,6},{14,7},{64,8},{72,9},{... | collective-permute-start | bytes 147464 | tf_op jit(solution)/shard_map/ppermute | solution.py:274
  151.0 2.9 %shard_map.124 = (bf16[384,512]{1,0:T(8,128)(2,1)}, bf16[384,512]{1,0:T(8,128)(2,1)}) custom-call(s32[1]{0:T(128)} %bitcast.where_ref, s32[1,256]{1,0:T(1,128)} %bitcast.7, s32[1,1]{1,0:T(1,128)} %bitcast.5.refs_1_, f32[1,256]{1,0:T(1,128)} %bitcast.9, bf16[2,256,512]{2,1,0:T(8,128)(2,1)} %get-tuple-element.36.refs_3_, bf16[2,256,512]{2,1,0:T(8,128)(2,1)} %copy-done.17, ...), custom_call_target="tpu_custom_call" | custom-call | flops 201326592 | bytes 2099204 | tf_op jit(solution)/shard_map/pallas_call | solution.py:99
  (54 shorter events, 8.6 us)
Async XLA Ops:
  1.4 13.8 %collective-permute-start = (bf16[192,128]{1,0:T(8,128)(2,1)S(1)}, bf16[192,128]{1,0:T(8,128)(2,1)S(1)}, u32[]{:S(2)}, u32[]{:S(2)}) collective-permute-start(bf16[192,128]{1,0:T(8,128)(2,1)S(1)} %pad_maximum_fusion), channel_id=1, source_target_pairs={{0,0},{1,8},{2,2},{3,10},{4,4},{5,12},{6,6},{7,14},{8,64},{9,72},{... | collective-permute-start | bytes 147464 | tf_op jit(solution)/shard_map/ppermute | solution.py:231
  16.8 10.7 %copy-start = (bf16[2,256,512]{2,1,0:T(8,128)(2,1)S(1)}, bf16[2,256,512]{2,1,0:T(8,128)(2,1)}, u32[]{:S(2)}) copy-start(bf16[2,256,512]{2,1,0:T(8,128)(2,1)} %shard_map.119.refs_1_.refs_0_) | copy-start | bytes 1572868
  16.8 47.4 %all-to-all-start = ((bf16[32,192,128]{2,1,0:T(8,128)(2,1)}), bf16[32,192,128]{2,1,0:T(8,128)(2,1)}, u32[]{:S(2)}, u32[]{:S(2)}) async-start(bf16[32,192,128]{2,1,0:T(8,128)(2,1)} %broadcast_in_dim.22), calls=%async_computation | async-start | bytes 3145728 | tf_op jit(solution)/shard_map/all_to_all | solution.py:241
  27.4 49.8 %copy-start.1 = (bf16[2,256,512]{2,1,0:T(8,128)(2,1)S(1)}, bf16[2,256,512]{2,1,0:T(8,128)(2,1)}, u32[]{:S(2)}) copy-start(bf16[2,256,512]{2,1,0:T(8,128)(2,1)} %shard_map.119.refs_1_.refs_0_) | copy-start | bytes 1572868
  27.5 15.3 %collective-permute-start.6 = (bf16[2,256,512]{2,1,0:T(8,128)(2,1)S(1)}, bf16[2,256,512]{2,1,0:T(8,128)(2,1)S(1)}, u32[]{:S(2)}, u32[]{:S(2)}) collective-permute-start(bf16[2,256,512]{2,1,0:T(8,128)(2,1)S(1)} %copy-done), channel_id=1, source_target_pairs={{0,2},{1,3},{2,4},{3,5},{4,6},{5,7},{6,0},{7,1},{8,10},{9,11},{10,... | collective-permute-start | bytes 1572872 | tf_op jit(solution)/shard_map/ppermute | solution.py:242
  30.7 24.3 %collective-permute-start.4 = (bf16[2,256,512]{2,1,0:T(8,128)(2,1)S(1)}, bf16[2,256,512]{2,1,0:T(8,128)(2,1)S(1)}, u32[]{:S(2)}, u32[]{:S(2)}) collective-permute-start(bf16[2,256,512]{2,1,0:T(8,128)(2,1)S(1)} %copy-done), channel_id=1, source_target_pairs={{0,4},{1,5},{2,6},{3,7},{4,0},{5,1},{6,2},{7,3},{8,12},{9,13},{10,... | collective-permute-start | bytes 1572872 | tf_op jit(solution)/shard_map/ppermute | solution.py:242
  35.1 24.1 %collective-permute-start.2 = (bf16[2,256,512]{2,1,0:T(8,128)(2,1)S(1)}, bf16[2,256,512]{2,1,0:T(8,128)(2,1)S(1)}, u32[]{:S(2)}, u32[]{:S(2)}) collective-permute-start(bf16[2,256,512]{2,1,0:T(8,128)(2,1)S(1)} %copy-done), channel_id=1, source_target_pairs={{0,6},{1,7},{2,0},{3,1},{4,2},{5,3},{6,4},{7,5},{8,14},{9,15},{10,... | collective-permute-start | bytes 1572872 | tf_op jit(solution)/shard_map/ppermute | solution.py:242
  38.2 23.0 %collective-permute-start.1 = (bf16[2,256,512]{2,1,0:T(8,128)(2,1)S(1)}, bf16[2,256,512]{2,1,0:T(8,128)(2,1)S(1)}, u32[]{:S(2)}, u32[]{:S(2)}) collective-permute-start(bf16[2,256,512]{2,1,0:T(8,128)(2,1)S(1)} %copy-done), channel_id=1, source_target_pairs={{0,8},{8,0},{16,24},{24,16},{32,40},{40,32},{48,56},{56,48},{64,72... | collective-permute-start | bytes 1572872 | tf_op jit(solution)/shard_map/ppermute | solution.py:244
  42.8 21.4 %copy-start.2 = (bf16[2,256,512]{2,1,0:T(8,128)(2,1)}, bf16[2,256,512]{2,1,0:T(8,128)(2,1)S(1)}, u32[]{:S(2)}) copy-start(bf16[2,256,512]{2,1,0:T(8,128)(2,1)S(1)} %collective-permute-done.6.refs_7_.refs_3_) | copy-start | bytes 1572868
  42.8 18.4 %collective-permute-start.7 = (bf16[2,256,512]{2,1,0:T(8,128)(2,1)S(1)}, bf16[2,256,512]{2,1,0:T(8,128)(2,1)S(1)}, u32[]{:S(2)}, u32[]{:S(2)}) collective-permute-start(bf16[2,256,512]{2,1,0:T(8,128)(2,1)S(1)} %collective-permute-done.6.refs_7_.refs_3_), channel_id=1, source_target_pairs={{0,8},{8,0},{16,24},{24,16},{32,40},{40,32},{48,56},{56,48},{64,72... | collective-permute-start | bytes 1572872 | tf_op jit(solution)/shard_map/ppermute | solution.py:244
  55.0 9.2 %copy-start.4 = (bf16[2,256,512]{2,1,0:T(8,128)(2,1)}, bf16[2,256,512]{2,1,0:T(8,128)(2,1)S(1)}, u32[]{:S(2)}) copy-start(bf16[2,256,512]{2,1,0:T(8,128)(2,1)S(1)} %collective-permute-done.4.refs_5_.refs_2_) | copy-start | bytes 1572868
  55.0 6.2 %collective-permute-start.5 = (bf16[2,256,512]{2,1,0:T(8,128)(2,1)S(1)}, bf16[2,256,512]{2,1,0:T(8,128)(2,1)S(1)}, u32[]{:S(2)}, u32[]{:S(2)}) collective-permute-start(bf16[2,256,512]{2,1,0:T(8,128)(2,1)S(1)} %collective-permute-done.4.refs_5_.refs_2_), channel_id=1, source_target_pairs={{0,8},{8,0},{16,24},{24,16},{32,40},{40,32},{48,56},{56,48},{64,72... | collective-permute-start | bytes 1572872 | tf_op jit(solution)/shard_map/ppermute | solution.py:244
  59.2 5.0 %copy-start.6 = (bf16[2,256,512]{2,1,0:T(8,128)(2,1)}, bf16[2,256,512]{2,1,0:T(8,128)(2,1)S(1)}, u32[]{:S(2)}) copy-start(bf16[2,256,512]{2,1,0:T(8,128)(2,1)S(1)} %collective-permute-done.2.refs_3_.refs_1_) | copy-start | bytes 1572868
  59.2 3.9 %collective-permute-start.3 = (bf16[2,256,512]{2,1,0:T(8,128)(2,1)S(1)}, bf16[2,256,512]{2,1,0:T(8,128)(2,1)}, u32[]{:S(2)}, u32[]{:S(2)}) collective-permute-start(bf16[2,256,512]{2,1,0:T(8,128)(2,1)S(1)} %collective-permute-done.2.refs_3_.refs_1_), channel_id=1, source_target_pairs={{0,8},{8,0},{16,24},{24,16},{32,40},{40,32},{48,56},{56,48},{64,72... | collective-permute-start | bytes 1572872 | tf_op jit(solution)/shard_map/ppermute | solution.py:244
  61.1 3.1 %copy-start.8 = (bf16[2,256,512]{2,1,0:T(8,128)(2,1)}, bf16[2,256,512]{2,1,0:T(8,128)(2,1)S(1)}, u32[]{:S(2)}) copy-start(bf16[2,256,512]{2,1,0:T(8,128)(2,1)S(1)} %collective-permute-done.1.refs_2_.refs_4_) | copy-start | bytes 1572868
  63.1 14.1 %copy-start.11 = (bf16[2,256,512]{2,1,0:T(8,128)(2,1)S(1)}, bf16[2,256,512]{2,1,0:T(8,128)(2,1)}, u32[]{:S(2)}) copy-start(bf16[2,256,512]{2,1,0:T(8,128)(2,1)} %copy-done.10) | copy-start | bytes 1572868
  64.2 13.1 %copy-start.13 = (bf16[2,256,512]{2,1,0:T(8,128)(2,1)S(1)}, bf16[2,256,512]{2,1,0:T(8,128)(2,1)}, u32[]{:S(2)}) copy-start(bf16[2,256,512]{2,1,0:T(8,128)(2,1)} %copy-done.12) | copy-start | bytes 1572868
  69.2 14.6 %collective-permute-start.8 = (bf16[512,384]{1,0:T(8,128)(2,1)}, bf16[512,384]{1,0:T(8,128)(2,1)S(1)}, u32[]{:S(2)}, u32[]{:S(2)}) collective-permute-start(bf16[512,384]{1,0:T(8,128)(2,1)} %get-tuple-element.26.refs_0_), channel_id=1, source_target_pairs={{0,1},{1,0},{2,3},{3,2},{4,5},{5,4},{6,7},{7,6},{8,9},{9,8},{10,11... | collective-permute-start | bytes 1179656 | tf_op jit(solution)/shard_map/ppermute | solution.py:258
  71.1 12.7 %collective-permute-start.9 = (bf16[2048,384]{1,0:T(8,128)(2,1)}, bf16[2048,384]{1,0:T(8,128)(2,1)S(1)}, u32[]{:S(2)}, u32[]{:S(2)}) collective-permute-start(bf16[2048,384]{1,0:T(8,128)(2,1)} %get-tuple-element.27.refs_1_), channel_id=1, source_target_pairs={{0,8},{8,0},{16,24},{24,16},{32,40},{40,32},{48,56},{56,48},{64,72... | collective-permute-start | bytes 4718600 | tf_op jit(solution)/shard_map/ppermute | solution.py:259
  77.3 1.0 copy-start.3
  78.3 1.0 copy-start.5
  79.3 1.0 copy-start.7
  80.4 1.0 copy-start.9
  81.4 3.6 %copy-start.14 = (bf16[512,384]{1,0:T(8,128)(2,1)S(1)}, bf16[512,384]{1,0:T(8,128)(2,1)}, u32[]{:S(2)}) copy-start(bf16[512,384]{1,0:T(8,128)(2,1)} %get-tuple-element.26.refs_0_) | copy-start | bytes 1179652
  83.8 1.1 copy-start.16
  88.7 56.3 %all-to-all-start.1 = ((bf16[32,192,128]{2,1,0:T(8,128)(2,1)}), bf16[32,192,128]{2,1,0:T(8,128)(2,1)S(1)}, u32[]{:S(2)}, u32[]{:S(2)}) async-start(bf16[32,192,128]{2,1,0:T(8,128)(2,1)} %get-tuple-element.42), calls=%async_computation.1 | async-start | bytes 3145728 | tf_op jit(solution)/shard_map/all_to_all | solution.py:272
  107.1 3.7 %collective-permute-start.10 = (bf16[256,384]{1,0:T(8,128)(2,1)S(1)}, bf16[256,384]{1,0:T(8,128)(2,1)S(1)}, u32[]{:S(2)}, u32[]{:S(2)}) collective-permute-start(bf16[256,384]{1,0:T(8,128)(2,1)S(1)} %get-tuple-element.34), channel_id=1, source_target_pairs={{0,8},{8,0},{16,24},{24,16},{32,40},{40,32},{48,56},{56,48},{64,72... | collective-permute-start | bytes 589832 | tf_op jit(solution)/shard_map/ppermute | solution.py:276
  115.8 34.0 %collective-permute-start.11 = (bf16[2,256,512]{2,1,0:T(8,128)(2,1)}, bf16[2,256,512]{2,1,0:T(8,128)(2,1)S(1)}, u32[]{:S(2)}, u32[]{:S(2)}) collective-permute-start(bf16[2,256,512]{2,1,0:T(8,128)(2,1)} %get-tuple-element.37), channel_id=1, source_target_pairs={{0,2},{1,3},{2,4},{3,5},{4,6},{5,7},{6,0},{7,1},{8,10},{9,11},{10,... | collective-permute-start | bytes 1572872 | tf_op jit(solution)/shard_map/ppermute | solution.py:284
  119.1 30.7 %collective-permute-start.12 = (bf16[2,256,512]{2,1,0:T(8,128)(2,1)}, bf16[2,256,512]{2,1,0:T(8,128)(2,1)S(1)}, u32[]{:S(2)}, u32[]{:S(2)}) collective-permute-start(bf16[2,256,512]{2,1,0:T(8,128)(2,1)} %get-tuple-element.38), channel_id=1, source_target_pairs={{0,4},{1,5},{2,6},{3,7},{4,0},{5,1},{6,2},{7,3},{8,12},{9,13},{10,... | collective-permute-start | bytes 1572872 | tf_op jit(solution)/shard_map/ppermute | solution.py:284
  122.4 27.4 %collective-permute-start.13 = (bf16[2,256,512]{2,1,0:T(8,128)(2,1)}, bf16[2,256,512]{2,1,0:T(8,128)(2,1)S(1)}, u32[]{:S(2)}, u32[]{:S(2)}) collective-permute-start(bf16[2,256,512]{2,1,0:T(8,128)(2,1)} %get-tuple-element.39), channel_id=1, source_target_pairs={{0,6},{1,7},{2,0},{3,1},{4,2},{5,3},{6,4},{7,5},{8,14},{9,15},{10,... | collective-permute-start | bytes 1572872 | tf_op jit(solution)/shard_map/ppermute | solution.py:284
  145.3 8.6 %collective-permute-start.14 = (bf16[192,128]{1,0:T(8,128)(2,1)S(1)}, bf16[192,128]{1,0:T(8,128)(2,1)S(1)}, u32[]{:S(2)}, u32[]{:S(2)}) collective-permute-start(bf16[192,128]{1,0:T(8,128)(2,1)S(1)} %reduce_sum.12), channel_id=1, source_target_pairs={{0,0},{8,1},{2,2},{10,3},{4,4},{12,5},{6,6},{14,7},{64,8},{72,9},{... | collective-permute-start | bytes 147464 | tf_op jit(solution)/shard_map/ppermute | solution.py:274
  149.9 1.1 copy-start.19
  (6 other events, 4.8 us)
